TPU v7x, 32 devices: a whole 2x2x4 slice. The times are simulated.
32 devices in a mesh: seq: 4 (over y, x), fsdp: 8 (over z, core).
Axes of the slice: x: 2, y: 2, z: 4, core: 2. Of those that a mesh axis runs over, the one named last changes fastest.
Arguments:
- tokens: bfloat16 [8, 1024, 2048], P('fsdp', 'seq'), may hold values from -6 to 6
- segment_ids: int32 [8, 1024], P('fsdp'), may hold values from 0 to 6, as said below
- input_gain: float32 [2048], replicated, may hold values from 0.5 to 1.5
- query_weight: bfloat16 [2048, 2048], P('fsdp'), may hold values from -0.125 to 0.125
- key_projection_weight: bfloat16 [2048, 1024], P('fsdp'), may hold values from -0.125 to 0.125
- value_projection_weight: bfloat16 [2048, 1024], P('fsdp'), may hold values from -0.125 to 0.125
- output_weight: bfloat16 [2048, 2048], P('fsdp'), may hold values from -2 to 2
- query_gain: float32 [128], replicated, may hold values from 0.25 to 1.75
- key_gain: float32 [128], replicated, may hold values from 0.25 to 1.75
- post_gain: float32 [2048], replicated, may hold values from 0.5 to 1.5
- gate_weight: bfloat16 [2048, 6144], P('fsdp'), may hold values from -0.125 to 0.125
- up_weight: bfloat16 [2048, 6144], P('fsdp'), may hold values from -0.125 to 0.125
- down_weight: bfloat16 [2048, 6144], P('fsdp'), may hold values from -0.078125 to 0.078125
- cotangent: bfloat16 [8, 1024, 2048], P('fsdp', 'seq'), may hold values from -6 to 6
Outputs:
- output: bfloat16 [8, 1024, 2048], P('fsdp', 'seq')
- input_grad: bfloat16 [8, 1024, 2048], P('fsdp', 'seq')
- input_gain_grad: float32 [2048], replicated
- query_weight_grad: float32 [2048, 2048], P('fsdp')
- key_weight_grad: float32 [2048, 1024], P('fsdp')
- value_weight_grad: float32 [2048, 1024], P('fsdp')
- output_weight_grad: float32 [2048, 2048], P('fsdp')
- query_gain_grad: float32 [128], replicated
- key_gain_grad: float32 [128], replicated
- post_gain_grad: float32 [2048], replicated
- gate_weight_grad: float32 [2048, 6144], P('fsdp')
- up_weight_grad: float32 [2048, 6144], P('fsdp')
- down_weight_grad: float32 [2048, 6144], P('fsdp')
Inputs may be any that keep to these rules, and one draw needn't show every extreme that they name: `segment_ids`: along each sequence the ids start at 0, never fall, and rise by one from one document to the next; documents after a sequence's first hold 200 to 2000 tokens, except the last, which the sequence's end may cut short; the first holds at most 2000. In one sequence of the batch, which one drawn from the seed, every id is 0; in another, documents after the first (the last aside) hold exactly 200 tokens and the largest id is reached.
All inputs are finite; a program needn't handle non-finite values.
Results may differ from a plain program's by a relative error of at most 0.02.
Values may be sent and summed in bfloat16 or wider, within the bound.
No kernel may reach another device: no remote copies, remote signals or barrier semaphores. Data moves between devices by JAX's collectives and lax.ppermute only.
A program may use at most 640 MiB of HBM per device.

v0:
```python
import jax
import jax.numpy as jnp
from jax import lax
from jax.sharding import PartitionSpec as P

QUERY_HEADS = 16
KEY_VALUE_HEADS = 8
HEAD_SIZE = 128
FF = 6144


NORM_EPSILON = 1e-06
ROPE_BASE = 1000000.0
SCORE_FLOOR = -1e30


def apply_norm(values_in, gain):
    return (
        values_in
        * lax.rsqrt(jnp.mean(values_in * values_in, axis=-1, keepdims=True) + NORM_EPSILON)
        * gain
    )


def positions(segments):
    index = jnp.arange(segments.shape[0], dtype=jnp.int32)
    first = jnp.concatenate([jnp.ones((1,), dtype=jnp.bool_), segments[1:] != segments[:-1]])
    starts = lax.cummax(jnp.where(first, index, jnp.zeros_like(index)), axis=0)
    return index - starts


def apply_rotary(values_in, position_index):
    size = values_in.shape[-1]
    half = size // 2
    freq = ROPE_BASE ** (-jnp.arange(half, dtype=jnp.float32) * 2.0 / size)
    angle = position_index.astype(jnp.float32)[:, None] * freq[None, :]
    shape = (values_in.shape[0],) + (1,) * (values_in.ndim - 2) + (size,)
    cosine = jnp.concatenate([jnp.cos(angle), jnp.cos(angle)], axis=-1).reshape(shape)
    sine = jnp.concatenate([jnp.sin(angle), jnp.sin(angle)], axis=-1).reshape(shape)
    turned = jnp.concatenate([-values_in[..., half:], values_in[..., :half]], axis=-1)
    return values_in * cosine + turned * sine


def norm_heads(query_heads, key_heads, query_gain_local, key_g, position_index):
    return (
        apply_rotary(apply_norm(query_heads, query_gain_local), position_index),
        apply_rotary(apply_norm(key_heads, key_g), position_index),
    )


def attention_weights(query_weight, key_projection_weight, value_projection_weight, output_weight):
    return (
        lax.all_gather(query_weight, "fsdp", axis=0, tiled=True),
        lax.all_gather(key_projection_weight, "fsdp", axis=0, tiled=True),
        lax.all_gather(value_projection_weight, "fsdp", axis=0, tiled=True),
        lax.all_gather(output_weight, "fsdp", axis=0, tiled=True),
    )


def mlp_weights(gate_weight, up_weight, down_weight):
    return (
        lax.all_gather(gate_weight, "fsdp", axis=0, tiled=True),
        lax.all_gather(up_weight, "fsdp", axis=0, tiled=True),
        lax.all_gather(down_weight, "fsdp", axis=0, tiled=True),
    )


def block_mask(segments, start, block):
    length_total = segments.shape[0]
    index = jnp.arange(length_total, dtype=jnp.int32)
    rows_now = start + jnp.arange(block, dtype=jnp.int32)
    seg_rows = lax.dynamic_slice_in_dim(segments, start, block, 0)
    return (seg_rows[:, None] == segments[None, :]) & (index[None, :] <= rows_now[:, None])


def attend(rotated_query, key_rot, value_rows, segments):
    length_total = rotated_query.shape[0]
    block = min(512, length_total)
    count = length_total // block
    scale = HEAD_SIZE ** (-0.5)

    def one_block(block_index):
        start = block_index * block
        query_block = lax.dynamic_slice_in_dim(rotated_query, start, block, 0)
        scores = (
            jnp.einsum("qgrd,kgd->grqk", query_block, key_rot, preferred_element_type=jnp.float32)
            * scale
        )
        scores = jnp.where(block_mask(segments, start, block), scores, SCORE_FLOOR)
        highest = jnp.max(scores, axis=-1, keepdims=True)
        weights = jnp.exp(scores - highest)
        total = jnp.sum(weights, axis=-1, keepdims=True)
        probs = (weights / total).astype(jnp.bfloat16)
        result = jnp.einsum("grqk,kgd->qgrd", probs, value_rows, preferred_element_type=jnp.float32)
        return (result.astype(jnp.bfloat16), (highest + jnp.log(total))[..., 0])

    results, lse = lax.map(one_block, jnp.arange(count, dtype=jnp.int32))
    return (results.reshape((length_total,) + results.shape[2:]), lse)


def attend_back(rotated_query, key_rot, value_rows, segments, lse, d_result):
    length_total = rotated_query.shape[0]
    block = min(512, length_total)
    count = length_total // block
    scale = HEAD_SIZE ** (-0.5)

    def one_block(carry, item):
        key_rows_gradient, value_rows_gradient = carry
        block_index, lse_block = item
        start = block_index * block
        query_block = lax.dynamic_slice_in_dim(rotated_query, start, block, 0)
        d_block = lax.dynamic_slice_in_dim(d_result, start, block, 0)
        scores = (
            jnp.einsum("qgrd,kgd->grqk", query_block, key_rot, preferred_element_type=jnp.float32)
            * scale
        )
        scores = jnp.where(block_mask(segments, start, block), scores, SCORE_FLOOR)
        probs = jnp.exp(scores - lse_block[..., None])
        d_probs = jnp.einsum(
            "qgrd,kgd->grqk", d_block, value_rows, preferred_element_type=jnp.float32
        )
        delta = jnp.sum(probs * d_probs, axis=-1, keepdims=True)
        d_scores = (probs * (d_probs - delta) * scale).astype(jnp.bfloat16)
        d_query = jnp.einsum(
            "grqk,kgd->qgrd", d_scores, key_rot, preferred_element_type=jnp.float32
        )
        key_rows_gradient = key_rows_gradient + jnp.einsum(
            "grqk,qgrd->kgd", d_scores, query_block, preferred_element_type=jnp.float32
        )
        value_rows_gradient = value_rows_gradient + jnp.einsum(
            "grqk,qgrd->kgd",
            probs.astype(jnp.bfloat16),
            d_block,
            preferred_element_type=jnp.float32,
        )
        return ((key_rows_gradient, value_rows_gradient), d_query)

    zeros = jnp.zeros(key_rot.shape, jnp.float32)
    (key_rows_gradient, value_rows_gradient), d_queries = lax.scan(
        one_block, (zeros, zeros), (jnp.arange(count, dtype=jnp.int32), lse)
    )
    return (
        d_queries.reshape((length_total,) + d_queries.shape[2:]),
        key_rows_gradient,
        value_rows_gradient,
    )


def row_terms(lefts, rights):
    parts = [
        jnp.einsum("cd,cf->df", left, right, preferred_element_type=jnp.float32)
        for left, right in zip(lefts, rights)
    ]
    return jnp.concatenate(parts, axis=1)


def reduce_rows(lefts, rights):
    share = lax.psum_scatter(
        row_terms(lefts, rights).astype(jnp.bfloat16), "fsdp", scatter_dimension=0, tiled=True
    )
    result = lax.psum(share, "seq").astype(jnp.float32)
    return result


def body(
    tokens,
    segment_ids,
    input_gain,
    query_weight,
    key_projection_weight,
    value_projection_weight,
    output_weight,
    query_gain,
    key_gain,
    post_gain,
    gate_weight,
    up_weight,
    down_weight,
    cotangent,
):
    stretch_factor = tokens.shape[1]
    paired_halves = QUERY_HEADS // KEY_VALUE_HEADS
    inputs = tokens[0].astype(jnp.float32)
    segments = segment_ids[0]
    position_index = positions(segments)
    normalized_input, norm_one_back = jax.vjp(apply_norm, inputs, input_gain)
    normed_low = normalized_input.astype(jnp.bfloat16)
    full_query, full_key, full_value, full_output = attention_weights(
        query_weight, key_projection_weight, value_projection_weight, output_weight
    )
    query_rows = jnp.dot(normed_low, full_query, preferred_element_type=jnp.float32).astype(
        jnp.bfloat16
    )
    key_rows = jnp.dot(normed_low, full_key, preferred_element_type=jnp.float32).astype(
        jnp.bfloat16
    )
    value_rows = jnp.dot(normed_low, full_value, preferred_element_type=jnp.float32).astype(
        jnp.bfloat16
    )
    packed = jnp.concatenate(
        [
            query_rows.reshape(stretch_factor, KEY_VALUE_HEADS, paired_halves, HEAD_SIZE),
            key_rows.reshape(stretch_factor, KEY_VALUE_HEADS, 1, HEAD_SIZE),
            value_rows.reshape(stretch_factor, KEY_VALUE_HEADS, 1, HEAD_SIZE),
        ],
        axis=2,
    )
    heads = lax.all_to_all(packed, "seq", split_axis=1, concat_axis=0, tiled=True)
    query_heads = heads[:, :, :paired_halves].astype(jnp.float32)
    key_heads = heads[:, :, paired_halves].astype(jnp.float32)
    value_heads = heads[:, :, paired_halves + 1]
    (query_normed, key_normed), rope_back = jax.vjp(
        lambda first, second, third, fourth: norm_heads(
            first, second, third, fourth, position_index
        ),
        query_heads,
        key_heads,
        query_gain,
        key_gain,
    )
    rotated_query = query_normed.astype(jnp.bfloat16)
    key_rot = key_normed.astype(jnp.bfloat16)
    attended, lse = attend(rotated_query, key_rot, value_heads, segments)
    merged = lax.all_to_all(attended, "seq", split_axis=0, concat_axis=1, tiled=True).reshape(
        stretch_factor, QUERY_HEADS * HEAD_SIZE
    )
    residual = inputs + jnp.einsum(
        "ce,de->cd", merged, full_output, preferred_element_type=jnp.float32
    )
    normed_two, norm_two_back = jax.vjp(apply_norm, residual, post_gain)
    normed_two_low = normed_two.astype(jnp.bfloat16)
    full_gate, full_up, full_down = mlp_weights(gate_weight, up_weight, down_weight)
    gate = jnp.dot(normed_two_low, full_gate, preferred_element_type=jnp.float32)
    upper = jnp.dot(normed_two_low, full_up, preferred_element_type=jnp.float32)
    hidden, act_back = jax.vjp(lambda first, second: jax.nn.silu(first) * second, gate, upper)
    hidden_low = hidden.astype(jnp.bfloat16)
    output = residual + jnp.einsum(
        "cf,df->cd", hidden_low, full_down, preferred_element_type=jnp.float32
    )
    d_output = cotangent[0]
    d_hidden = jnp.einsum("cd,df->cf", d_output, full_down, preferred_element_type=jnp.float32)
    d_gate, d_upper = act_back(d_hidden)
    d_gate_low = d_gate.astype(jnp.bfloat16)
    d_upper_low = d_upper.astype(jnp.bfloat16)
    d_normed_two = jnp.einsum(
        "cf,df->cd", d_gate_low, full_gate, preferred_element_type=jnp.float32
    ) + jnp.einsum("cf,df->cd", d_upper_low, full_up, preferred_element_type=jnp.float32)
    mlp_share = reduce_rows(
        (normed_two_low, d_output), (jnp.concatenate([d_gate_low, d_upper_low], axis=1), hidden_low)
    )
    d_resid_norm, d_post = norm_two_back(d_normed_two)
    d_residual = d_output.astype(jnp.float32) + d_resid_norm
    d_residual_low = d_residual.astype(jnp.bfloat16)
    full_query, full_key, full_value, full_output = attention_weights(
        query_weight, key_projection_weight, value_projection_weight, output_weight
    )
    attended_gradient = jnp.einsum(
        "cd,de->ce", d_residual_low, full_output, preferred_element_type=jnp.float32
    )
    attended_gradient = attended_gradient.astype(jnp.bfloat16).reshape(
        stretch_factor, KEY_VALUE_HEADS, paired_halves, HEAD_SIZE
    )
    d_heads = lax.all_to_all(attended_gradient, "seq", split_axis=1, concat_axis=0, tiled=True)
    d_query_rot, d_key_rot, d_value_heads = attend_back(
        rotated_query, key_rot, value_heads, segments, lse, d_heads
    )
    d_query_heads, d_key_heads, d_query_gain, d_key_gain = rope_back((d_query_rot, d_key_rot))
    d_packed = jnp.concatenate(
        [
            d_query_heads.astype(jnp.bfloat16),
            d_key_heads.astype(jnp.bfloat16)[:, :, None],
            d_value_heads.astype(jnp.bfloat16)[:, :, None],
        ],
        axis=2,
    )
    gradient_returned = lax.all_to_all(d_packed, "seq", split_axis=0, concat_axis=1, tiled=True)
    d_queries = gradient_returned[:, :, :paired_halves].reshape(
        stretch_factor, QUERY_HEADS * HEAD_SIZE
    )
    key_rows_gradient = gradient_returned[:, :, paired_halves].reshape(
        stretch_factor, KEY_VALUE_HEADS * HEAD_SIZE
    )
    value_rows_gradient = gradient_returned[:, :, paired_halves + 1].reshape(
        stretch_factor, KEY_VALUE_HEADS * HEAD_SIZE
    )
    d_normed = (
        jnp.einsum("ce,de->cd", d_queries, full_query, preferred_element_type=jnp.float32)
        + jnp.einsum("ce,de->cd", key_rows_gradient, full_key, preferred_element_type=jnp.float32)
        + jnp.einsum(
            "ce,de->cd", value_rows_gradient, full_value, preferred_element_type=jnp.float32
        )
    )
    attn_share = reduce_rows(
        (normed_low, d_residual_low),
        (jnp.concatenate([d_queries, key_rows_gradient, value_rows_gradient], axis=1), merged),
    )
    d_input_norm, d_input_gain = norm_one_back(d_normed)
    d_inputs = d_residual + d_input_norm
    gain_grads = lax.psum((d_input_gain, d_query_gain, d_key_gain, d_post), ("seq", "fsdp"))
    query_cols = QUERY_HEADS * HEAD_SIZE
    key_columns_split = KEY_VALUE_HEADS * HEAD_SIZE
    return (
        output.astype(jnp.bfloat16)[None],
        d_inputs.astype(jnp.bfloat16)[None],
        gain_grads[0],
        attn_share[:, :query_cols],
        attn_share[:, query_cols : query_cols + key_columns_split],
        attn_share[:, query_cols + key_columns_split : query_cols + 2 * key_columns_split],
        attn_share[:, query_cols + 2 * key_columns_split :],
        gain_grads[1],
        gain_grads[2],
        gain_grads[3],
        mlp_share[:, :FF],
        mlp_share[:, FF : 2 * FF],
        mlp_share[:, 2 * FF :],
    )


def solution(mesh):
    return jax.shard_map(
        body,
        mesh=mesh,
        in_specs=(
            P("fsdp", "seq", None),
            P("fsdp", None),
            P(),
            P("fsdp", None),
            P("fsdp", None),
            P("fsdp", None),
            P("fsdp", None),
            P(),
            P(),
            P(),
            P("fsdp", None),
            P("fsdp", None),
            P("fsdp", None),
            P("fsdp", "seq", None),
        ),
        out_specs=(
            P("fsdp", "seq", None),
            P("fsdp", "seq", None),
            P(),
            P("fsdp", None),
            P("fsdp", None),
            P("fsdp", None),
            P("fsdp", None),
            P(),
            P(),
            P(),
            P("fsdp", None),
            P("fsdp", None),
            P("fsdp", None),
        ),
        check_vma=False,
    )
```

profile of v0, /device:TPU:0, one launch (start us, length us, event | category | flops | bytes accessed | tf_op | source)
XLA Modules:
  0.0 2448.4 jit_solution(3762199663870759799)
XLA Ops:
  12.2 47.3 %all-gather.10.cloned.1.call-done = bf16[2048,1024]{1,0:T(8,128)(2,1)} async-done(((bf16[256,1024]{1,0:T(8,128)(2,1)}), bf16[2048,1024]{1,0:T(8,128)(2,1)}) %all-gather.10.cloned.1.call-update) | async-done | bytes 4194320 | tf_op jit(solution)/shard_map/all_gather | solution.py:54
  59.5 3.5 fusion.97
  63.9 43.1 %all-gather.12.cloned.1.call-done = bf16[2048,1024]{1,0:T(8,128)(2,1)} async-done(((bf16[256,1024]{1,0:T(8,128)(2,1)}), bf16[2048,1024]{1,0:T(8,128)(2,1)}) %all-gather.12.cloned.1.call-update) | async-done | bytes 4194320 | tf_op jit(solution)/shard_map/all_gather | solution.py:55
  107.0 3.5 fusion.98
  111.4 78.0 %all-gather.8.cloned.1.call-done = bf16[2048,2048]{1,0:T(8,128)(2,1)} async-done(((bf16[256,2048]{1,0:T(8,128)(2,1)}), bf16[2048,2048]{1,0:T(8,128)(2,1)}) %all-gather.8.cloned.1.call-update) | async-done | bytes 8388624 | tf_op jit(solution)/shard_map/all_gather | solution.py:53
  189.4 6.7 convolution_convert_fusion.4
  196.1 2.6 reshape.221
  198.8 5.6 pad_maximum_fusion.2
  204.4 4.8 all-to-all-start
  212.2 22.6 all-to-all-done
  243.4 24.0 while.27
  245.3 2.9 bitcast_reduce_fusion.2
  250.7 3.5 fusion.190
  257.1 2.9 bitcast_reduce_fusion.2
  262.4 3.5 fusion.190
  269.7 16.5 all_to_all.69
  287.6 6.4 multiply_reduce_fusion.2
  295.5 195.9 %all-gather.18.cloned.1.call-done = bf16[2048,6144]{1,0:T(8,128)(2,1)} async-done(((bf16[256,6144]{1,0:T(8,128)(2,1)}), bf16[2048,6144]{1,0:T(8,128)(2,1)}) %all-gather.18.cloned.1.call-update) | async-done | bytes 25165840 | tf_op jit(solution)/shard_map/all_gather | solution.py:63
  491.4 15.9 fusion.131
  507.3 203.7 %all-gather.16.cloned.1.call-done = bf16[2048,6144]{1,0:T(8,128)(2,1)} async-done(((bf16[256,6144]{1,0:T(8,128)(2,1)}), bf16[2048,6144]{1,0:T(8,128)(2,1)}) %all-gather.16.cloned.1.call-update) | async-done | bytes 25165840 | tf_op jit(solution)/shard_map/all_gather | solution.py:62
  711.0 16.0 fusion.130
  727.0 203.7 %all-gather.20.cloned.1.call-done = bf16[2048,6144]{1,0:T(8,128)(2,1)} async-done(((bf16[256,6144]{1,0:T(8,128)(2,1)}), bf16[2048,6144]{1,0:T(8,128)(2,1)}) %all-gather.20.cloned.1.call-update) | async-done | bytes 25165840 | tf_op jit(solution)/shard_map/all_gather | solution.py:64
  930.7 23.4 multiply_convert_fusion
  954.1 13.6 fusion.132
  967.7 14.8 multiply_reduce_fusion
  982.5 3.1 fusion.78
  985.6 7.4 convolution_convert_fusion.3
  993.1 2.6 reshape.227
  995.6 2.9 copy.112
  998.5 4.2 all-to-all-start.2
  1002.8 14.4 all-to-all-done.2
  1019.6 118.4 %while.28 = (s32[]{:T(128)}, f32[1024,2,128]{0,2,1:T(8,128)}, f32[1024,2,128]{0,2,1:T(8,128)}, f32[2,512,2,2,128]{4,1,0,3,2:T(8,128)}, s32[2]{0:T(128)S(1)}, /*i...) while((s32[]{:T(128)}, f32[1024,2,128]{0,2,1:T(8,128)}, ...), condition=%wide.region_13.14_spmd.clone, body=%wide.region_11.13_spmd.clone.sunk | while | flops 2741508608 | bytes 152639888 | solution.py:139
  1021.9 2.5 fusion.200
  1024.5 2.6 fusion.203
  1028.7 4.5 fusion.199
  1033.2 23.8 fusion.202
  1057.1 21.9 fusion.204
  1080.9 2.5 fusion.200
  1083.4 2.6 fusion.203
  1087.6 4.5 fusion.199
  1092.2 23.9 fusion.202
  1116.0 21.9 fusion.204
  1138.0 2.6 copy.115
  1146.6 2.6 fusion.77
  1151.6 2.9 copy.118
  1154.6 4.6 all-to-all-start.3
  1159.3 5.6 convolution_convert_fusion.2
  1164.9 19.1 all-to-all-done.3
  1191.7 10.0 convolution_convert_fusion.1
  1201.6 17.0 pad_maximum_fusion.1
  1219.9 13.8 convert_bitcast_fusion
  1233.7 22.3 convolution_convert_fusion
  1256.0 50.4 %pad_maximum_fusion = bf16[2048,18432]{1,0:T(8,128)(2,1)} fusion(bf16[2048,6144]{1,0:T(8,128)(2,1)} %convert_bitcast_fusion, bf16[2048,12288]{1,0:T(8,128)(2,1)} %convolution_convert_fusion), kind=kLoop, calls=%fused_computation.66 | loop fusion | flops 150994944 | bytes 150994944 | tf_op jit(solution)/shard_map/concatenate | solution.py:154
  1306.4 157.0 %reduce-scatter.3.cloned.1.call-done = bf16[256,6144]{1,0:T(8,128)(2,1)} async-done(((bf16[2048,6144]{1,0:T(8,128)(2,1)}), bf16[256,6144]{1,0:T(8,128)(2,1)}) %reduce-scatter.3.cloned.1.call-update) | async-done | bytes 3145744 | tf_op jit(solution)/shard_map/reduce_scatter | solution.py:158
  1463.4 719.6 %reduce-scatter.5.cloned.1.call-done = bf16[256,18432]{1,0:T(8,128)(2,1)} async-done(((bf16[2048,18432]{1,0:T(8,128)(2,1)}), bf16[256,18432]{1,0:T(8,128)(2,1)}) %reduce-scatter.5.cloned.1.call-update) | async-done | bytes 9437200 | tf_op jit(solution)/shard_map/reduce_scatter | solution.py:158
  2184.6 14.8 fusion.74
  2199.4 6.2 fusion.133
  2208.3 2.9 fusion.76
  2211.3 39.1 %all-reduce.4 = (f32[2048]{0:T(1024)}, f32[128]{0:T(128)}, f32[128]{0:T(128)}, f32[2048]{0:T(1024)}) all-reduce(f32[2048]{0:T(1024)S(1)} %get-tuple-element.196, f32[128]{0:T(128)S(1)} %copy-done.58, f32[128]{0:T(128)S(1)} %copy-done.57, f32[2048]{0:T(1024)S(1)} %copy-done.54), channel_id=1, replica_groups=mesh['seq'=4,'fsdp'=8] {'seq','fsdp'}, use_global_device_ids=true, to_apply=%region_18.19 | all-reduce | flops 4352 | bytes 34816 | tf_op jit(solution)/shard_map/psum | solution.py:299
  2250.3 3.3 fusion.103
  2253.6 173.4 %all-reduce.8.cloned.1.call-done = (bf16[256,6144]{1,0:T(8,128)(2,1)}, bf16[256,18432]{1,0:T(8,128)(2,1)}) async-done(((bf16[256,6144]{1,0:T(8,128)(2,1)}, bf16[256,18432]{1,0:T(8,128)(2,1)}), (bf16[256,6144]{1,0:T(8,128)(2,1)}, bf16[256,18432]{1,0:T(8,128)(2,1)})) %all-reduce.8.cloned.1.call-update) | async-done | bytes 12582928 | tf_op jit(solution)/shard_map/psum | solution.py:161
  2427.0 2.9 fusion.126
  2430.0 2.7 fusion.125
  2434.3 6.9 fusion.124
  (237 shorter events, 64.0 us)
Async XLA Ops:
  7.2 52.3 %all-gather.10.cloned.1.call-start = ((), (), s32[]{:S(2)}) async-start(), calls=%async_computation.7 | async-start | bytes 4718592 | tf_op jit(solution)/shard_map/all_gather | solution.py:54
  7.9 99.1 %all-gather.12.cloned.1.call-start = ((), (), s32[]{:S(2)}) async-start(), calls=%async_computation.8 | async-start | bytes 4718592 | tf_op jit(solution)/shard_map/all_gather | solution.py:55
  8.7 180.7 %all-gather.8.cloned.1.call-start = ((), (), s32[]{:S(2)}) async-start(), calls=%async_computation.6 | async-start | bytes 9437184 | tf_op jit(solution)/shard_map/all_gather | solution.py:53
  9.4 278.2 %all-gather.14.cloned.1.call-start = ((), (), s32[]{:S(2)}) async-start(), calls=%async_computation.9 | async-start | bytes 9437184 | tf_op jit(solution)/shard_map/all_gather | solution.py:56
  10.0 481.4 %all-gather.18.cloned.1.call-start = ((), (), s32[]{:S(2)}) async-start(), calls=%async_computation.11 | async-start | bytes 28311552 | tf_op jit(solution)/shard_map/all_gather | solution.py:63
  10.6 48.9 %copy-start.39 = (f32[2048]{0:T(1024)S(1)}, f32[2048]{0:T(1024)}, u32[]{:S(2)}) copy-start(f32[2048]{0:T(1024)} %param.20) | copy-start | bytes 24580
  10.6 700.4 %all-gather.16.cloned.1.call-start = ((), (), s32[]{:S(2)}) async-start(), calls=%async_computation.10 | async-start | bytes 28311552 | tf_op jit(solution)/shard_map/all_gather | solution.py:62
  11.2 919.6 %all-gather.20.cloned.1.call-start = ((), (), s32[]{:S(2)}) async-start(), calls=%async_computation.12 | async-start | bytes 28311552 | tf_op jit(solution)/shard_map/all_gather | solution.py:64
  12.2 50.8 %copy-start.50 = (f32[256]{0:T(256)}, f32[256]{0:T(256)S(1)}, u32[]{:S(2)}) copy-start(f32[256]{0:T(256)S(1)} %fusion.84) | copy-start | bytes 3076
  12.2 177.2 %copy-start.45 = (f32[256]{0:T(256)}, f32[256]{0:T(256)S(1)}, u32[]{:S(2)}) copy-start(f32[256]{0:T(256)S(1)} %fusion.115) | copy-start | bytes 3076
  204.3 4.9 copy-start.32
  204.4 30.5 %all-to-all-start = ((bf16[256,8,4,128]{3,2,0,1:T(4,128)(2,1)}), bf16[256,8,4,128]{3,2,0,1:T(4,128)(2,1)}, u32[]{:S(2)}, u32[]{:S(2)}) async-start(bf16[256,8,4,128]{3,2,0,1:T(4,128)(2,1)} %pad_maximum_fusion.2), calls=%async_computation | async-start | bytes 4194304 | tf_op jit(solution)/shard_map/all_to_all | solution.py:208
  212.2 29.1 %copy-start.9 = (f32[1024,128]{1,0:T(8,128)}, f32[1024,128]{1,0:T(8,128)S(1)}, u32[]{:S(2)}) copy-start(f32[1024,128]{1,0:T(8,128)S(1)} %get-tuple-element.276) | copy-start | bytes 1572868
  212.2 29.1 %copy-start.11 = (f32[1024,128]{1,0:T(8,128)}, f32[1024,128]{1,0:T(8,128)S(1)}, u32[]{:S(2)}) copy-start(f32[1024,128]{1,0:T(8,128)S(1)} %get-tuple-element.277) | copy-start | bytes 1572868
  234.8 3.8 copy-start.52
  236.9 4.4 copy-start.1
  237.3 4.0 copy-start.47
  238.5 2.8 copy-start.37
  248.2 2.5 copy-start.35
  259.9 2.5 copy-start.35
  287.6 7.7 copy-start.49
  295.5 415.5 %copy-start.24 = (bf16[256,2048]{1,0:T(8,128)(2,1)}, bf16[256,2048]{1,0:T(8,128)(2,1)S(1)}, u32[]{:S(2)}) copy-start(bf16[256,2048]{1,0:T(8,128)(2,1)S(1)} %multiply_convert_fusion.2) | copy-start | bytes 3145732
  507.3 423.4 %copy-start.26 = (bf16[1,256,2048]{2,1,0:T(8,128)(2,1)S(1)}, bf16[1,256,2048]{2,1,0:T(8,128)(2,1)}, u32[]{:S(2)}) copy-start(bf16[1,256,2048]{2,1,0:T(8,128)(2,1)} %param.31) | copy-start | bytes 3145732
  954.1 13.6 copy-start.17
  985.6 173.6 %copy-start.4 = (f32[256,2048]{1,0:T(8,128)}, f32[256,2048]{1,0:T(8,128)S(1)}, u32[]{:S(2)}) copy-start(f32[256,2048]{1,0:T(8,128)S(1)} %fusion.78) | copy-start | bytes 6291460
  998.5 18.7 all-to-all-start.2
  1021.9 2.6 copy-start.8
  1021.9 2.6 copy-start.13
  1021.9 2.6 copy-start.33
  1024.5 3.2 copy-start
  1080.8 2.6 copy-start.8
  1080.8 2.6 copy-start.13
  1080.9 2.6 copy-start.33
  1083.4 3.2 copy-start
  1138.0 4.1 copy-start.12
  1142.1 1.9 copy-start.2
  1142.2 2.0 copy-start.10
  1142.2 2.3 copy-start.15
  1142.2 2.3 copy-start.42
  1142.2 2.3 copy-start.53
  1144.0 1.7 copy-start.19
  1146.6 2.6 copy-start.44
  1154.6 4.7 copy-start.31
  1154.6 29.4 %all-to-all-start.3 = ((bf16[1024,2,4,128]{3,2,1,0:T(4,128)(2,1)}), bf16[1024,2,4,128]{3,2,1,0:T(4,128)(2,1)}, u32[]{:S(2)}, u32[]{:S(2)}) async-start(bf16[1024,2,4,128]{3,2,1,0:T(4,128)(2,1)} %copy.118), calls=%async_computation.3 | async-start | bytes 4194304 | tf_op jit(solution)/shard_map/all_to_all | solution.py:276
  1159.2 304.2 %reduce-scatter.3.cloned.1.call-start = ((), (), s32[]{:S(2)}) async-start(), calls=%async_computation.13 | async-start | bytes 28311552 | tf_op jit(solution)/shard_map/reduce_scatter | solution.py:158
  1187.2 4.5 copy-start.7
  1187.2 4.5 copy-start.40
  1187.2 4.5 copy-start.46
  1188.2 13.4 copy-start.20
  1190.0 11.6 copy-start.28
  1191.6 10.0 copy-start.22
  1218.7 964.3 %reduce-scatter.5.cloned.1.call-start = ((), (), s32[]{:S(2)}) async-start(), calls=%async_computation.14 | async-start | bytes 84934656 | tf_op jit(solution)/shard_map/reduce_scatter | solution.py:158
  1219.9 13.8 copy-start.25
  1306.4 1120.7 %all-reduce.8.cloned.1.call-start = ((), (), s32[]{:S(2)}) async-start(), calls=%async_computation.15 | async-start | bytes 25165824 | tf_op jit(solution)/shard_map/psum | solution.py:161
  2199.3 6.2 copy-start.23
  2199.3 6.3 copy-start.29
  2205.6 2.6 copy-start.30
  2208.3 3.0 copy-start.54
  2208.3 3.0 copy-start.57
  2208.3 3.0 copy-start.58
  2208.3 42.0 %copy-start.51 = (f32[256]{0:T(256)S(1)}, f32[256]{0:T(256)}, u32[]{:S(2)}) copy-start(f32[256]{0:T(256)} %copy-done.50) | copy-start | bytes 3076
  2208.3 42.0 %copy-start.5 = (f32[256,2048]{1,0:T(8,128)S(1)}, f32[256,2048]{1,0:T(8,128)}, u32[]{:S(2)}) copy-start(f32[256,2048]{1,0:T(8,128)} %copy-done.4) | copy-start | bytes 6291460
  2427.0 2.9 copy-start.14
  2427.0 7.2 copy-start.3
  (15 other events, 15.8 us)
Sparse Core Ops, SparseCore 0:
  9.6 49.8 all-gather.9
  61.1 45.8 all-gather.11
  108.6 80.7 all-gather.7
  190.9 80.5 all-gather.13
  273.0 218.3 all-gather.17
  492.9 218.0 all-gather.15
  712.6 218.0 all-gather.19
  1218.8 244.4 reduce-scatter.2
  1465.7 717.2 reduce-scatter.4
  2187.0 239.9 all-reduce.7
where the time goes:
time: 2460 us; the launch traced here: 2450 us
  waiting for transfers between devices  1880 us (76%)
  matrix products  312 us (13%)
  other arithmetic  105 us (4%)
  local copies, waits for them, and re-layouts  61.4 us (2%)
  blocking collectives  55.5 us (2%)
    reduce_scatter x2, waiting for transfers between devices, reduce_rows(): lax.psum_scatter(row_terms(lefts, rights).astype(jnp.bfloat16), 'fsdp', s...  877 us
    all_gather x1, waiting for transfers between devices, mlp_weights(): lax.all_gather(down_weight, 'fsdp', axis=0, tiled=True)  204 us
    all_gather x1, waiting for transfers between devices, mlp_weights(): lax.all_gather(gate_weight, 'fsdp', axis=0, tiled=True)  204 us
    all_gather x1, waiting for transfers between devices, mlp_weights(): lax.all_gather(up_weight, 'fsdp', axis=0, tiled=True)  196 us
    psum x1, waiting for transfers between devices, reduce_rows(): result = lax.psum(share, 'seq').astype(jnp.float32)  173 us
    all_gather x1, waiting for transfers between devices, attention_weights(): lax.all_gather(query_weight, 'fsdp', axis=0, tiled=True)  78 us
    concatenate x2, other arithmetic, row_terms(): return jnp.concatenate(parts, axis=1)  67.4 us
    dot_general x4, matrix products, row_terms(): jnp.einsum('cd,cf->df', left, right, preferred_element_type=jnp.float32)  51.7 us
  transfers between devices with their start and end apart: 13, of which 12 were waited for; matrix products, arithmetic and copies ran while one was open for 9% of the time, Pallas kernels for 0%

commit v1 on v0

v1 whole, which is shorter than its diff:
```python
import jax
import jax.numpy as jnp
from jax import lax
from jax.sharding import PartitionSpec as P

QUERY_HEADS = 16
KEY_VALUE_HEADS = 8
HEAD_SIZE = 128
NORM_EPSILON = 1e-06
ROPE_BASE = 1000000.0
SCORE_FLOOR = -1e30
F32 = jnp.float32
BF16 = jnp.bfloat16


def dot(a, b):
    return jnp.dot(a, b, preferred_element_type=F32)


def dot_nt(a, b):
    return lax.dot_general(a, b, (((1,), (1,)), ((), ())), preferred_element_type=F32)


def dot_tn(a, b):
    return lax.dot_general(a, b, (((0,), (0,)), ((), ())), preferred_element_type=F32)


def inverse_rms(u):
    return lax.rsqrt(jnp.mean(u * u, axis=-1, keepdims=True) + NORM_EPSILON)


def norm_back(u, gain, e):
    w = inverse_rms(u)
    n = u * w
    t = e * gain
    du = w * (t - n * jnp.mean(n * t, axis=-1, keepdims=True))
    return du, e * n


def positions(segments):
    index = jnp.arange(segments.shape[0], dtype=jnp.int32)
    first = jnp.concatenate([jnp.ones((1,), dtype=jnp.bool_), segments[1:] != segments[:-1]])
    starts = lax.cummax(jnp.where(first, index, jnp.zeros_like(index)), axis=0)
    return index - starts


def rotary_tables(position_index):
    half = HEAD_SIZE // 2
    freq = ROPE_BASE ** (-jnp.arange(half, dtype=F32) * 2.0 / HEAD_SIZE)
    angle = position_index.astype(F32)[:, None] * freq[None, :]
    cosine = jnp.concatenate([jnp.cos(angle), jnp.cos(angle)], axis=-1)
    sine = jnp.concatenate([jnp.sin(angle), jnp.sin(angle)], axis=-1)
    return cosine[:, None, :], sine[:, None, :]


def rotate(u, cosine, sine):
    half = HEAD_SIZE // 2
    turned = jnp.concatenate([-u[..., half:], u[..., :half]], axis=-1)
    return u * cosine + turned * sine


def rotate_back(e, cosine, sine):
    half = HEAD_SIZE // 2
    es = e * sine
    return e * cosine + jnp.concatenate([es[..., half:], -es[..., :half]], axis=-1)


def by_neighbours(count):
    return count == 4


def swap(x, side):
    return lax.ppermute(x, "seq", [(s, s ^ side) for s in range(4)])


def gather_slots(x, count):
    half = x.shape[0] // 2
    a, b = x[:half], x[half:]
    bx, ay = swap(b, 1), swap(a, 2)
    ax, by = swap(a, 1), swap(b, 2)
    ad = swap(ay, 1)
    bd = swap(bx, 2)
    return [[a, b], [ax, bx], [ay, by], [ad, bd]]


def gather_rows(x, count):
    if not by_neighbours(count):
        return lax.all_gather(x, "seq", axis=0, tiled=True)
    rows = x.shape[0]
    me = lax.axis_index("seq")
    out = jnp.zeros((count * rows,) + x.shape[1:], x.dtype)
    for k, pieces in enumerate(gather_slots(x, count)):
        for j, piece in enumerate(pieces):
            out = lax.dynamic_update_slice(out, piece, ((me ^ k) * rows + j * (rows // 2), 0))
    return out


def gather_columns(x, count):
    if not by_neighbours(count):
        return lax.all_gather(x, "seq", axis=1, tiled=True).astype(F32)
    rows, c = x.shape
    me = lax.axis_index("seq")
    out = jnp.zeros((rows, count * c), F32)
    for k, pieces in enumerate(gather_slots(x, count)):
        for j, piece in enumerate(pieces):
            out = lax.dynamic_update_slice(out, piece.astype(F32), (j * (rows // 2), (me ^ k) * c))
    return out


def scatter_sum(partial, count):
    if not by_neighbours(count):
        return lax.psum_scatter(
            partial.astype(BF16), "seq", scatter_dimension=0, tiled=True
        ).astype(F32)
    rows = partial.shape[0] // count
    half = rows // 2
    me = lax.axis_index("seq")
    low = partial.astype(BF16)

    def block(k, start, size):
        return lax.dynamic_slice(low, ((me ^ k) * rows + start, 0), (size, low.shape[1]))

    tx = swap(block(3, 0, half), 1)
    ty = swap(block(3, half, half), 2)
    ya = swap((block(2, 0, half).astype(F32) + tx.astype(F32)).astype(BF16), 2)
    yb = swap(block(2, half, half), 2)
    xa = swap(block(1, 0, half), 1)
    xb = swap((block(1, half, half).astype(F32) + ty.astype(F32)).astype(BF16), 1)
    top = block(0, 0, half).astype(F32) + ya.astype(F32) + xa.astype(F32)
    low_half = block(0, half, half).astype(F32) + yb.astype(F32) + xb.astype(F32)
    return jnp.concatenate([top, low_half], axis=0)


def scores_of(query, key, segments):
    length = query.shape[0]
    index = jnp.arange(length, dtype=jnp.int32)
    allowed = (segments[:, None] == segments[None, :]) & (index[None, :] <= index[:, None])
    s = dot_nt(query, key) * HEAD_SIZE ** (-0.5)
    return jnp.where(allowed, s, SCORE_FLOOR)


def attend(query, key, value, segments, ratio):
    outs, lses = [], []
    for h in range(query.shape[0]):
        s = scores_of(query[h], key[h // ratio], segments)
        top = jnp.max(s, axis=-1, keepdims=True)
        weights = jnp.exp(s - top)
        total = jnp.sum(weights, axis=-1, keepdims=True)
        probs = (weights / total).astype(BF16)
        outs.append(dot(probs, value[h // ratio]).astype(BF16))
        lses.append(top + jnp.log(total))
    return jnp.stack(outs), jnp.stack(lses)


def attend_back(query, key, value, segments, lse, d_out, ratio):
    dqs, dks, dvs = [], [], []
    for g in range(key.shape[0]):
        dk = dv = 0.0
        for h in range(g * ratio, (g + 1) * ratio):
            s = scores_of(query[h], key[g], segments)
            probs = jnp.exp(s - lse[h])
            dp = dot_nt(d_out[h], value[g])
            delta = jnp.sum(probs * dp, axis=-1, keepdims=True)
            ds = (probs * (dp - delta) * HEAD_SIZE ** (-0.5)).astype(BF16)
            dqs.append(dot(ds, key[g]))
            dk = dk + dot_tn(ds, query[h])
            dv = dv + dot_tn(probs.astype(BF16), d_out[h])
        dks.append(dk)
        dvs.append(dv)
    return jnp.stack(dqs), jnp.stack(dks), jnp.stack(dvs)


def make_body(seq_count):
    def body(
        tokens,
        segment_ids,
        input_gain,
        query_weight,
        key_projection_weight,
        value_projection_weight,
        output_weight,
        query_gain,
        key_gain,
        post_gain,
        gate_weight,
        up_weight,
        down_weight,
        cotangent,
    ):
        me = lax.axis_index("seq")
        q_heads = QUERY_HEADS // seq_count
        kv_heads = KEY_VALUE_HEADS // seq_count
        ratio = QUERY_HEADS // KEY_VALUE_HEADS
        q_cols, kv_cols = q_heads * HEAD_SIZE, kv_heads * HEAD_SIZE
        f_cols = gate_weight.shape[1] // seq_count

        def share(w, cols):
            return lax.dynamic_slice(w, (0, me * cols), (w.shape[0], cols))

        def gather_weight(w):
            return lax.all_gather(w, "fsdp", axis=0, tiled=True)

        def reduce_weight(terms):
            return lax.psum_scatter(terms.astype(BF16), "fsdp", scatter_dimension=0, tiled=True)

        w_qkv = gather_weight(
            jnp.concatenate(
                [
                    share(query_weight, q_cols),
                    share(key_projection_weight, kv_cols),
                    share(value_projection_weight, kv_cols),
                ],
                axis=1,
            )
        )
        w_out = gather_weight(share(output_weight, q_cols))
        w_gate = gather_weight(share(gate_weight, f_cols))
        w_up = gather_weight(share(up_weight, f_cols))
        w_down = gather_weight(share(down_weight, f_cols))

        inputs = tokens[0].astype(F32)
        segments = segment_ids[0]
        length = segments.shape[0]
        xa = gather_rows((inputs * inverse_rms(inputs) * input_gain).astype(BF16), seq_count)
        dy = gather_rows(cotangent[0], seq_count)

        cosine, sine = rotary_tables(positions(segments))
        qkv = dot(xa, w_qkv).astype(BF16)
        q = qkv[:, :q_cols].reshape(length, q_heads, HEAD_SIZE).astype(F32)
        k = qkv[:, q_cols : q_cols + kv_cols].reshape(length, kv_heads, HEAD_SIZE).astype(F32)
        v = qkv[:, q_cols + kv_cols :].reshape(length, kv_heads, HEAD_SIZE).transpose(1, 0, 2)
        qr = rotate(q * inverse_rms(q) * query_gain, cosine, sine).astype(BF16).transpose(1, 0, 2)
        kr = rotate(k * inverse_rms(k) * key_gain, cosine, sine).astype(BF16).transpose(1, 0, 2)
        o_heads, lse = attend(qr, kr, v, segments, ratio)
        o = o_heads.transpose(1, 0, 2).reshape(length, q_cols)

        resid = inputs + scatter_sum(dot_nt(o, w_out), seq_count)
        xb = gather_rows((resid * inverse_rms(resid) * post_gain).astype(BF16), seq_count)

        gate = dot(xb, w_gate)
        upper = dot(xb, w_up)
        d_hidden = dot(dy, w_down)
        sigma = 1.0 / (1.0 + jnp.exp(-gate))
        silu = gate * sigma
        hidden = (silu * upper).astype(BF16)
        d_gate = (d_hidden * upper * sigma * (1.0 + gate * (1.0 - sigma))).astype(BF16)
        d_up = (d_hidden * silu).astype(BF16)

        d_xb = scatter_sum(dot_nt(d_gate, w_gate) + dot_nt(d_up, w_up), seq_count)
        out = resid + scatter_sum(dot_nt(hidden, w_down), seq_count)

        g_gate = reduce_weight(dot_tn(xb, d_gate))
        g_up = reduce_weight(dot_tn(xb, d_up))
        g_down = reduce_weight(dot_tn(dy, hidden))

        du, post_terms = norm_back(resid, post_gain, d_xb)
        d_resid = cotangent[0].astype(F32) + du
        drl = gather_rows(d_resid.astype(BF16), seq_count)
        d_o = dot(drl, w_out).astype(BF16)
        g_out = reduce_weight(dot_tn(drl, o))

        d_o_heads = d_o.reshape(length, q_heads, HEAD_SIZE).transpose(1, 0, 2)
        dqr, dkr, dv = attend_back(qr, kr, v, segments, lse, d_o_heads, ratio)
        dq, q_terms = norm_back(q, query_gain, rotate_back(dqr.transpose(1, 0, 2), cosine, sine))
        dk, k_terms = norm_back(k, key_gain, rotate_back(dkr.transpose(1, 0, 2), cosine, sine))
        d_qkv = jnp.concatenate(
            [
                dq.astype(BF16).reshape(length, q_cols),
                dk.astype(BF16).reshape(length, kv_cols),
                dv.astype(BF16).transpose(1, 0, 2).reshape(length, kv_cols),
            ],
            axis=1,
        )
        g_qkv = reduce_weight(dot_tn(xa, d_qkv))
        d_xa = scatter_sum(dot_nt(d_qkv, w_qkv), seq_count)
        du, in_terms = norm_back(inputs, input_gain, d_xa)
        d_inputs = d_resid + du

        gains = lax.psum(
            (
                jnp.sum(in_terms, axis=0),
                jnp.sum(q_terms, axis=(0, 1)),
                jnp.sum(k_terms, axis=(0, 1)),
                jnp.sum(post_terms, axis=0),
            ),
            ("seq", "fsdp"),
        )
        return (
            out.astype(BF16)[None],
            d_inputs.astype(BF16)[None],
            gains[0],
            gather_columns(g_qkv[:, :q_cols], seq_count),
            gather_columns(g_qkv[:, q_cols : q_cols + kv_cols], seq_count),
            gather_columns(g_qkv[:, q_cols + kv_cols :], seq_count),
            gather_columns(g_out, seq_count),
            gains[1],
            gains[2],
            gains[3],
            gather_columns(g_gate, seq_count),
            gather_columns(g_up, seq_count),
            gather_columns(g_down, seq_count),
        )

    return body


def solution(mesh):
    rows, acts = P("fsdp", None), P("fsdp", "seq", None)
    return jax.shard_map(
        make_body(mesh.shape["seq"]),
        mesh=mesh,
        in_specs=(
            acts, rows, P(), rows, rows, rows, rows, P(), P(), P(), rows, rows, rows, acts,
        ),
        out_specs=(acts, acts, P(), rows, rows, rows, rows, P(), P(), P(), rows, rows, rows),
        check_vma=False,
    )
```

time: 2460 us -> 823 us (0.33)
  waiting for transfers between devices: 1880 us -> 328 us
  matrix products: 312 us -> 167 us
  starting transfers between devices: 14.1 us -> 99.7 us
    reduce_scatter x2 -> x5, waiting for transfers between devices: 877 us -> 14.8 us  [reduce_weight(): lax.psum_scatter(terms.astype(BF16), 'fsdp', scatter_dimension=0, tiled=T...]
    all_gather x7 -> x5, waiting for transfers between devices: 772 us -> 52.4 us  [gather_weight(): return lax.all_gather(w, 'fsdp', axis=0, tiled=True)]
    ppermute x0 -> x90, waiting for transfers between devices: none -> 260 us  [swap(): return lax.ppermute(x, 'seq', [(s, s ^ side) for s in range(4)])]
    psum x1 -> x0, waiting for transfers between devices: 173 us -> none  [reduce_rows(): result = lax.psum(share, 'seq').astype(jnp.float32)]
    dot_general x32 -> x39, matrix products: 312 us -> 167 us  [the longest x13 59.8 us: dot(): return jnp.dot(a, b, preferred_element_type=F32)]
    ppermute x0 -> x90, starting transfers between devices: none -> 98.9 us  [swap(): return lax.ppermute(x, 'seq', [(s, s ^ side) for s in range(4)])]
    concatenate x5 -> x4, other arithmetic: 73.6 us -> 8.13 us  [the longest x2 6.17 us: scatter_sum(): return jnp.concatenate([top, low_half], axis=0)]
    all_to_all x3 -> x0, waiting for transfers between devices: 56 us -> none  [the longest x1 22.6 us: body(): lax.all_to_all(packed, 'seq', split_axis=1, concat_axis=0, tiled=True)]
  transfers between devices with their start and end apart: 13 -> 100, of which waited for: 12 -> 55; matrix products, arithmetic and copies ran while one was open for 9% -> 29% of each run, Pallas kernels for 0% -> 0%
where the time goes in v1:
time: 823 us; the launch traced here: 812 us
  waiting for transfers between devices  328 us (40%)
  matrix products  167 us (20%)
  starting transfers between devices  99.7 us (12%)
  other arithmetic  84.4 us (10%)
  local copies, waits for them, and re-layouts  76.7 us (9%)
  blocking collectives  40.4 us (5%)
  between operations  16.5 us (2%)
    ppermute x90, waiting for transfers between devices, swap(): return lax.ppermute(x, 'seq', [(s, s ^ side) for s in range(4)])  260 us
    ppermute x90, starting transfers between devices, swap(): return lax.ppermute(x, 'seq', [(s, s ^ side) for s in range(4)])  98.9 us
    dot_general x13, matrix products, dot(): return jnp.dot(a, b, preferred_element_type=F32)  59.8 us
    dot_general x13, matrix products, dot_tn(): lax.dot_general(a, b, (((0,), (0,)), ((), ())), preferred_element_type=F32)  54.3 us
    all_gather x5, waiting for transfers between devices, gather_weight(): return lax.all_gather(w, 'fsdp', axis=0, tiled=True)  52.4 us
    dot_general x13, matrix products, dot_nt(): lax.dot_general(a, b, (((1,), (1,)), ((), ())), preferred_element_type=F32)  52.4 us
    psum x1, blocking collectives, body(): lax.psum((jnp.sum(in_terms, axis=0), jnp.sum(q_terms, axis=(0, 1)), jnp.s...  40.4 us
    dynamic_update_slice x55, other arithmetic, gather_columns(): lax.dynamic_update_slice(out, piece.astype(F32), (j * (rows // 2), (me ^...  38.4 us
  transfers between devices with their start and end apart: 100, of which 55 were waited for; matrix products, arithmetic and copies ran while one was open for 29% of the time, Pallas kernels for 0%

profile of v1, /device:TPU:0, one launch (start us, length us, event | category | flops | bytes accessed | tf_op | source)
XLA Modules:
  0.0 811.8 jit_solution(16544742240515405742)
XLA Ops:
  20.1 2.9 collective-permute-start
  39.7 7.5 collective-permute-done.1
  57.3 12.4 %collective-permute-done.4 = bf16[128,2048]{1,0:T(8,128)(2,1)S(1)} collective-permute-done((bf16[128,2048]{1,0:T(8,128)(2,1)}, bf16[128,2048]{1,0:T(8,128)(2,1)S(1)}, u32[]{:S(2)}, u32[]{:S(2)}) %collective-permute-start.4) | collective-permute-done | bytes 524320 | tf_op jit(solution)/shard_map/ppermute | solution.py:73
  71.4 8.1 convolution_convert_fusion.8
  95.0 4.3 convolution_convert_fusion.4
  107.5 10.3 %collective-permute-done.6 = bf16[128,2048]{1,0:T(8,128)(2,1)} collective-permute-done((bf16[128,2048]{1,0:T(8,128)(2,1)}, bf16[128,2048]{1,0:T(8,128)(2,1)}, u32[]{:S(2)}, u32[]{:S(2)}) %collective-permute-start.6) | collective-permute-done | bytes 524320 | tf_op jit(solution)/shard_map/ppermute | solution.py:73
  127.9 5.0 collective-permute-done.10
  135.0 9.2 %collective-permute-done.7 = bf16[128,2048]{1,0:T(8,128)(2,1)S(1)} collective-permute-done((bf16[128,2048]{1,0:T(8,128)(2,1)S(1)}, bf16[128,2048]{1,0:T(8,128)(2,1)S(1)}, u32[]{:S(2)}, u32[]{:S(2)}) %collective-permute-start.7) | collective-permute-done | bytes 524320 | tf_op jit(solution)/shard_map/ppermute | solution.py:73
  147.8 7.6 collective-permute-done.27
  155.6 16.1 %collective-permute-done.9 = bf16[128,2048]{1,0:T(8,128)(2,1)S(1)} collective-permute-done((bf16[128,2048]{1,0:T(8,128)(2,1)S(1)}, bf16[128,2048]{1,0:T(8,128)(2,1)S(1)}, u32[]{:S(2)}, u32[]{:S(2)}) %collective-permute-start.9) | collective-permute-done | bytes 524320 | tf_op jit(solution)/shard_map/ppermute | solution.py:73
  181.9 8.2 %collective-permute-done.14 = bf16[128,2048]{1,0:T(8,128)(2,1)S(1)} collective-permute-done((bf16[128,2048]{1,0:T(8,128)(2,1)S(1)}, bf16[128,2048]{1,0:T(8,128)(2,1)S(1)}, u32[]{:S(2)}, u32[]{:S(2)}) %collective-permute-start.14) | collective-permute-done | bytes 524320 | tf_op jit(solution)/shard_map/ppermute | solution.py:73
  192.5 8.8 %collective-permute-done.13 = bf16[128,2048]{1,0:T(8,128)(2,1)S(1)} collective-permute-done((bf16[128,2048]{1,0:T(8,128)(2,1)S(1)}, bf16[128,2048]{1,0:T(8,128)(2,1)S(1)}, u32[]{:S(2)}, u32[]{:S(2)}) %collective-permute-start.13) | collective-permute-done | bytes 524320 | tf_op jit(solution)/shard_map/ppermute | solution.py:73
  211.3 11.8 %fusion.125 = f32[1024,1536]{1,0:T(8,128)} fusion(bf16[1024,2048]{1,0:T(8,128)(2,1)} %constant_dynamic-update-slice_fusion.16, bf16[2048,1536]{1,0:T(8,128)(2,1)} %all-gather.10.cloned.1.call-done), kind=kOutput, calls=%fused_computation.352 | convolution fusion | flops 6442450944 | bytes 16777216 | tf_op jit(solution)/shard_map/dot_general | solution.py:17
  223.2 11.6 %fusion.126 = f32[1024,1536]{1,0:T(8,128)} fusion(bf16[1024,2048]{1,0:T(8,128)(2,1)} %constant_dynamic-update-slice_fusion.16, bf16[2048,1536]{1,0:T(8,128)(2,1)} %all-gather.12.cloned.1.call-done), kind=kOutput, calls=%fused_computation.353 | convolution fusion | flops 6442450944 | bytes 16777216 | tf_op jit(solution)/shard_map/dot_general | solution.py:17
  234.8 52.4 %all-gather.14.cloned.1.call-done = bf16[2048,1536]{1,0:T(8,128)(2,1)} async-done(((bf16[256,1536]{1,0:T(8,128)(2,1)}), bf16[2048,1536]{1,0:T(8,128)(2,1)}) %all-gather.14.cloned.1.call-update) | async-done | bytes 6291472 | tf_op jit(solution)/shard_map/all_gather | solution.py:201
  287.2 16.8 %multiply_convert_fusion = (bf16[1024,1536]{1,0:T(8,128)(2,1)}, bf16[1024,1536]{1,0:T(8,128)(2,1)}, bf16[1024,1536]{1,0:T(8,128)(2,1)}) fusion(f32[1024,1536]{1,0:T(8,128)} %fusion.125, f32[1024,1536]{1,0:T(8,128)} %fusion.126, bf16[1024,2048]{1,0:T(8,128)(2,1)} %copy-done.50, bf16[2048,1536]{1,0:T(8,128)(2,1)} %all-gather.14.cloned.1.call-done), kind=kOutput, calls=%fused_computation.4 | convolution fusion | flops 6466043904 | bytes 32505856 | tf_op jit(solution)/shard_map/dot_general | solution.py:17
  304.0 9.9 %fusion.127 = f32[1024,2048]{1,0:T(8,128)S(1)} fusion(bf16[1024,1536]{1,0:T(8,128)(2,1)} %get-tuple-element.28, bf16[2048,1536]{1,0:T(8,128)(2,1)} %all-gather.10.cloned.1.call-done), kind=kOutput, calls=%fused_computation.354 | convolution fusion | flops 6442450944 | bytes 17825792 | tf_op jit(solution)/shard_map/dot_general | solution.py:21
  314.0 8.7 %add_convert_fusion = bf16[1024,2048]{1,0:T(8,128)(2,1)S(1)} fusion(f32[1024,2048]{1,0:T(8,128)S(1)} %fusion.127, bf16[1024,1536]{1,0:T(8,128)(2,1)} %get-tuple-element.27, bf16[2048,1536]{1,0:T(8,128)(2,1)S(1)} %copy-done.86), kind=kOutput, calls=%fused_computation | convolution fusion | flops 6446645248 | bytes 22020096 | tf_op jit(solution)/shard_map/dot_general | solution.py:21
  326.5 11.2 %collective-permute-done.30 = bf16[128,2048]{1,0:T(8,128)(2,1)S(1)} collective-permute-done((bf16[128,2048]{1,0:T(8,128)(2,1)S(1)}, bf16[128,2048]{1,0:T(8,128)(2,1)S(1)}, u32[]{:S(2)}, u32[]{:S(2)}) %collective-permute-start.30) | collective-permute-done | bytes 524320 | tf_op jit(solution)/shard_map/ppermute | solution.py:73
  339.9 8.3 %collective-permute-done.32 = bf16[128,2048]{1,0:T(8,128)(2,1)S(1)} collective-permute-done((bf16[128,2048]{1,0:T(8,128)(2,1)S(1)}, bf16[128,2048]{1,0:T(8,128)(2,1)S(1)}, u32[]{:S(2)}, u32[]{:S(2)}) %collective-permute-start.32) | collective-permute-done | bytes 524320 | tf_op jit(solution)/shard_map/ppermute | solution.py:73
  348.3 4.5 collective-permute-done.31
  354.8 6.9 collective-permute-done.33
  369.4 12.2 %collective-permute-done.38 = bf16[128,2048]{1,0:T(8,128)(2,1)S(1)} collective-permute-done((bf16[128,2048]{1,0:T(8,128)(2,1)S(1)}, bf16[128,2048]{1,0:T(8,128)(2,1)S(1)}, u32[]{:S(2)}, u32[]{:S(2)}) %collective-permute-start.38) | collective-permute-done | bytes 524320 | tf_op jit(solution)/shard_map/ppermute | solution.py:73
  382.2 9.2 %collective-permute-done.37 = bf16[128,2048]{1,0:T(8,128)(2,1)S(1)} collective-permute-done((bf16[128,2048]{1,0:T(8,128)(2,1)S(1)}, bf16[128,2048]{1,0:T(8,128)(2,1)S(1)}, u32[]{:S(2)}, u32[]{:S(2)}) %collective-permute-start.37) | collective-permute-done | bytes 524320 | tf_op jit(solution)/shard_map/ppermute | solution.py:73
  393.2 5.3 collective-permute-done.40
  404.8 2.9 multiply_reduce_fusion
  409.6 2.9 multiply_reduce_fusion.2
  412.5 3.8 convolution_convert_fusion.7
  416.3 3.9 multiply_reduce_fusion.1
  451.5 9.6 %convolution_convert_fusion.5 = bf16[2048,1024]{1,0:T(8,128)(2,1)} fusion(bf16[1024,2048]{1,0:T(8,128)(2,1)} %constant_dynamic-update-slice_fusion.24, bf16[1024,256]{0,1:T(8,128)(2,1)S(1)} %bitcast.287, bf16[1024,256]{0,1:T(8,128)(2,1)S(1)} %bitcast.285, bf16[1024,512]{0,1:T(8,128)(2,1)S(1)} %bitcast.281), kind=kOutput, calls=%fused_computation.37 | convolution fusion | flops 4303355904 | bytes 10485760 | tf_op jit(solution)/shard_map/dot_general | solution.py:25
  461.2 11.5 %convolution_convert_fusion.2 = bf16[2048,1536]{1,0:T(8,128)(2,1)} fusion(bf16[1024,2048]{1,0:T(8,128)(2,1)} %constant_dynamic-update-slice_fusion.16, bf16[1024,1536]{1,0:T(8,128)(2,1)} %get-tuple-element.28), kind=kOutput, calls=%fused_computation.3 | convolution fusion | flops 6445596672 | bytes 13631488 | tf_op jit(solution)/shard_map/dot_general | solution.py:25
  472.8 11.5 %convolution_convert_fusion.1 = bf16[2048,1536]{1,0:T(8,128)(2,1)} fusion(bf16[1024,2048]{1,0:T(8,128)(2,1)} %constant_dynamic-update-slice_fusion.16, bf16[1024,1536]{1,0:T(8,128)(2,1)} %get-tuple-element.27), kind=kOutput, calls=%fused_computation.2 | convolution fusion | flops 6445596672 | bytes 13631488 | tf_op jit(solution)/shard_map/dot_general | solution.py:25
  484.6 9.9 %convolution_convert_fusion.3 = bf16[1024,2048]{1,0:T(8,128)(2,1)S(1)} fusion(bf16[1024,1536]{1,0:T(8,128)(2,1)} %get-tuple-element.29, bf16[2048,1536]{1,0:T(8,128)(2,1)} %all-gather.14.cloned.1.call-done), kind=kOutput, calls=%fused_computation.35 | convolution fusion | flops 6444548096 | bytes 13631488 | tf_op jit(solution)/shard_map/dot_general | solution.py:21
  497.2 4.8 convolution_convert_fusion.6
  506.9 3.2 collective-permute-done.18
  514.3 7.0 collective-permute-done.42
  523.8 8.8 %collective-permute-done.20 = bf16[128,2048]{1,0:T(8,128)(2,1)S(1)} collective-permute-done((bf16[128,2048]{1,0:T(8,128)(2,1)S(1)}, bf16[128,2048]{1,0:T(8,128)(2,1)S(1)}, u32[]{:S(2)}, u32[]{:S(2)}) %collective-permute-start.20) | collective-permute-done | bytes 524320 | tf_op jit(solution)/shard_map/ppermute | solution.py:73
  534.7 3.4 add_bitcast_fusion.1
  539.9 4.0 collective-permute-done.44
  545.3 9.1 %collective-permute-done.43 = bf16[128,2048]{1,0:T(8,128)(2,1)} collective-permute-done((bf16[128,2048]{1,0:T(8,128)(2,1)}, bf16[128,2048]{1,0:T(8,128)(2,1)}, u32[]{:S(2)}, u32[]{:S(2)}) %collective-permute-start.43) | collective-permute-done | bytes 524320 | tf_op jit(solution)/shard_map/ppermute | solution.py:73
  554.4 3.0 convert_add_fusion.3
  557.9 8.8 %convolution_convert_fusion = bf16[2048,1536]{1,0:T(8,128)(2,1)} fusion(bf16[1024,2048]{1,0:T(8,128)(2,1)S(1)} %copy-done.51, bf16[1024,1536]{1,0:T(8,128)(2,1)S(1)} %copy-done.89), kind=kOutput, calls=%fused_computation.1 | convolution fusion | flops 6445596672 | bytes 13631488 | tf_op jit(solution)/shard_map/dot_general | solution.py:25
  566.9 2.7 add_bitcast_fusion
  572.2 40.4 %all-reduce = (f32[2048]{0:T(1024)}, f32[128]{0:T(128)}, f32[128]{0:T(128)}, f32[2048]{0:T(1024)}) all-reduce(f32[2048]{0:T(1024)S(1)} %get-tuple-element.15, f32[128]{0:T(128)S(1)} %get-tuple-element.17, f32[128]{0:T(128)S(1)} %get-tuple-element.19, f32[2048]{0:T(1024)S(1)} %get-tuple-element.13), channel_id=1, replica_groups=mesh['seq'=4,'fsdp'=8] {'seq','fsdp'}, use_global_device_ids=true, to_apply=%region_23.24 | all-reduce | flops 4352 | bytes 34816 | tf_op jit(solution)/shard_map/psum | solution.py:279
  612.6 4.9 fusion.21
  651.2 2.8 collective-permute-done.55
  655.0 3.3 collective-permute-done.56
  659.2 3.3 collective-permute-done.57
  664.0 2.8 collective-permute-done.60
  668.2 2.8 collective-permute-done.61
  672.0 3.8 collective-permute-done.62
  676.5 3.6 collective-permute-done.63
  681.1 3.2 collective-permute-done.58
  685.1 3.6 collective-permute-done.59
  694.2 3.7 collective-permute-done.65
  714.8 3.4 broadcast.220.clone
  720.1 3.4 broadcast.220.clone.1
  725.5 14.8 %reduce-scatter.14.cloned.1.call-done = bf16[256,1536]{1,0:T(8,128)(2,1)} async-done(((bf16[2048,1536]{1,0:T(8,128)(2,1)}), bf16[256,1536]{1,0:T(8,128)(2,1)}) %reduce-scatter.14.cloned.1.call-update) | async-done | bytes 786448 | tf_op jit(solution)/shard_map/reduce_scatter | solution.py:204
  766.9 7.9 collective-permute-done.85
  784.2 3.8 collective-permute-done.77
  788.9 2.7 collective-permute-done.82
  792.6 3.8 collective-permute-done.83
  797.4 4.3 collective-permute-done.89
  801.8 2.7 copy-done.40
  (553 shorter events, 289.8 us)
Async XLA Ops:
  7.2 64.2 %all-gather.6.cloned.1.call-start = ((), (), s32[]{:S(2)}) async-start(), calls=%async_computation.5 | async-start | bytes 4718592 | tf_op jit(solution)/shard_map/all_gather | solution.py:201
  10.3 84.7 %all-gather.8.cloned.1.call-start = ((), (), s32[]{:S(2)}) async-start(), calls=%async_computation.6 | async-start | bytes 2359296 | tf_op jit(solution)/shard_map/all_gather | solution.py:201
  12.0 199.3 %all-gather.10.cloned.1.call-start = ((), (), s32[]{:S(2)}) async-start(), calls=%async_computation.7 | async-start | bytes 7077888 | tf_op jit(solution)/shard_map/all_gather | solution.py:201
  13.1 210.1 %all-gather.12.cloned.1.call-start = ((), (), s32[]{:S(2)}) async-start(), calls=%async_computation.8 | async-start | bytes 7077888 | tf_op jit(solution)/shard_map/all_gather | solution.py:201
  24.5 22.7 %collective-permute-start.1 = (bf16[128,2048]{1,0:T(8,128)(2,1)}, bf16[128,2048]{1,0:T(8,128)(2,1)S(1)}, u32[]{:S(2)}, u32[]{:S(2)}) collective-permute-start(bf16[128,2048]{1,0:T(8,128)(2,1)} %get-tuple-element.74), channel_id=1, source_target_pairs={{0,8},{8,0},{16,24},{24,16},{1,9},{9,1},{17,25},{25,17},{2,10},{10... | collective-permute-start | bytes 1572872 | tf_op jit(solution)/shard_map/ppermute | solution.py:73
  25.1 28.8 %collective-permute-start.3 = (bf16[128,2048]{1,0:T(8,128)(2,1)}, bf16[128,2048]{1,0:T(8,128)(2,1)}, u32[]{:S(2)}, u32[]{:S(2)}) collective-permute-start(bf16[128,2048]{1,0:T(8,128)(2,1)} %get-tuple-element.74), channel_id=1, source_target_pairs={{0,16},{8,24},{16,0},{24,8},{1,17},{9,25},{17,1},{25,9},{2,18},{10... | collective-permute-start | bytes 1572872 | tf_op jit(solution)/shard_map/ppermute | solution.py:73
  26.3 94.9 %collective-permute-start.24 = (bf16[128,2048]{1,0:T(8,128)(2,1)}, bf16[128,2048]{1,0:T(8,128)(2,1)}, u32[]{:S(2)}, u32[]{:S(2)}) collective-permute-start(bf16[128,2048]{1,0:T(8,128)(2,1)} %get-tuple-element.68), channel_id=1, source_target_pairs={{0,8},{8,0},{16,24},{24,16},{1,9},{9,1},{17,25},{25,17},{2,10},{10... | collective-permute-start | bytes 1572872 | tf_op jit(solution)/shard_map/ppermute | solution.py:73
  30.4 256.9 %all-gather.14.cloned.1.call-start = ((), (), s32[]{:S(2)}) async-start(), calls=%async_computation.9 | async-start | bytes 7077888 | tf_op jit(solution)/shard_map/all_gather | solution.py:201
  36.1 89.5 %collective-permute-start.26 = (bf16[128,2048]{1,0:T(8,128)(2,1)}, bf16[128,2048]{1,0:T(8,128)(2,1)}, u32[]{:S(2)}, u32[]{:S(2)}) collective-permute-start(bf16[128,2048]{1,0:T(8,128)(2,1)} %get-tuple-element.68), channel_id=1, source_target_pairs={{0,16},{8,24},{16,0},{24,8},{1,17},{9,25},{17,1},{25,9},{2,18},{10... | collective-permute-start | bytes 1572872 | tf_op jit(solution)/shard_map/ppermute | solution.py:73
  38.2 31.5 %collective-permute-start.4 = (bf16[128,2048]{1,0:T(8,128)(2,1)}, bf16[128,2048]{1,0:T(8,128)(2,1)S(1)}, u32[]{:S(2)}, u32[]{:S(2)}) collective-permute-start(bf16[128,2048]{1,0:T(8,128)(2,1)} %collective-permute-done.2), channel_id=1, source_target_pairs={{0,8},{8,0},{16,24},{24,16},{1,9},{9,1},{17,25},{25,17},{2,10},{10... | collective-permute-start | bytes 1572872 | tf_op jit(solution)/shard_map/ppermute | solution.py:73
  47.2 23.3 %collective-permute-start.5 = (bf16[128,2048]{1,0:T(8,128)(2,1)S(1)}, bf16[128,2048]{1,0:T(8,128)(2,1)S(1)}, u32[]{:S(2)}, u32[]{:S(2)}) collective-permute-start(bf16[128,2048]{1,0:T(8,128)(2,1)S(1)} %collective-permute-done.1), channel_id=1, source_target_pairs={{0,16},{8,24},{16,0},{24,8},{1,17},{9,25},{17,1},{25,9},{2,18},{10... | collective-permute-start | bytes 1572872 | tf_op jit(solution)/shard_map/ppermute | solution.py:73
  53.9 68.4 %collective-permute-start.25 = (bf16[128,2048]{1,0:T(8,128)(2,1)}, bf16[128,2048]{1,0:T(8,128)(2,1)}, u32[]{:S(2)}, u32[]{:S(2)}) collective-permute-start(bf16[128,2048]{1,0:T(8,128)(2,1)} %get-tuple-element.67), channel_id=1, source_target_pairs={{0,8},{8,0},{16,24},{24,16},{1,9},{9,1},{17,25},{25,17},{2,10},{10... | collective-permute-start | bytes 1572872 | tf_op jit(solution)/shard_map/ppermute | solution.py:73
  106.8 510.7 %reduce-scatter.8.cloned.1.call-start = ((), (), s32[]{:S(2)}) async-start(), calls=%async_computation.11 | async-start | bytes 2359296 | tf_op jit(solution)/shard_map/reduce_scatter | solution.py:204
  107.5 18.9 %collective-permute-start.8 = (bf16[128,2048]{1,0:T(8,128)(2,1)}, bf16[128,2048]{1,0:T(8,128)(2,1)S(1)}, u32[]{:S(2)}, u32[]{:S(2)}) collective-permute-start(bf16[128,2048]{1,0:T(8,128)(2,1)} %get-tuple-element.53), channel_id=1, source_target_pairs={{0,8},{8,0},{16,24},{24,16},{1,9},{9,1},{17,25},{25,17},{2,10},{10... | collective-permute-start | bytes 1572872 | tf_op jit(solution)/shard_map/ppermute | solution.py:73
  121.1 23.1 %collective-permute-start.7 = (bf16[128,2048]{1,0:T(8,128)(2,1)S(1)}, bf16[128,2048]{1,0:T(8,128)(2,1)S(1)}, u32[]{:S(2)}, u32[]{:S(2)}) collective-permute-start(bf16[128,2048]{1,0:T(8,128)(2,1)S(1)} %add_convert_fusion.8), channel_id=1, source_target_pairs={{0,16},{8,24},{16,0},{24,8},{1,17},{9,25},{17,1},{25,9},{2,18},{10... | collective-permute-start | bytes 1572872 | tf_op jit(solution)/shard_map/ppermute | solution.py:73
  122.4 33.1 %collective-permute-start.27 = (bf16[128,2048]{1,0:T(8,128)(2,1)S(1)}, bf16[128,2048]{1,0:T(8,128)(2,1)S(1)}, u32[]{:S(2)}, u32[]{:S(2)}) collective-permute-start(bf16[128,2048]{1,0:T(8,128)(2,1)S(1)} %copy-done.70), channel_id=1, source_target_pairs={{0,16},{8,24},{16,0},{24,8},{1,17},{9,25},{17,1},{25,9},{2,18},{10... | collective-permute-start | bytes 1572872 | tf_op jit(solution)/shard_map/ppermute | solution.py:73
  125.6 54.1 %collective-permute-start.29 = (bf16[128,2048]{1,0:T(8,128)(2,1)}, bf16[128,2048]{1,0:T(8,128)(2,1)S(1)}, u32[]{:S(2)}, u32[]{:S(2)}) collective-permute-start(bf16[128,2048]{1,0:T(8,128)(2,1)} %collective-permute-done.25), channel_id=1, source_target_pairs={{0,16},{8,24},{16,0},{24,8},{1,17},{9,25},{17,1},{25,9},{2,18},{10... | collective-permute-start | bytes 1572872 | tf_op jit(solution)/shard_map/ppermute | solution.py:73
  126.4 29.1 %collective-permute-start.28 = (bf16[128,2048]{1,0:T(8,128)(2,1)}, bf16[128,2048]{1,0:T(8,128)(2,1)S(1)}, u32[]{:S(2)}, u32[]{:S(2)}) collective-permute-start(bf16[128,2048]{1,0:T(8,128)(2,1)} %collective-permute-done.26), channel_id=1, source_target_pairs={{0,8},{8,0},{16,24},{24,16},{1,9},{9,1},{17,25},{25,17},{2,10},{10... | collective-permute-start | bytes 1572872 | tf_op jit(solution)/shard_map/ppermute | solution.py:73
  133.0 38.7 %collective-permute-start.9 = (bf16[128,2048]{1,0:T(8,128)(2,1)S(1)}, bf16[128,2048]{1,0:T(8,128)(2,1)S(1)}, u32[]{:S(2)}, u32[]{:S(2)}) collective-permute-start(bf16[128,2048]{1,0:T(8,128)(2,1)S(1)} %copy-done.71), channel_id=1, source_target_pairs={{0,16},{8,24},{16,0},{24,8},{1,17},{9,25},{17,1},{25,9},{2,18},{10... | collective-permute-start | bytes 1572872 | tf_op jit(solution)/shard_map/ppermute | solution.py:73
  144.7 27.0 %collective-permute-start.11 = (bf16[128,2048]{1,0:T(8,128)(2,1)S(1)}, bf16[128,2048]{1,0:T(8,128)(2,1)S(1)}, u32[]{:S(2)}, u32[]{:S(2)}) collective-permute-start(bf16[128,2048]{1,0:T(8,128)(2,1)S(1)} %get-tuple-element.49), channel_id=1, source_target_pairs={{0,8},{8,0},{16,24},{24,16},{1,9},{9,1},{17,25},{25,17},{2,10},{10... | collective-permute-start | bytes 1572872 | tf_op jit(solution)/shard_map/ppermute | solution.py:73
  176.7 24.6 %collective-permute-start.12 = (bf16[128,2048]{1,0:T(8,128)(2,1)S(1)}, bf16[128,2048]{1,0:T(8,128)(2,1)S(1)}, u32[]{:S(2)}, u32[]{:S(2)}) collective-permute-start(bf16[128,2048]{1,0:T(8,128)(2,1)S(1)} %get-tuple-element.71), channel_id=1, source_target_pairs={{0,8},{8,0},{16,24},{24,16},{1,9},{9,1},{17,25},{25,17},{2,10},{10... | collective-permute-start | bytes 1572872 | tf_op jit(solution)/shard_map/ppermute | solution.py:73
  179.1 22.2 %collective-permute-start.13 = (bf16[128,2048]{1,0:T(8,128)(2,1)S(1)}, bf16[128,2048]{1,0:T(8,128)(2,1)S(1)}, u32[]{:S(2)}, u32[]{:S(2)}) collective-permute-start(bf16[128,2048]{1,0:T(8,128)(2,1)S(1)} %get-tuple-element.69), channel_id=1, source_target_pairs={{0,8},{8,0},{16,24},{24,16},{1,9},{9,1},{17,25},{25,17},{2,10},{10... | collective-permute-start | bytes 1572872 | tf_op jit(solution)/shard_map/ppermute | solution.py:73
  179.8 24.1 %collective-permute-start.15 = (bf16[128,2048]{1,0:T(8,128)(2,1)S(1)}, bf16[128,2048]{1,0:T(8,128)(2,1)S(1)}, u32[]{:S(2)}, u32[]{:S(2)}) collective-permute-start(bf16[128,2048]{1,0:T(8,128)(2,1)S(1)} %get-tuple-element.69), channel_id=1, source_target_pairs={{0,16},{8,24},{16,0},{24,8},{1,17},{9,25},{17,1},{25,9},{2,18},{10... | collective-permute-start | bytes 1572872 | tf_op jit(solution)/shard_map/ppermute | solution.py:73
  190.1 16.8 %collective-permute-start.16 = (bf16[128,2048]{1,0:T(8,128)(2,1)S(1)}, bf16[128,2048]{1,0:T(8,128)(2,1)S(1)}, u32[]{:S(2)}, u32[]{:S(2)}) collective-permute-start(bf16[128,2048]{1,0:T(8,128)(2,1)S(1)} %collective-permute-done.14), channel_id=1, source_target_pairs={{0,8},{8,0},{16,24},{24,16},{1,9},{9,1},{17,25},{25,17},{2,10},{10... | collective-permute-start | bytes 1572872 | tf_op jit(solution)/shard_map/ppermute | solution.py:73
  324.4 23.8 %collective-permute-start.32 = (bf16[128,2048]{1,0:T(8,128)(2,1)S(1)}, bf16[128,2048]{1,0:T(8,128)(2,1)S(1)}, u32[]{:S(2)}, u32[]{:S(2)}) collective-permute-start(bf16[128,2048]{1,0:T(8,128)(2,1)S(1)} %get-tuple-element.41), channel_id=1, source_target_pairs={{0,8},{8,0},{16,24},{24,16},{1,9},{9,1},{17,25},{25,17},{2,10},{10... | collective-permute-start | bytes 1572872 | tf_op jit(solution)/shard_map/ppermute | solution.py:73
  325.0 23.3 %collective-permute-start.34 = (bf16[128,2048]{1,0:T(8,128)(2,1)S(1)}, bf16[128,2048]{1,0:T(8,128)(2,1)S(1)}, u32[]{:S(2)}, u32[]{:S(2)}) collective-permute-start(bf16[128,2048]{1,0:T(8,128)(2,1)S(1)} %get-tuple-element.39), channel_id=1, source_target_pairs={{0,16},{8,24},{16,0},{24,8},{1,17},{9,25},{17,1},{25,9},{2,18},{10... | collective-permute-start | bytes 1572872 | tf_op jit(solution)/shard_map/ppermute | solution.py:73
  339.4 22.3 %collective-permute-start.33 = (bf16[128,2048]{1,0:T(8,128)(2,1)S(1)}, bf16[128,2048]{1,0:T(8,128)(2,1)S(1)}, u32[]{:S(2)}, u32[]{:S(2)}) collective-permute-start(bf16[128,2048]{1,0:T(8,128)(2,1)S(1)} %get-tuple-element.40), channel_id=1, source_target_pairs={{0,16},{8,24},{16,0},{24,8},{1,17},{9,25},{17,1},{25,9},{2,18},{10... | collective-permute-start | bytes 1572872 | tf_op jit(solution)/shard_map/ppermute | solution.py:73
  365.3 27.6 %collective-permute-start.36 = (bf16[128,2048]{1,0:T(8,128)(2,1)S(1)}, bf16[128,2048]{1,0:T(8,128)(2,1)S(1)}, u32[]{:S(2)}, u32[]{:S(2)}) collective-permute-start(bf16[128,2048]{1,0:T(8,128)(2,1)S(1)} %get-tuple-element.66), channel_id=1, source_target_pairs={{0,8},{8,0},{16,24},{24,16},{1,9},{9,1},{17,25},{25,17},{2,10},{10... | collective-permute-start | bytes 1572872 | tf_op jit(solution)/shard_map/ppermute | solution.py:73
  368.3 23.2 %collective-permute-start.37 = (bf16[128,2048]{1,0:T(8,128)(2,1)S(1)}, bf16[128,2048]{1,0:T(8,128)(2,1)S(1)}, u32[]{:S(2)}, u32[]{:S(2)}) collective-permute-start(bf16[128,2048]{1,0:T(8,128)(2,1)S(1)} %get-tuple-element.64), channel_id=1, source_target_pairs={{0,8},{8,0},{16,24},{24,16},{1,9},{9,1},{17,25},{25,17},{2,10},{10... | collective-permute-start | bytes 1572872 | tf_op jit(solution)/shard_map/ppermute | solution.py:73
  368.8 24.2 %collective-permute-start.39 = (bf16[128,2048]{1,0:T(8,128)(2,1)S(1)}, bf16[128,2048]{1,0:T(8,128)(2,1)S(1)}, u32[]{:S(2)}, u32[]{:S(2)}) collective-permute-start(bf16[128,2048]{1,0:T(8,128)(2,1)S(1)} %get-tuple-element.64), channel_id=1, source_target_pairs={{0,16},{8,24},{16,0},{24,8},{1,17},{9,25},{17,1},{25,9},{2,18},{10... | collective-permute-start | bytes 1572872 | tf_op jit(solution)/shard_map/ppermute | solution.py:73
  381.7 16.8 %collective-permute-start.40 = (bf16[128,2048]{1,0:T(8,128)(2,1)S(1)}, bf16[128,2048]{1,0:T(8,128)(2,1)S(1)}, u32[]{:S(2)}, u32[]{:S(2)}) collective-permute-start(bf16[128,2048]{1,0:T(8,128)(2,1)S(1)} %collective-permute-done.38), channel_id=1, source_target_pairs={{0,8},{8,0},{16,24},{24,16},{1,9},{9,1},{17,25},{25,17},{2,10},{10... | collective-permute-start | bytes 1572872 | tf_op jit(solution)/shard_map/ppermute | solution.py:73
  441.7 191.3 %reduce-scatter.6.cloned.1.call-start = ((), (), s32[]{:S(2)}) async-start(), calls=%async_computation.10 | async-start | bytes 4718592 | tf_op jit(solution)/shard_map/reduce_scatter | solution.py:204
  461.2 245.3 %reduce-scatter.10.cloned.1.call-start = ((), (), s32[]{:S(2)}) async-start(), calls=%async_computation.12 | async-start | bytes 7077888 | tf_op jit(solution)/shard_map/reduce_scatter | solution.py:204
  472.8 239.7 %reduce-scatter.12.cloned.1.call-start = ((), (), s32[]{:S(2)}) async-start(), calls=%async_computation.13 | async-start | bytes 7077888 | tf_op jit(solution)/shard_map/reduce_scatter | solution.py:204
  484.3 255.9 %reduce-scatter.14.cloned.1.call-start = ((), (), s32[]{:S(2)}) async-start(), calls=%async_computation.14 | async-start | bytes 7077888 | tf_op jit(solution)/shard_map/reduce_scatter | solution.py:204
  503.5 17.9 %collective-permute-start.42 = (bf16[128,2048]{1,0:T(8,128)(2,1)S(1)}, bf16[128,2048]{1,0:T(8,128)(2,1)S(1)}, u32[]{:S(2)}, u32[]{:S(2)}) collective-permute-start(bf16[128,2048]{1,0:T(8,128)(2,1)S(1)} %get-tuple-element.32), channel_id=1, source_target_pairs={{0,8},{8,0},{16,24},{24,16},{1,9},{9,1},{17,25},{25,17},{2,10},{10... | collective-permute-start | bytes 1572872 | tf_op jit(solution)/shard_map/ppermute | solution.py:73
  504.0 28.6 %collective-permute-start.20 = (bf16[128,2048]{1,0:T(8,128)(2,1)S(1)}, bf16[128,2048]{1,0:T(8,128)(2,1)S(1)}, u32[]{:S(2)}, u32[]{:S(2)}) collective-permute-start(bf16[128,2048]{1,0:T(8,128)(2,1)S(1)} %get-tuple-element.47), channel_id=1, source_target_pairs={{0,8},{8,0},{16,24},{24,16},{1,9},{9,1},{17,25},{25,17},{2,10},{10... | collective-permute-start | bytes 1572872 | tf_op jit(solution)/shard_map/ppermute | solution.py:73
  505.5 28.6 %collective-permute-start.22 = (bf16[128,2048]{1,0:T(8,128)(2,1)}, bf16[128,2048]{1,0:T(8,128)(2,1)S(1)}, u32[]{:S(2)}, u32[]{:S(2)}) collective-permute-start(bf16[128,2048]{1,0:T(8,128)(2,1)} %get-tuple-element.45), channel_id=1, source_target_pairs={{0,16},{8,24},{16,0},{24,8},{1,17},{9,25},{17,1},{25,9},{2,18},{10... | collective-permute-start | bytes 1572872 | tf_op jit(solution)/shard_map/ppermute | solution.py:73
  511.1 23.6 %collective-permute-start.19 = (bf16[128,2048]{1,0:T(8,128)(2,1)}, bf16[128,2048]{1,0:T(8,128)(2,1)}, u32[]{:S(2)}, u32[]{:S(2)}) collective-permute-start(bf16[128,2048]{1,0:T(8,128)(2,1)} %add_convert_fusion.6), channel_id=1, source_target_pairs={{0,16},{8,24},{16,0},{24,8},{1,17},{9,25},{17,1},{25,9},{2,18},{10... | collective-permute-start | bytes 1572872 | tf_op jit(solution)/shard_map/ppermute | solution.py:73
  512.5 31.3 %collective-permute-start.44 = (bf16[128,2048]{1,0:T(8,128)(2,1)}, bf16[128,2048]{1,0:T(8,128)(2,1)S(1)}, u32[]{:S(2)}, u32[]{:S(2)}) collective-permute-start(bf16[128,2048]{1,0:T(8,128)(2,1)} %get-tuple-element.35), channel_id=1, source_target_pairs={{0,8},{8,0},{16,24},{24,16},{1,9},{9,1},{17,25},{25,17},{2,10},{10... | collective-permute-start | bytes 1572872 | tf_op jit(solution)/shard_map/ppermute | solution.py:73
  521.4 23.9 %collective-permute-start.46 = (bf16[128,2048]{1,0:T(8,128)(2,1)}, bf16[128,2048]{1,0:T(8,128)(2,1)S(1)}, u32[]{:S(2)}, u32[]{:S(2)}) collective-permute-start(bf16[128,2048]{1,0:T(8,128)(2,1)} %get-tuple-element.33), channel_id=1, source_target_pairs={{0,16},{8,24},{16,0},{24,8},{1,17},{9,25},{17,1},{25,9},{2,18},{10... | collective-permute-start | bytes 1572872 | tf_op jit(solution)/shard_map/ppermute | solution.py:73
  532.6 21.8 %collective-permute-start.43 = (bf16[128,2048]{1,0:T(8,128)(2,1)}, bf16[128,2048]{1,0:T(8,128)(2,1)}, u32[]{:S(2)}, u32[]{:S(2)}) collective-permute-start(bf16[128,2048]{1,0:T(8,128)(2,1)} %add_convert_fusion.2), channel_id=1, source_target_pairs={{0,16},{8,24},{16,0},{24,8},{1,17},{9,25},{17,1},{25,9},{2,18},{10... | collective-permute-start | bytes 1572872 | tf_op jit(solution)/shard_map/ppermute | solution.py:73
  534.0 32.8 %collective-permute-start.21 = (bf16[128,2048]{1,0:T(8,128)(2,1)}, bf16[128,2048]{1,0:T(8,128)(2,1)}, u32[]{:S(2)}, u32[]{:S(2)}) collective-permute-start(bf16[128,2048]{1,0:T(8,128)(2,1)} %get-tuple-element.46), channel_id=1, source_target_pairs={{0,16},{8,24},{16,0},{24,8},{1,17},{9,25},{17,1},{25,9},{2,18},{10... | collective-permute-start | bytes 1572872 | tf_op jit(solution)/shard_map/ppermute | solution.py:73
  538.1 28.7 %collective-permute-start.23 = (bf16[128,2048]{1,0:T(8,128)(2,1)}, bf16[128,2048]{1,0:T(8,128)(2,1)}, u32[]{:S(2)}, u32[]{:S(2)}) collective-permute-start(bf16[128,2048]{1,0:T(8,128)(2,1)} %get-tuple-element.43), channel_id=1, source_target_pairs={{0,8},{8,0},{16,24},{24,16},{1,9},{9,1},{17,25},{25,17},{2,10},{10... | collective-permute-start | bytes 1572872 | tf_op jit(solution)/shard_map/ppermute | solution.py:73
  543.8 25.8 %collective-permute-start.45 = (bf16[128,2048]{1,0:T(8,128)(2,1)}, bf16[128,2048]{1,0:T(8,128)(2,1)}, u32[]{:S(2)}, u32[]{:S(2)}) collective-permute-start(bf16[128,2048]{1,0:T(8,128)(2,1)} %get-tuple-element.34), channel_id=1, source_target_pairs={{0,16},{8,24},{16,0},{24,8},{1,17},{9,25},{17,1},{25,9},{2,18},{10... | collective-permute-start | bytes 1572872 | tf_op jit(solution)/shard_map/ppermute | solution.py:73
  634.4 65.5 %collective-permute-start.48 = (bf16[128,512]{1,0:T(8,128)(2,1)S(1)}, bf16[128,512]{1,0:T(8,128)(2,1)S(1)}, u32[]{:S(2)}, u32[]{:S(2)}) collective-permute-start(bf16[128,512]{1,0:T(8,128)(2,1)S(1)} %get-tuple-element.90), channel_id=1, source_target_pairs={{0,8},{8,0},{16,24},{24,16},{1,9},{9,1},{17,25},{25,17},{2,10},{10... | collective-permute-start | bytes 393224 | tf_op jit(solution)/shard_map/ppermute | solution.py:73
  635.7 62.9 %collective-permute-start.50 = (bf16[128,512]{1,0:T(8,128)(2,1)S(1)}, bf16[128,512]{1,0:T(8,128)(2,1)S(1)}, u32[]{:S(2)}, u32[]{:S(2)}) collective-permute-start(bf16[128,512]{1,0:T(8,128)(2,1)S(1)} %get-tuple-element.90), channel_id=1, source_target_pairs={{0,16},{8,24},{16,0},{24,8},{1,17},{9,25},{17,1},{25,9},{2,18},{10... | collective-permute-start | bytes 393224 | tf_op jit(solution)/shard_map/ppermute | solution.py:73
  636.0 63.6 %collective-permute-start.49 = (bf16[128,512]{1,0:T(8,128)(2,1)S(1)}, bf16[128,512]{1,0:T(8,128)(2,1)S(1)}, u32[]{:S(2)}, u32[]{:S(2)}) collective-permute-start(bf16[128,512]{1,0:T(8,128)(2,1)S(1)} %get-tuple-element.89), channel_id=1, source_target_pairs={{0,8},{8,0},{16,24},{24,16},{1,9},{9,1},{17,25},{25,17},{2,10},{10... | collective-permute-start | bytes 393224 | tf_op jit(solution)/shard_map/ppermute | solution.py:73
  636.9 65.2 %collective-permute-start.51 = (bf16[128,512]{1,0:T(8,128)(2,1)S(1)}, bf16[128,512]{1,0:T(8,128)(2,1)S(1)}, u32[]{:S(2)}, u32[]{:S(2)}) collective-permute-start(bf16[128,512]{1,0:T(8,128)(2,1)S(1)} %get-tuple-element.89), channel_id=1, source_target_pairs={{0,16},{8,24},{16,0},{24,8},{1,17},{9,25},{17,1},{25,9},{2,18},{10... | collective-permute-start | bytes 393224 | tf_op jit(solution)/shard_map/ppermute | solution.py:73
  708.4 34.0 %collective-permute-start.72 = (bf16[128,1536]{1,0:T(8,128)(2,1)}, bf16[128,1536]{1,0:T(8,128)(2,1)}, u32[]{:S(2)}, u32[]{:S(2)}) collective-permute-start(bf16[128,1536]{1,0:T(8,128)(2,1)} %get-tuple-element.82), channel_id=1, source_target_pairs={{0,8},{8,0},{16,24},{24,16},{1,9},{9,1},{17,25},{25,17},{2,10},{10... | collective-permute-start | bytes 1179656 | tf_op jit(solution)/shard_map/ppermute | solution.py:73
  709.5 38.8 %collective-permute-start.74 = (bf16[128,1536]{1,0:T(8,128)(2,1)}, bf16[128,1536]{1,0:T(8,128)(2,1)}, u32[]{:S(2)}, u32[]{:S(2)}) collective-permute-start(bf16[128,1536]{1,0:T(8,128)(2,1)} %get-tuple-element.82), channel_id=1, source_target_pairs={{0,16},{8,24},{16,0},{24,8},{1,17},{9,25},{17,1},{25,9},{2,18},{10... | collective-permute-start | bytes 1179656 | tf_op jit(solution)/shard_map/ppermute | solution.py:73
  710.1 35.8 %collective-permute-start.73 = (bf16[128,1536]{1,0:T(8,128)(2,1)S(1)}, bf16[128,1536]{1,0:T(8,128)(2,1)S(1)}, u32[]{:S(2)}, u32[]{:S(2)}) collective-permute-start(bf16[128,1536]{1,0:T(8,128)(2,1)S(1)} %get-tuple-element.81), channel_id=1, source_target_pairs={{0,8},{8,0},{16,24},{24,16},{1,9},{9,1},{17,25},{25,17},{2,10},{10... | collective-permute-start | bytes 1179656 | tf_op jit(solution)/shard_map/ppermute | solution.py:73
  711.1 39.7 %collective-permute-start.75 = (bf16[128,1536]{1,0:T(8,128)(2,1)S(1)}, bf16[128,1536]{1,0:T(8,128)(2,1)S(1)}, u32[]{:S(2)}, u32[]{:S(2)}) collective-permute-start(bf16[128,1536]{1,0:T(8,128)(2,1)S(1)} %get-tuple-element.81), channel_id=1, source_target_pairs={{0,16},{8,24},{16,0},{24,8},{1,17},{9,25},{17,1},{25,9},{2,18},{10... | collective-permute-start | bytes 1179656 | tf_op jit(solution)/shard_map/ppermute | solution.py:73
  713.7 38.7 %collective-permute-start.78 = (bf16[128,1536]{1,0:T(8,128)(2,1)S(1)}, bf16[128,1536]{1,0:T(8,128)(2,1)}, u32[]{:S(2)}, u32[]{:S(2)}) collective-permute-start(bf16[128,1536]{1,0:T(8,128)(2,1)S(1)} %get-tuple-element.80), channel_id=1, source_target_pairs={{0,8},{8,0},{16,24},{24,16},{1,9},{9,1},{17,25},{25,17},{2,10},{10... | collective-permute-start | bytes 1179656 | tf_op jit(solution)/shard_map/ppermute | solution.py:73
  742.4 18.0 %collective-permute-start.80 = (bf16[128,1536]{1,0:T(8,128)(2,1)S(1)}, bf16[128,1536]{1,0:T(8,128)(2,1)S(1)}, u32[]{:S(2)}, u32[]{:S(2)}) collective-permute-start(bf16[128,1536]{1,0:T(8,128)(2,1)S(1)} %get-tuple-element.80), channel_id=1, source_target_pairs={{0,16},{8,24},{16,0},{24,8},{1,17},{9,25},{17,1},{25,9},{2,18},{10... | collective-permute-start | bytes 1179656 | tf_op jit(solution)/shard_map/ppermute | solution.py:73
  752.3 24.0 %collective-permute-start.86 = (bf16[128,1536]{1,0:T(8,128)(2,1)S(1)}, bf16[128,1536]{1,0:T(8,128)(2,1)S(1)}, u32[]{:S(2)}, u32[]{:S(2)}) collective-permute-start(bf16[128,1536]{1,0:T(8,128)(2,1)S(1)} %get-tuple-element.78), channel_id=1, source_target_pairs={{0,16},{8,24},{16,0},{24,8},{1,17},{9,25},{17,1},{25,9},{2,18},{10... | collective-permute-start | bytes 1179656 | tf_op jit(solution)/shard_map/ppermute | solution.py:73
  757.9 16.9 %collective-permute-start.85 = (bf16[128,1536]{1,0:T(8,128)(2,1)S(1)}, bf16[128,1536]{1,0:T(8,128)(2,1)S(1)}, u32[]{:S(2)}, u32[]{:S(2)}) collective-permute-start(bf16[128,1536]{1,0:T(8,128)(2,1)S(1)} %get-tuple-element.77), channel_id=1, source_target_pairs={{0,8},{8,0},{16,24},{24,16},{1,9},{9,1},{17,25},{25,17},{2,10},{10... | collective-permute-start | bytes 1179656 | tf_op jit(solution)/shard_map/ppermute | solution.py:73
  760.4 19.2 %collective-permute-start.87 = (bf16[128,1536]{1,0:T(8,128)(2,1)S(1)}, bf16[128,1536]{1,0:T(8,128)(2,1)S(1)}, u32[]{:S(2)}, u32[]{:S(2)}) collective-permute-start(bf16[128,1536]{1,0:T(8,128)(2,1)S(1)} %get-tuple-element.77), channel_id=1, source_target_pairs={{0,16},{8,24},{16,0},{24,8},{1,17},{9,25},{17,1},{25,9},{2,18},{10... | collective-permute-start | bytes 1179656 | tf_op jit(solution)/shard_map/ppermute | solution.py:73
  762.7 20.5 %collective-permute-start.76 = (bf16[128,1536]{1,0:T(8,128)(2,1)}, bf16[128,1536]{1,0:T(8,128)(2,1)S(1)}, u32[]{:S(2)}, u32[]{:S(2)}) collective-permute-start(bf16[128,1536]{1,0:T(8,128)(2,1)} %collective-permute-done.74), channel_id=1, source_target_pairs={{0,8},{8,0},{16,24},{24,16},{1,9},{9,1},{17,25},{25,17},{2,10},{10... | collective-permute-start | bytes 1179656 | tf_op jit(solution)/shard_map/ppermute | solution.py:73
  766.4 21.6 %collective-permute-start.77 = (bf16[128,1536]{1,0:T(8,128)(2,1)S(1)}, bf16[128,1536]{1,0:T(8,128)(2,1)S(1)}, u32[]{:S(2)}, u32[]{:S(2)}) collective-permute-start(bf16[128,1536]{1,0:T(8,128)(2,1)S(1)} %collective-permute-done.73), channel_id=1, source_target_pairs={{0,16},{8,24},{16,0},{24,8},{1,17},{9,25},{17,1},{25,9},{2,18},{10... | collective-permute-start | bytes 1179656 | tf_op jit(solution)/shard_map/ppermute | solution.py:73
  774.8 16.9 %collective-permute-start.82 = (bf16[128,1536]{1,0:T(8,128)(2,1)S(1)}, bf16[128,1536]{1,0:T(8,128)(2,1)S(1)}, u32[]{:S(2)}, u32[]{:S(2)}) collective-permute-start(bf16[128,1536]{1,0:T(8,128)(2,1)S(1)} %collective-permute-done.80), channel_id=1, source_target_pairs={{0,8},{8,0},{16,24},{24,16},{1,9},{9,1},{17,25},{25,17},{2,10},{10... | collective-permute-start | bytes 1179656 | tf_op jit(solution)/shard_map/ppermute | solution.py:73
  776.3 20.0 %collective-permute-start.83 = (bf16[128,1536]{1,0:T(8,128)(2,1)S(1)}, bf16[128,1536]{1,0:T(8,128)(2,1)S(1)}, u32[]{:S(2)}, u32[]{:S(2)}) collective-permute-start(bf16[128,1536]{1,0:T(8,128)(2,1)S(1)} %collective-permute-done.79), channel_id=1, source_target_pairs={{0,16},{8,24},{16,0},{24,8},{1,17},{9,25},{17,1},{25,9},{2,18},{10... | collective-permute-start | bytes 1179656 | tf_op jit(solution)/shard_map/ppermute | solution.py:73
  779.5 17.8 %collective-permute-start.88 = (bf16[128,1536]{1,0:T(8,128)(2,1)S(1)}, bf16[128,1536]{1,0:T(8,128)(2,1)S(1)}, u32[]{:S(2)}, u32[]{:S(2)}) collective-permute-start(bf16[128,1536]{1,0:T(8,128)(2,1)S(1)} %collective-permute-done.86), channel_id=1, source_target_pairs={{0,8},{8,0},{16,24},{24,16},{1,9},{9,1},{17,25},{25,17},{2,10},{10... | collective-permute-start | bytes 1179656 | tf_op jit(solution)/shard_map/ppermute | solution.py:73
  783.2 18.5 %collective-permute-start.89 = (bf16[128,1536]{1,0:T(8,128)(2,1)S(1)}, bf16[128,1536]{1,0:T(8,128)(2,1)S(1)}, u32[]{:S(2)}, u32[]{:S(2)}) collective-permute-start(bf16[128,1536]{1,0:T(8,128)(2,1)S(1)} %collective-permute-done.85), channel_id=1, source_target_pairs={{0,16},{8,24},{16,0},{24,8},{1,17},{9,25},{17,1},{25,9},{2,18},{10... | collective-permute-start | bytes 1179656 | tf_op jit(solution)/shard_map/ppermute | solution.py:73
  (127 other events, 1506.5 us)
Sparse Core Ops, SparseCore 0:
  10.4 49.8 all-gather.5
  62.4 27.8 all-gather.7
  92.5 64.2 all-gather.9
  158.9 63.3 all-gather.11
  223.8 63.3 all-gather.13
  441.9 34.4 reduce-scatter.7
  478.6 48.6 reduce-scatter.5
  530.1 68.6 reduce-scatter.9
  601.7 68.1 reduce-scatter.11
  672.0 68.1 reduce-scatter.13

commit v2 on v1

v2 whole, which is shorter than its diff:
```python
import functools

import jax
import jax.numpy as jnp
from jax import lax
from jax.experimental import pallas as pl
from jax.experimental.pallas import tpu as pltpu
from jax.sharding import PartitionSpec as P

QUERY_HEADS = 16
KEY_VALUE_HEADS = 8
HEAD_SIZE = 128
NORM_EPSILON = 1e-06
ROPE_BASE = 1000000.0
SCORE_FLOOR = -1e30
F32 = jnp.float32
BF16 = jnp.bfloat16
TINY = pl.CostEstimate(flops=1000, bytes_accessed=1000, transcendentals=0)


def dot(a, b):
    return jnp.dot(a, b, preferred_element_type=F32)


def dot_nt(a, b):
    return lax.dot_general(a, b, (((1,), (1,)), ((), ())), preferred_element_type=F32)


def dot_tn(a, b):
    return lax.dot_general(a, b, (((0,), (0,)), ((), ())), preferred_element_type=F32)


def inverse_rms(u):
    return lax.rsqrt(jnp.mean(u * u, axis=-1, keepdims=True) + NORM_EPSILON)


def norm_back(u, gain, e):
    w = inverse_rms(u)
    n = u * w
    t = e * gain
    du = w * (t - n * jnp.mean(n * t, axis=-1, keepdims=True))
    return du, e * n


def positions(segments):
    index = jnp.arange(segments.shape[0], dtype=jnp.int32)
    first = jnp.concatenate([jnp.ones((1,), dtype=jnp.bool_), segments[1:] != segments[:-1]])
    starts = lax.cummax(jnp.where(first, index, jnp.zeros_like(index)), axis=0)
    return index - starts


def rotary_tables(position_index):
    half = HEAD_SIZE // 2
    freq = ROPE_BASE ** (-jnp.arange(half, dtype=F32) * 2.0 / HEAD_SIZE)
    angle = position_index.astype(F32)[:, None] * freq[None, :]
    cosine, sine = jnp.cos(angle), jnp.sin(angle)
    return jnp.concatenate([cosine, cosine], axis=-1), jnp.concatenate([-sine, sine], axis=-1)


def by_neighbours(count):
    return count == 4


def swap(x, side):
    return lax.ppermute(x, "seq", [(s, s ^ side) for s in range(4)])


class Scatter:
    def __init__(self, partial, count):
        self.partial, self.count = partial, count
        self.square = by_neighbours(count)
        self.rows = partial.shape[0] // count
        self.me = lax.axis_index("seq")

    def block(self, k, start, size):
        at = ((self.me ^ k) * self.rows + start, 0)
        return lax.dynamic_slice(self.partial, at, (size, self.partial.shape[1]))

    def first(self):
        if not self.square:
            return [self.partial]
        half = self.rows // 2
        self.tx = swap(self.block(3, 0, half), 1)
        self.ty = swap(self.block(3, half, half), 2)
        return [self.tx, self.ty]

    def second(self, *others):
        if not self.square:
            self.sent = [self.partial]
            self.sum = lax.psum_scatter(self.partial, "seq", scatter_dimension=0, tiled=True)
            return [self.sum]
        zero = jnp.zeros((self.rows // 2, self.partial.shape[1]), F32)
        sx = self.block(1, 0, self.rows).astype(F32) + jnp.concatenate([zero, self.ty.astype(F32)])
        sy = self.block(2, 0, self.rows).astype(F32) + jnp.concatenate([self.tx.astype(F32), zero])
        sx, sy = sx.astype(BF16), sy.astype(BF16)
        if others:
            sx, sy, *_ = lax.optimization_barrier((sx, sy, *others))
        self.sent = [sx, sy]
        self.rx, self.ry = swap(sx, 1), swap(sy, 2)
        return [self.rx, self.ry]

    def finish(self):
        if not self.square:
            return self.sum.astype(F32)
        own = self.block(0, 0, self.rows).astype(F32)
        return own + self.rx.astype(F32) + self.ry.astype(F32)


class Gather:
    def __init__(self, x, count):
        self.x, self.count = x, count
        self.square = by_neighbours(count)
        self.me = lax.axis_index("seq")

    def first(self):
        if not self.square:
            return [self.x]
        self.bx, self.by = swap(self.x, 1), swap(self.x, 2)
        return [self.bx, self.by]

    def second(self, *others):
        if not self.square:
            self.sent = self.x
            return [self.x]
        half = self.x.shape[0] // 2
        ahead, below = self.by[:half], self.bx[half:]
        if others:
            ahead, below, *_ = lax.optimization_barrier((ahead, below, *others))
        self.sent = ahead
        self.ad, self.bd = swap(ahead, 1), swap(below, 2)
        return [self.ad, self.bd]

    def column(self):
        if not self.square:
            return lax.all_gather(self.x, "seq", axis=0, tiled=True)
        rows = self.x.shape[0]
        out = jnp.zeros((self.count * rows,) + self.x.shape[1:], self.x.dtype)
        pieces = (
            (0, 0, self.x),
            (1, 0, self.bx),
            (2, 0, self.by),
            (3, 0, self.ad),
            (3, rows // 2, self.bd),
        )
        for k, start, piece in pieces:
            out = lax.dynamic_update_slice(out, piece, ((self.me ^ k) * rows + start, 0))
        return out

    def slots(self):
        if not self.square:
            every = lax.all_gather(self.x, "seq", axis=0, tiled=False)
            return [every[k] for k in range(self.count)]
        return [self.x, self.bx, self.by, jnp.concatenate([self.ad, self.bd], axis=0)]


def after(x, *others):
    return lax.optimization_barrier((x, *others))[0]


def in_line(count):
    return count == 8


def gather_weight(w):
    return lax.all_gather(w, "fsdp", axis=0, tiled=True)


def terms_kernel(starts, order_ref, *refs):
    count = len(starts)
    x_refs, d_ref = refs[:count], refs[count]
    out_ref = refs[-1]
    j = pl.program_id(0)
    for n, x_ref in enumerate(x_refs):
        last = starts[n + 1] if n + 1 < count else pl.num_programs(0)

        @pl.when((j >= starts[n]) & (j < last))
        def _():
            total = dot_tn(x_ref[...], d_ref[...])
            if len(refs) == count + 3:
                total = total + refs[count + 1][0].astype(F32)
            out_ref[0] = total.astype(BF16)


def weight_terms(xs, d, rows, order, got=None):
    length, blocks = d.shape[0], order.shape[0]
    tiles = sum(n for _, n in xs)
    width = d.shape[1] // tiles
    starts = [sum(n for _, n in xs[:m]) for m in range(len(xs))]

    def x_map(first, n):
        def index(j, i, order_ref):
            here = (j >= first) & (j < first + n)
            return 0, order_ref[jnp.where(here, i, jnp.where(j < first, 0, blocks - 1))]

        return index

    def out_map(j, i, order_ref):
        return i, 0, j

    in_specs = [
        pl.BlockSpec((length, rows), x_map(first, n)) for first, (_, n) in zip(starts, xs)
    ] + [pl.BlockSpec((length, width), lambda j, i, order_ref: (0, j))]
    operands = [x for x, _ in xs] + [d]
    if got is not None:
        in_specs.append(pl.BlockSpec((1, rows, width), out_map))
        operands.append(got)
    return pl.pallas_call(
        functools.partial(terms_kernel, starts),
        grid_spec=pltpu.PrefetchScalarGridSpec(
            num_scalar_prefetch=1,
            grid=(tiles, blocks),
            in_specs=in_specs,
            out_specs=pl.BlockSpec((1, rows, width), out_map),
        ),
        out_shape=jax.ShapeDtypeStruct((blocks, rows, d.shape[1]), BF16),
        compiler_params=pltpu.CompilerParams(vmem_limit_bytes=40 << 20),
        cost_estimate=TINY,
        name="weight_terms",
    )(order, *operands)


def all_terms(xs, d, rows, count):
    terms = weight_terms(xs, d, rows, jnp.arange(count, dtype=jnp.int32))
    return terms.reshape(count * rows, d.shape[1])


def sum_terms(terms):
    return lax.psum_scatter(terms, "fsdp", scatter_dimension=0, tiled=True)


def sum_all(x, axis, count):
    if count & (count - 1):
        return lax.psum(x, axis)
    bit = 1
    while bit < count:
        x = x + lax.ppermute(x, axis, [(i, i ^ bit) for i in range(count)])
        bit *= 2
    return x


ROWS = 256
SCALE = HEAD_SIZE ** (-0.5)


def head_norm_rope(u, gain, cosine, sine):
    w = inverse_rms(u)
    t = u * w * gain
    return (t * cosine + pltpu.roll(t, HEAD_SIZE // 2, 1) * sine).astype(BF16)


def head_norm_rope_back(u, gain, cosine, sine, e):
    e = e * cosine - pltpu.roll(e, HEAD_SIZE // 2, 1) * sine
    return norm_back(u, gain, e)


def heads_of(refs, gains, cosine, sine, ratio):
    q_ref, k_ref = refs
    queries = [
        head_norm_rope(
            q_ref[:, h * HEAD_SIZE : (h + 1) * HEAD_SIZE].astype(F32), gains[0], cosine, sine
        )
        for h in range(ratio)
    ]
    return queries, head_norm_rope(k_ref[...].astype(F32), gains[1], cosine, sine)


def softmax_rows(queries, key, column, row, i, keys):
    stacked = jnp.concatenate([q[i * ROWS : (i + 1) * ROWS] for q in queries], axis=0)
    s = dot_nt(stacked, key[:keys]) * SCALE
    ids = jnp.concatenate([column[i * ROWS : (i + 1) * ROWS]] * len(queries), axis=0)
    place = lax.broadcasted_iota(jnp.int32, s.shape, 0) % ROWS + i * ROWS
    allowed = (ids == row[:, :keys]) & (lax.broadcasted_iota(jnp.int32, s.shape, 1) <= place)
    s = jnp.where(allowed, s, SCORE_FLOOR)
    p = jnp.exp(s - jnp.max(s, axis=-1, keepdims=True))
    return stacked, p * (1.0 / jnp.sum(p, axis=-1, keepdims=True))


def attend_kernel(
    ratio, q_ref, k_ref, v_ref, cos_ref, sin_ref, col_ref, row_ref, qg_ref, kg_ref, o_ref
):
    gains = qg_ref[...], kg_ref[...]
    queries, key = heads_of((q_ref, k_ref), gains, cos_ref[...], sin_ref[...], ratio)
    column, row = col_ref[...], row_ref[...]
    for i in range(q_ref.shape[0] // ROWS):
        keys = (i + 1) * ROWS
        _, p = softmax_rows(queries, key, column, row, i, keys)
        o = dot(p.astype(BF16), v_ref[:keys, :])
        for h in range(ratio):
            o_ref[i * ROWS : keys, h * HEAD_SIZE : (h + 1) * HEAD_SIZE] = o[
                h * ROWS : (h + 1) * ROWS
            ].astype(BF16)


def attend_back_kernel(
    ratio,
    q_ref,
    k_ref,
    v_ref,
    cos_ref,
    sin_ref,
    col_ref,
    row_ref,
    qg_ref,
    kg_ref,
    do_ref,
    dq_ref,
    dk_ref,
    dv_ref,
    qgg_ref,
    kgg_ref,
    dq_all,
    dk_all,
    dv_all,
):
    gains = qg_ref[...], kg_ref[...]
    cosine, sine = cos_ref[...], sin_ref[...]
    queries, key = heads_of((q_ref, k_ref), gains, cosine, sine, ratio)
    column, row = col_ref[...], row_ref[...]
    dk_all[...] = jnp.zeros_like(dk_all)
    dv_all[...] = jnp.zeros_like(dv_all)
    for i in range(q_ref.shape[0] // ROWS):
        keys = (i + 1) * ROWS
        stacked, p = softmax_rows(queries, key, column, row, i, keys)
        do = jnp.concatenate(
            [do_ref[i * ROWS : keys, h * HEAD_SIZE : (h + 1) * HEAD_SIZE] for h in range(ratio)],
            axis=0,
        )
        dp = dot_nt(do, v_ref[:keys, :])
        delta = jnp.sum(p * dp, axis=-1, keepdims=True)
        ds = (p * (dp - delta) * SCALE).astype(BF16)
        dq = dot(ds, key[:keys])
        for h in range(ratio):
            dq_all[h, i * ROWS : keys, :] = dq[h * ROWS : (h + 1) * ROWS]
        dk_all[:keys, :] += dot_tn(ds, stacked)
        dv_all[:keys, :] += dot_tn(p.astype(BF16), do)

    q_terms = jnp.zeros((1, HEAD_SIZE), F32)
    for h in range(ratio):
        columns = slice(h * HEAD_SIZE, (h + 1) * HEAD_SIZE)
        du, terms = head_norm_rope_back(
            q_ref[:, columns].astype(F32), gains[0], cosine, sine, dq_all[h]
        )
        dq_ref[:, columns] = du.astype(BF16)
        q_terms = q_terms + jnp.sum(terms, axis=0, keepdims=True)
    du, terms = head_norm_rope_back(k_ref[...].astype(F32), gains[1], cosine, sine, dk_all[...])
    dk_ref[...] = du.astype(BF16)
    dv_ref[...] = dv_all[...].astype(BF16)
    qgg_ref[0] = q_terms
    kgg_ref[0] = jnp.sum(terms, axis=0, keepdims=True)


def attention_specs(length, q_heads, kv_heads):
    ratio = q_heads // kv_heads
    wide = pl.BlockSpec((length, ratio * HEAD_SIZE), lambda g: (0, g))
    narrow = pl.BlockSpec((length, HEAD_SIZE), lambda g: (0, g))
    table = pl.BlockSpec((length, HEAD_SIZE), lambda g: (0, 0))
    gain = pl.BlockSpec((1, HEAD_SIZE), lambda g: (0, 0))
    inputs = [
        wide,
        pl.BlockSpec((length, HEAD_SIZE), lambda g: (0, q_heads + g)),
        pl.BlockSpec((length, HEAD_SIZE), lambda g: (0, q_heads + kv_heads + g)),
        table,
        table,
        pl.BlockSpec((length, 1), lambda g: (0, 0)),
        pl.BlockSpec((1, length), lambda g: (0, 0)),
        gain,
        gain,
    ]
    return ratio, wide, narrow, inputs


def attention_cost(length, q_heads, products):
    flops = products * q_heads * length * length * HEAD_SIZE
    return pl.CostEstimate(
        flops=flops, bytes_accessed=16 * length * q_heads * HEAD_SIZE, transcendentals=q_heads * length * length
    )


def attend(qkv, tables, ids, gains, q_heads, kv_heads):
    length = qkv.shape[0]
    ratio, wide, _, inputs = attention_specs(length, q_heads, kv_heads)
    return pl.pallas_call(
        functools.partial(attend_kernel, ratio),
        grid=(kv_heads,),
        in_specs=inputs,
        out_specs=wide,
        out_shape=jax.ShapeDtypeStruct((length, q_heads * HEAD_SIZE), BF16),
        compiler_params=pltpu.CompilerParams(vmem_limit_bytes=56 << 20),
        cost_estimate=TINY,
        name="attend",
    )(qkv, qkv, qkv, *tables, *ids, *gains)


def attend_back(qkv, tables, ids, gains, d_o, q_heads, kv_heads):
    length = qkv.shape[0]
    ratio, wide, narrow, inputs = attention_specs(length, q_heads, kv_heads)
    gain_spec = pl.BlockSpec((1, 1, HEAD_SIZE), lambda g: (g, 0, 0))
    gain_shape = jax.ShapeDtypeStruct((kv_heads, 1, HEAD_SIZE), F32)
    kv_shape = jax.ShapeDtypeStruct((length, kv_heads * HEAD_SIZE), BF16)
    return pl.pallas_call(
        functools.partial(attend_back_kernel, ratio),
        grid=(kv_heads,),
        in_specs=inputs + [wide],
        out_specs=(wide, narrow, narrow, gain_spec, gain_spec),
        out_shape=(
            jax.ShapeDtypeStruct((length, q_heads * HEAD_SIZE), BF16),
            kv_shape,
            kv_shape,
            gain_shape,
            gain_shape,
        ),
        scratch_shapes=[
            pltpu.VMEM((ratio, length, HEAD_SIZE), F32),
            pltpu.VMEM((length, HEAD_SIZE), F32),
            pltpu.VMEM((length, HEAD_SIZE), F32),
        ],
        compiler_params=pltpu.CompilerParams(vmem_limit_bytes=56 << 20),
        cost_estimate=TINY,
        name="attend_back",
    )(qkv, qkv, qkv, *tables, *ids, *gains, d_o)


def feed_forward_kernel(carried, piece, xb_ref, dy_ref, w_ref, *refs):
    sums = refs[:2] if carried else (None, None)
    d_ref, dxb_ref, out_ref = refs[-3:]
    xb, dy = xb_ref[...], dy_ref[...]
    gate = dot(xb, w_ref[:, :piece])
    upper = dot(xb, w_ref[:, piece : 2 * piece])
    d_hidden = dot(dy, w_ref[:, 2 * piece :])
    sigma = 1.0 / (1.0 + jnp.exp(-gate))
    silu = gate * sigma
    hidden = (silu * upper).astype(BF16)
    d_gate = (d_hidden * upper * sigma * (1.0 + gate * (1.0 - sigma))).astype(BF16)
    d_up = (d_hidden * silu).astype(BF16)
    d_ref[:, :piece] = d_gate
    d_ref[:, piece : 2 * piece] = d_up
    d_ref[:, 2 * piece :] = hidden
    d_xb = dot_nt(d_gate, w_ref[:, :piece]) + dot_nt(d_up, w_ref[:, piece : 2 * piece])
    out = dot_nt(hidden, w_ref[:, 2 * piece :])
    if carried:
        d_xb = d_xb + sums[0][...]
        out = out + sums[1][...]
    dxb_ref[...] = d_xb.astype(dxb_ref.dtype)
    out_ref[...] = out.astype(out_ref.dtype)


def feed_forward(xb, dy, w, sums, last):
    length, width = xb.shape
    piece = w.shape[1] // 3
    rows = pl.BlockSpec((ROWS, width), lambda i: (i, 0))
    whole = pl.BlockSpec(w.shape, lambda i: (0, 0), pipeline_mode=pl.Buffered(1))
    total = jax.ShapeDtypeStruct((length, width), BF16 if last else F32)
    return pl.pallas_call(
        functools.partial(feed_forward_kernel, bool(sums), piece),
        grid=(length // ROWS,),
        in_specs=[rows, rows, whole] + [rows] * len(sums),
        out_specs=(pl.BlockSpec((ROWS, 3 * piece), lambda i: (i, 0)), rows, rows),
        out_shape=(jax.ShapeDtypeStruct((length, 3 * piece), BF16), total, total),
        compiler_params=pltpu.CompilerParams(vmem_limit_bytes=60 << 20),
        cost_estimate=TINY,
        name="feed_forward",
    )(xb, dy, w, *sums)


def place_kernel(widths, tiles, me_ref, *refs):
    outs = refs[-len(widths) :]
    k, t = pl.program_id(0), pl.program_id(1)
    for n in range(pl.num_programs(0)):
        for m in range(tiles):

            @pl.when((k == n) & (t == m))
            def _():
                start = 0
                for out_ref, width in zip(outs, widths):
                    size = width // tiles
                    at = start + m * size
                    out_ref[...] = refs[n][:, at : at + size].astype(F32)
                    start += width


def place(slots, widths, tiles, first, every, outs, me, count):
    rows = slots[0].shape[0]
    square = by_neighbours(count)

    def out_map(k, t, me_ref):
        member = jnp.bitwise_xor(me_ref[0], k) if square else k
        return 0, member * every + first + t

    any_spec = pl.BlockSpec(memory_space=pl.ANY)
    n = len(slots)
    return pl.pallas_call(
        functools.partial(place_kernel, widths, tiles),
        grid_spec=pltpu.PrefetchScalarGridSpec(
            num_scalar_prefetch=1,
            grid=(count, tiles),
            in_specs=[pl.BlockSpec(s.shape, lambda k, t, me_ref: (0, 0)) for s in slots]
            + [any_spec] * len(outs),
            out_specs=[pl.BlockSpec((rows, w // tiles), out_map) for w in widths],
        ),
        out_shape=[
            jax.ShapeDtypeStruct((rows, w // tiles * every * count), F32) for w in widths
        ],
        input_output_aliases={1 + n + m: m for m in range(len(outs))},
        compiler_params=pltpu.CompilerParams(vmem_limit_bytes=40 << 20),
        name="place",
        cost_estimate=TINY,
    )(jnp.reshape(me, (1,)).astype(jnp.int32), *slots, *outs)


def make_body(counts):
    seq_count, fsdp_count = counts["seq"], counts["fsdp"]

    def body(
        tokens,
        segment_ids,
        input_gain,
        query_weight,
        key_projection_weight,
        value_projection_weight,
        output_weight,
        query_gain,
        key_gain,
        post_gain,
        gate_weight,
        up_weight,
        down_weight,
        cotangent,
    ):
        me = lax.axis_index("seq")
        rows = query_weight.shape[0]
        q_heads = QUERY_HEADS // seq_count
        kv_heads = KEY_VALUE_HEADS // seq_count
        ratio = QUERY_HEADS // KEY_VALUE_HEADS
        q_cols, kv_cols = q_heads * HEAD_SIZE, kv_heads * HEAD_SIZE
        qkv_cols = q_cols + 2 * kv_cols
        f_cols = gate_weight.shape[1] // seq_count
        pieces = (f_cols // 3 * 2, f_cols // 3)
        def share(w, cols, start=0, size=None):
            return lax.dynamic_slice(w, (0, me * cols + start), (rows, size or cols))

        w_attn = gather_weight(
            jnp.concatenate(
                [
                    share(query_weight, q_cols),
                    share(key_projection_weight, kv_cols),
                    share(value_projection_weight, kv_cols),
                    share(output_weight, q_cols),
                ],
                axis=1,
            )
        )
        w_qkv, w_out = w_attn[:, :qkv_cols], w_attn[:, qkv_cols:]
        w_mlp = [
            gather_weight(
                jnp.concatenate(
                    [share(w, f_cols, start, size) for w in (gate_weight, up_weight, down_weight)],
                    axis=1,
                )
            )
            for start, size in zip((0, pieces[0]), pieces)
        ]

        inputs = tokens[0].astype(F32)
        segments = segment_ids[0]
        get_dy = Gather(cotangent[0], seq_count)
        get_xa = Gather((inputs * inverse_rms(inputs) * input_gain).astype(BF16), seq_count)
        got = get_xa.first()
        get_dy.x = after(get_dy.x, *got)
        get_xa.second()
        get_dy.first()
        xa = get_xa.column()

        tables = rotary_tables(positions(segments))
        ids = segments[:, None], segments[None, :]
        head_gains = query_gain[None, :], key_gain[None, :]
        qkv = dot(xa, w_qkv).astype(BF16)
        get_dy.second(qkv)
        dy = get_dy.column()
        o = attend(qkv, tables, ids, head_gains, q_heads, kv_heads)
        sum_r = Scatter(dot_nt(after(o, dy), w_out).astype(BF16), seq_count)
        sum_r.first()
        sum_r.second()
        resid = inputs + sum_r.finish()
        get_xb = Gather((resid * inverse_rms(resid) * post_gain).astype(BF16), seq_count)
        get_xb.first()
        get_xb.second()
        xb = get_xb.column()

        d1, *sums = feed_forward(xb, dy, w_mlp[0], (), False)
        terms1 = all_terms([(xb, 2), (dy, 1)], d1, rows, fsdp_count)
        share1 = sum_terms(terms1)
        d2, d_xb, out = feed_forward(after(xb, terms1), dy, w_mlp[1], tuple(sums), True)
        sum_dxb = Scatter(d_xb, seq_count)
        sum_dxb.first()
        got = sum_dxb.second()
        terms2 = all_terms([(xb, 2), (dy, 1)], after(d2, *sum_dxb.sent), rows, fsdp_count)
        du, post_terms = norm_back(resid, post_gain, after(sum_dxb.finish(), terms2))
        d_resid = cotangent[0].astype(F32) + du
        get_drl = Gather(d_resid.astype(BF16), seq_count)
        get_drl.first()
        get_drl.second()
        drl = get_drl.column()
        sum_out = Scatter(after(out, drl), seq_count)
        sum_out.first()
        d_o = dot(drl, w_out).astype(BF16)
        got = sum_out.second(d_o)
        share2 = sum_terms(after(terms2, share1, *sum_out.sent))
        dq, dk, dv, q_terms, k_terms = attend_back(
            qkv, tables, ids, head_gains, after(d_o, *sum_out.sent), q_heads, kv_heads
        )
        d_attn = jnp.concatenate([dq, dk, dv, o], axis=1)
        out = resid + sum_out.finish()
        d_attn, out = lax.optimization_barrier((d_attn, out))
        sum_dxa = Scatter(dot_nt(d_attn[:, :qkv_cols], w_qkv).astype(BF16), seq_count)
        sum_dxa.first()
        sum_dxa.second()
        terms3 = all_terms([(xa, 2), (drl, 1)], after(d_attn, *sum_dxa.sent), rows, fsdp_count)
        share3 = sum_terms(after(terms3, share2))
        du, in_terms = norm_back(inputs, input_gain, after(sum_dxa.finish(), terms3))
        d_inputs = d_resid + du

        gains = jnp.concatenate(
            [
                jnp.sum(in_terms, axis=0),
                jnp.sum(post_terms, axis=0),
                jnp.sum(q_terms, axis=(0, 1)),
                jnp.sum(k_terms, axis=(0, 1)),
            ]
        )
        width = post_gain.shape[0]
        get1 = Gather(after(share1, in_terms), seq_count)
        get1.first()
        gains = sum_all(gains, "fsdp", fsdp_count)
        get1.second(gains)
        get2 = Gather(after(share2, *get1.slots()), seq_count)
        get2.first()
        mlp = place(get1.slots(), (pieces[0],) * 3, 2, 0, 3, (), me, seq_count)
        gains = sum_all(after(gains, *get1.slots()), "seq", seq_count)
        get2.second(gains, *mlp)
        mlp = place(get2.slots(), (pieces[1],) * 3, 1, 2, 3, mlp, me, seq_count)
        get3 = Gather(after(share3, *get2.slots()), seq_count)
        get3.first()
        get3.second(*mlp)
        widths = (q_cols, kv_cols, kv_cols, q_cols)
        g_q, g_k, g_v, g_out = place(get3.slots(), widths, 1, 0, 1, (), me, seq_count)
        return (
            out.astype(BF16)[None],
            d_inputs.astype(BF16)[None],
            gains[:width],
            g_q,
            g_k,
            g_v,
            g_out,
            gains[2 * width : 2 * width + HEAD_SIZE],
            gains[2 * width + HEAD_SIZE :],
            gains[width : 2 * width],
            *mlp,
        )

    return body


def solution(mesh):
    rows, acts = P("fsdp", None), P("fsdp", "seq", None)
    return jax.shard_map(
        make_body({"seq": mesh.shape["seq"], "fsdp": mesh.shape["fsdp"]}),
        mesh=mesh,
        in_specs=(
            acts, rows, P(), rows, rows, rows, rows, P(), P(), P(), rows, rows, rows, acts,
        ),
        out_specs=(acts, acts, P(), rows, rows, rows, rows, P(), P(), P(), rows, rows, rows),
        check_vma=False,
    )
```

time: 823 us -> 642 us (0.78)
  Pallas kernels: 0 us -> 176 us
  matrix products: 167 us -> 27.5 us
  other arithmetic: 84.4 us -> 32.6 us
  waiting for transfers between devices: 328 us -> 277 us
  starting transfers between devices: 99.7 us -> 56.6 us
  blocking collectives: 40.4 us -> 0 us
  local copies, waits for them, and re-layouts: 76.7 us -> 45.9 us
    pallas_call x0 -> x10, Pallas kernels: none -> 176 us  [the longest x3 67.8 us: weight_terms(): pl.pallas_call(functools.partial(terms_kernel, starts), grid_spec=pltpu.P...]
    dot_general x13 -> x0, matrix products: 54.3 us -> none  [dot_tn(): lax.dot_general(a, b, (((0,), (0,)), ((), ())), preferred_element_type=F32)]
    all_gather x5 -> x3, waiting for transfers between devices: 52.4 us -> 0.02 us  [gather_weight(): return lax.all_gather(w, 'fsdp', axis=0, tiled=True)]
    ppermute x90 -> x44, starting transfers between devices: 98.9 us -> 47.2 us  [swap(): return lax.ppermute(x, 'seq', [(s, s ^ side) for s in range(4)])]
    dot_general x13 -> x2, matrix products: 59.8 us -> 14.8 us  [dot(): return jnp.dot(a, b, preferred_element_type=F32)]
    psum x1 -> x0, blocking collectives: 40.4 us -> none  [body(): lax.psum((jnp.sum(in_terms, axis=0), jnp.sum(q_terms, axis=(0, 1)), jnp.s...]
    dot_general x13 -> x2, matrix products: 52.4 us -> 12.7 us  [dot_nt(): lax.dot_general(a, b, (((1,), (1,)), ((), ())), preferred_element_type=F32)]
    dynamic_update_slice x55 -> x3, other arithmetic: 38.4 us -> 3.47 us  [column(): lax.dynamic_update_slice(out, piece, ((self.me ^ k) * rows + start, 0))]
  transfers between devices with their start and end apart: 100 -> 55, of which waited for: 55 -> 36; matrix products, arithmetic and copies ran while one was open for 29% -> 15% of each run, Pallas kernels for 0% -> 27%
where the time goes in v2:
time: 642 us; the launch traced here: 630 us
  waiting for transfers between devices  277 us (43%)
  Pallas kernels  176 us (27%)
  starting transfers between devices  56.6 us (9%)
  local copies, waits for them, and re-layouts  45.9 us (7%)
  other arithmetic  32.6 us (5%)
  matrix products  27.5 us (4%)
  between operations  15.1 us (2%)
    ppermute x44, waiting for transfers between devices, swap(): return lax.ppermute(x, 'seq', [(s, s ^ side) for s in range(4)])  243 us
    pallas_call x3, Pallas kernels, weight_terms(): pl.pallas_call(functools.partial(terms_kernel, starts), grid_spec=pltpu.P...  67.8 us
    pallas_call x2, Pallas kernels, feed_forward(): pl.pallas_call(functools.partial(feed_forward_kernel, bool(sums), piece),...  56.5 us
    ppermute x44, starting transfers between devices, swap(): return lax.ppermute(x, 'seq', [(s, s ^ side) for s in range(4)])  47.2 us
    pallas_call x1, Pallas kernels, attend_back(): pl.pallas_call(functools.partial(attend_back_kernel, ratio), grid=(kv_hea...  22.8 us
    ppermute x5, waiting for transfers between devices, sum_all(): x = x + lax.ppermute(x, axis, [(i, i ^ bit) for i in range(count)])  20.1 us
    pallas_call x1, Pallas kernels, attend(): pl.pallas_call(functools.partial(attend_kernel, ratio), grid=(kv_heads,),...  15.5 us
    dynamic_update_slice x17, local copies, waits for them, and re-layouts, column(): lax.dynamic_update_slice(out, piece, ((self.me ^ k) * rows + start, 0))  15.3 us
  transfers between devices with their start and end apart: 55, of which 36 were waited for; matrix products, arithmetic and copies ran while one was open for 15% of the time, Pallas kernels for 27%

profile of v2, /device:TPU:0, one launch (start us, length us, event | category | flops | bytes accessed | tf_op | source)
XLA Modules:
  0.0 629.9 jit_solution(6296394473215159903)
XLA Ops:
  15.7 2.5 broadcast.80.clone
  19.8 2.9 collective-permute-start
  25.1 1.9 fusion.25
  27.0 19.2 %collective-permute-done = bf16[256,2048]{1,0:T(8,128)(2,1)S(1)} collective-permute-done((bf16[256,2048]{1,0:T(8,128)(2,1)}, bf16[256,2048]{1,0:T(8,128)(2,1)S(1)}, u32[]{:S(2)}, u32[]{:S(2)}) %collective-permute-start) | collective-permute-done | bytes 1048608 | tf_op jit(solution)/shard_map/ppermute | solution.py:65
  50.4 1.9 slice.103
  57.2 2.3 constant_dynamic-update-slice_fusion.18
  59.5 2.3 constant_dynamic-update-slice_fusion.17
  61.8 22.3 %collective-permute-done.2 = bf16[128,2048]{1,0:T(8,128)(2,1)} collective-permute-done((bf16[128,2048]{1,0:T(8,128)(2,1)}, bf16[128,2048]{1,0:T(8,128)(2,1)}, u32[]{:S(2)}, u32[]{:S(2)}) %collective-permute-start.2) | collective-permute-done | bytes 524320 | tf_op jit(solution)/shard_map/ppermute | solution.py:65
  84.1 1.9 constant_dynamic-update-slice_fusion.16
  87.7 1.9 slice.108
  89.6 9.5 %fusion.15.q_ref.k_ref.v_ref = bf16[1024,1024]{1,0:T(8,128)(2,1)} fusion(bf16[1024,2048]{1,0:T(8,128)(2,1)} %constant_dynamic-update-slice_fusion.15.refs_0_, bf16[2048,1536]{1,0:T(8,128)(2,1)} %all-gather.4.cloned.1.call-done), kind=kOutput, calls=%fused_computation.37 | convolution fusion | flops 4296015872 | bytes 10485760 | tf_op jit(solution)/shard_map/dot_general | solution.py:22
  104.9 15.5 %attend.1 = bf16[1024,512]{1,0:T(8,128)(2,1)} custom-call(bf16[1024,1024]{1,0:T(8,128)(2,1)} %fusion.15.q_ref.k_ref.v_ref, bf16[1024,1024]{1,0:T(8,128)(2,1)} %fusion.15.q_ref.k_ref.v_ref, bf16[1024,1024]{1,0:T(8,128)(2,1)} %fusion.15.q_ref.k_ref.v_ref, f32[1024,128]{1,0:T(8,128)} %get-tuple-element.149.cos_ref, f32[1024,128]{1,0:T(8,128)} %get-tuple-element.150.sin_ref, ...), custom_call_target="tpu_custom_call" | custom-call | flops 1000 | bytes 1000 | tf_op jit(solution)/shard_map/attend/pallas_call | solution.py:382
  122.7 5.5 convolution_convert_fusion
  129.8 10.0 %collective-permute-done.10 = bf16[128,2048]{1,0:T(8,128)(2,1)S(1)} collective-permute-done((bf16[128,2048]{1,0:T(8,128)(2,1)S(1)}, bf16[128,2048]{1,0:T(8,128)(2,1)S(1)}, u32[]{:S(2)}, u32[]{:S(2)}) %collective-permute-start.10) | collective-permute-done | bytes 524320 | tf_op jit(solution)/shard_map/ppermute | solution.py:65
  140.4 1.8 collective-permute-start.11
  142.1 1.7 collective-permute-start.9
  143.8 19.2 %collective-permute-done.11 = bf16[256,2048]{1,0:T(8,128)(2,1)S(1)} collective-permute-done((bf16[256,2048]{1,0:T(8,128)(2,1)S(1)}, bf16[256,2048]{1,0:T(8,128)(2,1)S(1)}, u32[]{:S(2)}, u32[]{:S(2)}) %collective-permute-start.11) | collective-permute-done | bytes 1048608 | tf_op jit(solution)/shard_map/ppermute | solution.py:65
  165.3 2.7 broadcast.80.clone.1
  171.0 20.4 %collective-permute-done.13 = bf16[256,2048]{1,0:T(8,128)(2,1)S(1)} collective-permute-done((bf16[256,2048]{1,0:T(8,128)(2,1)S(1)}, bf16[256,2048]{1,0:T(8,128)(2,1)S(1)}, u32[]{:S(2)}, u32[]{:S(2)}) %collective-permute-start.13) | collective-permute-done | bytes 1048608 | tf_op jit(solution)/shard_map/ppermute | solution.py:65
  193.1 2.0 collective-permute-start.15
  197.3 4.9 collective-permute-done.14
  203.8 35.2 %feed_forward.2 = (bf16[1024,3072]{1,0:T(8,128)(2,1)}, f32[1024,2048]{1,0:T(8,128)}, f32[1024,2048]{1,0:T(8,128)}) custom-call(bf16[1024,2048]{1,0:T(8,128)(2,1)} %constant_dynamic-update-slice_fusion.5.xb_ref.refs_0_, bf16[1024,2048]{1,0:T(8,128)(2,1)} %copy-done.2, bf16[2048,3072]{1,0:T(8,128)(2,1)} %all-gather.6.cloned.1.call-done.w_ref), custom_call_target="tpu_custom_call" | custom-call | flops 1000 | bytes 1000 | tf_op jit(solution)/shard_map/feed_forward/pallas_call | solution.py:453
  239.1 2.3 copy-done.3
  241.3 27.6 %weight_terms.3 = bf16[8,256,3072]{2,1,0:T(8,128)(2,1)} custom-call(s32[8]{0:T(128)S(1)} %iota.39.order_ref, bf16[1024,2048]{1,0:T(8,128)(2,1)} %constant_dynamic-update-slice_fusion.5.xb_ref.refs_0_, bf16[1024,2048]{1,0:T(8,128)(2,1)S(1)} %copy-done.3, bf16[1024,3072]{1,0:T(8,128)(2,1)} %get-tuple-element.65.refs_2_), custom_call_target="tpu_custom_call" | custom-call | flops 1000 | bytes 1000 | tf_op jit(solution)/shard_map/weight_terms/pallas_call | solution.py:207
  269.1 21.3 %feed_forward.3 = (bf16[1024,1536]{1,0:T(8,128)(2,1)}, bf16[1024,2048]{1,0:T(8,128)(2,1)}, bf16[1024,2048]{1,0:T(8,128)(2,1)}) custom-call(bf16[1024,2048]{1,0:T(8,128)(2,1)} %constant_dynamic-update-slice_fusion.5.xb_ref.refs_0_, bf16[1024,2048]{1,0:T(8,128)(2,1)} %copy-done.2, bf16[2048,1536]{1,0:T(8,128)(2,1)} %all-gather.8.cloned.1.call-done.w_ref, ...), custom_call_target="tpu_custom_call" | custom-call | flops 1000 | bytes 1000 | tf_op jit(solution)/shard_map/feed_forward/pallas_call | solution.py:453
  294.7 8.6 %collective-permute-done.16 = bf16[128,2048]{1,0:T(8,128)(2,1)S(1)} collective-permute-done((bf16[128,2048]{1,0:T(8,128)(2,1)S(1)}, bf16[128,2048]{1,0:T(8,128)(2,1)S(1)}, u32[]{:S(2)}, u32[]{:S(2)}) %collective-permute-start.16) | collective-permute-done | bytes 524320 | tf_op jit(solution)/shard_map/ppermute | solution.py:65
  304.7 2.0 add_convert_fusion.5
  306.7 1.7 collective-permute-start.17
  308.8 20.0 %weight_terms.4 = bf16[8,256,1536]{2,1,0:T(8,128)(2,1)} custom-call(s32[8]{0:T(128)S(1)} %iota.40.order_ref, bf16[1024,2048]{1,0:T(8,128)(2,1)} %constant_dynamic-update-slice_fusion.5.xb_ref.refs_0_, bf16[1024,2048]{1,0:T(8,128)(2,1)S(1)} %copy-done.4, bf16[1024,1536]{1,0:T(8,128)(2,1)S(1)} %copy-done.7), custom_call_target="tpu_custom_call" | custom-call | flops 1000 | bytes 1000 | tf_op jit(solution)/shard_map/weight_terms/pallas_call | solution.py:207
  330.3 3.1 convert_add_fusion.2
  333.4 2.2 multiply_reduce_fusion
  339.3 21.2 %collective-permute-done.21 = bf16[256,2048]{1,0:T(8,128)(2,1)S(1)} collective-permute-done((bf16[256,2048]{1,0:T(8,128)(2,1)S(1)}, bf16[256,2048]{1,0:T(8,128)(2,1)S(1)}, u32[]{:S(2)}, u32[]{:S(2)}) %collective-permute-start.21) | collective-permute-done | bytes 1048608 | tf_op jit(solution)/shard_map/ppermute | solution.py:65
  360.8 1.9 collective-permute-done.20
  363.9 7.7 %collective-permute-done.22 = bf16[128,2048]{1,0:T(8,128)(2,1)S(1)} collective-permute-done((bf16[128,2048]{1,0:T(8,128)(2,1)S(1)}, bf16[128,2048]{1,0:T(8,128)(2,1)S(1)}, u32[]{:S(2)}, u32[]{:S(2)}) %collective-permute-start.22) | collective-permute-done | bytes 524320 | tf_op jit(solution)/shard_map/ppermute | solution.py:65
  371.6 2.3 collective-permute-done.23
  375.0 5.3 fusion.21.do_ref
  380.3 3.0 collective-permute-done.24
  384.1 1.8 add_convert_fusion.2
  385.9 13.3 %reduce-scatter.4.cloned.1.call-done.refs_0_ = bf16[256,3072]{1,0:T(8,128)(2,1)} async-done(((bf16[2048,3072]{1,0:T(8,128)(2,1)}), bf16[256,3072]{1,0:T(8,128)(2,1)}) %reduce-scatter.4.cloned.1.call-update) | async-done | bytes 1572880 | tf_op jit(solution)/shard_map/reduce_scatter | solution.py:228
  402.3 22.8 %attend_back.1 = (bf16[1024,512]{1,0:T(8,128)(2,1)}, bf16[1024,256]{1,0:T(8,128)(2,1)}, bf16[1024,256]{1,0:T(8,128)(2,1)}, f32[2,1,128]{2,1,0:T(1,128)}, f32[2,1,128]{2,1,0:T(1,128)}) custom-call(bf16[1024,1024]{1,0:T(8,128)(2,1)} %fusion.15.q_ref.k_ref.v_ref, bf16[1024,1024]{1,0:T(8,128)(2,1)} %fusion.15.q_ref.k_ref.v_ref, ...), custom_call_target="tpu_custom_call" | custom-call | flops 1000 | bytes 1000 | tf_op jit(solution)/shard_map/attend_back/pallas_call | solution.py:400
  425.2 1.8 pad_maximum_fusion.refs_2_
  427.5 2.9 add_add_fusion
  430.4 7.2 %convolution_convert_fusion.1 = bf16[1024,2048]{1,0:T(8,128)(2,1)S(1)} fusion(bf16[2048,1536]{1,0:T(8,128)(2,1)} %all-gather.4.cloned.1.call-done, bf16[1024,1536]{1,0:T(8,128)(2,1)S(1)} %pad_maximum_fusion.refs_2_), kind=kOutput, calls=%fused_computation.1 | convolution fusion | flops 4297064448 | bytes 10485760 | tf_op jit(solution)/shard_map/dot_general | solution.py:26
  438.9 9.8 %collective-permute-done.28 = bf16[128,2048]{1,0:T(8,128)(2,1)S(1)} collective-permute-done((bf16[128,2048]{1,0:T(8,128)(2,1)S(1)}, bf16[128,2048]{1,0:T(8,128)(2,1)S(1)}, u32[]{:S(2)}, u32[]{:S(2)}) %collective-permute-start.28) | collective-permute-done | bytes 524320 | tf_op jit(solution)/shard_map/ppermute | solution.py:65
  449.0 1.9 add_convert_fusion.1
  450.8 20.2 %weight_terms.5 = bf16[8,256,1536]{2,1,0:T(8,128)(2,1)} custom-call(s32[8]{0:T(128)S(1)} %iota.41.order_ref, bf16[1024,2048]{1,0:T(8,128)(2,1)} %constant_dynamic-update-slice_fusion.15.refs_0_, bf16[1024,2048]{1,0:T(8,128)(2,1)S(1)} %copy-done.6, bf16[1024,1536]{1,0:T(8,128)(2,1)S(1)} %pad_maximum_fusion.refs_2_), custom_call_target="tpu_custom_call" | custom-call | flops 1000 | bytes 1000 | tf_op jit(solution)/shard_map/weight_terms/pallas_call | solution.py:207
  474.3 19.8 %collective-permute-done.29 = bf16[256,2048]{1,0:T(8,128)(2,1)S(1)} collective-permute-done((bf16[256,2048]{1,0:T(8,128)(2,1)S(1)}, bf16[256,2048]{1,0:T(8,128)(2,1)S(1)}, u32[]{:S(2)}, u32[]{:S(2)}) %collective-permute-start.29) | collective-permute-done | bytes 1048608 | tf_op jit(solution)/shard_map/ppermute | solution.py:65
  495.3 1.9 convert_add_fusion.1
  499.2 2.4 fusion.29
  504.9 4.9 collective-permute-start.33
  509.8 2.7 collective-permute-done.33
  512.5 2.1 collective-permute-start.34
  514.6 3.5 collective-permute-done.34
  518.1 16.8 %collective-permute-done.36.refs_2_ = bf16[256,3072]{1,0:T(8,128)(2,1)S(1)} collective-permute-done((bf16[256,3072]{1,0:T(8,128)(2,1)}, bf16[256,3072]{1,0:T(8,128)(2,1)S(1)}, u32[]{:S(2)}, u32[]{:S(2)}) %collective-permute-start.36) | collective-permute-done | bytes 1572896 | tf_op jit(solution)/shard_map/ppermute | solution.py:65
  535.0 2.6 collective-permute-done.35.refs_1_
  538.7 16.2 %collective-permute-done.37 = bf16[128,3072]{1,0:T(8,128)(2,1)S(1)} collective-permute-done((bf16[128,3072]{1,0:T(8,128)(2,1)S(1)}, bf16[128,3072]{1,0:T(8,128)(2,1)S(1)}, u32[]{:S(2)}, u32[]{:S(2)}) %collective-permute-start.37) | collective-permute-done | bytes 786464 | tf_op jit(solution)/shard_map/ppermute | solution.py:65
  557.4 12.7 %collective-permute-done.39 = f32[4352]{0:T(1024)S(1)} collective-permute-done((f32[4352]{0:T(1024)S(1)}, f32[4352]{0:T(1024)S(1)}, u32[]{:S(2)}, u32[]{:S(2)}) %collective-permute-start.39) | collective-permute-done | bytes 17440 | tf_op jit(solution)/shard_map/ppermute | solution.py:236
  570.6 6.9 %place.3 = (f32[256,6144]{1,0:T(8,128)}, f32[256,6144]{1,0:T(8,128)}, f32[256,6144]{1,0:T(8,128)}) custom-call(s32[1]{0:T(128)} %bitcast.13.me_ref, bf16[256,3072]{1,0:T(8,128)(2,1)} %reduce-scatter.4.cloned.1.call-done.refs_0_, bf16[256,3072]{1,0:T(8,128)(2,1)S(1)} %collective-permute-done.35.refs_1_, ...), custom_call_target="tpu_custom_call" | custom-call | flops 1000 | bytes 1000 | tf_op jit(solution)/shard_map/place/pallas_call | solution.py:491
  581.4 8.8 %collective-permute-done.43 = bf16[128,1536]{1,0:T(8,128)(2,1)S(1)} collective-permute-done((bf16[128,1536]{1,0:T(8,128)(2,1)S(1)}, bf16[128,1536]{1,0:T(8,128)(2,1)S(1)}, u32[]{:S(2)}, u32[]{:S(2)}) %collective-permute-start.43) | collective-permute-done | bytes 393248 | tf_op jit(solution)/shard_map/ppermute | solution.py:65
  590.2 1.6 collective-permute-done.44
  594.9 3.1 place.4
  598.0 10.4 %collective-permute-done.46.refs_2_ = bf16[256,1536]{1,0:T(8,128)(2,1)S(1)} collective-permute-done((bf16[256,1536]{1,0:T(8,128)(2,1)}, bf16[256,1536]{1,0:T(8,128)(2,1)S(1)}, u32[]{:S(2)}, u32[]{:S(2)}) %collective-permute-start.46) | collective-permute-done | bytes 786464 | tf_op jit(solution)/shard_map/ppermute | solution.py:65
  612.6 5.1 collective-permute-done.47
  619.8 3.0 place.5
  (241 shorter events, 90.9 us)
Async XLA Ops:
  7.2 82.4 %all-gather.4.cloned.1.call-start = ((), (), s32[]{:S(2)}) async-start(), calls=%async_computation.3 | async-start | bytes 7077888 | tf_op jit(solution)/shard_map/all_gather | solution.py:165
  10.4 193.4 %all-gather.6.cloned.1.call-start = ((), (), s32[]{:S(2)}) async-start(), calls=%async_computation.4 | async-start | bytes 14155776 | tf_op jit(solution)/shard_map/all_gather | solution.py:165
  13.1 256.0 %all-gather.8.cloned.1.call-start = ((), (), s32[]{:S(2)}) async-start(), calls=%async_computation.5 | async-start | bytes 7077888 | tf_op jit(solution)/shard_map/all_gather | solution.py:165
  15.3 383.9 %reduce-scatter.4.cloned.1.call-start = ((), (), s32[]{:S(2)}) async-start(), calls=%async_computation.6 | async-start | bytes 14155776 | tf_op jit(solution)/shard_map/reduce_scatter | solution.py:228
  18.2 29.5 %copy-start.23 = (bf16[1,256,2048]{2,1,0:T(8,128)(2,1)S(1)}, bf16[1,256,2048]{2,1,0:T(8,128)(2,1)}, u32[]{:S(2)}) copy-start(bf16[1,256,2048]{2,1,0:T(8,128)(2,1)} %param.27) | copy-start | bytes 3145732
  19.8 26.3 %collective-permute-start = (bf16[256,2048]{1,0:T(8,128)(2,1)}, bf16[256,2048]{1,0:T(8,128)(2,1)S(1)}, u32[]{:S(2)}, u32[]{:S(2)}) collective-permute-start(bf16[256,2048]{1,0:T(8,128)(2,1)} %get-tuple-element.120), channel_id=1, source_target_pairs={{0,8},{8,0},{16,24},{24,16},{1,9},{9,1},{17,25},{25,17},{2,10},{10... | collective-permute-start | bytes 3145736 | tf_op jit(solution)/shard_map/ppermute | solution.py:65
  22.8 24.9 %collective-permute-start.1 = (bf16[256,2048]{1,0:T(8,128)(2,1)}, bf16[256,2048]{1,0:T(8,128)(2,1)}, u32[]{:S(2)}, u32[]{:S(2)}) collective-permute-start(bf16[256,2048]{1,0:T(8,128)(2,1)} %get-tuple-element.120), channel_id=1, source_target_pairs={{0,16},{8,24},{16,0},{24,8},{1,17},{9,25},{17,1},{25,9},{2,18},{10... | collective-permute-start | bytes 3145736 | tf_op jit(solution)/shard_map/ppermute | solution.py:65
  47.7 39.1 %collective-permute-start.5 = (bf16[256,2048]{1,0:T(8,128)(2,1)S(1)}, bf16[256,2048]{1,0:T(8,128)(2,1)S(1)}, u32[]{:S(2)}, u32[]{:S(2)}) collective-permute-start(bf16[256,2048]{1,0:T(8,128)(2,1)S(1)} %bitcast.44), channel_id=1, source_target_pairs={{0,16},{8,24},{16,0},{24,8},{1,17},{9,25},{17,1},{25,9},{2,18},{10... | collective-permute-start | bytes 3145736 | tf_op jit(solution)/shard_map/ppermute | solution.py:65
  49.3 38.4 %collective-permute-start.4 = (bf16[256,2048]{1,0:T(8,128)(2,1)S(1)}, bf16[256,2048]{1,0:T(8,128)(2,1)}, u32[]{:S(2)}, u32[]{:S(2)}) collective-permute-start(bf16[256,2048]{1,0:T(8,128)(2,1)S(1)} %bitcast.45), channel_id=1, source_target_pairs={{0,8},{8,0},{16,24},{24,16},{1,9},{9,1},{17,25},{25,17},{2,10},{10... | collective-permute-start | bytes 3145736 | tf_op jit(solution)/shard_map/ppermute | solution.py:65
  52.3 31.8 %collective-permute-start.2 = (bf16[128,2048]{1,0:T(8,128)(2,1)}, bf16[128,2048]{1,0:T(8,128)(2,1)}, u32[]{:S(2)}, u32[]{:S(2)}) collective-permute-start(bf16[128,2048]{1,0:T(8,128)(2,1)} %slice.103), channel_id=1, source_target_pairs={{0,8},{8,0},{16,24},{24,16},{1,9},{9,1},{17,25},{25,17},{2,10},{10... | collective-permute-start | bytes 1572872 | tf_op jit(solution)/shard_map/ppermute | solution.py:65
  56.6 29.4 %collective-permute-start.3 = (bf16[128,2048]{1,0:T(8,128)(2,1)S(1)}, bf16[128,2048]{1,0:T(8,128)(2,1)S(1)}, u32[]{:S(2)}, u32[]{:S(2)}) collective-permute-start(bf16[128,2048]{1,0:T(8,128)(2,1)S(1)} %slice.104), channel_id=1, source_target_pairs={{0,16},{8,24},{16,0},{24,8},{1,17},{9,25},{17,1},{25,9},{2,18},{10... | collective-permute-start | bytes 1572872 | tf_op jit(solution)/shard_map/ppermute | solution.py:65
  99.1 21.3 %collective-permute-start.6 = (bf16[128,2048]{1,0:T(8,128)(2,1)}, bf16[128,2048]{1,0:T(8,128)(2,1)}, u32[]{:S(2)}, u32[]{:S(2)}) collective-permute-start(bf16[128,2048]{1,0:T(8,128)(2,1)} %slice.107), channel_id=1, source_target_pairs={{0,8},{8,0},{16,24},{24,16},{1,9},{9,1},{17,25},{25,17},{2,10},{10... | collective-permute-start | bytes 1572872 | tf_op jit(solution)/shard_map/ppermute | solution.py:65
  102.2 19.4 %collective-permute-start.7 = (bf16[128,2048]{1,0:T(8,128)(2,1)S(1)}, bf16[128,2048]{1,0:T(8,128)(2,1)}, u32[]{:S(2)}, u32[]{:S(2)}) collective-permute-start(bf16[128,2048]{1,0:T(8,128)(2,1)S(1)} %copy-done.33), channel_id=1, source_target_pairs={{0,16},{8,24},{16,0},{24,8},{1,17},{9,25},{17,1},{25,9},{2,18},{10... | collective-permute-start | bytes 1572872 | tf_op jit(solution)/shard_map/ppermute | solution.py:65
  128.3 11.5 %collective-permute-start.10 = (bf16[128,2048]{1,0:T(8,128)(2,1)S(1)}, bf16[128,2048]{1,0:T(8,128)(2,1)S(1)}, u32[]{:S(2)}, u32[]{:S(2)}) collective-permute-start(bf16[128,2048]{1,0:T(8,128)(2,1)S(1)} %get-tuple-element.136), channel_id=1, source_target_pairs={{0,8},{8,0},{16,24},{24,16},{1,9},{9,1},{17,25},{25,17},{2,10},{10... | collective-permute-start | bytes 1572872 | tf_op jit(solution)/shard_map/ppermute | solution.py:65
  129.0 10.8 %collective-permute-start.8 = (bf16[128,2048]{1,0:T(8,128)(2,1)S(1)}, bf16[128,2048]{1,0:T(8,128)(2,1)S(1)}, u32[]{:S(2)}, u32[]{:S(2)}) collective-permute-start(bf16[128,2048]{1,0:T(8,128)(2,1)S(1)} %get-tuple-element.135), channel_id=1, source_target_pairs={{0,16},{8,24},{16,0},{24,8},{1,17},{9,25},{17,1},{25,9},{2,18},{10... | collective-permute-start | bytes 1572872 | tf_op jit(solution)/shard_map/ppermute | solution.py:65
  140.4 22.6 %collective-permute-start.11 = (bf16[256,2048]{1,0:T(8,128)(2,1)S(1)}, bf16[256,2048]{1,0:T(8,128)(2,1)S(1)}, u32[]{:S(2)}, u32[]{:S(2)}) collective-permute-start(bf16[256,2048]{1,0:T(8,128)(2,1)S(1)} %get-tuple-element.134), channel_id=1, source_target_pairs={{0,16},{8,24},{16,0},{24,8},{1,17},{9,25},{17,1},{25,9},{2,18},{10... | collective-permute-start | bytes 3145736 | tf_op jit(solution)/shard_map/ppermute | solution.py:65
  142.1 22.3 %collective-permute-start.9 = (bf16[256,2048]{1,0:T(8,128)(2,1)S(1)}, bf16[256,2048]{1,0:T(8,128)(2,1)S(1)}, u32[]{:S(2)}, u32[]{:S(2)}) collective-permute-start(bf16[256,2048]{1,0:T(8,128)(2,1)S(1)} %get-tuple-element.133), channel_id=1, source_target_pairs={{0,8},{8,0},{16,24},{24,16},{1,9},{9,1},{17,25},{25,17},{2,10},{10... | collective-permute-start | bytes 3145736 | tf_op jit(solution)/shard_map/ppermute | solution.py:65
  169.2 22.2 %collective-permute-start.13 = (bf16[256,2048]{1,0:T(8,128)(2,1)S(1)}, bf16[256,2048]{1,0:T(8,128)(2,1)S(1)}, u32[]{:S(2)}, u32[]{:S(2)}) collective-permute-start(bf16[256,2048]{1,0:T(8,128)(2,1)S(1)} %get-tuple-element.116), channel_id=1, source_target_pairs={{0,16},{8,24},{16,0},{24,8},{1,17},{9,25},{17,1},{25,9},{2,18},{10... | collective-permute-start | bytes 3145736 | tf_op jit(solution)/shard_map/ppermute | solution.py:65
  169.5 23.5 %collective-permute-start.12 = (bf16[256,2048]{1,0:T(8,128)(2,1)S(1)}, bf16[256,2048]{1,0:T(8,128)(2,1)S(1)}, u32[]{:S(2)}, u32[]{:S(2)}) collective-permute-start(bf16[256,2048]{1,0:T(8,128)(2,1)S(1)} %get-tuple-element.116), channel_id=1, source_target_pairs={{0,8},{8,0},{16,24},{24,16},{1,9},{9,1},{17,25},{25,17},{2,10},{10... | collective-permute-start | bytes 3145736 | tf_op jit(solution)/shard_map/ppermute | solution.py:65
  191.4 10.7 %collective-permute-start.14 = (bf16[128,2048]{1,0:T(8,128)(2,1)S(1)}, bf16[128,2048]{1,0:T(8,128)(2,1)S(1)}, u32[]{:S(2)}, u32[]{:S(2)}) collective-permute-start(bf16[128,2048]{1,0:T(8,128)(2,1)S(1)} %slice.110), channel_id=1, source_target_pairs={{0,8},{8,0},{16,24},{24,16},{1,9},{9,1},{17,25},{25,17},{2,10},{10... | collective-permute-start | bytes 1572872 | tf_op jit(solution)/shard_map/ppermute | solution.py:65
  193.1 9.9 %collective-permute-start.15 = (bf16[128,2048]{1,0:T(8,128)(2,1)S(1)}, bf16[128,2048]{1,0:T(8,128)(2,1)S(1)}, u32[]{:S(2)}, u32[]{:S(2)}) collective-permute-start(bf16[128,2048]{1,0:T(8,128)(2,1)S(1)} %slice.111), channel_id=1, source_target_pairs={{0,16},{8,24},{16,0},{24,8},{1,17},{9,25},{17,1},{25,9},{2,18},{10... | collective-permute-start | bytes 1572872 | tf_op jit(solution)/shard_map/ppermute | solution.py:65
  269.0 202.0 %reduce-scatter.6.cloned.1.call-start = ((), (), s32[]{:S(2)}) async-start(), calls=%async_computation.7 | async-start | bytes 7077888 | tf_op jit(solution)/shard_map/reduce_scatter | solution.py:228
  290.3 18.5 %copy-start.7 = (bf16[1024,1536]{1,0:T(8,128)(2,1)S(1)}, bf16[1024,1536]{1,0:T(8,128)(2,1)}, u32[]{:S(2)}) copy-start(bf16[1024,1536]{1,0:T(8,128)(2,1)} %get-tuple-element.71.refs_2_) | copy-start | bytes 9437188
  291.7 11.5 %collective-permute-start.16 = (bf16[128,2048]{1,0:T(8,128)(2,1)S(1)}, bf16[128,2048]{1,0:T(8,128)(2,1)S(1)}, u32[]{:S(2)}, u32[]{:S(2)}) collective-permute-start(bf16[128,2048]{1,0:T(8,128)(2,1)S(1)} %get-tuple-element.131), channel_id=1, source_target_pairs={{0,16},{8,24},{16,0},{24,8},{1,17},{9,25},{17,1},{25,9},{2,18},{10... | collective-permute-start | bytes 1572872 | tf_op jit(solution)/shard_map/ppermute | solution.py:65
  293.3 11.4 %collective-permute-start.18 = (bf16[128,2048]{1,0:T(8,128)(2,1)S(1)}, bf16[128,2048]{1,0:T(8,128)(2,1)S(1)}, u32[]{:S(2)}, u32[]{:S(2)}) collective-permute-start(bf16[128,2048]{1,0:T(8,128)(2,1)S(1)} %get-tuple-element.132), channel_id=1, source_target_pairs={{0,8},{8,0},{16,24},{24,16},{1,9},{9,1},{17,25},{25,17},{2,10},{10... | collective-permute-start | bytes 1572872 | tf_op jit(solution)/shard_map/ppermute | solution.py:65
  306.7 22.1 %collective-permute-start.17 = (bf16[256,2048]{1,0:T(8,128)(2,1)S(1)}, bf16[256,2048]{1,0:T(8,128)(2,1)S(1)}, u32[]{:S(2)}, u32[]{:S(2)}) collective-permute-start(bf16[256,2048]{1,0:T(8,128)(2,1)S(1)} %get-tuple-element.129), channel_id=1, source_target_pairs={{0,8},{8,0},{16,24},{24,16},{1,9},{9,1},{17,25},{25,17},{2,10},{10... | collective-permute-start | bytes 3145736 | tf_op jit(solution)/shard_map/ppermute | solution.py:65
  308.4 21.9 %collective-permute-start.19 = (bf16[256,2048]{1,0:T(8,128)(2,1)S(1)}, bf16[256,2048]{1,0:T(8,128)(2,1)S(1)}, u32[]{:S(2)}, u32[]{:S(2)}) collective-permute-start(bf16[256,2048]{1,0:T(8,128)(2,1)S(1)} %get-tuple-element.130), channel_id=1, source_target_pairs={{0,16},{8,24},{16,0},{24,8},{1,17},{9,25},{17,1},{25,9},{2,18},{10... | collective-permute-start | bytes 3145736 | tf_op jit(solution)/shard_map/ppermute | solution.py:65
  338.1 22.4 %collective-permute-start.21 = (bf16[256,2048]{1,0:T(8,128)(2,1)S(1)}, bf16[256,2048]{1,0:T(8,128)(2,1)S(1)}, u32[]{:S(2)}, u32[]{:S(2)}) collective-permute-start(bf16[256,2048]{1,0:T(8,128)(2,1)S(1)} %get-tuple-element.114), channel_id=1, source_target_pairs={{0,16},{8,24},{16,0},{24,8},{1,17},{9,25},{17,1},{25,9},{2,18},{10... | collective-permute-start | bytes 3145736 | tf_op jit(solution)/shard_map/ppermute | solution.py:65
  338.9 23.7 %collective-permute-start.20 = (bf16[256,2048]{1,0:T(8,128)(2,1)S(1)}, bf16[256,2048]{1,0:T(8,128)(2,1)S(1)}, u32[]{:S(2)}, u32[]{:S(2)}) collective-permute-start(bf16[256,2048]{1,0:T(8,128)(2,1)S(1)} %get-tuple-element.114), channel_id=1, source_target_pairs={{0,8},{8,0},{16,24},{24,16},{1,9},{9,1},{17,25},{25,17},{2,10},{10... | collective-permute-start | bytes 3145736 | tf_op jit(solution)/shard_map/ppermute | solution.py:65
  360.5 11.1 %collective-permute-start.22 = (bf16[128,2048]{1,0:T(8,128)(2,1)S(1)}, bf16[128,2048]{1,0:T(8,128)(2,1)S(1)}, u32[]{:S(2)}, u32[]{:S(2)}) collective-permute-start(bf16[128,2048]{1,0:T(8,128)(2,1)S(1)} %slice.112), channel_id=1, source_target_pairs={{0,8},{8,0},{16,24},{24,16},{1,9},{9,1},{17,25},{25,17},{2,10},{10... | collective-permute-start | bytes 1572872 | tf_op jit(solution)/shard_map/ppermute | solution.py:65
  362.7 11.2 %collective-permute-start.23 = (bf16[128,2048]{1,0:T(8,128)(2,1)S(1)}, bf16[128,2048]{1,0:T(8,128)(2,1)S(1)}, u32[]{:S(2)}, u32[]{:S(2)}) collective-permute-start(bf16[128,2048]{1,0:T(8,128)(2,1)S(1)} %slice.113), channel_id=1, source_target_pairs={{0,16},{8,24},{16,0},{24,8},{1,17},{9,25},{17,1},{25,9},{2,18},{10... | collective-permute-start | bytes 1572872 | tf_op jit(solution)/shard_map/ppermute | solution.py:65
  374.1 9.2 %collective-permute-start.24 = (bf16[128,2048]{1,0:T(8,128)(2,1)S(1)}, bf16[128,2048]{1,0:T(8,128)(2,1)S(1)}, u32[]{:S(2)}, u32[]{:S(2)}) collective-permute-start(bf16[128,2048]{1,0:T(8,128)(2,1)S(1)} %get-tuple-element.128), channel_id=1, source_target_pairs={{0,16},{8,24},{16,0},{24,8},{1,17},{9,25},{17,1},{25,9},{2,18},{10... | collective-permute-start | bytes 1572872 | tf_op jit(solution)/shard_map/ppermute | solution.py:65
  375.0 9.2 %collective-permute-start.25 = (bf16[128,2048]{1,0:T(8,128)(2,1)S(1)}, bf16[128,2048]{1,0:T(8,128)(2,1)S(1)}, u32[]{:S(2)}, u32[]{:S(2)}) collective-permute-start(bf16[128,2048]{1,0:T(8,128)(2,1)S(1)} %get-tuple-element.127), channel_id=1, source_target_pairs={{0,8},{8,0},{16,24},{24,16},{1,9},{9,1},{17,25},{25,17},{2,10},{10... | collective-permute-start | bytes 1572872 | tf_op jit(solution)/shard_map/ppermute | solution.py:65
  399.3 192.6 %reduce-scatter.8.cloned.1.call-start = ((), (), s32[]{:S(2)}) async-start(), calls=%async_computation.8 | async-start | bytes 7077888 | tf_op jit(solution)/shard_map/reduce_scatter | solution.py:228
  399.3 25.8 %copy-start.28 = (bf16[1024,512]{1,0:T(8,128)(2,1)S(1)}, bf16[1024,512]{1,0:T(8,128)(2,1)}, u32[]{:S(2)}) copy-start(bf16[1024,512]{1,0:T(8,128)(2,1)} %attend.1) | copy-start | bytes 3145732
  399.3 27.7 %collective-permute-start.26 = (bf16[256,2048]{1,0:T(8,128)(2,1)}, bf16[256,2048]{1,0:T(8,128)(2,1)S(1)}, u32[]{:S(2)}, u32[]{:S(2)}) collective-permute-start(bf16[256,2048]{1,0:T(8,128)(2,1)} %get-tuple-element.75), channel_id=1, source_target_pairs={{0,8},{8,0},{16,24},{24,16},{1,9},{9,1},{17,25},{25,17},{2,10},{10... | collective-permute-start | bytes 3145736 | tf_op jit(solution)/shard_map/ppermute | solution.py:65
  400.8 26.2 %collective-permute-start.27 = (bf16[256,2048]{1,0:T(8,128)(2,1)}, bf16[256,2048]{1,0:T(8,128)(2,1)S(1)}, u32[]{:S(2)}, u32[]{:S(2)}) collective-permute-start(bf16[256,2048]{1,0:T(8,128)(2,1)} %get-tuple-element.76), channel_id=1, source_target_pairs={{0,16},{8,24},{16,0},{24,8},{1,17},{9,25},{17,1},{25,9},{2,18},{10... | collective-permute-start | bytes 3145736 | tf_op jit(solution)/shard_map/ppermute | solution.py:65
  437.7 11.0 %collective-permute-start.28 = (bf16[128,2048]{1,0:T(8,128)(2,1)S(1)}, bf16[128,2048]{1,0:T(8,128)(2,1)S(1)}, u32[]{:S(2)}, u32[]{:S(2)}) collective-permute-start(bf16[128,2048]{1,0:T(8,128)(2,1)S(1)} %get-tuple-element.123), channel_id=1, source_target_pairs={{0,16},{8,24},{16,0},{24,8},{1,17},{9,25},{17,1},{25,9},{2,18},{10... | collective-permute-start | bytes 1572872 | tf_op jit(solution)/shard_map/ppermute | solution.py:65
  438.3 10.7 %collective-permute-start.30 = (bf16[128,2048]{1,0:T(8,128)(2,1)S(1)}, bf16[128,2048]{1,0:T(8,128)(2,1)S(1)}, u32[]{:S(2)}, u32[]{:S(2)}) collective-permute-start(bf16[128,2048]{1,0:T(8,128)(2,1)S(1)} %get-tuple-element.124), channel_id=1, source_target_pairs={{0,8},{8,0},{16,24},{24,16},{1,9},{9,1},{17,25},{25,17},{2,10},{10... | collective-permute-start | bytes 1572872 | tf_op jit(solution)/shard_map/ppermute | solution.py:65
  472.2 25.0 %copy-start.22 = (bf16[1,256,2048]{2,1,0:T(8,128)(2,1)S(1)}, bf16[1,256,2048]{2,1,0:T(8,128)(2,1)}, u32[]{:S(2)}) copy-start(bf16[1,256,2048]{2,1,0:T(8,128)(2,1)} %param.14) | copy-start | bytes 3145732
  472.3 21.9 %collective-permute-start.29 = (bf16[256,2048]{1,0:T(8,128)(2,1)S(1)}, bf16[256,2048]{1,0:T(8,128)(2,1)S(1)}, u32[]{:S(2)}, u32[]{:S(2)}) collective-permute-start(bf16[256,2048]{1,0:T(8,128)(2,1)S(1)} %copy-done.32), channel_id=1, source_target_pairs={{0,8},{8,0},{16,24},{24,16},{1,9},{9,1},{17,25},{25,17},{2,10},{10... | collective-permute-start | bytes 3145736 | tf_op jit(solution)/shard_map/ppermute | solution.py:65
  472.9 22.5 %collective-permute-start.31 = (bf16[256,2048]{1,0:T(8,128)(2,1)S(1)}, bf16[256,2048]{1,0:T(8,128)(2,1)S(1)}, u32[]{:S(2)}, u32[]{:S(2)}) collective-permute-start(bf16[256,2048]{1,0:T(8,128)(2,1)S(1)} %copy-done.31), channel_id=1, source_target_pairs={{0,16},{8,24},{16,0},{24,8},{1,17},{9,25},{17,1},{25,9},{2,18},{10... | collective-permute-start | bytes 3145736 | tf_op jit(solution)/shard_map/ppermute | solution.py:65
  501.6 33.3 %collective-permute-start.36 = (bf16[256,3072]{1,0:T(8,128)(2,1)}, bf16[256,3072]{1,0:T(8,128)(2,1)S(1)}, u32[]{:S(2)}, u32[]{:S(2)}) collective-permute-start(bf16[256,3072]{1,0:T(8,128)(2,1)} %reduce-scatter.4.cloned.1.call-done.refs_0_), channel_id=1, source_target_pairs={{0,16},{8,24},{16,0},{24,8},{1,17},{9,25},{17,1},{25,9},{2,18},{10... | collective-permute-start | bytes 4718600 | tf_op jit(solution)/shard_map/ppermute | solution.py:65
  503.1 34.5 %collective-permute-start.35 = (bf16[256,3072]{1,0:T(8,128)(2,1)}, bf16[256,3072]{1,0:T(8,128)(2,1)S(1)}, u32[]{:S(2)}, u32[]{:S(2)}) collective-permute-start(bf16[256,3072]{1,0:T(8,128)(2,1)} %reduce-scatter.4.cloned.1.call-done.refs_0_), channel_id=1, source_target_pairs={{0,8},{8,0},{16,24},{24,16},{1,9},{9,1},{17,25},{25,17},{2,10},{10... | collective-permute-start | bytes 4718600 | tf_op jit(solution)/shard_map/ppermute | solution.py:65
  503.7 1.3 collective-permute-start.32
  504.9 7.5 %collective-permute-start.33 = (f32[4352]{0:T(1024)S(1)}, f32[4352]{0:T(1024)S(1)}, u32[]{:S(2)}, u32[]{:S(2)}) collective-permute-start(f32[4352]{0:T(1024)S(1)} %fusion.27), channel_id=1, source_target_pairs={{0,2},{1,3},{2,0},{3,1},{4,6},{5,7},{6,4},{7,5},{8,10},{9,11},{10,... | collective-permute-start | bytes 52232 | tf_op jit(solution)/shard_map/ppermute | solution.py:236
  512.5 5.6 collective-permute-start.34
  535.0 20.0 %copy-start.12 = (bf16[256,1536]{1,0:T(8,128)(2,1)S(1)}, bf16[256,1536]{1,0:T(8,128)(2,1)}, u32[]{:S(2)}) copy-start(bf16[256,1536]{1,0:T(8,128)(2,1)} %reduce-scatter.6.cloned.1.call-done.refs_0_) | copy-start | bytes 2359300
  537.7 17.2 %collective-permute-start.37 = (bf16[128,3072]{1,0:T(8,128)(2,1)S(1)}, bf16[128,3072]{1,0:T(8,128)(2,1)S(1)}, u32[]{:S(2)}, u32[]{:S(2)}) collective-permute-start(bf16[128,3072]{1,0:T(8,128)(2,1)S(1)} %slice.114), channel_id=1, source_target_pairs={{0,8},{8,0},{16,24},{24,16},{1,9},{9,1},{17,25},{25,17},{2,10},{10... | collective-permute-start | bytes 2359304 | tf_op jit(solution)/shard_map/ppermute | solution.py:65
  538.3 16.7 %collective-permute-start.38 = (bf16[128,3072]{1,0:T(8,128)(2,1)S(1)}, bf16[128,3072]{1,0:T(8,128)(2,1)S(1)}, u32[]{:S(2)}, u32[]{:S(2)}) collective-permute-start(bf16[128,3072]{1,0:T(8,128)(2,1)S(1)} %slice.115), channel_id=1, source_target_pairs={{0,16},{8,24},{16,0},{24,8},{1,17},{9,25},{17,1},{25,9},{2,18},{10... | collective-permute-start | bytes 2359304 | tf_op jit(solution)/shard_map/ppermute | solution.py:65
  555.1 22.5 %collective-permute-start.42 = (bf16[256,1536]{1,0:T(8,128)(2,1)S(1)}, bf16[256,1536]{1,0:T(8,128)(2,1)S(1)}, u32[]{:S(2)}, u32[]{:S(2)}) collective-permute-start(bf16[256,1536]{1,0:T(8,128)(2,1)S(1)} %copy-done.12), channel_id=1, source_target_pairs={{0,16},{8,24},{16,0},{24,8},{1,17},{9,25},{17,1},{25,9},{2,18},{10... | collective-permute-start | bytes 2359304 | tf_op jit(solution)/shard_map/ppermute | solution.py:65
  555.3 23.1 %collective-permute-start.41 = (bf16[256,1536]{1,0:T(8,128)(2,1)S(1)}, bf16[256,1536]{1,0:T(8,128)(2,1)S(1)}, u32[]{:S(2)}, u32[]{:S(2)}) collective-permute-start(bf16[256,1536]{1,0:T(8,128)(2,1)S(1)} %copy-done.12), channel_id=1, source_target_pairs={{0,8},{8,0},{16,24},{24,16},{1,9},{9,1},{17,25},{25,17},{2,10},{10... | collective-permute-start | bytes 2359304 | tf_op jit(solution)/shard_map/ppermute | solution.py:65
  555.8 14.2 %collective-permute-start.39 = (f32[4352]{0:T(1024)S(1)}, f32[4352]{0:T(1024)S(1)}, u32[]{:S(2)}, u32[]{:S(2)}) collective-permute-start(f32[4352]{0:T(1024)S(1)} %add.235), channel_id=1, source_target_pairs={{0,8},{8,0},{16,24},{24,16},{1,9},{9,1},{17,25},{25,17},{2,10},{10... | collective-permute-start | bytes 52232 | tf_op jit(solution)/shard_map/ppermute | solution.py:236
  570.1 7.4 %collective-permute-start.40 = (f32[4352]{0:T(1024)S(1)}, f32[4352]{0:T(1024)S(1)}, u32[]{:S(2)}, u32[]{:S(2)}) collective-permute-start(f32[4352]{0:T(1024)S(1)} %add.236), channel_id=1, source_target_pairs={{0,16},{8,24},{16,0},{24,8},{1,17},{9,25},{17,1},{25,9},{2,18},{10... | collective-permute-start | bytes 52232 | tf_op jit(solution)/shard_map/ppermute | solution.py:236
  577.5 17.4 %copy-start.13 = (bf16[256,1536]{1,0:T(8,128)(2,1)S(1)}, bf16[256,1536]{1,0:T(8,128)(2,1)}, u32[]{:S(2)}) copy-start(bf16[256,1536]{1,0:T(8,128)(2,1)} %reduce-scatter.6.cloned.1.call-done.refs_0_) | copy-start | bytes 2359300
  578.4 16.5 %copy-start.9 = (bf16[256,1536]{1,0:T(8,128)(2,1)S(1)}, bf16[256,1536]{1,0:T(8,128)(2,1)}, u32[]{:S(2)}) copy-start(bf16[256,1536]{1,0:T(8,128)(2,1)} %copy-done.8) | copy-start | bytes 2359300
  579.4 15.6 %copy-start.11 = (bf16[256,1536]{1,0:T(8,128)(2,1)S(1)}, bf16[256,1536]{1,0:T(8,128)(2,1)}, u32[]{:S(2)}) copy-start(bf16[256,1536]{1,0:T(8,128)(2,1)} %copy-done.10) | copy-start | bytes 2359300
  579.4 10.8 %collective-permute-start.43 = (bf16[128,1536]{1,0:T(8,128)(2,1)S(1)}, bf16[128,1536]{1,0:T(8,128)(2,1)S(1)}, u32[]{:S(2)}, u32[]{:S(2)}) collective-permute-start(bf16[128,1536]{1,0:T(8,128)(2,1)S(1)} %slice.117), channel_id=1, source_target_pairs={{0,8},{8,0},{16,24},{24,16},{1,9},{9,1},{17,25},{25,17},{2,10},{10... | collective-permute-start | bytes 1179656 | tf_op jit(solution)/shard_map/ppermute | solution.py:65
  579.9 12.0 %collective-permute-start.44 = (bf16[128,1536]{1,0:T(8,128)(2,1)S(1)}, bf16[128,1536]{1,0:T(8,128)(2,1)S(1)}, u32[]{:S(2)}, u32[]{:S(2)}) collective-permute-start(bf16[128,1536]{1,0:T(8,128)(2,1)S(1)} %slice.118), channel_id=1, source_target_pairs={{0,16},{8,24},{16,0},{24,8},{1,17},{9,25},{17,1},{25,9},{2,18},{10... | collective-permute-start | bytes 1179656 | tf_op jit(solution)/shard_map/ppermute | solution.py:65
  591.9 16.5 %collective-permute-start.46 = (bf16[256,1536]{1,0:T(8,128)(2,1)}, bf16[256,1536]{1,0:T(8,128)(2,1)S(1)}, u32[]{:S(2)}, u32[]{:S(2)}) collective-permute-start(bf16[256,1536]{1,0:T(8,128)(2,1)} %reduce-scatter.8.cloned.1.call-done.refs_0_), channel_id=1, source_target_pairs={{0,16},{8,24},{16,0},{24,8},{1,17},{9,25},{17,1},{25,9},{2,18},{10... | collective-permute-start | bytes 2359304 | tf_op jit(solution)/shard_map/ppermute | solution.py:65
  593.4 16.4 %collective-permute-start.45 = (bf16[256,1536]{1,0:T(8,128)(2,1)}, bf16[256,1536]{1,0:T(8,128)(2,1)S(1)}, u32[]{:S(2)}, u32[]{:S(2)}) collective-permute-start(bf16[256,1536]{1,0:T(8,128)(2,1)} %reduce-scatter.8.cloned.1.call-done.refs_0_), channel_id=1, source_target_pairs={{0,8},{8,0},{16,24},{24,16},{1,9},{9,1},{17,25},{25,17},{2,10},{10... | collective-permute-start | bytes 2359304 | tf_op jit(solution)/shard_map/ppermute | solution.py:65
  598.0 21.8 %copy-start.14 = (bf16[256,1536]{1,0:T(8,128)(2,1)S(1)}, bf16[256,1536]{1,0:T(8,128)(2,1)}, u32[]{:S(2)}) copy-start(bf16[256,1536]{1,0:T(8,128)(2,1)} %reduce-scatter.8.cloned.1.call-done.refs_0_) | copy-start | bytes 2359300
  609.9 7.8 %collective-permute-start.47 = (bf16[128,1536]{1,0:T(8,128)(2,1)S(1)}, bf16[128,1536]{1,0:T(8,128)(2,1)S(1)}, u32[]{:S(2)}, u32[]{:S(2)}) collective-permute-start(bf16[128,1536]{1,0:T(8,128)(2,1)S(1)} %slice.119), channel_id=1, source_target_pairs={{0,8},{8,0},{16,24},{24,16},{1,9},{9,1},{17,25},{25,17},{2,10},{10... | collective-permute-start | bytes 1179656 | tf_op jit(solution)/shard_map/ppermute | solution.py:65
  611.4 7.8 %collective-permute-start.48 = (bf16[128,1536]{1,0:T(8,128)(2,1)S(1)}, bf16[128,1536]{1,0:T(8,128)(2,1)S(1)}, u32[]{:S(2)}, u32[]{:S(2)}) collective-permute-start(bf16[128,1536]{1,0:T(8,128)(2,1)S(1)} %slice.120), channel_id=1, source_target_pairs={{0,16},{8,24},{16,0},{24,8},{1,17},{9,25},{17,1},{25,9},{2,18},{10... | collective-permute-start | bytes 1179656 | tf_op jit(solution)/shard_map/ppermute | solution.py:65
  (30 other events, 131.0 us)
Sparse Core Ops, SparseCore 0:
  10.6 67.4 all-gather.3
  80.3 115.3 all-gather.5
  197.9 62.9 all-gather.7
  269.1 130.0 reduce-scatter.3
  402.0 68.1 reduce-scatter.5
  472.3 69.0 reduce-scatter.7

commit v3 on v2

--- a/solution.py
+++ b/solution.py
@@ -12,7 +12,6 @@
 HEAD_SIZE = 128
 NORM_EPSILON = 1e-06
 ROPE_BASE = 1000000.0
-SCORE_FLOOR = -1e30
 F32 = jnp.float32
 BF16 = jnp.bfloat16
 TINY = pl.CostEstimate(flops=1000, bytes_accessed=1000, transcendentals=0)
@@ -65,36 +64,59 @@
     return lax.ppermute(x, "seq", [(s, s ^ side) for s in range(4)])
 
 
+def put_rows_kernel(count, order_ref, *refs):
+    for n in range(count):
+
+        @pl.when(pl.program_id(0) == n)
+        def _():
+            refs[-1][...] = refs[n][...]
+
+
+def put_rows(pieces, offsets, parts, out):
+    me = lax.axis_index("seq")
+    blocks = [(me ^ k) * parts + n % parts for n, k in enumerate(offsets)]
+    rows, c = pieces[0].shape
+    kept = [] if out is None else [out]
+    return pl.pallas_call(
+        functools.partial(put_rows_kernel, len(pieces)),
+        grid_spec=pltpu.PrefetchScalarGridSpec(
+            num_scalar_prefetch=1,
+            grid=(len(pieces),),
+            in_specs=[pl.BlockSpec((rows, c), lambda n, order: (0, 0))] * len(pieces)
+            + [pl.BlockSpec(memory_space=pl.ANY)] * len(kept),
+            out_specs=pl.BlockSpec((rows, c), lambda n, order: (order[n], 0)),
+        ),
+        out_shape=jax.ShapeDtypeStruct((4 * parts * rows, c), pieces[0].dtype),
+        input_output_aliases={1 + len(pieces): 0} if kept else {},
+        compiler_params=pltpu.CompilerParams(vmem_limit_bytes=60 << 20),
+        cost_estimate=TINY,
+        name="put_rows",
+    )(jnp.stack(blocks).astype(jnp.int32), *pieces, *kept)
+
+
 class Scatter:
-    def __init__(self, partial, count):
-        self.partial, self.count = partial, count
+    def __init__(self, count):
         self.square = by_neighbours(count)
-        self.rows = partial.shape[0] // count
-        self.me = lax.axis_index("seq")
-
-    def block(self, k, start, size):
-        at = ((self.me ^ k) * self.rows + start, 0)
-        return lax.dynamic_slice(self.partial, at, (size, self.partial.shape[1]))
-
-    def first(self):
+
+    def first(self, last):
         if not self.square:
-            return [self.partial]
-        half = self.rows // 2
-        self.tx = swap(self.block(3, 0, half), 1)
-        self.ty = swap(self.block(3, half, half), 2)
+            return [last]
+        half = last.shape[0] // 2
+        self.tx, self.ty = swap(last[:half], 1), swap(last[half:], 2)
         return [self.tx, self.ty]
 
-    def second(self, *others):
+    def second(self, slots):
+        self.slots = slots
         if not self.square:
-            self.sent = [self.partial]
-            self.sum = lax.psum_scatter(self.partial, "seq", scatter_dimension=0, tiled=True)
+            every = slots.reshape(-1, slots.shape[-1])
+            self.sum = lax.psum_scatter(every, "seq", scatter_dimension=0, tiled=True)
+            self.sent = [every]
             return [self.sum]
-        zero = jnp.zeros((self.rows // 2, self.partial.shape[1]), F32)
-        sx = self.block(1, 0, self.rows).astype(F32) + jnp.concatenate([zero, self.ty.astype(F32)])
-        sy = self.block(2, 0, self.rows).astype(F32) + jnp.concatenate([self.tx.astype(F32), zero])
-        sx, sy = sx.astype(BF16), sy.astype(BF16)
-        if others:
-            sx, sy, *_ = lax.optimization_barrier((sx, sy, *others))
+        half = self.tx.shape[0]
+        top, low = slots[1, :half], slots[1, half:]
+        sx = jnp.concatenate([top, add(low, self.ty)])
+        top, low = slots[2, :half], slots[2, half:]
+        sy = jnp.concatenate([add(top, self.tx), low])
         self.sent = [sx, sy]
         self.rx, self.ry = swap(sx, 1), swap(sy, 2)
         return [self.rx, self.ry]
@@ -102,8 +124,39 @@
     def finish(self):
         if not self.square:
             return self.sum.astype(F32)
-        own = self.block(0, 0, self.rows).astype(F32)
-        return own + self.rx.astype(F32) + self.ry.astype(F32)
+        return self.slots[0].astype(F32) + self.rx.astype(F32) + self.ry.astype(F32)
+
+
+def add(a, b):
+    return (a.astype(F32) + b.astype(F32)).astype(BF16)
+
+
+def slot_order(count):
+    me = lax.axis_index("seq")
+    members = [me ^ k if by_neighbours(count) else jnp.int32(k) for k in range(count)]
+    return jnp.stack(members).astype(jnp.int32)
+
+
+def slot_rows(x, order, count, slots):
+    rows = x.shape[0] // count
+    return jnp.concatenate(
+        [lax.dynamic_slice_in_dim(x, order[k] * rows, rows, 0) for k in slots], axis=0
+    )
+
+
+def scattered_product(x, w, order, count, *others):
+    total = Scatter(count)
+    rows = x.shape[0] // count
+    if not total.square:
+        terms = dot_nt(x, w).astype(BF16)
+        total.last = terms
+        total.second(terms.reshape(count, rows, w.shape[0]))
+        return total, [terms]
+    total.last = dot_nt(slot_rows(x, order, count, (3,)), w).astype(BF16)
+    got = total.first(total.last)
+    rest = dot_nt(slot_rows(x, order, count, (0, 1, 2)), w).astype(BF16)
+    total.second(after(rest, *others).reshape(3, rows, w.shape[0]))
+    return total, got
 
 
 class Gather:
@@ -133,18 +186,8 @@
     def column(self):
         if not self.square:
             return lax.all_gather(self.x, "seq", axis=0, tiled=True)
-        rows = self.x.shape[0]
-        out = jnp.zeros((self.count * rows,) + self.x.shape[1:], self.x.dtype)
-        pieces = (
-            (0, 0, self.x),
-            (1, 0, self.bx),
-            (2, 0, self.by),
-            (3, 0, self.ad),
-            (3, rows // 2, self.bd),
-        )
-        for k, start, piece in pieces:
-            out = lax.dynamic_update_slice(out, piece, ((self.me ^ k) * rows + start, 0))
-        return out
+        near = put_rows((self.x, self.bx, self.by), (0, 1, 2), 1, None)
+        return put_rows((self.ad, self.bd), (3, 3), 2, near)
 
     def slots(self):
         if not self.square:
@@ -165,63 +208,37 @@
     return lax.all_gather(w, "fsdp", axis=0, tiled=True)
 
 
-def terms_kernel(starts, order_ref, *refs):
+def terms_kernel(starts, *refs):
     count = len(starts)
-    x_refs, d_ref = refs[:count], refs[count]
-    out_ref = refs[-1]
+    x_refs, d_ref, out_ref = refs[:count], refs[count], refs[-1]
     j = pl.program_id(0)
+    rows = 512
     for n, x_ref in enumerate(x_refs):
         last = starts[n + 1] if n + 1 < count else pl.num_programs(0)
 
         @pl.when((j >= starts[n]) & (j < last))
         def _():
-            total = dot_tn(x_ref[...], d_ref[...])
-            if len(refs) == count + 3:
-                total = total + refs[count + 1][0].astype(F32)
-            out_ref[0] = total.astype(BF16)
-
-
-def weight_terms(xs, d, rows, order, got=None):
-    length, blocks = d.shape[0], order.shape[0]
+            for at in range(0, out_ref.shape[0], rows):
+                here = slice(at, at + rows)
+                out_ref[here, :] = dot_tn(x_ref[:, here], d_ref[...]).astype(BF16)
+
+
+def weight_terms(xs, d):
+    length, columns = xs[0][0].shape
     tiles = sum(n for _, n in xs)
     width = d.shape[1] // tiles
     starts = [sum(n for _, n in xs[:m]) for m in range(len(xs))]
-
-    def x_map(first, n):
-        def index(j, i, order_ref):
-            here = (j >= first) & (j < first + n)
-            return 0, order_ref[jnp.where(here, i, jnp.where(j < first, 0, blocks - 1))]
-
-        return index
-
-    def out_map(j, i, order_ref):
-        return i, 0, j
-
-    in_specs = [
-        pl.BlockSpec((length, rows), x_map(first, n)) for first, (_, n) in zip(starts, xs)
-    ] + [pl.BlockSpec((length, width), lambda j, i, order_ref: (0, j))]
-    operands = [x for x, _ in xs] + [d]
-    if got is not None:
-        in_specs.append(pl.BlockSpec((1, rows, width), out_map))
-        operands.append(got)
+    whole = pl.BlockSpec((length, columns), lambda j: (0, 0), pipeline_mode=pl.Buffered(1))
     return pl.pallas_call(
         functools.partial(terms_kernel, starts),
-        grid_spec=pltpu.PrefetchScalarGridSpec(
-            num_scalar_prefetch=1,
-            grid=(tiles, blocks),
-            in_specs=in_specs,
-            out_specs=pl.BlockSpec((1, rows, width), out_map),
-        ),
-        out_shape=jax.ShapeDtypeStruct((blocks, rows, d.shape[1]), BF16),
-        compiler_params=pltpu.CompilerParams(vmem_limit_bytes=40 << 20),
+        grid=(tiles,),
+        in_specs=[whole] * len(xs) + [pl.BlockSpec((length, width), lambda j: (0, j))],
+        out_specs=pl.BlockSpec((columns, width), lambda j: (0, j)),
+        out_shape=jax.ShapeDtypeStruct((columns, d.shape[1]), BF16),
+        compiler_params=pltpu.CompilerParams(vmem_limit_bytes=58 << 20),
         cost_estimate=TINY,
         name="weight_terms",
-    )(order, *operands)
-
-
-def all_terms(xs, d, rows, count):
-    terms = weight_terms(xs, d, rows, jnp.arange(count, dtype=jnp.int32))
-    return terms.reshape(count * rows, d.shape[1])
+    )(*[x for x, _ in xs], d)
 
 
 def sum_terms(terms):
@@ -239,7 +256,9 @@
 
 
 ROWS = 256
+FORWARD_ROWS = 128
 SCALE = HEAD_SIZE ** (-0.5)
+LOG2_E = 1.4426950408889634
 
 
 def head_norm_rope(u, gain, cosine, sine):
@@ -264,31 +283,37 @@
     return queries, head_norm_rope(k_ref[...].astype(F32), gains[1], cosine, sine)
 
 
-def softmax_rows(queries, key, column, row, i, keys):
-    stacked = jnp.concatenate([q[i * ROWS : (i + 1) * ROWS] for q in queries], axis=0)
-    s = dot_nt(stacked, key[:keys]) * SCALE
-    ids = jnp.concatenate([column[i * ROWS : (i + 1) * ROWS]] * len(queries), axis=0)
-    place = lax.broadcasted_iota(jnp.int32, s.shape, 0) % ROWS + i * ROWS
-    allowed = (ids == row[:, :keys]) & (lax.broadcasted_iota(jnp.int32, s.shape, 1) <= place)
-    s = jnp.where(allowed, s, SCORE_FLOOR)
-    p = jnp.exp(s - jnp.max(s, axis=-1, keepdims=True))
-    return stacked, p * (1.0 / jnp.sum(p, axis=-1, keepdims=True))
+def softmax_rows(queries, key, start, block, i):
+    before, keys = i * block, (i + 1) * block
+    stacked = jnp.concatenate([q[before:keys] for q in queries], axis=0)
+    s = dot_nt(stacked, key[:keys]) * (SCALE * LOG2_E)
+    first = jnp.concatenate([start[before:keys]] * len(queries), axis=0)
+    here = (s.shape[0], block)
+    place = lax.broadcasted_iota(jnp.int32, here, 0) % block
+    index = lax.broadcasted_iota(jnp.int32, here, 1)
+    allowed = (index <= place) & (index + before >= first)
+    e = jnp.where(allowed, jnp.exp2(s[:, before:]), 0.0)
+    if before:
+        index = lax.broadcasted_iota(jnp.int32, (s.shape[0], before), 1)
+        earlier = jnp.where(index >= first, jnp.exp2(s[:, :before]), 0.0)
+        e = jnp.concatenate([earlier, e], axis=1)
+    return stacked, e * (1.0 / jnp.sum(e, axis=-1, keepdims=True))
 
 
 def attend_kernel(
-    ratio, q_ref, k_ref, v_ref, cos_ref, sin_ref, col_ref, row_ref, qg_ref, kg_ref, o_ref
+    ratio, q_ref, k_ref, v_ref, cos_ref, sin_ref, start_ref, qg_ref, kg_ref, o_ref
 ):
     gains = qg_ref[...], kg_ref[...]
     queries, key = heads_of((q_ref, k_ref), gains, cos_ref[...], sin_ref[...], ratio)
-    column, row = col_ref[...], row_ref[...]
-    for i in range(q_ref.shape[0] // ROWS):
-        keys = (i + 1) * ROWS
-        _, p = softmax_rows(queries, key, column, row, i, keys)
-        o = dot(p.astype(BF16), v_ref[:keys, :])
+    start, block = start_ref[...], FORWARD_ROWS
+    for i in range(q_ref.shape[0] // block):
+        keys = (i + 1) * block
+        _, p = softmax_rows(queries, key, start, block, i)
+        o = dot(p.astype(BF16), v_ref[:keys, :]).astype(BF16)
         for h in range(ratio):
-            o_ref[i * ROWS : keys, h * HEAD_SIZE : (h + 1) * HEAD_SIZE] = o[
-                h * ROWS : (h + 1) * ROWS
-            ].astype(BF16)
+            o_ref[i * block : keys, h * HEAD_SIZE : (h + 1) * HEAD_SIZE] = o[
+                h * block : (h + 1) * block
+            ]
 
 
 def attend_back_kernel(
@@ -298,8 +323,7 @@
     v_ref,
     cos_ref,
     sin_ref,
-    col_ref,
-    row_ref,
+    start_ref,
     qg_ref,
     kg_ref,
     do_ref,
@@ -315,12 +339,12 @@
     gains = qg_ref[...], kg_ref[...]
     cosine, sine = cos_ref[...], sin_ref[...]
     queries, key = heads_of((q_ref, k_ref), gains, cosine, sine, ratio)
-    column, row = col_ref[...], row_ref[...]
+    start = start_ref[...]
     dk_all[...] = jnp.zeros_like(dk_all)
     dv_all[...] = jnp.zeros_like(dv_all)
     for i in range(q_ref.shape[0] // ROWS):
         keys = (i + 1) * ROWS
-        stacked, p = softmax_rows(queries, key, column, row, i, keys)
+        stacked, p = softmax_rows(queries, key, start, ROWS, i)
         do = jnp.concatenate(
             [do_ref[i * ROWS : keys, h * HEAD_SIZE : (h + 1) * HEAD_SIZE] for h in range(ratio)],
             axis=0,
@@ -362,7 +386,6 @@
         table,
         table,
         pl.BlockSpec((length, 1), lambda g: (0, 0)),
-        pl.BlockSpec((1, length), lambda g: (0, 0)),
         gain,
         gain,
     ]
@@ -376,7 +399,7 @@
     )
 
 
-def attend(qkv, tables, ids, gains, q_heads, kv_heads):
+def attend(qkv, tables, start, gains, q_heads, kv_heads):
     length = qkv.shape[0]
     ratio, wide, _, inputs = attention_specs(length, q_heads, kv_heads)
     return pl.pallas_call(
@@ -388,10 +411,10 @@
         compiler_params=pltpu.CompilerParams(vmem_limit_bytes=56 << 20),
         cost_estimate=TINY,
         name="attend",
-    )(qkv, qkv, qkv, *tables, *ids, *gains)
-
-
-def attend_back(qkv, tables, ids, gains, d_o, q_heads, kv_heads):
+    )(qkv, qkv, qkv, *tables, start, *gains)
+
+
+def attend_back(qkv, tables, start, gains, d_o, q_heads, kv_heads):
     length = qkv.shape[0]
     ratio, wide, narrow, inputs = attention_specs(length, q_heads, kv_heads)
     gain_spec = pl.BlockSpec((1, 1, HEAD_SIZE), lambda g: (g, 0, 0))
@@ -417,10 +440,10 @@
         compiler_params=pltpu.CompilerParams(vmem_limit_bytes=56 << 20),
         cost_estimate=TINY,
         name="attend_back",
-    )(qkv, qkv, qkv, *tables, *ids, *gains, d_o)
-
-
-def feed_forward_kernel(carried, piece, xb_ref, dy_ref, w_ref, *refs):
+    )(qkv, qkv, qkv, *tables, start, *gains, d_o)
+
+
+def feed_forward_kernel(carried, piece, order_ref, xb_ref, dy_ref, w_ref, *refs):
     sums = refs[:2] if carried else (None, None)
     d_ref, dxb_ref, out_ref = refs[-3:]
     xb, dy = xb_ref[...], dy_ref[...]
@@ -438,28 +461,38 @@
     d_xb = dot_nt(d_gate, w_ref[:, :piece]) + dot_nt(d_up, w_ref[:, piece : 2 * piece])
     out = dot_nt(hidden, w_ref[:, 2 * piece :])
     if carried:
-        d_xb = d_xb + sums[0][...]
-        out = out + sums[1][...]
-    dxb_ref[...] = d_xb.astype(dxb_ref.dtype)
-    out_ref[...] = out.astype(out_ref.dtype)
-
-
-def feed_forward(xb, dy, w, sums, last):
+        d_xb = d_xb + sums[0][0]
+        out = out + sums[1][0]
+    dxb_ref[0] = d_xb.astype(dxb_ref.dtype)
+    out_ref[0] = out.astype(out_ref.dtype)
+
+
+def feed_forward(xb, dy, w, order, sums, kind):
     length, width = xb.shape
     piece = w.shape[1] // 3
-    rows = pl.BlockSpec((ROWS, width), lambda i: (i, 0))
-    whole = pl.BlockSpec(w.shape, lambda i: (0, 0), pipeline_mode=pl.Buffered(1))
-    total = jax.ShapeDtypeStruct((length, width), BF16 if last else F32)
+    count = order.shape[0]
+    block = length // count
+    rows = pl.BlockSpec((block, width), lambda i, order: (order[i], 0))
+    whole = pl.BlockSpec(w.shape, lambda i, order: (0, 0), pipeline_mode=pl.Buffered(1))
+    summed = pl.BlockSpec((1, block, width), lambda i, order: (i, 0, 0))
+    total = jax.ShapeDtypeStruct((count, block, width), kind)
     return pl.pallas_call(
         functools.partial(feed_forward_kernel, bool(sums), piece),
-        grid=(length // ROWS,),
-        in_specs=[rows, rows, whole] + [rows] * len(sums),
-        out_specs=(pl.BlockSpec((ROWS, 3 * piece), lambda i: (i, 0)), rows, rows),
+        grid_spec=pltpu.PrefetchScalarGridSpec(
+            num_scalar_prefetch=1,
+            grid=(count,),
+            in_specs=[rows, rows, whole] + [summed] * len(sums),
+            out_specs=(
+                pl.BlockSpec((block, 3 * piece), lambda i, order: (order[i], 0)),
+                summed,
+                summed,
+            ),
+        ),
         out_shape=(jax.ShapeDtypeStruct((length, 3 * piece), BF16), total, total),
         compiler_params=pltpu.CompilerParams(vmem_limit_bytes=60 << 20),
         cost_estimate=TINY,
         name="feed_forward",
-    )(xb, dy, w, *sums)
+    )(order, xb, dy, w, *sums)
 
 
 def place_kernel(widths, tiles, me_ref, *refs):
@@ -562,61 +595,62 @@
 
         inputs = tokens[0].astype(F32)
         segments = segment_ids[0]
+        order = slot_order(seq_count)
         get_dy = Gather(cotangent[0], seq_count)
+        get_dy.first()
         get_xa = Gather((inputs * inverse_rms(inputs) * input_gain).astype(BF16), seq_count)
-        got = get_xa.first()
-        get_dy.x = after(get_dy.x, *got)
+        get_xa.first()
         get_xa.second()
-        get_dy.first()
         xa = get_xa.column()
 
-        tables = rotary_tables(positions(segments))
-        ids = segments[:, None], segments[None, :]
+        place_in_document = positions(segments)
+        tables = rotary_tables(place_in_document)
+        start = (jnp.arange(segments.shape[0], dtype=jnp.int32) - place_in_document)[:, None]
         head_gains = query_gain[None, :], key_gain[None, :]
         qkv = dot(xa, w_qkv).astype(BF16)
         get_dy.second(qkv)
         dy = get_dy.column()
-        o = attend(qkv, tables, ids, head_gains, q_heads, kv_heads)
-        sum_r = Scatter(dot_nt(after(o, dy), w_out).astype(BF16), seq_count)
-        sum_r.first()
-        sum_r.second()
+        o = attend(qkv, tables, start, head_gains, q_heads, kv_heads)
+        sum_r, _ = scattered_product(after(o, dy), w_out, order, seq_count)
         resid = inputs + sum_r.finish()
         get_xb = Gather((resid * inverse_rms(resid) * post_gain).astype(BF16), seq_count)
         get_xb.first()
         get_xb.second()
         xb = get_xb.column()
 
-        d1, *sums = feed_forward(xb, dy, w_mlp[0], (), False)
-        terms1 = all_terms([(xb, 2), (dy, 1)], d1, rows, fsdp_count)
+        d1, *sums = feed_forward(xb, dy, w_mlp[0], order, (), F32)
+        terms1 = weight_terms([(xb, 2), (dy, 1)], d1)
         share1 = sum_terms(terms1)
-        d2, d_xb, out = feed_forward(after(xb, terms1), dy, w_mlp[1], tuple(sums), True)
-        sum_dxb = Scatter(d_xb, seq_count)
-        sum_dxb.first()
-        got = sum_dxb.second()
-        terms2 = all_terms([(xb, 2), (dy, 1)], after(d2, *sum_dxb.sent), rows, fsdp_count)
+        xb2 = after(xb, terms1)
+        d2, d_xb, out = feed_forward(xb2, dy, w_mlp[1], order, tuple(sums), BF16)
+        sum_dxb = Scatter(seq_count)
+        sum_dxb.first(d_xb[-1])
+        sum_dxb.second(d_xb)
+        terms2 = weight_terms([(xb, 2), (dy, 1)], after(d2, *sum_dxb.sent))
         du, post_terms = norm_back(resid, post_gain, after(sum_dxb.finish(), terms2))
         d_resid = cotangent[0].astype(F32) + du
         get_drl = Gather(d_resid.astype(BF16), seq_count)
         get_drl.first()
         get_drl.second()
         drl = get_drl.column()
-        sum_out = Scatter(after(out, drl), seq_count)
-        sum_out.first()
+        share2 = sum_terms(after(terms2, drl))
+        sum_out = Scatter(seq_count)
+        got = sum_out.first(after(out, drl)[-1])
         d_o = dot(drl, w_out).astype(BF16)
-        got = sum_out.second(d_o)
-        share2 = sum_terms(after(terms2, share1, *sum_out.sent))
+        sum_out.second(after(out, d_o))
         dq, dk, dv, q_terms, k_terms = attend_back(
-            qkv, tables, ids, head_gains, after(d_o, *sum_out.sent), q_heads, kv_heads
+            qkv, tables, start, head_gains, after(d_o, *sum_out.sent), q_heads, kv_heads
         )
+        out = resid + sum_out.finish()
+        dq, out = lax.optimization_barrier((dq, out))
+        get1 = Gather(after(share1, dq), seq_count)
+        near = get1.first()
         d_attn = jnp.concatenate([dq, dk, dv, o], axis=1)
-        out = resid + sum_out.finish()
-        d_attn, out = lax.optimization_barrier((d_attn, out))
-        sum_dxa = Scatter(dot_nt(d_attn[:, :qkv_cols], w_qkv).astype(BF16), seq_count)
-        sum_dxa.first()
-        sum_dxa.second()
-        terms3 = all_terms([(xa, 2), (drl, 1)], after(d_attn, *sum_dxa.sent), rows, fsdp_count)
-        share3 = sum_terms(after(terms3, share2))
-        du, in_terms = norm_back(inputs, input_gain, after(sum_dxa.finish(), terms3))
+        sum_dxa, got = scattered_product(d_attn[:, :qkv_cols], w_qkv, order, seq_count, *near)
+        terms3 = weight_terms([(xa, 2), (drl, 1)], after(d_attn, sum_dxa.last))
+        get1.second(*got)
+        share3 = sum_terms(after(terms3, share2, *sum_dxa.sent))
+        du, in_terms = norm_back(inputs, input_gain, after(sum_dxa.finish(), *get1.slots()))
         d_inputs = d_resid + du
 
         gains = jnp.concatenate(
@@ -628,19 +662,16 @@
             ]
         )
         width = post_gain.shape[0]
-        get1 = Gather(after(share1, in_terms), seq_count)
-        get1.first()
+        get2 = Gather(after(share2, in_terms), seq_count)
+        get2.first()
         gains = sum_all(gains, "fsdp", fsdp_count)
-        get1.second(gains)
-        get2 = Gather(after(share2, *get1.slots()), seq_count)
-        get2.first()
         mlp = place(get1.slots(), (pieces[0],) * 3, 2, 0, 3, (), me, seq_count)
-        gains = sum_all(after(gains, *get1.slots()), "seq", seq_count)
         get2.second(gains, *mlp)
-        mlp = place(get2.slots(), (pieces[1],) * 3, 1, 2, 3, mlp, me, seq_count)
         get3 = Gather(after(share3, *get2.slots()), seq_count)
         get3.first()
-        get3.second(*mlp)
+        mlp = place(get2.slots(), (pieces[1],) * 3, 1, 2, 3, mlp, me, seq_count)
+        gains = sum_all(after(gains, *get2.slots()), "seq", seq_count)
+        get3.second(gains, *mlp)
         widths = (q_cols, kv_cols, kv_cols, q_cols)
         g_q, g_k, g_v, g_out = place(get3.slots(), widths, 1, 0, 1, (), me, seq_count)
         return (

time: 642 us -> 597 us (0.930)
  waiting for transfers between devices: 277 us -> 231 us
  local copies, waits for them, and re-layouts: 45.9 us -> 38.1 us
  matrix products: 27.5 us -> 35.2 us
    ppermute x44, waiting for transfers between devices: 243 us -> 200 us  [swap(): return lax.ppermute(x, 'seq', [(s, s ^ side) for s in range(4)])]
    dynamic_update_slice x17 -> x0, local copies, waits for them, and re-layouts: 15.3 us -> none  [column(): lax.dynamic_update_slice(out, piece, ((self.me ^ k) * rows + start, 0))]
    reduce_scatter x3, waiting for transfers between devices: 13.3 us -> 0.02 us  [sum_terms(): return lax.psum_scatter(terms, 'fsdp', scatter_dimension=0, tiled=True)]
    all_gather x3, waiting for transfers between devices: 0.02 us -> 10.4 us  [gather_weight(): return lax.all_gather(w, 'fsdp', axis=0, tiled=True)]
    pallas_call x3 -> x11, Pallas kernels: 67.8 us -> 75.6 us  [the longest x3 45.2 us: weight_terms(): pl.pallas_call(functools.partial(terms_kernel, starts), grid=(tiles,), in...]
    slice x14, local copies, waits for them, and re-layouts: 6.11 us -> 13.4 us  [second(): ahead, below = (self.by[:half], self.bx[half:])]
    dot_general x2 -> x4, matrix products: 12.7 us -> 19.8 us  [dot_nt(): lax.dot_general(a, b, (((1,), (1,)), ((), ())), preferred_element_type=F32)]
    ppermute x5, starting transfers between devices: 9.12 us -> 2.34 us  [sum_all(): x = x + lax.ppermute(x, axis, [(i, i ^ bit) for i in range(count)])]
  transfers between devices with their start and end apart: 55 -> 55, of which waited for: 36 -> 37; matrix products, arithmetic and copies ran while one was open for 15% -> 16% of each run, Pallas kernels for 27% -> 30%
where the time goes in v3:
time: 597 us; the launch traced here: 587 us
  waiting for transfers between devices  231 us (39%)
  Pallas kernels  181 us (30%)
  starting transfers between devices  51.2 us (9%)
  local copies, waits for them, and re-layouts  38.1 us (6%)
  other arithmetic  35.5 us (6%)
  matrix products  35.2 us (6%)
  between operations  15.1 us (3%)
    ppermute x44, waiting for transfers between devices, swap(): return lax.ppermute(x, 'seq', [(s, s ^ side) for s in range(4)])  200 us
    pallas_call x2, Pallas kernels, feed_forward(): pl.pallas_call(functools.partial(feed_forward_kernel, bool(sums), piece),...  56.8 us
    ppermute x44, starting transfers between devices, swap(): return lax.ppermute(x, 'seq', [(s, s ^ side) for s in range(4)])  48.6 us
    pallas_call x3, Pallas kernels, weight_terms(): pl.pallas_call(functools.partial(terms_kernel, starts), grid=(tiles,), in...  45.2 us
    pallas_call x8, Pallas kernels, put_rows(): pl.pallas_call(functools.partial(put_rows_kernel, len(pieces)), grid_spec...  30.4 us
    pallas_call x1, Pallas kernels, attend_back(): pl.pallas_call(functools.partial(attend_back_kernel, ratio), grid=(kv_hea...  22.6 us
    ppermute x5, waiting for transfers between devices, sum_all(): x = x + lax.ppermute(x, axis, [(i, i ^ bit) for i in range(count)])  21.4 us
    dot_general x4, matrix products, dot_nt(): lax.dot_general(a, b, (((1,), (1,)), ((), ())), preferred_element_type=F32)  19.8 us
  transfers between devices with their start and end apart: 55, of which 37 were waited for; matrix products, arithmetic and copies ran while one was open for 16% of the time, Pallas kernels for 30%

profile of v3, /device:TPU:0, one launch (start us, length us, event | category | flops | bytes accessed | tf_op | source)
XLA Modules:
  0.0 587.2 jit_solution(14514126552736602488)
XLA Ops:
  16.0 3.0 collective-permute-start.2
  21.8 21.3 %collective-permute-done.2.refs_1_ = bf16[256,2048]{1,0:T(8,128)(2,1)} collective-permute-done((bf16[256,2048]{1,0:T(8,128)(2,1)S(1)}, bf16[256,2048]{1,0:T(8,128)(2,1)}, u32[]{:S(2)}, u32[]{:S(2)}) %collective-permute-start.2) | collective-permute-done | bytes 1048608 | tf_op jit(solution)/shard_map/ppermute | solution.py:64
  43.1 1.9 slice.238
  45.0 2.0 collective-permute-start.3
  47.1 1.9 slice.237
  52.7 4.6 put_rows.8.refs_2_
  57.4 8.2 %collective-permute-done.5.refs_1_ = bf16[256,2048]{1,0:T(8,128)(2,1)} collective-permute-done((bf16[256,2048]{1,0:T(8,128)(2,1)S(1)}, bf16[256,2048]{1,0:T(8,128)(2,1)}, u32[]{:S(2)}, u32[]{:S(2)}) %collective-permute-start.5) | collective-permute-done | bytes 1048608 | tf_op jit(solution)/shard_map/ppermute | solution.py:64
  65.6 1.9 slice.242
  67.7 1.9 slice.241
  69.6 7.9 %collective-permute-done.3.refs_1_ = bf16[128,2048]{1,0:T(8,128)(2,1)} collective-permute-done((bf16[128,2048]{1,0:T(8,128)(2,1)}, bf16[128,2048]{1,0:T(8,128)(2,1)}, u32[]{:S(2)}, u32[]{:S(2)}) %collective-permute-start.3) | collective-permute-done | bytes 524320 | tf_op jit(solution)/shard_map/ppermute | solution.py:64
  77.5 2.9 put_rows.9.refs_0_
  80.3 9.3 %fusion.22.q_ref.k_ref.v_ref = bf16[1024,1024]{1,0:T(8,128)(2,1)} fusion(bf16[1024,2048]{1,0:T(8,128)(2,1)} %put_rows.9.refs_0_, bf16[2048,1536]{1,0:T(8,128)(2,1)} %all-gather.4.cloned.1.call-done), kind=kOutput, calls=%fused_computation.35 | convolution fusion | flops 4296015872 | bytes 10485760 | tf_op jit(solution)/shard_map/dot_general | solution.py:21
  90.0 1.7 collective-permute-start.7
  91.7 1.9 fusion.53
  95.8 4.7 put_rows.10.refs_2_
  100.5 12.7 %attend.1 = bf16[1024,512]{1,0:T(8,128)(2,1)} custom-call(bf16[1024,1024]{1,0:T(8,128)(2,1)} %fusion.22.q_ref.k_ref.v_ref, bf16[1024,1024]{1,0:T(8,128)(2,1)} %fusion.22.q_ref.k_ref.v_ref, bf16[1024,1024]{1,0:T(8,128)(2,1)} %fusion.22.q_ref.k_ref.v_ref, f32[1024,128]{1,0:T(8,128)} %get-tuple-element.157.cos_ref, f32[1024,128]{1,0:T(8,128)} %get-tuple-element.158.sin_ref, ...), custom_call_target="tpu_custom_call" | custom-call | flops 1000 | bytes 1000 | tf_op jit(solution)/shard_map/attend/pallas_call | solution.py:405
  114.0 3.1 put_rows.11.dy_ref.refs_1_
  117.1 2.3 convolution_convert_fusion.2
  120.0 1.7 collective-permute-start.10
  121.7 3.4 convolution_convert_fusion
  125.3 6.5 %collective-permute-done.8 = bf16[128,2048]{1,0:T(8,128)(2,1)S(1)} collective-permute-done((bf16[128,2048]{1,0:T(8,128)(2,1)S(1)}, bf16[128,2048]{1,0:T(8,128)(2,1)S(1)}, u32[]{:S(2)}, u32[]{:S(2)}) %collective-permute-start.8) | collective-permute-done | bytes 524320 | tf_op jit(solution)/shard_map/ppermute | solution.py:64
  135.6 19.4 %collective-permute-done.11 = bf16[256,2048]{1,0:T(8,128)(2,1)S(1)} collective-permute-done((bf16[256,2048]{1,0:T(8,128)(2,1)S(1)}, bf16[256,2048]{1,0:T(8,128)(2,1)S(1)}, u32[]{:S(2)}, u32[]{:S(2)}) %collective-permute-start.11) | collective-permute-done | bytes 1048608 | tf_op jit(solution)/shard_map/ppermute | solution.py:64
  159.2 19.5 %collective-permute-done.14.refs_1_ = bf16[256,2048]{1,0:T(8,128)(2,1)S(1)} collective-permute-done((bf16[256,2048]{1,0:T(8,128)(2,1)S(1)}, bf16[256,2048]{1,0:T(8,128)(2,1)S(1)}, u32[]{:S(2)}, u32[]{:S(2)}) %collective-permute-start.14) | collective-permute-done | bytes 1048608 | tf_op jit(solution)/shard_map/ppermute | solution.py:64
  183.7 4.6 put_rows.12.refs_2_
  188.3 2.2 collective-permute-done.15.refs_1_
  191.3 2.9 put_rows.13.xb_ref.refs_0_
  195.7 35.3 %feed_forward.2 = (bf16[1024,3072]{1,0:T(8,128)(2,1)}, f32[4,256,2048]{2,1,0:T(8,128)}, f32[4,256,2048]{2,1,0:T(8,128)}) custom-call(s32[4]{0:T(128)} %pad_add_fusion.2.order_ref, bf16[1024,2048]{1,0:T(8,128)(2,1)} %put_rows.13.xb_ref.refs_0_, bf16[1024,2048]{1,0:T(8,128)(2,1)} %put_rows.11.dy_ref.refs_1_, bf16[2048,3072]{1,0:T(8,128)(2,1)} %all-gather.6.cloned.1.call-done.w_ref), custom_call_target="tpu_custom_call" | custom-call | flops 1000 | bytes 1000 | tf_op jit(solution)/shard_map/feed_forward/pallas_call | solution.py:479
  231.0 20.4 %weight_terms.3 = bf16[2048,3072]{1,0:T(8,128)(2,1)} custom-call(bf16[1024,2048]{1,0:T(8,128)(2,1)} %put_rows.13.xb_ref.refs_0_, bf16[1024,2048]{1,0:T(8,128)(2,1)} %put_rows.11.dy_ref.refs_1_, bf16[1024,3072]{1,0:T(8,128)(2,1)} %get-tuple-element.63.refs_2_), custom_call_target="tpu_custom_call" | custom-call | flops 1000 | bytes 1000 | tf_op jit(solution)/shard_map/weight_terms/pallas_call | solution.py:232
  251.4 8.9 %all-gather.8.cloned.1.call-done.w_ref = bf16[2048,1536]{1,0:T(8,128)(2,1)} async-done(((bf16[256,1536]{1,0:T(8,128)(2,1)}), bf16[2048,1536]{1,0:T(8,128)(2,1)}) %all-gather.8.cloned.1.call-update) | async-done | bytes 6291472 | tf_op jit(solution)/shard_map/all_gather | solution.py:208
  260.3 21.5 %feed_forward.3 = (bf16[1024,1536]{1,0:T(8,128)(2,1)}, bf16[4,256,2048]{2,1,0:T(8,128)(2,1)}, bf16[4,256,2048]{2,1,0:T(8,128)(2,1)}) custom-call(s32[4]{0:T(128)} %pad_add_fusion.2.order_ref, bf16[1024,2048]{1,0:T(8,128)(2,1)} %put_rows.13.xb_ref.refs_0_, bf16[1024,2048]{1,0:T(8,128)(2,1)} %put_rows.11.dy_ref.refs_1_, ...), custom_call_target="tpu_custom_call" | custom-call | flops 1000 | bytes 1000 | tf_op jit(solution)/shard_map/feed_forward/pallas_call | solution.py:479
  281.8 1.7 slice_bitcast_fusion.15
  286.6 11.2 %collective-permute-done.18 = bf16[128,2048]{1,0:T(8,128)(2,1)S(1)} collective-permute-done((bf16[128,2048]{1,0:T(8,128)(2,1)S(1)}, bf16[128,2048]{1,0:T(8,128)(2,1)S(1)}, u32[]{:S(2)}, u32[]{:S(2)}) %collective-permute-start.18) | collective-permute-done | bytes 524320 | tf_op jit(solution)/shard_map/ppermute | solution.py:64
  304.8 12.4 %weight_terms.4 = bf16[2048,1536]{1,0:T(8,128)(2,1)} custom-call(bf16[1024,2048]{1,0:T(8,128)(2,1)} %put_rows.13.xb_ref.refs_0_, bf16[1024,2048]{1,0:T(8,128)(2,1)} %put_rows.11.dy_ref.refs_1_, bf16[1024,1536]{1,0:T(8,128)(2,1)} %get-tuple-element.69.refs_2_), custom_call_target="tpu_custom_call" | custom-call | flops 1000 | bytes 1000 | tf_op jit(solution)/shard_map/weight_terms/pallas_call | solution.py:232
  317.2 9.2 %collective-permute-done.19 = bf16[256,2048]{1,0:T(8,128)(2,1)} collective-permute-done((bf16[256,2048]{1,0:T(8,128)(2,1)}, bf16[256,2048]{1,0:T(8,128)(2,1)}, u32[]{:S(2)}, u32[]{:S(2)}) %collective-permute-start.19) | collective-permute-done | bytes 1048608 | tf_op jit(solution)/shard_map/ppermute | solution.py:64
  326.4 2.1 collective-permute-done.17
  328.5 2.1 fusion.21
  334.8 21.8 %collective-permute-done.22.refs_1_ = bf16[256,2048]{1,0:T(8,128)(2,1)S(1)} collective-permute-done((bf16[256,2048]{1,0:T(8,128)(2,1)S(1)}, bf16[256,2048]{1,0:T(8,128)(2,1)S(1)}, u32[]{:S(2)}, u32[]{:S(2)}) %collective-permute-start.22) | collective-permute-done | bytes 1048608 | tf_op jit(solution)/shard_map/ppermute | solution.py:64
  360.6 4.6 put_rows.14.refs_2_
  365.3 3.8 collective-permute-done.23.refs_1_
  369.0 2.2 collective-permute-done.21.refs_0_
  371.2 2.9 put_rows.15.refs_1_
  377.7 6.2 %fusion.34.do_ref = bf16[1024,512]{1,0:T(8,128)(2,1)} fusion(bf16[1024,2048]{1,0:T(8,128)(2,1)} %put_rows.15.refs_1_, bf16[2048,1536]{1,0:T(8,128)(2,1)} %all-gather.4.cloned.1.call-done), kind=kOutput, calls=%fused_computation.46 | convolution fusion | flops 2148007936 | bytes 7340032 | tf_op jit(solution)/shard_map/dot_general | solution.py:21
  384.0 1.8 collective-permute-done.25
  391.4 22.6 %attend_back.1 = (bf16[1024,512]{1,0:T(8,128)(2,1)}, bf16[1024,256]{1,0:T(8,128)(2,1)}, bf16[1024,256]{1,0:T(8,128)(2,1)}, f32[2,1,128]{2,1,0:T(1,128)}, f32[2,1,128]{2,1,0:T(1,128)}) custom-call(bf16[1024,1024]{1,0:T(8,128)(2,1)} %fusion.22.q_ref.k_ref.v_ref, bf16[1024,1024]{1,0:T(8,128)(2,1)} %fusion.22.q_ref.k_ref.v_ref, ...), custom_call_target="tpu_custom_call" | custom-call | flops 1000 | bytes 1000 | tf_op jit(solution)/shard_map/attend_back/pallas_call | solution.py:423
  414.0 3.3 fusion.20
  418.6 5.2 fusion.9
  425.1 2.3 fusion.63
  430.3 8.8 %convolution_convert_fusion.1 = bf16[768,2048]{1,0:T(8,128)(2,1)} fusion(bf16[2048,1536]{1,0:T(8,128)(2,1)} %all-gather.4.cloned.1.call-done, bf16[256,1024]{1,0:T(8,128)(2,1)S(1)} %get-tuple-element.137, bf16[256,1024]{1,0:T(8,128)(2,1)S(1)} %get-tuple-element.138, bf16[256,1024]{1,0:T(8,128)(2,1)S(1)} %get-tuple-element.136), kind=kOutput, calls=%fused_computation.1 | convolution fusion | flops 3227516928 | bytes 8912896 | tf_op jit(solution)/shard_map/dot_general | solution.py:25
  439.1 1.9 pad_maximum_fusion.refs_2_
  441.0 12.4 %weight_terms.5 = bf16[2048,1536]{1,0:T(8,128)(2,1)} custom-call(bf16[1024,2048]{1,0:T(8,128)(2,1)} %put_rows.9.refs_0_, bf16[1024,2048]{1,0:T(8,128)(2,1)} %put_rows.15.refs_1_, bf16[1024,1536]{1,0:T(8,128)(2,1)} %pad_maximum_fusion.refs_2_), custom_call_target="tpu_custom_call" | custom-call | flops 1000 | bytes 1000 | tf_op jit(solution)/shard_map/weight_terms/pallas_call | solution.py:232
  453.4 7.2 %collective-permute-done.29.refs_2_ = bf16[256,3072]{1,0:T(8,128)(2,1)S(1)} collective-permute-done((bf16[256,3072]{1,0:T(8,128)(2,1)}, bf16[256,3072]{1,0:T(8,128)(2,1)S(1)}, u32[]{:S(2)}, u32[]{:S(2)}) %collective-permute-start.29) | collective-permute-done | bytes 1572896 | tf_op jit(solution)/shard_map/ppermute | solution.py:64
  462.2 4.2 collective-permute-done.30
  466.5 1.9 fusion.39
  474.9 16.4 %collective-permute-done.34 = bf16[128,3072]{1,0:T(8,128)(2,1)S(1)} collective-permute-done((bf16[128,3072]{1,0:T(8,128)(2,1)S(1)}, bf16[128,3072]{1,0:T(8,128)(2,1)S(1)}, u32[]{:S(2)}, u32[]{:S(2)}) %collective-permute-start.34) | collective-permute-done | bytes 786464 | tf_op jit(solution)/shard_map/ppermute | solution.py:64
  493.2 13.5 %collective-permute-done.33 = bf16[256,2048]{1,0:T(8,128)(2,1)S(1)} collective-permute-done((bf16[256,2048]{1,0:T(8,128)(2,1)S(1)}, bf16[256,2048]{1,0:T(8,128)(2,1)S(1)}, u32[]{:S(2)}, u32[]{:S(2)}) %collective-permute-start.33) | collective-permute-done | bytes 1048608 | tf_op jit(solution)/shard_map/ppermute | solution.py:64
  506.7 1.9 convert_add_fusion.3
  510.5 2.4 fusion.61
  517.1 4.4 collective-permute-done.37
  524.6 5.5 place.3
  533.4 8.9 %collective-permute-done.41 = bf16[128,1536]{1,0:T(8,128)(2,1)S(1)} collective-permute-done((bf16[128,1536]{1,0:T(8,128)(2,1)S(1)}, bf16[128,1536]{1,0:T(8,128)(2,1)S(1)}, u32[]{:S(2)}, u32[]{:S(2)}) %collective-permute-start.41) | collective-permute-done | bytes 393248 | tf_op jit(solution)/shard_map/ppermute | solution.py:64
  545.5 15.8 %collective-permute-done.43 = f32[4352]{0:T(1024)S(1)} collective-permute-done((f32[4352]{0:T(1024)S(1)}, f32[4352]{0:T(1024)S(1)}, u32[]{:S(2)}, u32[]{:S(2)}) %collective-permute-start.43) | collective-permute-done | bytes 17440 | tf_op jit(solution)/shard_map/ppermute | solution.py:253
  562.7 4.6 place.4
  570.1 5.1 collective-permute-done.47
  577.2 3.0 place.5
  (257 shorter events, 99.2 us)
Async XLA Ops:
  7.2 73.2 %all-gather.4.cloned.1.call-start = ((), (), s32[]{:S(2)}) async-start(), calls=%async_computation.3 | async-start | bytes 7077888 | tf_op jit(solution)/shard_map/all_gather | solution.py:208
  10.4 185.2 %all-gather.6.cloned.1.call-start = ((), (), s32[]{:S(2)}) async-start(), calls=%async_computation.4 | async-start | bytes 14155776 | tf_op jit(solution)/shard_map/all_gather | solution.py:208
  13.1 247.2 %all-gather.8.cloned.1.call-start = ((), (), s32[]{:S(2)}) async-start(), calls=%async_computation.5 | async-start | bytes 7077888 | tf_op jit(solution)/shard_map/all_gather | solution.py:208
  15.3 408.5 %reduce-scatter.4.cloned.1.call-start = ((), (), s32[]{:S(2)}) async-start(), calls=%async_computation.6 | async-start | bytes 14155776 | tf_op jit(solution)/shard_map/reduce_scatter | solution.py:245
  16.0 36.8 %copy-start.21 = (bf16[256,2048]{1,0:T(8,128)(2,1)}, bf16[256,2048]{1,0:T(8,128)(2,1)S(1)}, u32[]{:S(2)}) copy-start(bf16[256,2048]{1,0:T(8,128)(2,1)S(1)} %fusion.12.refs_0_) | copy-start | bytes 3145732
  16.0 27.1 %collective-permute-start.2 = (bf16[256,2048]{1,0:T(8,128)(2,1)S(1)}, bf16[256,2048]{1,0:T(8,128)(2,1)}, u32[]{:S(2)}, u32[]{:S(2)}) collective-permute-start(bf16[256,2048]{1,0:T(8,128)(2,1)S(1)} %fusion.12.refs_0_), channel_id=1, source_target_pairs={{0,8},{8,0},{16,24},{24,16},{1,9},{9,1},{17,25},{25,17},{2,10},{10... | collective-permute-start | bytes 3145736 | tf_op jit(solution)/shard_map/ppermute | solution.py:64
  19.0 28.1 %collective-permute-start = (bf16[256,2048]{1,0:T(8,128)(2,1)S(1)}, bf16[256,2048]{1,0:T(8,128)(2,1)}, u32[]{:S(2)}, u32[]{:S(2)}) collective-permute-start(bf16[256,2048]{1,0:T(8,128)(2,1)S(1)} %fusion.12.refs_0_), channel_id=1, source_target_pairs={{0,16},{8,24},{16,0},{24,8},{1,17},{9,25},{17,1},{25,9},{2,18},{10... | collective-permute-start | bytes 3145736 | tf_op jit(solution)/shard_map/ppermute | solution.py:64
  20.5 45.0 %collective-permute-start.5 = (bf16[256,2048]{1,0:T(8,128)(2,1)S(1)}, bf16[256,2048]{1,0:T(8,128)(2,1)}, u32[]{:S(2)}, u32[]{:S(2)}) collective-permute-start(bf16[256,2048]{1,0:T(8,128)(2,1)S(1)} %bitcast.105), channel_id=1, source_target_pairs={{0,8},{8,0},{16,24},{24,16},{1,9},{9,1},{17,25},{25,17},{2,10},{10... | collective-permute-start | bytes 3145736 | tf_op jit(solution)/shard_map/ppermute | solution.py:64
  21.1 46.6 %collective-permute-start.4 = (bf16[256,2048]{1,0:T(8,128)(2,1)S(1)}, bf16[256,2048]{1,0:T(8,128)(2,1)}, u32[]{:S(2)}, u32[]{:S(2)}) collective-permute-start(bf16[256,2048]{1,0:T(8,128)(2,1)S(1)} %bitcast.106), channel_id=1, source_target_pairs={{0,16},{8,24},{16,0},{24,8},{1,17},{9,25},{17,1},{25,9},{2,18},{10... | collective-permute-start | bytes 3145736 | tf_op jit(solution)/shard_map/ppermute | solution.py:64
  45.0 32.4 %collective-permute-start.3 = (bf16[128,2048]{1,0:T(8,128)(2,1)}, bf16[128,2048]{1,0:T(8,128)(2,1)}, u32[]{:S(2)}, u32[]{:S(2)}) collective-permute-start(bf16[128,2048]{1,0:T(8,128)(2,1)} %slice.238), channel_id=1, source_target_pairs={{0,16},{8,24},{16,0},{24,8},{1,17},{9,25},{17,1},{25,9},{2,18},{10... | collective-permute-start | bytes 1572872 | tf_op jit(solution)/shard_map/ppermute | solution.py:64
  49.0 28.5 %collective-permute-start.1 = (bf16[128,2048]{1,0:T(8,128)(2,1)}, bf16[128,2048]{1,0:T(8,128)(2,1)}, u32[]{:S(2)}, u32[]{:S(2)}) collective-permute-start(bf16[128,2048]{1,0:T(8,128)(2,1)} %slice.237), channel_id=1, source_target_pairs={{0,8},{8,0},{16,24},{24,16},{1,9},{9,1},{17,25},{25,17},{2,10},{10... | collective-permute-start | bytes 1572872 | tf_op jit(solution)/shard_map/ppermute | solution.py:64
  89.6 23.5 %collective-permute-start.6 = (bf16[128,2048]{1,0:T(8,128)(2,1)}, bf16[128,2048]{1,0:T(8,128)(2,1)S(1)}, u32[]{:S(2)}, u32[]{:S(2)}) collective-permute-start(bf16[128,2048]{1,0:T(8,128)(2,1)} %slice.241), channel_id=1, source_target_pairs={{0,8},{8,0},{16,24},{24,16},{1,9},{9,1},{17,25},{25,17},{2,10},{10... | collective-permute-start | bytes 1572872 | tf_op jit(solution)/shard_map/ppermute | solution.py:64
  90.0 23.2 %collective-permute-start.7 = (bf16[128,2048]{1,0:T(8,128)(2,1)}, bf16[128,2048]{1,0:T(8,128)(2,1)}, u32[]{:S(2)}, u32[]{:S(2)}) collective-permute-start(bf16[128,2048]{1,0:T(8,128)(2,1)} %slice.242), channel_id=1, source_target_pairs={{0,16},{8,24},{16,0},{24,8},{1,17},{9,25},{17,1},{25,9},{2,18},{10... | collective-permute-start | bytes 1572872 | tf_op jit(solution)/shard_map/ppermute | solution.py:64
  119.5 12.2 %collective-permute-start.8 = (bf16[128,2048]{1,0:T(8,128)(2,1)S(1)}, bf16[128,2048]{1,0:T(8,128)(2,1)S(1)}, u32[]{:S(2)}, u32[]{:S(2)}) collective-permute-start(bf16[128,2048]{1,0:T(8,128)(2,1)S(1)} %get-tuple-element.141), channel_id=1, source_target_pairs={{0,16},{8,24},{16,0},{24,8},{1,17},{9,25},{17,1},{25,9},{2,18},{10... | collective-permute-start | bytes 1572872 | tf_op jit(solution)/shard_map/ppermute | solution.py:64
  120.0 12.0 %collective-permute-start.10 = (bf16[128,2048]{1,0:T(8,128)(2,1)S(1)}, bf16[128,2048]{1,0:T(8,128)(2,1)S(1)}, u32[]{:S(2)}, u32[]{:S(2)}) collective-permute-start(bf16[128,2048]{1,0:T(8,128)(2,1)S(1)} %get-tuple-element.142), channel_id=1, source_target_pairs={{0,8},{8,0},{16,24},{24,16},{1,9},{9,1},{17,25},{25,17},{2,10},{10... | collective-permute-start | bytes 1572872 | tf_op jit(solution)/shard_map/ppermute | solution.py:64
  132.5 22.5 %collective-permute-start.11 = (bf16[256,2048]{1,0:T(8,128)(2,1)S(1)}, bf16[256,2048]{1,0:T(8,128)(2,1)S(1)}, u32[]{:S(2)}, u32[]{:S(2)}) collective-permute-start(bf16[256,2048]{1,0:T(8,128)(2,1)S(1)} %pad_maximum_fusion.3), channel_id=1, source_target_pairs={{0,16},{8,24},{16,0},{24,8},{1,17},{9,25},{17,1},{25,9},{2,18},{10... | collective-permute-start | bytes 3145736 | tf_op jit(solution)/shard_map/ppermute | solution.py:64
  134.2 23.0 %copy-start.39 = (f32[2048]{0:T(1024)S(1)}, f32[2048]{0:T(1024)}, u32[]{:S(2)}) copy-start(f32[2048]{0:T(1024)} %param.23) | copy-start | bytes 24580
  134.2 22.1 %collective-permute-start.9 = (bf16[256,2048]{1,0:T(8,128)(2,1)S(1)}, bf16[256,2048]{1,0:T(8,128)(2,1)S(1)}, u32[]{:S(2)}, u32[]{:S(2)}) collective-permute-start(bf16[256,2048]{1,0:T(8,128)(2,1)S(1)} %pad_maximum_fusion.2), channel_id=1, source_target_pairs={{0,8},{8,0},{16,24},{24,16},{1,9},{9,1},{17,25},{25,17},{2,10},{10... | collective-permute-start | bytes 3145736 | tf_op jit(solution)/shard_map/ppermute | solution.py:64
  157.1 256.8 %copy-start.6 = (f32[256,2048]{1,0:T(8,128)}, f32[256,2048]{1,0:T(8,128)S(1)}, u32[]{:S(2)}) copy-start(f32[256,2048]{1,0:T(8,128)S(1)} %get-tuple-element.112) | copy-start | bytes 6291460
  157.4 26.2 %copy-start.20 = (bf16[256,2048]{1,0:T(8,128)(2,1)}, bf16[256,2048]{1,0:T(8,128)(2,1)S(1)}, u32[]{:S(2)}) copy-start(bf16[256,2048]{1,0:T(8,128)(2,1)S(1)} %multiply_convert_fusion.refs_0_) | copy-start | bytes 3145732
  157.4 21.3 %collective-permute-start.14 = (bf16[256,2048]{1,0:T(8,128)(2,1)S(1)}, bf16[256,2048]{1,0:T(8,128)(2,1)S(1)}, u32[]{:S(2)}, u32[]{:S(2)}) collective-permute-start(bf16[256,2048]{1,0:T(8,128)(2,1)S(1)} %multiply_convert_fusion.refs_0_), channel_id=1, source_target_pairs={{0,8},{8,0},{16,24},{24,16},{1,9},{9,1},{17,25},{25,17},{2,10},{10... | collective-permute-start | bytes 3145736 | tf_op jit(solution)/shard_map/ppermute | solution.py:64
  158.8 21.8 %collective-permute-start.12 = (bf16[256,2048]{1,0:T(8,128)(2,1)S(1)}, bf16[256,2048]{1,0:T(8,128)(2,1)S(1)}, u32[]{:S(2)}, u32[]{:S(2)}) collective-permute-start(bf16[256,2048]{1,0:T(8,128)(2,1)S(1)} %multiply_convert_fusion.refs_0_), channel_id=1, source_target_pairs={{0,16},{8,24},{16,0},{24,8},{1,17},{9,25},{17,1},{25,9},{2,18},{10... | collective-permute-start | bytes 3145736 | tf_op jit(solution)/shard_map/ppermute | solution.py:64
  179.7 10.8 %collective-permute-start.15 = (bf16[128,2048]{1,0:T(8,128)(2,1)}, bf16[128,2048]{1,0:T(8,128)(2,1)S(1)}, u32[]{:S(2)}, u32[]{:S(2)}) collective-permute-start(bf16[128,2048]{1,0:T(8,128)(2,1)} %slice.252), channel_id=1, source_target_pairs={{0,16},{8,24},{16,0},{24,8},{1,17},{9,25},{17,1},{25,9},{2,18},{10... | collective-permute-start | bytes 1572872 | tf_op jit(solution)/shard_map/ppermute | solution.py:64
  181.7 9.5 %collective-permute-start.13 = (bf16[128,2048]{1,0:T(8,128)(2,1)}, bf16[128,2048]{1,0:T(8,128)(2,1)}, u32[]{:S(2)}, u32[]{:S(2)}) collective-permute-start(bf16[128,2048]{1,0:T(8,128)(2,1)} %slice.251), channel_id=1, source_target_pairs={{0,8},{8,0},{16,24},{24,16},{1,9},{9,1},{17,25},{25,17},{2,10},{10... | collective-permute-start | bytes 1572872 | tf_op jit(solution)/shard_map/ppermute | solution.py:64
  251.4 219.2 %reduce-scatter.6.cloned.1.call-start = ((), (), s32[]{:S(2)}) async-start(), calls=%async_computation.7 | async-start | bytes 7077888 | tf_op jit(solution)/shard_map/reduce_scatter | solution.py:245
  283.5 14.2 %collective-permute-start.18 = (bf16[128,2048]{1,0:T(8,128)(2,1)S(1)}, bf16[128,2048]{1,0:T(8,128)(2,1)S(1)}, u32[]{:S(2)}, u32[]{:S(2)}) collective-permute-start(bf16[128,2048]{1,0:T(8,128)(2,1)S(1)} %get-tuple-element.123), channel_id=1, source_target_pairs={{0,8},{8,0},{16,24},{24,16},{1,9},{9,1},{17,25},{25,17},{2,10},{10... | collective-permute-start | bytes 1572872 | tf_op jit(solution)/shard_map/ppermute | solution.py:64
  285.1 13.9 %collective-permute-start.16 = (bf16[128,2048]{1,0:T(8,128)(2,1)S(1)}, bf16[128,2048]{1,0:T(8,128)(2,1)S(1)}, u32[]{:S(2)}, u32[]{:S(2)}) collective-permute-start(bf16[128,2048]{1,0:T(8,128)(2,1)S(1)} %get-tuple-element.124), channel_id=1, source_target_pairs={{0,16},{8,24},{16,0},{24,8},{1,17},{9,25},{17,1},{25,9},{2,18},{10... | collective-permute-start | bytes 1572872 | tf_op jit(solution)/shard_map/ppermute | solution.py:64
  301.7 24.7 %collective-permute-start.19 = (bf16[256,2048]{1,0:T(8,128)(2,1)}, bf16[256,2048]{1,0:T(8,128)(2,1)}, u32[]{:S(2)}, u32[]{:S(2)}) collective-permute-start(bf16[256,2048]{1,0:T(8,128)(2,1)} %pad_maximum_fusion.5), channel_id=1, source_target_pairs={{0,16},{8,24},{16,0},{24,8},{1,17},{9,25},{17,1},{25,9},{2,18},{10... | collective-permute-start | bytes 3145736 | tf_op jit(solution)/shard_map/ppermute | solution.py:64
  304.2 24.3 %collective-permute-start.17 = (bf16[256,2048]{1,0:T(8,128)(2,1)}, bf16[256,2048]{1,0:T(8,128)(2,1)S(1)}, u32[]{:S(2)}, u32[]{:S(2)}) collective-permute-start(bf16[256,2048]{1,0:T(8,128)(2,1)} %pad_maximum_fusion.4), channel_id=1, source_target_pairs={{0,8},{8,0},{16,24},{24,16},{1,9},{9,1},{17,25},{25,17},{2,10},{10... | collective-permute-start | bytes 3145736 | tf_op jit(solution)/shard_map/ppermute | solution.py:64
  333.3 23.4 %collective-permute-start.22 = (bf16[256,2048]{1,0:T(8,128)(2,1)S(1)}, bf16[256,2048]{1,0:T(8,128)(2,1)S(1)}, u32[]{:S(2)}, u32[]{:S(2)}) collective-permute-start(bf16[256,2048]{1,0:T(8,128)(2,1)S(1)} %fusion.60.refs_0_), channel_id=1, source_target_pairs={{0,8},{8,0},{16,24},{24,16},{1,9},{9,1},{17,25},{25,17},{2,10},{10... | collective-permute-start | bytes 3145736 | tf_op jit(solution)/shard_map/ppermute | solution.py:64
  334.2 23.9 %collective-permute-start.20 = (bf16[256,2048]{1,0:T(8,128)(2,1)S(1)}, bf16[256,2048]{1,0:T(8,128)(2,1)S(1)}, u32[]{:S(2)}, u32[]{:S(2)}) collective-permute-start(bf16[256,2048]{1,0:T(8,128)(2,1)S(1)} %fusion.60.refs_0_), channel_id=1, source_target_pairs={{0,16},{8,24},{16,0},{24,8},{1,17},{9,25},{17,1},{25,9},{2,18},{10... | collective-permute-start | bytes 3145736 | tf_op jit(solution)/shard_map/ppermute | solution.py:64
  357.6 11.5 %collective-permute-start.23 = (bf16[128,2048]{1,0:T(8,128)(2,1)}, bf16[128,2048]{1,0:T(8,128)(2,1)S(1)}, u32[]{:S(2)}, u32[]{:S(2)}) collective-permute-start(bf16[128,2048]{1,0:T(8,128)(2,1)} %slice.254), channel_id=1, source_target_pairs={{0,16},{8,24},{16,0},{24,8},{1,17},{9,25},{17,1},{25,9},{2,18},{10... | collective-permute-start | bytes 1572872 | tf_op jit(solution)/shard_map/ppermute | solution.py:64
  359.9 11.3 %collective-permute-start.21 = (bf16[128,2048]{1,0:T(8,128)(2,1)}, bf16[128,2048]{1,0:T(8,128)(2,1)}, u32[]{:S(2)}, u32[]{:S(2)}) collective-permute-start(bf16[128,2048]{1,0:T(8,128)(2,1)} %slice.253), channel_id=1, source_target_pairs={{0,8},{8,0},{16,24},{24,16},{1,9},{9,1},{17,25},{25,17},{2,10},{10... | collective-permute-start | bytes 1572872 | tf_op jit(solution)/shard_map/ppermute | solution.py:64
  374.2 168.7 %reduce-scatter.8.cloned.1.call-start = ((), (), s32[]{:S(2)}) async-start(), calls=%async_computation.8 | async-start | bytes 7077888 | tf_op jit(solution)/shard_map/reduce_scatter | solution.py:245
  375.5 10.3 %collective-permute-start.25 = (bf16[128,2048]{1,0:T(8,128)(2,1)S(1)}, bf16[128,2048]{1,0:T(8,128)(2,1)S(1)}, u32[]{:S(2)}, u32[]{:S(2)}) collective-permute-start(bf16[128,2048]{1,0:T(8,128)(2,1)S(1)} %get-tuple-element.117), channel_id=1, source_target_pairs={{0,8},{8,0},{16,24},{24,16},{1,9},{9,1},{17,25},{25,17},{2,10},{10... | collective-permute-start | bytes 1572872 | tf_op jit(solution)/shard_map/ppermute | solution.py:64
  376.3 9.8 %collective-permute-start.24 = (bf16[128,2048]{1,0:T(8,128)(2,1)S(1)}, bf16[128,2048]{1,0:T(8,128)(2,1)S(1)}, u32[]{:S(2)}, u32[]{:S(2)}) collective-permute-start(bf16[128,2048]{1,0:T(8,128)(2,1)S(1)} %get-tuple-element.118), channel_id=1, source_target_pairs={{0,16},{8,24},{16,0},{24,8},{1,17},{9,25},{17,1},{25,9},{2,18},{10... | collective-permute-start | bytes 1572872 | tf_op jit(solution)/shard_map/ppermute | solution.py:64
  387.5 26.5 %collective-permute-start.26 = (bf16[256,2048]{1,0:T(8,128)(2,1)}, bf16[256,2048]{1,0:T(8,128)(2,1)}, u32[]{:S(2)}, u32[]{:S(2)}) collective-permute-start(bf16[256,2048]{1,0:T(8,128)(2,1)} %pad_maximum_fusion.6), channel_id=1, source_target_pairs={{0,8},{8,0},{16,24},{24,16},{1,9},{9,1},{17,25},{25,17},{2,10},{10... | collective-permute-start | bytes 3145736 | tf_op jit(solution)/shard_map/ppermute | solution.py:64
  389.9 24.0 %collective-permute-start.27 = (bf16[256,2048]{1,0:T(8,128)(2,1)}, bf16[256,2048]{1,0:T(8,128)(2,1)}, u32[]{:S(2)}, u32[]{:S(2)}) collective-permute-start(bf16[256,2048]{1,0:T(8,128)(2,1)} %pad_maximum_fusion.7), channel_id=1, source_target_pairs={{0,16},{8,24},{16,0},{24,8},{1,17},{9,25},{17,1},{25,9},{2,18},{10... | collective-permute-start | bytes 3145736 | tf_op jit(solution)/shard_map/ppermute | solution.py:64
  423.8 36.8 %collective-permute-start.29 = (bf16[256,3072]{1,0:T(8,128)(2,1)}, bf16[256,3072]{1,0:T(8,128)(2,1)S(1)}, u32[]{:S(2)}, u32[]{:S(2)}) collective-permute-start(bf16[256,3072]{1,0:T(8,128)(2,1)} %reduce-scatter.4.cloned.1.call-done.refs_0_), channel_id=1, source_target_pairs={{0,16},{8,24},{16,0},{24,8},{1,17},{9,25},{17,1},{25,9},{2,18},{10... | collective-permute-start | bytes 4718600 | tf_op jit(solution)/shard_map/ppermute | solution.py:64
  424.4 36.4 %collective-permute-start.28 = (bf16[256,3072]{1,0:T(8,128)(2,1)}, bf16[256,3072]{1,0:T(8,128)(2,1)S(1)}, u32[]{:S(2)}, u32[]{:S(2)}) collective-permute-start(bf16[256,3072]{1,0:T(8,128)(2,1)} %reduce-scatter.4.cloned.1.call-done.refs_0_), channel_id=1, source_target_pairs={{0,8},{8,0},{16,24},{24,16},{1,9},{9,1},{17,25},{25,17},{2,10},{10... | collective-permute-start | bytes 4718600 | tf_op jit(solution)/shard_map/ppermute | solution.py:64
  427.4 38.9 %collective-permute-start.30 = (bf16[128,2048]{1,0:T(8,128)(2,1)}, bf16[128,2048]{1,0:T(8,128)(2,1)}, u32[]{:S(2)}, u32[]{:S(2)}) collective-permute-start(bf16[128,2048]{1,0:T(8,128)(2,1)} %get-tuple-element.139), channel_id=1, source_target_pairs={{0,16},{8,24},{16,0},{24,8},{1,17},{9,25},{17,1},{25,9},{2,18},{10... | collective-permute-start | bytes 1572872 | tf_op jit(solution)/shard_map/ppermute | solution.py:64
  428.9 37.6 %collective-permute-start.32 = (bf16[128,2048]{1,0:T(8,128)(2,1)}, bf16[128,2048]{1,0:T(8,128)(2,1)}, u32[]{:S(2)}, u32[]{:S(2)}) collective-permute-start(bf16[128,2048]{1,0:T(8,128)(2,1)} %get-tuple-element.140), channel_id=1, source_target_pairs={{0,8},{8,0},{16,24},{24,16},{1,9},{9,1},{17,25},{25,17},{2,10},{10... | collective-permute-start | bytes 1572872 | tf_op jit(solution)/shard_map/ppermute | solution.py:64
  430.3 8.8 %copy-start.16 = (bf16[1024,512]{1,0:T(8,128)(2,1)S(1)}, bf16[1024,512]{1,0:T(8,128)(2,1)}, u32[]{:S(2)}) copy-start(bf16[1024,512]{1,0:T(8,128)(2,1)} %attend.1) | copy-start | bytes 3145732
  430.3 8.8 %copy-start.19 = (bf16[1024,512]{1,0:T(8,128)(2,1)S(1)}, bf16[1024,512]{1,0:T(8,128)(2,1)}, u32[]{:S(2)}) copy-start(bf16[1024,512]{1,0:T(8,128)(2,1)} %get-tuple-element.77) | copy-start | bytes 3145732
  470.8 20.5 %collective-permute-start.34 = (bf16[128,3072]{1,0:T(8,128)(2,1)S(1)}, bf16[128,3072]{1,0:T(8,128)(2,1)S(1)}, u32[]{:S(2)}, u32[]{:S(2)}) collective-permute-start(bf16[128,3072]{1,0:T(8,128)(2,1)S(1)} %slice.261), channel_id=1, source_target_pairs={{0,8},{8,0},{16,24},{24,16},{1,9},{9,1},{17,25},{25,17},{2,10},{10... | collective-permute-start | bytes 2359304 | tf_op jit(solution)/shard_map/ppermute | solution.py:64
  471.5 20.5 %collective-permute-start.35 = (bf16[128,3072]{1,0:T(8,128)(2,1)S(1)}, bf16[128,3072]{1,0:T(8,128)(2,1)S(1)}, u32[]{:S(2)}, u32[]{:S(2)}) collective-permute-start(bf16[128,3072]{1,0:T(8,128)(2,1)S(1)} %slice.262), channel_id=1, source_target_pairs={{0,16},{8,24},{16,0},{24,8},{1,17},{9,25},{17,1},{25,9},{2,18},{10... | collective-permute-start | bytes 2359304 | tf_op jit(solution)/shard_map/ppermute | solution.py:64
  473.1 33.6 %collective-permute-start.33 = (bf16[256,2048]{1,0:T(8,128)(2,1)S(1)}, bf16[256,2048]{1,0:T(8,128)(2,1)S(1)}, u32[]{:S(2)}, u32[]{:S(2)}) collective-permute-start(bf16[256,2048]{1,0:T(8,128)(2,1)S(1)} %copy-done.35), channel_id=1, source_target_pairs={{0,16},{8,24},{16,0},{24,8},{1,17},{9,25},{17,1},{25,9},{2,18},{10... | collective-permute-start | bytes 3145736 | tf_op jit(solution)/shard_map/ppermute | solution.py:64
  473.5 33.2 %collective-permute-start.31 = (bf16[256,2048]{1,0:T(8,128)(2,1)S(1)}, bf16[256,2048]{1,0:T(8,128)(2,1)S(1)}, u32[]{:S(2)}, u32[]{:S(2)}) collective-permute-start(bf16[256,2048]{1,0:T(8,128)(2,1)S(1)} %copy-done.34), channel_id=1, source_target_pairs={{0,8},{8,0},{16,24},{24,16},{1,9},{9,1},{17,25},{25,17},{2,10},{10... | collective-permute-start | bytes 3145736 | tf_op jit(solution)/shard_map/ppermute | solution.py:64
  493.2 15.4 %copy-start.11 = (bf16[1,256,2048]{2,1,0:T(8,128)(2,1)S(1)}, bf16[1,256,2048]{2,1,0:T(8,128)(2,1)}, u32[]{:S(2)}) copy-start(bf16[1,256,2048]{2,1,0:T(8,128)(2,1)} %param.14) | copy-start | bytes 3145732
  512.9 17.2 %collective-permute-start.40 = (bf16[256,1536]{1,0:T(8,128)(2,1)}, bf16[256,1536]{1,0:T(8,128)(2,1)}, u32[]{:S(2)}, u32[]{:S(2)}) collective-permute-start(bf16[256,1536]{1,0:T(8,128)(2,1)} %reduce-scatter.6.cloned.1.call-done.refs_0_), channel_id=1, source_target_pairs={{0,16},{8,24},{16,0},{24,8},{1,17},{9,25},{17,1},{25,9},{2,18},{10... | collective-permute-start | bytes 2359304 | tf_op jit(solution)/shard_map/ppermute | solution.py:64
  514.4 16.8 %collective-permute-start.39 = (bf16[256,1536]{1,0:T(8,128)(2,1)}, bf16[256,1536]{1,0:T(8,128)(2,1)}, u32[]{:S(2)}, u32[]{:S(2)}) collective-permute-start(bf16[256,1536]{1,0:T(8,128)(2,1)} %reduce-scatter.6.cloned.1.call-done.refs_0_), channel_id=1, source_target_pairs={{0,8},{8,0},{16,24},{24,16},{1,9},{9,1},{17,25},{25,17},{2,10},{10... | collective-permute-start | bytes 2359304 | tf_op jit(solution)/shard_map/ppermute | solution.py:64
  515.8 1.3 collective-permute-start.36
  517.1 4.5 collective-permute-start.37
  521.6 8.5 %collective-permute-start.38 = (f32[4352]{0:T(1024)S(1)}, f32[4352]{0:T(1024)S(1)}, u32[]{:S(2)}, u32[]{:S(2)}) collective-permute-start(f32[4352]{0:T(1024)S(1)} %add.177), channel_id=1, source_target_pairs={{0,4},{1,5},{2,6},{3,7},{4,0},{5,1},{6,2},{7,3},{8,12},{9,13},{10,... | collective-permute-start | bytes 52232 | tf_op jit(solution)/shard_map/ppermute | solution.py:253
  532.1 10.2 %collective-permute-start.41 = (bf16[128,1536]{1,0:T(8,128)(2,1)S(1)}, bf16[128,1536]{1,0:T(8,128)(2,1)S(1)}, u32[]{:S(2)}, u32[]{:S(2)}) collective-permute-start(bf16[128,1536]{1,0:T(8,128)(2,1)S(1)} %slice.263), channel_id=1, source_target_pairs={{0,8},{8,0},{16,24},{24,16},{1,9},{9,1},{17,25},{25,17},{2,10},{10... | collective-permute-start | bytes 1179656 | tf_op jit(solution)/shard_map/ppermute | solution.py:64
  532.9 9.9 %collective-permute-start.42 = (bf16[128,1536]{1,0:T(8,128)(2,1)S(1)}, bf16[128,1536]{1,0:T(8,128)(2,1)S(1)}, u32[]{:S(2)}, u32[]{:S(2)}) collective-permute-start(bf16[128,1536]{1,0:T(8,128)(2,1)S(1)} %slice.264), channel_id=1, source_target_pairs={{0,16},{8,24},{16,0},{24,8},{1,17},{9,25},{17,1},{25,9},{2,18},{10... | collective-permute-start | bytes 1179656 | tf_op jit(solution)/shard_map/ppermute | solution.py:64
  542.8 24.5 %collective-permute-start.46 = (bf16[256,1536]{1,0:T(8,128)(2,1)}, bf16[256,1536]{1,0:T(8,128)(2,1)S(1)}, u32[]{:S(2)}, u32[]{:S(2)}) collective-permute-start(bf16[256,1536]{1,0:T(8,128)(2,1)} %reduce-scatter.8.cloned.1.call-done.refs_0_), channel_id=1, source_target_pairs={{0,16},{8,24},{16,0},{24,8},{1,17},{9,25},{17,1},{25,9},{2,18},{10... | collective-permute-start | bytes 2359304 | tf_op jit(solution)/shard_map/ppermute | solution.py:64
  543.4 23.9 %collective-permute-start.45 = (bf16[256,1536]{1,0:T(8,128)(2,1)}, bf16[256,1536]{1,0:T(8,128)(2,1)S(1)}, u32[]{:S(2)}, u32[]{:S(2)}) collective-permute-start(bf16[256,1536]{1,0:T(8,128)(2,1)} %reduce-scatter.8.cloned.1.call-done.refs_0_), channel_id=1, source_target_pairs={{0,8},{8,0},{16,24},{24,16},{1,9},{9,1},{17,25},{25,17},{2,10},{10... | collective-permute-start | bytes 2359304 | tf_op jit(solution)/shard_map/ppermute | solution.py:64
  544.8 16.4 %collective-permute-start.43 = (f32[4352]{0:T(1024)S(1)}, f32[4352]{0:T(1024)S(1)}, u32[]{:S(2)}, u32[]{:S(2)}) collective-permute-start(f32[4352]{0:T(1024)S(1)} %add.178), channel_id=1, source_target_pairs={{0,8},{8,0},{16,24},{24,16},{1,9},{9,1},{17,25},{25,17},{2,10},{10... | collective-permute-start | bytes 52232 | tf_op jit(solution)/shard_map/ppermute | solution.py:253
  561.3 6.0 %collective-permute-start.44 = (f32[4352]{0:T(1024)S(1)}, f32[4352]{0:T(1024)S(1)}, u32[]{:S(2)}, u32[]{:S(2)}) collective-permute-start(f32[4352]{0:T(1024)S(1)} %add.179), channel_id=1, source_target_pairs={{0,16},{8,24},{16,0},{24,8},{1,17},{9,25},{17,1},{25,9},{2,18},{10... | collective-permute-start | bytes 52232 | tf_op jit(solution)/shard_map/ppermute | solution.py:253
  567.3 9.9 %copy-start.5 = (bf16[256,1536]{1,0:T(8,128)(2,1)S(1)}, bf16[256,1536]{1,0:T(8,128)(2,1)}, u32[]{:S(2)}) copy-start(bf16[256,1536]{1,0:T(8,128)(2,1)} %reduce-scatter.8.cloned.1.call-done.refs_0_) | copy-start | bytes 2359300
  567.4 7.8 %collective-permute-start.47 = (bf16[128,1536]{1,0:T(8,128)(2,1)S(1)}, bf16[128,1536]{1,0:T(8,128)(2,1)S(1)}, u32[]{:S(2)}, u32[]{:S(2)}) collective-permute-start(bf16[128,1536]{1,0:T(8,128)(2,1)S(1)} %slice.266), channel_id=1, source_target_pairs={{0,8},{8,0},{16,24},{24,16},{1,9},{9,1},{17,25},{25,17},{2,10},{10... | collective-permute-start | bytes 1179656 | tf_op jit(solution)/shard_map/ppermute | solution.py:64
  568.8 7.8 %collective-permute-start.48 = (bf16[128,1536]{1,0:T(8,128)(2,1)S(1)}, bf16[128,1536]{1,0:T(8,128)(2,1)S(1)}, u32[]{:S(2)}, u32[]{:S(2)}) collective-permute-start(bf16[128,1536]{1,0:T(8,128)(2,1)S(1)} %slice.267), channel_id=1, source_target_pairs={{0,16},{8,24},{16,0},{24,8},{1,17},{9,25},{17,1},{25,9},{2,18},{10... | collective-permute-start | bytes 1179656 | tf_op jit(solution)/shard_map/ppermute | solution.py:64
  569.5 10.7 %copy-start.1 = (bf16[256,6144]{1,0:T(8,128)(2,1)S(1)}, bf16[256,6144]{1,0:T(8,128)(2,1)}, u32[]{:S(2)}) copy-start(bf16[256,6144]{1,0:T(8,128)(2,1)} %param.24) | copy-start | bytes 9437188
  (35 other events, 110.4 us)
Sparse Core Ops, SparseCore 0:
  10.6 67.4 all-gather.3
  80.3 115.3 all-gather.5
  197.3 62.9 all-gather.7
  262.5 127.8 reduce-scatter.3
  393.1 68.1 reduce-scatter.5
  470.8 68.1 reduce-scatter.7

commit v4 on v3

--- a/solution.py
+++ b/solution.py
@@ -121,6 +121,9 @@
         self.rx, self.ry = swap(sx, 1), swap(sy, 2)
         return [self.rx, self.ry]
 
+    def arrived(self):
+        return [self.rx, self.ry] if self.square else [self.sum]
+
     def finish(self):
         if not self.square:
             return self.sum.astype(F32)
@@ -144,18 +147,24 @@
     )
 
 
-def scattered_product(x, w, order, count, *others):
+def scattered_product(x, w, order, count, *others, early=True):
     total = Scatter(count)
     rows = x.shape[0] // count
     if not total.square:
-        terms = dot_nt(x, w).astype(BF16)
-        total.last = terms
+        total.last = terms = dot_nt(x, w).astype(BF16)
         total.second(terms.reshape(count, rows, w.shape[0]))
         return total, [terms]
-    total.last = dot_nt(slot_rows(x, order, count, (3,)), w).astype(BF16)
+    if early:
+        last = dot_nt(slot_rows(x, order, count, (3,)), w).astype(BF16)
+        rest = dot_nt(slot_rows(x, order, count, (0, 1, 2)), w).astype(BF16)
+        rest = rest.reshape(3, rows, w.shape[0])
+    else:
+        rest = dot_nt(slot_rows(x, order, count, range(4)), w).astype(BF16)
+        rest = rest.reshape(4, rows, w.shape[0])
+        last = rest[3]
+    total.last = after(last, *others)
     got = total.first(total.last)
-    rest = dot_nt(slot_rows(x, order, count, (0, 1, 2)), w).astype(BF16)
-    total.second(after(rest, *others).reshape(3, rows, w.shape[0]))
+    total.second(rest)
     return total, got
 
 
@@ -173,13 +182,13 @@
 
     def second(self, *others):
         if not self.square:
-            self.sent = self.x
+            self.sent = [self.x]
             return [self.x]
         half = self.x.shape[0] // 2
         ahead, below = self.by[:half], self.bx[half:]
         if others:
             ahead, below, *_ = lax.optimization_barrier((ahead, below, *others))
-        self.sent = ahead
+        self.sent = [ahead, below]
         self.ad, self.bd = swap(ahead, 1), swap(below, 2)
         return [self.ad, self.bd]
 
@@ -623,33 +632,34 @@
         share1 = sum_terms(terms1)
         xb2 = after(xb, terms1)
         d2, d_xb, out = feed_forward(xb2, dy, w_mlp[1], order, tuple(sums), BF16)
-        sum_dxb = Scatter(seq_count)
-        sum_dxb.first(d_xb[-1])
-        sum_dxb.second(d_xb)
+        sum_dxb, sum_out = Scatter(seq_count), Scatter(seq_count)
+        got = sum_dxb.first(d_xb[-1]) + sum_out.first(out[-1])
+        sum_dxb.second(after(d_xb, *got))
         terms2 = weight_terms([(xb, 2), (dy, 1)], after(d2, *sum_dxb.sent))
         du, post_terms = norm_back(resid, post_gain, after(sum_dxb.finish(), terms2))
         d_resid = cotangent[0].astype(F32) + du
         get_drl = Gather(d_resid.astype(BF16), seq_count)
         get_drl.first()
         get_drl.second()
+        share2 = sum_terms(after(terms2, *get_drl.sent))
         drl = get_drl.column()
-        share2 = sum_terms(after(terms2, drl))
-        sum_out = Scatter(seq_count)
-        got = sum_out.first(after(out, drl)[-1])
+        halves = sum_out.second(after(out, drl))
         d_o = dot(drl, w_out).astype(BF16)
-        sum_out.second(after(out, d_o))
         dq, dk, dv, q_terms, k_terms = attend_back(
             qkv, tables, start, head_gains, after(d_o, *sum_out.sent), q_heads, kv_heads
         )
-        out = resid + sum_out.finish()
-        dq, out = lax.optimization_barrier((dq, out))
+        dq = after(dq, *halves)
         get1 = Gather(after(share1, dq), seq_count)
         near = get1.first()
         d_attn = jnp.concatenate([dq, dk, dv, o], axis=1)
-        sum_dxa, got = scattered_product(d_attn[:, :qkv_cols], w_qkv, order, seq_count, *near)
-        terms3 = weight_terms([(xa, 2), (drl, 1)], after(d_attn, sum_dxa.last))
+        terms3 = weight_terms([(xa, 2), (drl, 1)], d_attn)
+        d_qkv = after(d_attn, terms3)[:, :qkv_cols]
+        sum_dxa, got = scattered_product(
+            d_qkv, w_qkv, order, seq_count, *near, early=False
+        )
         get1.second(*got)
-        share3 = sum_terms(after(terms3, share2, *sum_dxa.sent))
+        out = resid + after(sum_out.finish(), *got)
+        share3 = sum_terms(after(terms3, share2, *got))
         du, in_terms = norm_back(inputs, input_gain, after(sum_dxa.finish(), *get1.slots()))
         d_inputs = d_resid + du
 
@@ -662,7 +672,7 @@
             ]
         )
         width = post_gain.shape[0]
-        get2 = Gather(after(share2, in_terms), seq_count)
+        get2 = Gather(after(share2, *get1.slots(), *sum_dxa.arrived()), seq_count)
         get2.first()
         gains = sum_all(gains, "fsdp", fsdp_count)
         mlp = place(get1.slots(), (pieces[0],) * 3, 2, 0, 3, (), me, seq_count)

time: 597 us -> 587 us (0.983)
  matrix products: 35.2 us -> 28.8 us
    ppermute x5, waiting for transfers between devices: 21.4 us -> 12.9 us  [sum_all(): x = x + lax.ppermute(x, axis, [(i, i ^ bit) for i in range(count)])]
    reduce_scatter x3, waiting for transfers between devices: 0.02 us -> 6.89 us  [sum_terms(): return lax.psum_scatter(terms, 'fsdp', scatter_dimension=0, tiled=True)]
    dot_general x4 -> x3, matrix products: 19.8 us -> 14.6 us  [dot_nt(): lax.dot_general(a, b, (((1,), (1,)), ((), ())), preferred_element_type=F32)]
  transfers between devices with their start and end apart: 55 -> 55, of which waited for: 37 -> 40; matrix products, arithmetic and copies ran while one was open for 16% -> 15% of each run, Pallas kernels for 30% -> 31%
where the time goes in v4:
time: 587 us; the launch traced here: 577 us
  waiting for transfers between devices  226 us (39%)
  Pallas kernels  180 us (31%)
  starting transfers between devices  55.7 us (9%)
  local copies, waits for them, and re-layouts  36.7 us (6%)
  other arithmetic  35 us (6%)
  matrix products  28.8 us (5%)
  between operations  15.4 us (3%)
    ppermute x44, waiting for transfers between devices, swap(): return lax.ppermute(x, 'seq', [(s, s ^ side) for s in range(4)])  196 us
    pallas_call x2, Pallas kernels, feed_forward(): pl.pallas_call(functools.partial(feed_forward_kernel, bool(sums), piece),...  56.8 us
    ppermute x44, starting transfers between devices, swap(): return lax.ppermute(x, 'seq', [(s, s ^ side) for s in range(4)])  51.1 us
    pallas_call x3, Pallas kernels, weight_terms(): pl.pallas_call(functools.partial(terms_kernel, starts), grid=(tiles,), in...  45.3 us
    pallas_call x8, Pallas kernels, put_rows(): pl.pallas_call(functools.partial(put_rows_kernel, len(pieces)), grid_spec...  30.6 us
    pallas_call x1, Pallas kernels, attend_back(): pl.pallas_call(functools.partial(attend_back_kernel, ratio), grid=(kv_hea...  22.1 us
    dot_general x3, matrix products, dot_nt(): lax.dot_general(a, b, (((1,), (1,)), ((), ())), preferred_element_type=F32)  14.6 us
    dot_general x2, matrix products, dot(): return jnp.dot(a, b, preferred_element_type=F32)  14.3 us
  transfers between devices with their start and end apart: 55, of which 40 were waited for; matrix products, arithmetic and copies ran while one was open for 15% of the time, Pallas kernels for 31%

profile of v4, /device:TPU:0, one launch (start us, length us, event | category | flops | bytes accessed | tf_op | source)
XLA Modules:
  0.0 577.4 jit_solution(198575776563579446)
XLA Ops:
  16.0 3.0 collective-permute-start.2
  21.8 21.3 %collective-permute-done.2.refs_1_ = bf16[256,2048]{1,0:T(8,128)(2,1)} collective-permute-done((bf16[256,2048]{1,0:T(8,128)(2,1)S(1)}, bf16[256,2048]{1,0:T(8,128)(2,1)}, u32[]{:S(2)}, u32[]{:S(2)}) %collective-permute-start.2) | collective-permute-done | bytes 1048608 | tf_op jit(solution)/shard_map/ppermute | solution.py:64
  43.1 1.9 slice.245
  45.0 2.0 collective-permute-start.3
  47.1 1.9 slice.244
  52.8 4.6 put_rows.8.refs_2_
  57.4 8.2 %collective-permute-done.5.refs_1_ = bf16[256,2048]{1,0:T(8,128)(2,1)} collective-permute-done((bf16[256,2048]{1,0:T(8,128)(2,1)S(1)}, bf16[256,2048]{1,0:T(8,128)(2,1)}, u32[]{:S(2)}, u32[]{:S(2)}) %collective-permute-start.5) | collective-permute-done | bytes 1048608 | tf_op jit(solution)/shard_map/ppermute | solution.py:64
  65.6 1.9 slice.249
  67.7 1.9 slice.248
  69.6 7.9 %collective-permute-done.3.refs_1_ = bf16[128,2048]{1,0:T(8,128)(2,1)} collective-permute-done((bf16[128,2048]{1,0:T(8,128)(2,1)}, bf16[128,2048]{1,0:T(8,128)(2,1)}, u32[]{:S(2)}, u32[]{:S(2)}) %collective-permute-start.3) | collective-permute-done | bytes 524320 | tf_op jit(solution)/shard_map/ppermute | solution.py:64
  77.5 2.9 put_rows.9.refs_0_
  80.4 9.3 %fusion.24.q_ref.k_ref.v_ref = bf16[1024,1024]{1,0:T(8,128)(2,1)} fusion(bf16[1024,2048]{1,0:T(8,128)(2,1)} %put_rows.9.refs_0_, bf16[2048,1536]{1,0:T(8,128)(2,1)} %all-gather.4.cloned.1.call-done), kind=kOutput, calls=%fused_computation.40 | convolution fusion | flops 4296015872 | bytes 10485760 | tf_op jit(solution)/shard_map/dot_general | solution.py:21
  90.0 1.7 collective-permute-start.7
  91.7 1.9 fusion.50
  95.8 4.7 put_rows.10.refs_2_
  100.5 12.7 %attend.1 = bf16[1024,512]{1,0:T(8,128)(2,1)} custom-call(bf16[1024,1024]{1,0:T(8,128)(2,1)} %fusion.24.q_ref.k_ref.v_ref, bf16[1024,1024]{1,0:T(8,128)(2,1)} %fusion.24.q_ref.k_ref.v_ref, bf16[1024,1024]{1,0:T(8,128)(2,1)} %fusion.24.q_ref.k_ref.v_ref, f32[1024,128]{1,0:T(8,128)} %get-tuple-element.159.cos_ref, f32[1024,128]{1,0:T(8,128)} %get-tuple-element.160.sin_ref, ...), custom_call_target="tpu_custom_call" | custom-call | flops 1000 | bytes 1000 | tf_op jit(solution)/shard_map/attend/pallas_call | solution.py:414
  114.0 3.1 put_rows.11.dy_ref.refs_1_
  117.1 2.3 convolution_convert_fusion.2
  120.0 1.6 collective-permute-start.10
  121.7 3.4 convolution_convert_fusion.1
  125.2 6.5 %collective-permute-done.8 = bf16[128,2048]{1,0:T(8,128)(2,1)S(1)} collective-permute-done((bf16[128,2048]{1,0:T(8,128)(2,1)S(1)}, bf16[128,2048]{1,0:T(8,128)(2,1)S(1)}, u32[]{:S(2)}, u32[]{:S(2)}) %collective-permute-start.8) | collective-permute-done | bytes 524320 | tf_op jit(solution)/shard_map/ppermute | solution.py:64
  132.5 1.5 collective-permute-start.11
  135.5 19.5 %collective-permute-done.11 = bf16[256,2048]{1,0:T(8,128)(2,1)S(1)} collective-permute-done((bf16[256,2048]{1,0:T(8,128)(2,1)S(1)}, bf16[256,2048]{1,0:T(8,128)(2,1)S(1)}, u32[]{:S(2)}, u32[]{:S(2)}) %collective-permute-start.11) | collective-permute-done | bytes 1048608 | tf_op jit(solution)/shard_map/ppermute | solution.py:64
  159.2 19.5 %collective-permute-done.14.refs_1_ = bf16[256,2048]{1,0:T(8,128)(2,1)S(1)} collective-permute-done((bf16[256,2048]{1,0:T(8,128)(2,1)S(1)}, bf16[256,2048]{1,0:T(8,128)(2,1)S(1)}, u32[]{:S(2)}, u32[]{:S(2)}) %collective-permute-start.14) | collective-permute-done | bytes 1048608 | tf_op jit(solution)/shard_map/ppermute | solution.py:64
  183.6 4.6 put_rows.12.refs_2_
  188.2 2.2 collective-permute-done.15.refs_1_
  191.3 2.9 put_rows.13.xb_ref.refs_0_
  195.7 35.3 %feed_forward.2 = (bf16[1024,3072]{1,0:T(8,128)(2,1)}, f32[4,256,2048]{2,1,0:T(8,128)}, f32[4,256,2048]{2,1,0:T(8,128)}) custom-call(s32[4]{0:T(128)} %pad_add_fusion.2.order_ref, bf16[1024,2048]{1,0:T(8,128)(2,1)} %put_rows.13.xb_ref.refs_0_, bf16[1024,2048]{1,0:T(8,128)(2,1)} %put_rows.11.dy_ref.refs_1_, bf16[2048,3072]{1,0:T(8,128)(2,1)} %all-gather.6.cloned.1.call-done.w_ref), custom_call_target="tpu_custom_call" | custom-call | flops 1000 | bytes 1000 | tf_op jit(solution)/shard_map/feed_forward/pallas_call | solution.py:488
  231.0 20.4 %weight_terms.3 = bf16[2048,3072]{1,0:T(8,128)(2,1)} custom-call(bf16[1024,2048]{1,0:T(8,128)(2,1)} %put_rows.13.xb_ref.refs_0_, bf16[1024,2048]{1,0:T(8,128)(2,1)} %put_rows.11.dy_ref.refs_1_, bf16[1024,3072]{1,0:T(8,128)(2,1)} %get-tuple-element.63.refs_2_), custom_call_target="tpu_custom_call" | custom-call | flops 1000 | bytes 1000 | tf_op jit(solution)/shard_map/weight_terms/pallas_call | solution.py:241
  251.4 8.9 %all-gather.8.cloned.1.call-done.w_ref = bf16[2048,1536]{1,0:T(8,128)(2,1)} async-done(((bf16[256,1536]{1,0:T(8,128)(2,1)}), bf16[2048,1536]{1,0:T(8,128)(2,1)}) %all-gather.8.cloned.1.call-update) | async-done | bytes 6291472 | tf_op jit(solution)/shard_map/all_gather | solution.py:217
  260.3 21.5 %feed_forward.3 = (bf16[1024,1536]{1,0:T(8,128)(2,1)}, bf16[4,256,2048]{2,1,0:T(8,128)(2,1)}, bf16[4,256,2048]{2,1,0:T(8,128)(2,1)}) custom-call(s32[4]{0:T(128)} %pad_add_fusion.2.order_ref, bf16[1024,2048]{1,0:T(8,128)(2,1)} %put_rows.13.xb_ref.refs_0_, bf16[1024,2048]{1,0:T(8,128)(2,1)} %put_rows.11.dy_ref.refs_1_, ...), custom_call_target="tpu_custom_call" | custom-call | flops 1000 | bytes 1000 | tf_op jit(solution)/shard_map/feed_forward/pallas_call | solution.py:488
  283.3 1.6 collective-permute-start.19
  288.8 9.3 %collective-permute-done.19 = bf16[128,2048]{1,0:T(8,128)(2,1)S(1)} collective-permute-done((bf16[128,2048]{1,0:T(8,128)(2,1)S(1)}, bf16[128,2048]{1,0:T(8,128)(2,1)S(1)}, u32[]{:S(2)}, u32[]{:S(2)}) %collective-permute-start.19) | collective-permute-done | bytes 524320 | tf_op jit(solution)/shard_map/ppermute | solution.py:64
  299.7 9.1 %collective-permute-done.17 = bf16[128,2048]{1,0:T(8,128)(2,1)S(1)} collective-permute-done((bf16[128,2048]{1,0:T(8,128)(2,1)S(1)}, bf16[128,2048]{1,0:T(8,128)(2,1)S(1)}, u32[]{:S(2)}, u32[]{:S(2)}) %collective-permute-start.17) | collective-permute-done | bytes 524320 | tf_op jit(solution)/shard_map/ppermute | solution.py:64
  314.6 12.3 %weight_terms.4 = bf16[2048,1536]{1,0:T(8,128)(2,1)} custom-call(bf16[1024,2048]{1,0:T(8,128)(2,1)} %put_rows.13.xb_ref.refs_0_, bf16[1024,2048]{1,0:T(8,128)(2,1)} %put_rows.11.dy_ref.refs_1_, bf16[1024,1536]{1,0:T(8,128)(2,1)} %get-tuple-element.71.refs_2_), custom_call_target="tpu_custom_call" | custom-call | flops 1000 | bytes 1000 | tf_op jit(solution)/shard_map/weight_terms/pallas_call | solution.py:241
  326.9 9.3 %collective-permute-done.21 = bf16[256,2048]{1,0:T(8,128)(2,1)} collective-permute-done((bf16[256,2048]{1,0:T(8,128)(2,1)}, bf16[256,2048]{1,0:T(8,128)(2,1)}, u32[]{:S(2)}, u32[]{:S(2)}) %collective-permute-start.21) | collective-permute-done | bytes 1048608 | tf_op jit(solution)/shard_map/ppermute | solution.py:64
  337.5 2.1 fusion.23
  342.3 1.5 collective-permute-start.24
  345.2 20.4 %collective-permute-done.24.refs_1_ = bf16[256,2048]{1,0:T(8,128)(2,1)S(1)} collective-permute-done((bf16[256,2048]{1,0:T(8,128)(2,1)S(1)}, bf16[256,2048]{1,0:T(8,128)(2,1)S(1)}, u32[]{:S(2)}, u32[]{:S(2)}) %collective-permute-start.24) | collective-permute-done | bytes 1048608 | tf_op jit(solution)/shard_map/ppermute | solution.py:64
  370.3 4.8 put_rows.14.refs_2_
  375.2 3.7 collective-permute-done.25.refs_1_
  380.5 3.0 put_rows.15.refs_1_
  385.0 1.6 fusion.39
  389.5 5.0 fusion.31.do_ref
  394.5 22.1 %attend_back.1 = (bf16[1024,512]{1,0:T(8,128)(2,1)}, bf16[1024,256]{1,0:T(8,128)(2,1)}, bf16[1024,256]{1,0:T(8,128)(2,1)}, f32[2,1,128]{2,1,0:T(1,128)}, f32[2,1,128]{2,1,0:T(1,128)}) custom-call(bf16[1024,1024]{1,0:T(8,128)(2,1)} %fusion.24.q_ref.k_ref.v_ref, bf16[1024,1024]{1,0:T(8,128)(2,1)} %fusion.24.q_ref.k_ref.v_ref, ...), custom_call_target="tpu_custom_call" | custom-call | flops 1000 | bytes 1000 | tf_op jit(solution)/shard_map/attend_back/pallas_call | solution.py:432
  419.7 3.1 pad_maximum_fusion.refs_2_
  422.8 12.7 %weight_terms.5 = bf16[2048,1536]{1,0:T(8,128)(2,1)} custom-call(bf16[1024,2048]{1,0:T(8,128)(2,1)} %put_rows.9.refs_0_, bf16[1024,2048]{1,0:T(8,128)(2,1)} %put_rows.15.refs_1_, bf16[1024,1536]{1,0:T(8,128)(2,1)} %pad_maximum_fusion.refs_2_), custom_call_target="tpu_custom_call" | custom-call | flops 1000 | bytes 1000 | tf_op jit(solution)/shard_map/weight_terms/pallas_call | solution.py:241
  435.5 1.6 slice-done
  437.3 8.8 %convolution_convert_fusion = bf16[1024,2048]{1,0:T(8,128)(2,1)S(1)} fusion(bf16[2048,1536]{1,0:T(8,128)(2,1)} %all-gather.4.cloned.1.call-done, bf16[256,1024]{1,0:T(8,128)(2,1)S(1)} %get-tuple-element.138, bf16[256,1024]{1,0:T(8,128)(2,1)S(1)} %get-tuple-element.139, bf16[256,1024]{1,0:T(8,128)(2,1)S(1)} %get-tuple-element.140, ...), kind=kOutput, calls=%fused_computation | convolution fusion | flops 4305453056 | bytes 10485760 | tf_op jit(solution)/shard_map/dot_general | solution.py:25
  446.2 4.9 collective-permute-done.29.refs_2_
  454.4 6.9 %reduce-scatter.6.cloned.1.call-done.refs_0_ = bf16[256,1536]{1,0:T(8,128)(2,1)} async-done(((bf16[2048,1536]{1,0:T(8,128)(2,1)}), bf16[256,1536]{1,0:T(8,128)(2,1)}) %reduce-scatter.6.cloned.1.call-update) | async-done | bytes 786448 | tf_op jit(solution)/shard_map/reduce_scatter | solution.py:254
  468.4 1.9 fusion.37
  474.4 12.2 %collective-permute-done.34 = bf16[128,3072]{1,0:T(8,128)(2,1)} collective-permute-done((bf16[128,3072]{1,0:T(8,128)(2,1)}, bf16[128,3072]{1,0:T(8,128)(2,1)}, u32[]{:S(2)}, u32[]{:S(2)}) %collective-permute-start.34) | collective-permute-done | bytes 786464 | tf_op jit(solution)/shard_map/ppermute | solution.py:64
  489.1 18.4 %collective-permute-done.33 = bf16[256,2048]{1,0:T(8,128)(2,1)} collective-permute-done((bf16[256,2048]{1,0:T(8,128)(2,1)}, bf16[256,2048]{1,0:T(8,128)(2,1)}, u32[]{:S(2)}, u32[]{:S(2)}) %collective-permute-start.33) | collective-permute-done | bytes 1048608 | tf_op jit(solution)/shard_map/ppermute | solution.py:64
  509.4 2.5 convert_add_fusion.3
  515.1 3.7 collective-permute-done.37
  520.3 5.5 place.3
  528.9 8.0 %collective-permute-done.41 = bf16[128,1536]{1,0:T(8,128)(2,1)S(1)} collective-permute-done((bf16[128,1536]{1,0:T(8,128)(2,1)S(1)}, bf16[128,1536]{1,0:T(8,128)(2,1)S(1)}, u32[]{:S(2)}, u32[]{:S(2)}) %collective-permute-start.41) | collective-permute-done | bytes 393248 | tf_op jit(solution)/shard_map/ppermute | solution.py:64
  540.9 2.4 fusion.22
  544.8 3.6 place.4
  548.5 8.1 %collective-permute-done.44 = f32[4352]{0:T(1024)S(1)} collective-permute-done((f32[4352]{0:T(1024)S(1)}, f32[4352]{0:T(1024)S(1)}, u32[]{:S(2)}, u32[]{:S(2)}) %collective-permute-start.44) | collective-permute-done | bytes 17440 | tf_op jit(solution)/shard_map/ppermute | solution.py:262
  560.2 2.6 fusion.35
  563.4 1.6 collective-permute-done.47
  567.1 3.0 place.5
  (267 shorter events, 103.7 us)
Async XLA Ops:
  7.2 73.2 %all-gather.4.cloned.1.call-start = ((), (), s32[]{:S(2)}) async-start(), calls=%async_computation.3 | async-start | bytes 7077888 | tf_op jit(solution)/shard_map/all_gather | solution.py:217
  10.4 185.2 %all-gather.6.cloned.1.call-start = ((), (), s32[]{:S(2)}) async-start(), calls=%async_computation.4 | async-start | bytes 14155776 | tf_op jit(solution)/shard_map/all_gather | solution.py:217
  13.1 247.2 %all-gather.8.cloned.1.call-start = ((), (), s32[]{:S(2)}) async-start(), calls=%async_computation.5 | async-start | bytes 7077888 | tf_op jit(solution)/shard_map/all_gather | solution.py:217
  15.3 402.6 %reduce-scatter.4.cloned.1.call-start = ((), (), s32[]{:S(2)}) async-start(), calls=%async_computation.6 | async-start | bytes 14155776 | tf_op jit(solution)/shard_map/reduce_scatter | solution.py:254
  16.0 36.8 %copy-start.27 = (bf16[256,2048]{1,0:T(8,128)(2,1)}, bf16[256,2048]{1,0:T(8,128)(2,1)S(1)}, u32[]{:S(2)}) copy-start(bf16[256,2048]{1,0:T(8,128)(2,1)S(1)} %fusion.7.refs_0_) | copy-start | bytes 3145732
  16.0 27.1 %collective-permute-start.2 = (bf16[256,2048]{1,0:T(8,128)(2,1)S(1)}, bf16[256,2048]{1,0:T(8,128)(2,1)}, u32[]{:S(2)}, u32[]{:S(2)}) collective-permute-start(bf16[256,2048]{1,0:T(8,128)(2,1)S(1)} %fusion.7.refs_0_), channel_id=1, source_target_pairs={{0,8},{8,0},{16,24},{24,16},{1,9},{9,1},{17,25},{25,17},{2,10},{10... | collective-permute-start | bytes 3145736 | tf_op jit(solution)/shard_map/ppermute | solution.py:64
  19.0 28.1 %collective-permute-start = (bf16[256,2048]{1,0:T(8,128)(2,1)S(1)}, bf16[256,2048]{1,0:T(8,128)(2,1)}, u32[]{:S(2)}, u32[]{:S(2)}) collective-permute-start(bf16[256,2048]{1,0:T(8,128)(2,1)S(1)} %fusion.7.refs_0_), channel_id=1, source_target_pairs={{0,16},{8,24},{16,0},{24,8},{1,17},{9,25},{17,1},{25,9},{2,18},{10... | collective-permute-start | bytes 3145736 | tf_op jit(solution)/shard_map/ppermute | solution.py:64
  20.5 45.0 %collective-permute-start.5 = (bf16[256,2048]{1,0:T(8,128)(2,1)S(1)}, bf16[256,2048]{1,0:T(8,128)(2,1)}, u32[]{:S(2)}, u32[]{:S(2)}) collective-permute-start(bf16[256,2048]{1,0:T(8,128)(2,1)S(1)} %bitcast.103), channel_id=1, source_target_pairs={{0,8},{8,0},{16,24},{24,16},{1,9},{9,1},{17,25},{25,17},{2,10},{10... | collective-permute-start | bytes 3145736 | tf_op jit(solution)/shard_map/ppermute | solution.py:64
  21.1 46.6 %collective-permute-start.4 = (bf16[256,2048]{1,0:T(8,128)(2,1)S(1)}, bf16[256,2048]{1,0:T(8,128)(2,1)}, u32[]{:S(2)}, u32[]{:S(2)}) collective-permute-start(bf16[256,2048]{1,0:T(8,128)(2,1)S(1)} %bitcast.104), channel_id=1, source_target_pairs={{0,16},{8,24},{16,0},{24,8},{1,17},{9,25},{17,1},{25,9},{2,18},{10... | collective-permute-start | bytes 3145736 | tf_op jit(solution)/shard_map/ppermute | solution.py:64
  45.0 32.4 %collective-permute-start.3 = (bf16[128,2048]{1,0:T(8,128)(2,1)}, bf16[128,2048]{1,0:T(8,128)(2,1)}, u32[]{:S(2)}, u32[]{:S(2)}) collective-permute-start(bf16[128,2048]{1,0:T(8,128)(2,1)} %slice.245), channel_id=1, source_target_pairs={{0,16},{8,24},{16,0},{24,8},{1,17},{9,25},{17,1},{25,9},{2,18},{10... | collective-permute-start | bytes 1572872 | tf_op jit(solution)/shard_map/ppermute | solution.py:64
  49.0 28.5 %collective-permute-start.1 = (bf16[128,2048]{1,0:T(8,128)(2,1)}, bf16[128,2048]{1,0:T(8,128)(2,1)}, u32[]{:S(2)}, u32[]{:S(2)}) collective-permute-start(bf16[128,2048]{1,0:T(8,128)(2,1)} %slice.244), channel_id=1, source_target_pairs={{0,8},{8,0},{16,24},{24,16},{1,9},{9,1},{17,25},{25,17},{2,10},{10... | collective-permute-start | bytes 1572872 | tf_op jit(solution)/shard_map/ppermute | solution.py:64
  89.6 23.5 %collective-permute-start.6 = (bf16[128,2048]{1,0:T(8,128)(2,1)}, bf16[128,2048]{1,0:T(8,128)(2,1)S(1)}, u32[]{:S(2)}, u32[]{:S(2)}) collective-permute-start(bf16[128,2048]{1,0:T(8,128)(2,1)} %slice.248), channel_id=1, source_target_pairs={{0,8},{8,0},{16,24},{24,16},{1,9},{9,1},{17,25},{25,17},{2,10},{10... | collective-permute-start | bytes 1572872 | tf_op jit(solution)/shard_map/ppermute | solution.py:64
  90.0 23.2 %collective-permute-start.7 = (bf16[128,2048]{1,0:T(8,128)(2,1)}, bf16[128,2048]{1,0:T(8,128)(2,1)}, u32[]{:S(2)}, u32[]{:S(2)}) collective-permute-start(bf16[128,2048]{1,0:T(8,128)(2,1)} %slice.249), channel_id=1, source_target_pairs={{0,16},{8,24},{16,0},{24,8},{1,17},{9,25},{17,1},{25,9},{2,18},{10... | collective-permute-start | bytes 1572872 | tf_op jit(solution)/shard_map/ppermute | solution.py:64
  119.5 12.2 %collective-permute-start.8 = (bf16[128,2048]{1,0:T(8,128)(2,1)S(1)}, bf16[128,2048]{1,0:T(8,128)(2,1)S(1)}, u32[]{:S(2)}, u32[]{:S(2)}) collective-permute-start(bf16[128,2048]{1,0:T(8,128)(2,1)S(1)} %get-tuple-element.143), channel_id=1, source_target_pairs={{0,16},{8,24},{16,0},{24,8},{1,17},{9,25},{17,1},{25,9},{2,18},{10... | collective-permute-start | bytes 1572872 | tf_op jit(solution)/shard_map/ppermute | solution.py:64
  120.0 12.0 %collective-permute-start.10 = (bf16[128,2048]{1,0:T(8,128)(2,1)S(1)}, bf16[128,2048]{1,0:T(8,128)(2,1)S(1)}, u32[]{:S(2)}, u32[]{:S(2)}) collective-permute-start(bf16[128,2048]{1,0:T(8,128)(2,1)S(1)} %get-tuple-element.144), channel_id=1, source_target_pairs={{0,8},{8,0},{16,24},{24,16},{1,9},{9,1},{17,25},{25,17},{2,10},{10... | collective-permute-start | bytes 1572872 | tf_op jit(solution)/shard_map/ppermute | solution.py:64
  132.5 22.5 %collective-permute-start.11 = (bf16[256,2048]{1,0:T(8,128)(2,1)S(1)}, bf16[256,2048]{1,0:T(8,128)(2,1)S(1)}, u32[]{:S(2)}, u32[]{:S(2)}) collective-permute-start(bf16[256,2048]{1,0:T(8,128)(2,1)S(1)} %pad_maximum_fusion.3), channel_id=1, source_target_pairs={{0,16},{8,24},{16,0},{24,8},{1,17},{9,25},{17,1},{25,9},{2,18},{10... | collective-permute-start | bytes 3145736 | tf_op jit(solution)/shard_map/ppermute | solution.py:64
  134.2 23.0 %copy-start.44 = (f32[2048]{0:T(1024)S(1)}, f32[2048]{0:T(1024)}, u32[]{:S(2)}) copy-start(f32[2048]{0:T(1024)} %param.23) | copy-start | bytes 24580
  134.2 22.1 %collective-permute-start.9 = (bf16[256,2048]{1,0:T(8,128)(2,1)S(1)}, bf16[256,2048]{1,0:T(8,128)(2,1)S(1)}, u32[]{:S(2)}, u32[]{:S(2)}) collective-permute-start(bf16[256,2048]{1,0:T(8,128)(2,1)S(1)} %pad_maximum_fusion.2), channel_id=1, source_target_pairs={{0,8},{8,0},{16,24},{24,16},{1,9},{9,1},{17,25},{25,17},{2,10},{10... | collective-permute-start | bytes 3145736 | tf_op jit(solution)/shard_map/ppermute | solution.py:64
  157.1 183.2 %copy-start.10 = (f32[256,2048]{1,0:T(8,128)}, f32[256,2048]{1,0:T(8,128)S(1)}, u32[]{:S(2)}) copy-start(f32[256,2048]{1,0:T(8,128)S(1)} %get-tuple-element.112) | copy-start | bytes 6291460
  157.4 26.2 %copy-start.26 = (bf16[256,2048]{1,0:T(8,128)(2,1)}, bf16[256,2048]{1,0:T(8,128)(2,1)S(1)}, u32[]{:S(2)}) copy-start(bf16[256,2048]{1,0:T(8,128)(2,1)S(1)} %multiply_convert_fusion.refs_0_) | copy-start | bytes 3145732
  157.4 21.3 %collective-permute-start.14 = (bf16[256,2048]{1,0:T(8,128)(2,1)S(1)}, bf16[256,2048]{1,0:T(8,128)(2,1)S(1)}, u32[]{:S(2)}, u32[]{:S(2)}) collective-permute-start(bf16[256,2048]{1,0:T(8,128)(2,1)S(1)} %multiply_convert_fusion.refs_0_), channel_id=1, source_target_pairs={{0,8},{8,0},{16,24},{24,16},{1,9},{9,1},{17,25},{25,17},{2,10},{10... | collective-permute-start | bytes 3145736 | tf_op jit(solution)/shard_map/ppermute | solution.py:64
  158.8 21.9 %collective-permute-start.12 = (bf16[256,2048]{1,0:T(8,128)(2,1)S(1)}, bf16[256,2048]{1,0:T(8,128)(2,1)S(1)}, u32[]{:S(2)}, u32[]{:S(2)}) collective-permute-start(bf16[256,2048]{1,0:T(8,128)(2,1)S(1)} %multiply_convert_fusion.refs_0_), channel_id=1, source_target_pairs={{0,16},{8,24},{16,0},{24,8},{1,17},{9,25},{17,1},{25,9},{2,18},{10... | collective-permute-start | bytes 3145736 | tf_op jit(solution)/shard_map/ppermute | solution.py:64
  179.6 10.9 %collective-permute-start.15 = (bf16[128,2048]{1,0:T(8,128)(2,1)}, bf16[128,2048]{1,0:T(8,128)(2,1)S(1)}, u32[]{:S(2)}, u32[]{:S(2)}) collective-permute-start(bf16[128,2048]{1,0:T(8,128)(2,1)} %slice.259), channel_id=1, source_target_pairs={{0,16},{8,24},{16,0},{24,8},{1,17},{9,25},{17,1},{25,9},{2,18},{10... | collective-permute-start | bytes 1572872 | tf_op jit(solution)/shard_map/ppermute | solution.py:64
  181.8 9.5 %collective-permute-start.13 = (bf16[128,2048]{1,0:T(8,128)(2,1)}, bf16[128,2048]{1,0:T(8,128)(2,1)}, u32[]{:S(2)}, u32[]{:S(2)}) collective-permute-start(bf16[128,2048]{1,0:T(8,128)(2,1)} %slice.258), channel_id=1, source_target_pairs={{0,8},{8,0},{16,24},{24,16},{1,9},{9,1},{17,25},{25,17},{2,10},{10... | collective-permute-start | bytes 1572872 | tf_op jit(solution)/shard_map/ppermute | solution.py:64
  251.3 210.0 %reduce-scatter.6.cloned.1.call-start = ((), (), s32[]{:S(2)}) async-start(), calls=%async_computation.7 | async-start | bytes 7077888 | tf_op jit(solution)/shard_map/reduce_scatter | solution.py:254
  281.8 28.1 %copy-start.25 = (bf16[4,256,2048]{2,1,0:T(8,128)(2,1)S(1)}, bf16[4,256,2048]{2,1,0:T(8,128)(2,1)}, u32[]{:S(2)}) copy-start(bf16[4,256,2048]{2,1,0:T(8,128)(2,1)} %get-tuple-element.69) | copy-start | bytes 12582916
  283.3 14.8 %collective-permute-start.19 = (bf16[128,2048]{1,0:T(8,128)(2,1)S(1)}, bf16[128,2048]{1,0:T(8,128)(2,1)S(1)}, u32[]{:S(2)}, u32[]{:S(2)}) collective-permute-start(bf16[128,2048]{1,0:T(8,128)(2,1)S(1)} %get-tuple-element.127), channel_id=1, source_target_pairs={{0,16},{8,24},{16,0},{24,8},{1,17},{9,25},{17,1},{25,9},{2,18},{10... | collective-permute-start | bytes 1572872 | tf_op jit(solution)/shard_map/ppermute | solution.py:64
  284.9 14.8 %collective-permute-start.18 = (bf16[128,2048]{1,0:T(8,128)(2,1)S(1)}, bf16[128,2048]{1,0:T(8,128)(2,1)S(1)}, u32[]{:S(2)}, u32[]{:S(2)}) collective-permute-start(bf16[128,2048]{1,0:T(8,128)(2,1)S(1)} %get-tuple-element.128), channel_id=1, source_target_pairs={{0,8},{8,0},{16,24},{24,16},{1,9},{9,1},{17,25},{25,17},{2,10},{10... | collective-permute-start | bytes 1572872 | tf_op jit(solution)/shard_map/ppermute | solution.py:64
  287.6 21.1 %collective-permute-start.17 = (bf16[128,2048]{1,0:T(8,128)(2,1)S(1)}, bf16[128,2048]{1,0:T(8,128)(2,1)S(1)}, u32[]{:S(2)}, u32[]{:S(2)}) collective-permute-start(bf16[128,2048]{1,0:T(8,128)(2,1)S(1)} %get-tuple-element.129), channel_id=1, source_target_pairs={{0,16},{8,24},{16,0},{24,8},{1,17},{9,25},{17,1},{25,9},{2,18},{10... | collective-permute-start | bytes 1572872 | tf_op jit(solution)/shard_map/ppermute | solution.py:64
  288.2 21.8 %collective-permute-start.16 = (bf16[128,2048]{1,0:T(8,128)(2,1)S(1)}, bf16[128,2048]{1,0:T(8,128)(2,1)S(1)}, u32[]{:S(2)}, u32[]{:S(2)}) collective-permute-start(bf16[128,2048]{1,0:T(8,128)(2,1)S(1)} %get-tuple-element.130), channel_id=1, source_target_pairs={{0,8},{8,0},{16,24},{24,16},{1,9},{9,1},{17,25},{25,17},{2,10},{10... | collective-permute-start | bytes 1572872 | tf_op jit(solution)/shard_map/ppermute | solution.py:64
  311.5 24.6 %collective-permute-start.21 = (bf16[256,2048]{1,0:T(8,128)(2,1)}, bf16[256,2048]{1,0:T(8,128)(2,1)}, u32[]{:S(2)}, u32[]{:S(2)}) collective-permute-start(bf16[256,2048]{1,0:T(8,128)(2,1)} %pad_maximum_fusion.5), channel_id=1, source_target_pairs={{0,16},{8,24},{16,0},{24,8},{1,17},{9,25},{17,1},{25,9},{2,18},{10... | collective-permute-start | bytes 3145736 | tf_op jit(solution)/shard_map/ppermute | solution.py:64
  313.2 24.3 %collective-permute-start.20 = (bf16[256,2048]{1,0:T(8,128)(2,1)}, bf16[256,2048]{1,0:T(8,128)(2,1)S(1)}, u32[]{:S(2)}, u32[]{:S(2)}) collective-permute-start(bf16[256,2048]{1,0:T(8,128)(2,1)} %pad_maximum_fusion.4), channel_id=1, source_target_pairs={{0,8},{8,0},{16,24},{24,16},{1,9},{9,1},{17,25},{25,17},{2,10},{10... | collective-permute-start | bytes 3145736 | tf_op jit(solution)/shard_map/ppermute | solution.py:64
  342.3 23.4 %collective-permute-start.24 = (bf16[256,2048]{1,0:T(8,128)(2,1)S(1)}, bf16[256,2048]{1,0:T(8,128)(2,1)S(1)}, u32[]{:S(2)}, u32[]{:S(2)}) collective-permute-start(bf16[256,2048]{1,0:T(8,128)(2,1)S(1)} %fusion.56.refs_0_), channel_id=1, source_target_pairs={{0,8},{8,0},{16,24},{24,16},{1,9},{9,1},{17,25},{25,17},{2,10},{10... | collective-permute-start | bytes 3145736 | tf_op jit(solution)/shard_map/ppermute | solution.py:64
  343.8 23.1 %collective-permute-start.22 = (bf16[256,2048]{1,0:T(8,128)(2,1)S(1)}, bf16[256,2048]{1,0:T(8,128)(2,1)S(1)}, u32[]{:S(2)}, u32[]{:S(2)}) collective-permute-start(bf16[256,2048]{1,0:T(8,128)(2,1)S(1)} %fusion.56.refs_0_), channel_id=1, source_target_pairs={{0,16},{8,24},{16,0},{24,8},{1,17},{9,25},{17,1},{25,9},{2,18},{10... | collective-permute-start | bytes 3145736 | tf_op jit(solution)/shard_map/ppermute | solution.py:64
  367.8 171.0 %reduce-scatter.8.cloned.1.call-start = ((), (), s32[]{:S(2)}) async-start(), calls=%async_computation.8 | async-start | bytes 7077888 | tf_op jit(solution)/shard_map/reduce_scatter | solution.py:254
  367.8 11.0 %collective-permute-start.25 = (bf16[128,2048]{1,0:T(8,128)(2,1)S(1)}, bf16[128,2048]{1,0:T(8,128)(2,1)S(1)}, u32[]{:S(2)}, u32[]{:S(2)}) collective-permute-start(bf16[128,2048]{1,0:T(8,128)(2,1)S(1)} %slice.261), channel_id=1, source_target_pairs={{0,16},{8,24},{16,0},{24,8},{1,17},{9,25},{17,1},{25,9},{2,18},{10... | collective-permute-start | bytes 1572872 | tf_op jit(solution)/shard_map/ppermute | solution.py:64
  369.1 10.6 %collective-permute-start.23 = (bf16[128,2048]{1,0:T(8,128)(2,1)S(1)}, bf16[128,2048]{1,0:T(8,128)(2,1)S(1)}, u32[]{:S(2)}, u32[]{:S(2)}) collective-permute-start(bf16[128,2048]{1,0:T(8,128)(2,1)S(1)} %slice.260), channel_id=1, source_target_pairs={{0,8},{8,0},{16,24},{24,16},{1,9},{9,1},{17,25},{25,17},{2,10},{10... | collective-permute-start | bytes 1572872 | tf_op jit(solution)/shard_map/ppermute | solution.py:64
  386.8 29.8 %collective-permute-start.27 = (bf16[256,2048]{1,0:T(8,128)(2,1)S(1)}, bf16[256,2048]{1,0:T(8,128)(2,1)S(1)}, u32[]{:S(2)}, u32[]{:S(2)}) collective-permute-start(bf16[256,2048]{1,0:T(8,128)(2,1)S(1)} %pad_maximum_fusion.7), channel_id=1, source_target_pairs={{0,16},{8,24},{16,0},{24,8},{1,17},{9,25},{17,1},{25,9},{2,18},{10... | collective-permute-start | bytes 3145736 | tf_op jit(solution)/shard_map/ppermute | solution.py:64
  388.0 28.7 %collective-permute-start.26 = (bf16[256,2048]{1,0:T(8,128)(2,1)S(1)}, bf16[256,2048]{1,0:T(8,128)(2,1)S(1)}, u32[]{:S(2)}, u32[]{:S(2)}) collective-permute-start(bf16[256,2048]{1,0:T(8,128)(2,1)S(1)} %pad_maximum_fusion.6), channel_id=1, source_target_pairs={{0,8},{8,0},{16,24},{24,16},{1,9},{9,1},{17,25},{25,17},{2,10},{10... | collective-permute-start | bytes 3145736 | tf_op jit(solution)/shard_map/ppermute | solution.py:64
  417.9 33.1 %collective-permute-start.29 = (bf16[256,3072]{1,0:T(8,128)(2,1)}, bf16[256,3072]{1,0:T(8,128)(2,1)S(1)}, u32[]{:S(2)}, u32[]{:S(2)}) collective-permute-start(bf16[256,3072]{1,0:T(8,128)(2,1)} %reduce-scatter.4.cloned.1.call-done.refs_0_), channel_id=1, source_target_pairs={{0,16},{8,24},{16,0},{24,8},{1,17},{9,25},{17,1},{25,9},{2,18},{10... | collective-permute-start | bytes 4718600 | tf_op jit(solution)/shard_map/ppermute | solution.py:64
  418.9 32.3 %collective-permute-start.28 = (bf16[256,3072]{1,0:T(8,128)(2,1)}, bf16[256,3072]{1,0:T(8,128)(2,1)S(1)}, u32[]{:S(2)}, u32[]{:S(2)}) collective-permute-start(bf16[256,3072]{1,0:T(8,128)(2,1)} %reduce-scatter.4.cloned.1.call-done.refs_0_), channel_id=1, source_target_pairs={{0,8},{8,0},{16,24},{24,16},{1,9},{9,1},{17,25},{25,17},{2,10},{10... | collective-permute-start | bytes 4718600 | tf_op jit(solution)/shard_map/ppermute | solution.py:64
  452.3 9.5 %collective-permute-start.31 = (bf16[128,2048]{1,0:T(8,128)(2,1)}, bf16[128,2048]{1,0:T(8,128)(2,1)}, u32[]{:S(2)}, u32[]{:S(2)}) collective-permute-start(bf16[128,2048]{1,0:T(8,128)(2,1)} %get-tuple-element.141), channel_id=1, source_target_pairs={{0,16},{8,24},{16,0},{24,8},{1,17},{9,25},{17,1},{25,9},{2,18},{10... | collective-permute-start | bytes 1572872 | tf_op jit(solution)/shard_map/ppermute | solution.py:64
  453.2 9.5 %collective-permute-start.30 = (bf16[128,2048]{1,0:T(8,128)(2,1)}, bf16[128,2048]{1,0:T(8,128)(2,1)}, u32[]{:S(2)}, u32[]{:S(2)}) collective-permute-start(bf16[128,2048]{1,0:T(8,128)(2,1)} %get-tuple-element.142), channel_id=1, source_target_pairs={{0,8},{8,0},{16,24},{24,16},{1,9},{9,1},{17,25},{25,17},{2,10},{10... | collective-permute-start | bytes 1572872 | tf_op jit(solution)/shard_map/ppermute | solution.py:64
  465.9 20.8 %collective-permute-start.34 = (bf16[128,3072]{1,0:T(8,128)(2,1)}, bf16[128,3072]{1,0:T(8,128)(2,1)}, u32[]{:S(2)}, u32[]{:S(2)}) collective-permute-start(bf16[128,3072]{1,0:T(8,128)(2,1)} %slice.268), channel_id=1, source_target_pairs={{0,8},{8,0},{16,24},{24,16},{1,9},{9,1},{17,25},{25,17},{2,10},{10... | collective-permute-start | bytes 2359304 | tf_op jit(solution)/shard_map/ppermute | solution.py:64
  467.1 20.8 %collective-permute-start.35 = (bf16[128,3072]{1,0:T(8,128)(2,1)}, bf16[128,3072]{1,0:T(8,128)(2,1)}, u32[]{:S(2)}, u32[]{:S(2)}) collective-permute-start(bf16[128,3072]{1,0:T(8,128)(2,1)} %slice.269), channel_id=1, source_target_pairs={{0,16},{8,24},{16,0},{24,8},{1,17},{9,25},{17,1},{25,9},{2,18},{10... | collective-permute-start | bytes 2359304 | tf_op jit(solution)/shard_map/ppermute | solution.py:64
  471.4 36.1 %collective-permute-start.33 = (bf16[256,2048]{1,0:T(8,128)(2,1)}, bf16[256,2048]{1,0:T(8,128)(2,1)}, u32[]{:S(2)}, u32[]{:S(2)}) collective-permute-start(bf16[256,2048]{1,0:T(8,128)(2,1)} %pad_maximum_fusion.9), channel_id=1, source_target_pairs={{0,16},{8,24},{16,0},{24,8},{1,17},{9,25},{17,1},{25,9},{2,18},{10... | collective-permute-start | bytes 3145736 | tf_op jit(solution)/shard_map/ppermute | solution.py:64
  473.5 34.0 %collective-permute-start.32 = (bf16[256,2048]{1,0:T(8,128)(2,1)}, bf16[256,2048]{1,0:T(8,128)(2,1)}, u32[]{:S(2)}, u32[]{:S(2)}) collective-permute-start(bf16[256,2048]{1,0:T(8,128)(2,1)} %pad_maximum_fusion.8), channel_id=1, source_target_pairs={{0,8},{8,0},{16,24},{24,16},{1,9},{9,1},{17,25},{25,17},{2,10},{10... | collective-permute-start | bytes 3145736 | tf_op jit(solution)/shard_map/ppermute | solution.py:64
  474.4 33.1 %copy-start.7 = (bf16[256,1536]{1,0:T(8,128)(2,1)S(1)}, bf16[256,1536]{1,0:T(8,128)(2,1)}, u32[]{:S(2)}) copy-start(bf16[256,1536]{1,0:T(8,128)(2,1)} %reduce-scatter.6.cloned.1.call-done.refs_0_) | copy-start | bytes 2359300
  489.1 22.7 %copy-start.16 = (bf16[1,256,2048]{2,1,0:T(8,128)(2,1)S(1)}, bf16[1,256,2048]{2,1,0:T(8,128)(2,1)}, u32[]{:S(2)}) copy-start(bf16[1,256,2048]{2,1,0:T(8,128)(2,1)} %param.14) | copy-start | bytes 3145732
  507.5 18.3 %collective-permute-start.40 = (bf16[256,1536]{1,0:T(8,128)(2,1)S(1)}, bf16[256,1536]{1,0:T(8,128)(2,1)S(1)}, u32[]{:S(2)}, u32[]{:S(2)}) collective-permute-start(bf16[256,1536]{1,0:T(8,128)(2,1)S(1)} %copy-done.7), channel_id=1, source_target_pairs={{0,16},{8,24},{16,0},{24,8},{1,17},{9,25},{17,1},{25,9},{2,18},{10... | collective-permute-start | bytes 2359304 | tf_op jit(solution)/shard_map/ppermute | solution.py:64
  508.8 17.9 %collective-permute-start.39 = (bf16[256,1536]{1,0:T(8,128)(2,1)S(1)}, bf16[256,1536]{1,0:T(8,128)(2,1)S(1)}, u32[]{:S(2)}, u32[]{:S(2)}) collective-permute-start(bf16[256,1536]{1,0:T(8,128)(2,1)S(1)} %copy-done.7), channel_id=1, source_target_pairs={{0,8},{8,0},{16,24},{24,16},{1,9},{9,1},{17,25},{25,17},{2,10},{10... | collective-permute-start | bytes 2359304 | tf_op jit(solution)/shard_map/ppermute | solution.py:64
  513.2 1.2 collective-permute-start.36
  514.4 4.4 collective-permute-start.37
  518.8 7.0 %collective-permute-start.38 = (f32[4352]{0:T(1024)S(1)}, f32[4352]{0:T(1024)S(1)}, u32[]{:S(2)}, u32[]{:S(2)}) collective-permute-start(f32[4352]{0:T(1024)S(1)} %add.177), channel_id=1, source_target_pairs={{0,4},{1,5},{2,6},{3,7},{4,0},{5,1},{6,2},{7,3},{8,12},{9,13},{10,... | collective-permute-start | bytes 52232 | tf_op jit(solution)/shard_map/ppermute | solution.py:262
  526.8 10.2 %collective-permute-start.41 = (bf16[128,1536]{1,0:T(8,128)(2,1)S(1)}, bf16[128,1536]{1,0:T(8,128)(2,1)S(1)}, u32[]{:S(2)}, u32[]{:S(2)}) collective-permute-start(bf16[128,1536]{1,0:T(8,128)(2,1)S(1)} %slice.270), channel_id=1, source_target_pairs={{0,8},{8,0},{16,24},{24,16},{1,9},{9,1},{17,25},{25,17},{2,10},{10... | collective-permute-start | bytes 1179656 | tf_op jit(solution)/shard_map/ppermute | solution.py:64
  528.3 9.8 %collective-permute-start.42 = (bf16[128,1536]{1,0:T(8,128)(2,1)S(1)}, bf16[128,1536]{1,0:T(8,128)(2,1)S(1)}, u32[]{:S(2)}, u32[]{:S(2)}) collective-permute-start(bf16[128,1536]{1,0:T(8,128)(2,1)S(1)} %slice.271), channel_id=1, source_target_pairs={{0,16},{8,24},{16,0},{24,8},{1,17},{9,25},{17,1},{25,9},{2,18},{10... | collective-permute-start | bytes 1179656 | tf_op jit(solution)/shard_map/ppermute | solution.py:64
  538.2 5.1 collective-permute-start.43
  538.8 17.8 %collective-permute-start.46 = (bf16[256,1536]{1,0:T(8,128)(2,1)}, bf16[256,1536]{1,0:T(8,128)(2,1)S(1)}, u32[]{:S(2)}, u32[]{:S(2)}) collective-permute-start(bf16[256,1536]{1,0:T(8,128)(2,1)} %reduce-scatter.8.cloned.1.call-done.refs_0_), channel_id=1, source_target_pairs={{0,16},{8,24},{16,0},{24,8},{1,17},{9,25},{17,1},{25,9},{2,18},{10... | collective-permute-start | bytes 2359304 | tf_op jit(solution)/shard_map/ppermute | solution.py:64
  539.4 17.8 %collective-permute-start.45 = (bf16[256,1536]{1,0:T(8,128)(2,1)}, bf16[256,1536]{1,0:T(8,128)(2,1)S(1)}, u32[]{:S(2)}, u32[]{:S(2)}) collective-permute-start(bf16[256,1536]{1,0:T(8,128)(2,1)} %reduce-scatter.8.cloned.1.call-done.refs_0_), channel_id=1, source_target_pairs={{0,8},{8,0},{16,24},{24,16},{1,9},{9,1},{17,25},{25,17},{2,10},{10... | collective-permute-start | bytes 2359304 | tf_op jit(solution)/shard_map/ppermute | solution.py:64
  543.3 13.3 %collective-permute-start.44 = (f32[4352]{0:T(1024)S(1)}, f32[4352]{0:T(1024)S(1)}, u32[]{:S(2)}, u32[]{:S(2)}) collective-permute-start(f32[4352]{0:T(1024)S(1)} %add.179), channel_id=1, source_target_pairs={{0,16},{8,24},{16,0},{24,8},{1,17},{9,25},{17,1},{25,9},{2,18},{10... | collective-permute-start | bytes 52232 | tf_op jit(solution)/shard_map/ppermute | solution.py:262
  544.8 15.4 %copy-start.11 = (f32[256,2048]{1,0:T(8,128)S(1)}, f32[256,2048]{1,0:T(8,128)}, u32[]{:S(2)}) copy-start(f32[256,2048]{1,0:T(8,128)} %copy-done.10) | copy-start | bytes 6291460
  544.8 15.4 %copy-start.14 = (f32[256,2048]{1,0:T(8,128)S(1)}, f32[256,2048]{1,0:T(8,128)}, u32[]{:S(2)}) copy-start(f32[256,2048]{1,0:T(8,128)} %copy-done.13) | copy-start | bytes 6291460
  557.2 7.9 %collective-permute-start.47 = (bf16[128,1536]{1,0:T(8,128)(2,1)S(1)}, bf16[128,1536]{1,0:T(8,128)(2,1)S(1)}, u32[]{:S(2)}, u32[]{:S(2)}) collective-permute-start(bf16[128,1536]{1,0:T(8,128)(2,1)S(1)} %slice.273), channel_id=1, source_target_pairs={{0,8},{8,0},{16,24},{24,16},{1,9},{9,1},{17,25},{25,17},{2,10},{10... | collective-permute-start | bytes 1179656 | tf_op jit(solution)/shard_map/ppermute | solution.py:64
  558.7 7.8 %collective-permute-start.48 = (bf16[128,1536]{1,0:T(8,128)(2,1)S(1)}, bf16[128,1536]{1,0:T(8,128)(2,1)S(1)}, u32[]{:S(2)}, u32[]{:S(2)}) collective-permute-start(bf16[128,1536]{1,0:T(8,128)(2,1)S(1)} %slice.274), channel_id=1, source_target_pairs={{0,16},{8,24},{16,0},{24,8},{1,17},{9,25},{17,1},{25,9},{2,18},{10... | collective-permute-start | bytes 1179656 | tf_op jit(solution)/shard_map/ppermute | solution.py:64
  (41 other events, 179.6 us)
Sparse Core Ops, SparseCore 0:
  10.6 67.4 all-gather.3
  80.3 115.3 all-gather.5
  197.3 62.9 all-gather.7
  262.5 127.8 reduce-scatter.3
  393.1 68.1 reduce-scatter.5
  463.5 69.0 reduce-scatter.7

commit v5 on v4

--- a/solution.py
+++ b/solution.py
@@ -98,11 +98,10 @@
     def __init__(self, count):
         self.square = by_neighbours(count)
 
-    def first(self, last):
+    def first(self, top, low):
         if not self.square:
-            return [last]
-        half = last.shape[0] // 2
-        self.tx, self.ty = swap(last[:half], 1), swap(last[half:], 2)
+            return [top]
+        self.tx, self.ty = swap(top, 1), swap(low, 2)
         return [self.tx, self.ty]
 
     def second(self, slots):
@@ -112,11 +111,7 @@
             self.sum = lax.psum_scatter(every, "seq", scatter_dimension=0, tiled=True)
             self.sent = [every]
             return [self.sum]
-        half = self.tx.shape[0]
-        top, low = slots[1, :half], slots[1, half:]
-        sx = jnp.concatenate([top, add(low, self.ty)])
-        top, low = slots[2, :half], slots[2, half:]
-        sy = jnp.concatenate([add(top, self.tx), low])
+        sx, sy = add_halves(slots, self.tx, self.ty)
         self.sent = [sx, sy]
         self.rx, self.ry = swap(sx, 1), swap(sy, 2)
         return [self.rx, self.ry]
@@ -130,8 +125,33 @@
         return self.slots[0].astype(F32) + self.rx.astype(F32) + self.ry.astype(F32)
 
 
-def add(a, b):
-    return (a.astype(F32) + b.astype(F32)).astype(BF16)
+def add_halves_kernel(one_ref, two_ref, tx_ref, ty_ref, sx_ref, sy_ref):
+    half = tx_ref.shape[0]
+    sx_ref[:half] = one_ref[0, :half]
+    sx_ref[half:] = (one_ref[0, half:].astype(F32) + ty_ref[...].astype(F32)).astype(BF16)
+    sy_ref[:half] = (two_ref[0, :half].astype(F32) + tx_ref[...].astype(F32)).astype(BF16)
+    sy_ref[half:] = two_ref[0, half:]
+
+
+def add_halves(slots, tx, ty):
+    _, rows, c = slots.shape
+    half = pl.BlockSpec((rows // 2, c), lambda i: (0, 0))
+    whole = pl.BlockSpec((rows, c), lambda i: (0, 0))
+    return pl.pallas_call(
+        add_halves_kernel,
+        grid=(1,),
+        in_specs=[
+            pl.BlockSpec((1, rows, c), lambda i: (1, 0, 0)),
+            pl.BlockSpec((1, rows, c), lambda i: (2, 0, 0)),
+            half,
+            half,
+        ],
+        out_specs=(whole, whole),
+        out_shape=[jax.ShapeDtypeStruct((rows, c), slots.dtype)] * 2,
+        compiler_params=pltpu.CompilerParams(vmem_limit_bytes=60 << 20),
+        cost_estimate=TINY,
+        name="add_halves",
+    )(slots, slots, tx, ty)
 
 
 def slot_order(count):
@@ -163,7 +183,7 @@
         rest = rest.reshape(4, rows, w.shape[0])
         last = rest[3]
     total.last = after(last, *others)
-    got = total.first(total.last)
+    got = total.first(total.last[: rows // 2], total.last[rows // 2 :])
     total.second(rest)
     return total, got
 
@@ -173,6 +193,7 @@
         self.x, self.count = x, count
         self.square = by_neighbours(count)
         self.me = lax.axis_index("seq")
+        self.halves = None
 
     def first(self):
         if not self.square:
@@ -180,12 +201,19 @@
         self.bx, self.by = swap(self.x, 1), swap(self.x, 2)
         return [self.bx, self.by]
 
+    def cut(self):
+        if not self.square:
+            return [self.x]
+        if not self.halves:
+            half = self.x.shape[0] // 2
+            self.halves = [self.by[:half], self.bx[half:]]
+        return self.halves
+
     def second(self, *others):
         if not self.square:
             self.sent = [self.x]
             return [self.x]
-        half = self.x.shape[0] // 2
-        ahead, below = self.by[:half], self.bx[half:]
+        ahead, below = self.cut()
         if others:
             ahead, below, *_ = lax.optimization_barrier((ahead, below, *others))
         self.sent = [ahead, below]
@@ -198,11 +226,22 @@
         near = put_rows((self.x, self.bx, self.by), (0, 1, 2), 1, None)
         return put_rows((self.ad, self.bd), (3, 3), 2, near)
 
-    def slots(self):
+    def arrived(self):
+        return [piece for _, rows in self.all() for piece in rows]
+
+    def near(self):
         if not self.square:
             every = lax.all_gather(self.x, "seq", axis=0, tiled=False)
-            return [every[k] for k in range(self.count)]
-        return [self.x, self.bx, self.by, jnp.concatenate([self.ad, self.bd], axis=0)]
+            return [(jnp.int32(k), (every[k],)) for k in range(self.count)]
+        return [(self.me ^ k, (x,)) for k, x in enumerate((self.x, self.bx, self.by))]
+
+    def all(self):
+        return self.near() + [
+            (member, (jnp.concatenate(rows, axis=0),)) for member, rows in self.far()
+        ]
+
+    def far(self):
+        return [(self.me ^ 3, (self.ad, self.bd))] if self.square else []
 
 
 def after(x, *others):
@@ -217,41 +256,83 @@
     return lax.all_gather(w, "fsdp", axis=0, tiled=True)
 
 
-def terms_kernel(starts, *refs):
+def other_core(x):
+    return lax.ppermute(x, "fsdp", [(f, f ^ 1) for f in range(8)])
+
+
+def terms_kernel(starts, blocks, stride, parity_ref, *refs):
     count = len(starts)
     x_refs, d_ref, out_ref = refs[:count], refs[count], refs[-1]
+    rows = out_ref.shape[0] // blocks
     j = pl.program_id(0)
-    rows = 512
     for n, x_ref in enumerate(x_refs):
         last = starts[n + 1] if n + 1 < count else pl.num_programs(0)
 
         @pl.when((j >= starts[n]) & (j < last))
         def _():
-            for at in range(0, out_ref.shape[0], rows):
-                here = slice(at, at + rows)
-                out_ref[here, :] = dot_tn(x_ref[:, here], d_ref[...]).astype(BF16)
-
-
-def weight_terms(xs, d):
+            for i in range(blocks):
+                at = pl.multiple_of((stride * i + parity_ref[0]) * rows, rows)
+                terms = dot_tn(x_ref[:, pl.ds(at, rows)], d_ref[...])
+                here = slice(i * rows, (i + 1) * rows)
+                if len(refs) == count + 3:
+                    terms = terms + refs[count + 1][here].astype(F32)
+                out_ref[here] = terms.astype(BF16)
+
+
+def weight_terms(xs, d, blocks, stride, parity, got=None):
     length, columns = xs[0][0].shape
     tiles = sum(n for _, n in xs)
     width = d.shape[1] // tiles
     starts = [sum(n for _, n in xs[:m]) for m in range(len(xs))]
-    whole = pl.BlockSpec((length, columns), lambda j: (0, 0), pipeline_mode=pl.Buffered(1))
+    whole = pl.BlockSpec(
+        (length, columns), lambda j, parity: (0, 0), pipeline_mode=pl.Buffered(1)
+    )
+    terms = pl.BlockSpec((columns // stride, width), lambda j, parity: (0, j))
+    operands = [x for x, _ in xs] + [d] + ([] if got is None else [got])
     return pl.pallas_call(
-        functools.partial(terms_kernel, starts),
-        grid=(tiles,),
-        in_specs=[whole] * len(xs) + [pl.BlockSpec((length, width), lambda j: (0, j))],
-        out_specs=pl.BlockSpec((columns, width), lambda j: (0, j)),
-        out_shape=jax.ShapeDtypeStruct((columns, d.shape[1]), BF16),
+        functools.partial(terms_kernel, starts, blocks, stride),
+        grid_spec=pltpu.PrefetchScalarGridSpec(
+            num_scalar_prefetch=1,
+            grid=(tiles,),
+            in_specs=[whole] * len(xs)
+            + [pl.BlockSpec((length, width), lambda j, parity: (0, j))]
+            + ([] if got is None else [terms]),
+            out_specs=terms,
+        ),
+        out_shape=jax.ShapeDtypeStruct((columns // stride, d.shape[1]), BF16),
         compiler_params=pltpu.CompilerParams(vmem_limit_bytes=58 << 20),
         cost_estimate=TINY,
         name="weight_terms",
-    )(*[x for x, _ in xs], d)
-
-
-def sum_terms(terms):
-    return lax.psum_scatter(terms, "fsdp", scatter_dimension=0, tiled=True)
+    )(jnp.reshape(parity, (1,)).astype(jnp.int32), *operands)
+
+
+class Reduction:
+    def __init__(self, xs, d, count, by_core=False):
+        self.xs, self.d, self.count = xs, d, count
+        self.line = by_core and in_line(count)
+        self.core = lax.axis_index("fsdp") % 2
+
+    def odd(self, *others):
+        d = after(self.d, *others)
+        if self.line:
+            self.terms = weight_terms(self.xs, d, 4, 2, 1 - self.core)
+            self.got = other_core(self.terms)
+        else:
+            self.terms = self.got = weight_terms(self.xs, d, 4, 1, jnp.int32(0))
+        return self.terms
+
+    def even(self, *others):
+        if self.line:
+            d = after(self.d, *others)
+            self.terms = weight_terms(self.xs, d, 4, 2, self.core, self.got)
+        return self.terms
+
+    def total(self, *others):
+        terms = after(self.terms, *others)
+        groups = [[0, 2, 4, 6], [1, 3, 5, 7]] if self.line else None
+        return lax.psum_scatter(
+            terms, "fsdp", scatter_dimension=0, axis_index_groups=groups, tiled=True
+        )
 
 
 def sum_all(x, axis, count):
@@ -264,8 +345,7 @@
     return x
 
 
-ROWS = 256
-FORWARD_ROWS = 128
+BLOCK = 128
 SCALE = HEAD_SIZE ** (-0.5)
 LOG2_E = 1.4426950408889634
 
@@ -314,7 +394,7 @@
 ):
     gains = qg_ref[...], kg_ref[...]
     queries, key = heads_of((q_ref, k_ref), gains, cos_ref[...], sin_ref[...], ratio)
-    start, block = start_ref[...], FORWARD_ROWS
+    start, block = start_ref[...], BLOCK
     for i in range(q_ref.shape[0] // block):
         keys = (i + 1) * block
         _, p = softmax_rows(queries, key, start, block, i)
@@ -336,6 +416,7 @@
     qg_ref,
     kg_ref,
     do_ref,
+    o_ref,
     dq_ref,
     dk_ref,
     dv_ref,
@@ -351,19 +432,22 @@
     start = start_ref[...]
     dk_all[...] = jnp.zeros_like(dk_all)
     dv_all[...] = jnp.zeros_like(dv_all)
-    for i in range(q_ref.shape[0] // ROWS):
-        keys = (i + 1) * ROWS
-        stacked, p = softmax_rows(queries, key, start, ROWS, i)
+    products = do_ref[...].astype(F32) * o_ref[...].astype(F32)
+    deltas = [
+        jnp.sum(products[:, h * HEAD_SIZE : (h + 1) * HEAD_SIZE], axis=-1, keepdims=True)
+        for h in range(ratio)
+    ]
+    for i in range(q_ref.shape[0] // BLOCK):
+        before, keys = i * BLOCK, (i + 1) * BLOCK
+        stacked, p = softmax_rows(queries, key, start, BLOCK, i)
         do = jnp.concatenate(
-            [do_ref[i * ROWS : keys, h * HEAD_SIZE : (h + 1) * HEAD_SIZE] for h in range(ratio)],
-            axis=0,
+            [do_ref[before:keys, h * HEAD_SIZE : (h + 1) * HEAD_SIZE] for h in range(ratio)], axis=0
         )
-        dp = dot_nt(do, v_ref[:keys, :])
-        delta = jnp.sum(p * dp, axis=-1, keepdims=True)
-        ds = (p * (dp - delta) * SCALE).astype(BF16)
-        dq = dot(ds, key[:keys])
+        delta = jnp.concatenate([x[before:keys] for x in deltas], axis=0)
+        ds = (p * (dot_nt(do, v_ref[:keys, :]) - delta)).astype(BF16)
+        dq = dot(ds, key[:keys]) * SCALE
         for h in range(ratio):
-            dq_all[h, i * ROWS : keys, :] = dq[h * ROWS : (h + 1) * ROWS]
+            dq_all[h, before:keys, :] = dq[h * BLOCK : (h + 1) * BLOCK]
         dk_all[:keys, :] += dot_tn(ds, stacked)
         dv_all[:keys, :] += dot_tn(p.astype(BF16), do)
 
@@ -375,7 +459,9 @@
         )
         dq_ref[:, columns] = du.astype(BF16)
         q_terms = q_terms + jnp.sum(terms, axis=0, keepdims=True)
-    du, terms = head_norm_rope_back(k_ref[...].astype(F32), gains[1], cosine, sine, dk_all[...])
+    du, terms = head_norm_rope_back(
+        k_ref[...].astype(F32), gains[1], cosine, sine, dk_all[...] * SCALE
+    )
     dk_ref[...] = du.astype(BF16)
     dv_ref[...] = dv_all[...].astype(BF16)
     qgg_ref[0] = q_terms
@@ -423,7 +509,7 @@
     )(qkv, qkv, qkv, *tables, start, *gains)
 
 
-def attend_back(qkv, tables, start, gains, d_o, q_heads, kv_heads):
+def attend_back(qkv, tables, start, gains, d_o, o, q_heads, kv_heads):
     length = qkv.shape[0]
     ratio, wide, narrow, inputs = attention_specs(length, q_heads, kv_heads)
     gain_spec = pl.BlockSpec((1, 1, HEAD_SIZE), lambda g: (g, 0, 0))
@@ -432,7 +518,7 @@
     return pl.pallas_call(
         functools.partial(attend_back_kernel, ratio),
         grid=(kv_heads,),
-        in_specs=inputs + [wide],
+        in_specs=inputs + [wide, wide],
         out_specs=(wide, narrow, narrow, gain_spec, gain_spec),
         out_shape=(
             jax.ShapeDtypeStruct((length, q_heads * HEAD_SIZE), BF16),
@@ -449,7 +535,7 @@
         compiler_params=pltpu.CompilerParams(vmem_limit_bytes=56 << 20),
         cost_estimate=TINY,
         name="attend_back",
-    )(qkv, qkv, qkv, *tables, start, *gains, d_o)
+    )(qkv, qkv, qkv, *tables, start, *gains, d_o, o)
 
 
 def feed_forward_kernel(carried, piece, order_ref, xb_ref, dy_ref, w_ref, *refs):
@@ -504,10 +590,11 @@
     )(order, xb, dy, w, *sums)
 
 
-def place_kernel(widths, tiles, me_ref, *refs):
+def place_kernel(widths, tiles, pieces, order_ref, *refs):
     outs = refs[-len(widths) :]
     k, t = pl.program_id(0), pl.program_id(1)
     for n in range(pl.num_programs(0)):
+        mine = refs[sum(pieces[:n]) : sum(pieces[: n + 1])]
         for m in range(tiles):
 
             @pl.when((k == n) & (t == m))
@@ -515,27 +602,29 @@
                 start = 0
                 for out_ref, width in zip(outs, widths):
                     size = width // tiles
-                    at = start + m * size
-                    out_ref[...] = refs[n][:, at : at + size].astype(F32)
+                    at, row = start + m * size, 0
+                    for piece in mine:
+                        rows = piece.shape[0]
+                        out_ref[row : row + rows, :] = piece[:, at : at + size].astype(F32)
+                        row += rows
                     start += width
 
 
-def place(slots, widths, tiles, first, every, outs, me, count):
-    rows = slots[0].shape[0]
-    square = by_neighbours(count)
-
-    def out_map(k, t, me_ref):
-        member = jnp.bitwise_xor(me_ref[0], k) if square else k
-        return 0, member * every + first + t
+def place(blocks, widths, tiles, first, every, outs, count):
+    pieces = [piece for _, rows in blocks for piece in rows]
+    rows = sum(piece.shape[0] for piece in blocks[0][1])
+
+    def out_map(k, t, order_ref):
+        return 0, order_ref[k] * every + first + t
 
     any_spec = pl.BlockSpec(memory_space=pl.ANY)
-    n = len(slots)
+    n = len(pieces)
     return pl.pallas_call(
-        functools.partial(place_kernel, widths, tiles),
+        functools.partial(place_kernel, widths, tiles, [len(x) for _, x in blocks]),
         grid_spec=pltpu.PrefetchScalarGridSpec(
             num_scalar_prefetch=1,
-            grid=(count, tiles),
-            in_specs=[pl.BlockSpec(s.shape, lambda k, t, me_ref: (0, 0)) for s in slots]
+            grid=(len(blocks), tiles),
+            in_specs=[pl.BlockSpec(x.shape, lambda k, t, order_ref: (0, 0)) for x in pieces]
             + [any_spec] * len(outs),
             out_specs=[pl.BlockSpec((rows, w // tiles), out_map) for w in widths],
         ),
@@ -546,7 +635,7 @@
         compiler_params=pltpu.CompilerParams(vmem_limit_bytes=40 << 20),
         name="place",
         cost_estimate=TINY,
-    )(jnp.reshape(me, (1,)).astype(jnp.int32), *slots, *outs)
+    )(jnp.stack([k for k, _ in blocks]).astype(jnp.int32), *pieces, *outs)
 
 
 def make_body(counts):
@@ -628,39 +717,44 @@
         xb = get_xb.column()
 
         d1, *sums = feed_forward(xb, dy, w_mlp[0], order, (), F32)
-        terms1 = weight_terms([(xb, 2), (dy, 1)], d1)
-        share1 = sum_terms(terms1)
+        red1 = Reduction([(xb, 2), (dy, 1)], d1, fsdp_count)
+        terms1 = red1.odd()
+        share1 = red1.total()
         xb2 = after(xb, terms1)
         d2, d_xb, out = feed_forward(xb2, dy, w_mlp[1], order, tuple(sums), BF16)
         sum_dxb, sum_out = Scatter(seq_count), Scatter(seq_count)
-        got = sum_dxb.first(d_xb[-1]) + sum_out.first(out[-1])
+        half = d_xb.shape[1] // 2
+        got = sum_dxb.first(d_xb[-1, :half], d_xb[-1, half:])
+        got += sum_out.first(out[-1, :half], out[-1, half:])
         sum_dxb.second(after(d_xb, *got))
-        terms2 = weight_terms([(xb, 2), (dy, 1)], after(d2, *sum_dxb.sent))
+        red2 = Reduction([(xb, 2), (dy, 1)], d2, fsdp_count)
+        terms2 = red2.odd(*sum_dxb.sent)
         du, post_terms = norm_back(resid, post_gain, after(sum_dxb.finish(), terms2))
         d_resid = cotangent[0].astype(F32) + du
         get_drl = Gather(d_resid.astype(BF16), seq_count)
         get_drl.first()
         get_drl.second()
-        share2 = sum_terms(after(terms2, *get_drl.sent))
+        share2 = red2.total(*get_drl.sent)
         drl = get_drl.column()
         halves = sum_out.second(after(out, drl))
         d_o = dot(drl, w_out).astype(BF16)
         dq, dk, dv, q_terms, k_terms = attend_back(
-            qkv, tables, start, head_gains, after(d_o, *sum_out.sent), q_heads, kv_heads
+            qkv, tables, start, head_gains, after(d_o, *sum_out.sent), o, q_heads, kv_heads
         )
         dq = after(dq, *halves)
         get1 = Gather(after(share1, dq), seq_count)
         near = get1.first()
         d_attn = jnp.concatenate([dq, dk, dv, o], axis=1)
-        terms3 = weight_terms([(xa, 2), (drl, 1)], d_attn)
+        red3 = Reduction([(xa, 2), (drl, 1)], d_attn, fsdp_count)
+        terms3 = red3.odd()
         d_qkv = after(d_attn, terms3)[:, :qkv_cols]
         sum_dxa, got = scattered_product(
-            d_qkv, w_qkv, order, seq_count, *near, early=False
+            d_qkv, w_qkv, order, seq_count, *near, *get1.cut(), early=False
         )
         get1.second(*got)
         out = resid + after(sum_out.finish(), *got)
-        share3 = sum_terms(after(terms3, share2, *got))
-        du, in_terms = norm_back(inputs, input_gain, after(sum_dxa.finish(), *get1.slots()))
+        share3 = red3.total(share2, *got)
+        du, in_terms = norm_back(inputs, input_gain, after(sum_dxa.finish(), *get1.arrived()))
         d_inputs = d_resid + du
 
         gains = jnp.concatenate(
@@ -672,18 +766,21 @@
             ]
         )
         width = post_gain.shape[0]
-        get2 = Gather(after(share2, *get1.slots(), *sum_dxa.arrived()), seq_count)
+        get2 = Gather(after(share2, *get1.arrived(), *sum_dxa.arrived()), seq_count)
         get2.first()
         gains = sum_all(gains, "fsdp", fsdp_count)
-        mlp = place(get1.slots(), (pieces[0],) * 3, 2, 0, 3, (), me, seq_count)
+        mlp = place(get1.all(), (pieces[0],) * 3, 2, 0, 3, (), seq_count)
         get2.second(gains, *mlp)
-        get3 = Gather(after(share3, *get2.slots()), seq_count)
+        get3 = Gather(after(share3, *get2.arrived()), seq_count)
         get3.first()
-        mlp = place(get2.slots(), (pieces[1],) * 3, 1, 2, 3, mlp, me, seq_count)
-        gains = sum_all(after(gains, *get2.slots()), "seq", seq_count)
+        mlp = place(get2.all(), (pieces[1],) * 3, 1, 2, 3, mlp, seq_count)
+        gains = sum_all(after(gains, *get2.arrived()), "seq", seq_count)
         get3.second(gains, *mlp)
         widths = (q_cols, kv_cols, kv_cols, q_cols)
-        g_q, g_k, g_v, g_out = place(get3.slots(), widths, 1, 0, 1, (), me, seq_count)
+        attn = place(get3.near(), widths, 1, 0, 1, (), seq_count)
+        if get3.far():
+            attn = place(get3.far(), widths, 1, 0, 1, attn, seq_count)
+        g_q, g_k, g_v, g_out = attn
         return (
             out.astype(BF16)[None],
             d_inputs.astype(BF16)[None],

time: 587 us -> 582 us (level)
  Pallas kernels: 180 us -> 195 us
  waiting for transfers between devices: 226 us -> 213 us
    pallas_call x6 -> x11, Pallas kernels: 57.4 us -> 73.4 us  [the longest x3 45.5 us: weight_terms(): pl.pallas_call(functools.partial(terms_kernel, starts, blocks, stride), g...]
    all_gather x3, waiting for transfers between devices: 10.4 us -> 3.22 us  [gather_weight(): return lax.all_gather(w, 'fsdp', axis=0, tiled=True)]
    slice x19 -> x17, local copies, waits for them, and re-layouts: 15.4 us -> 12.6 us  [the longest x14 11.4 us: cut(): self.halves = [self.by[:half], self.bx[half:]]]
  transfers between devices with their start and end apart: 55 -> 55, of which waited for: 40 -> 39; matrix products, arithmetic and copies ran while one was open for 15% -> 15% of each run, Pallas kernels for 31% -> 34%
where the time goes in v5:
time: 582 us; the launch traced here: 572 us
  waiting for transfers between devices  213 us (37%)
  Pallas kernels  195 us (34%)
  starting transfers between devices  50.7 us (9%)
  local copies, waits for them, and re-layouts  34.3 us (6%)
  other arithmetic  32 us (5%)
  matrix products  31.7 us (5%)
  between operations  15.3 us (3%)
    ppermute x44, waiting for transfers between devices, swap(): return lax.ppermute(x, 'seq', [(s, s ^ side) for s in range(4)])  192 us
    pallas_call x2, Pallas kernels, feed_forward(): pl.pallas_call(functools.partial(feed_forward_kernel, bool(sums), piece),...  57.8 us
    ppermute x44, starting transfers between devices, swap(): return lax.ppermute(x, 'seq', [(s, s ^ side) for s in range(4)])  46.9 us
    pallas_call x3, Pallas kernels, weight_terms(): pl.pallas_call(functools.partial(terms_kernel, starts, blocks, stride), g...  45.5 us
    pallas_call x8, Pallas kernels, put_rows(): pl.pallas_call(functools.partial(put_rows_kernel, len(pieces)), grid_spec...  30.5 us
    pallas_call x1, Pallas kernels, attend_back(): pl.pallas_call(functools.partial(attend_back_kernel, ratio), grid=(kv_hea...  19.9 us
    dot_general x3, matrix products, dot_nt(): lax.dot_general(a, b, (((1,), (1,)), ((), ())), preferred_element_type=F32)  16.2 us
    dot_general x2, matrix products, dot(): return jnp.dot(a, b, preferred_element_type=F32)  15.5 us
  transfers between devices with their start and end apart: 55, of which 39 were waited for; matrix products, arithmetic and copies ran while one was open for 15% of the time, Pallas kernels for 34%

profile of v5, /device:TPU:0, one launch (start us, length us, event | category | flops | bytes accessed | tf_op | source)
XLA Modules:
  0.0 571.9 jit_solution(7284410681078101376)
XLA Ops:
  16.0 3.0 collective-permute-start.2
  21.8 21.3 %collective-permute-done.2.refs_1_ = bf16[256,2048]{1,0:T(8,128)(2,1)} collective-permute-done((bf16[256,2048]{1,0:T(8,128)(2,1)S(1)}, bf16[256,2048]{1,0:T(8,128)(2,1)}, u32[]{:S(2)}, u32[]{:S(2)}) %collective-permute-start.2) | collective-permute-done | bytes 1048608 | tf_op jit(solution)/shard_map/ppermute | solution.py:64
  43.1 1.9 slice.159
  45.0 2.0 collective-permute-start.3
  47.1 1.9 slice.158
  52.8 4.6 put_rows.8.refs_2_
  57.5 8.1 %collective-permute-done.5.refs_1_ = bf16[256,2048]{1,0:T(8,128)(2,1)} collective-permute-done((bf16[256,2048]{1,0:T(8,128)(2,1)S(1)}, bf16[256,2048]{1,0:T(8,128)(2,1)}, u32[]{:S(2)}, u32[]{:S(2)}) %collective-permute-start.5) | collective-permute-done | bytes 1048608 | tf_op jit(solution)/shard_map/ppermute | solution.py:64
  65.6 1.9 slice.163
  67.7 1.9 slice.162
  69.6 7.9 %collective-permute-done.3.refs_1_ = bf16[128,2048]{1,0:T(8,128)(2,1)} collective-permute-done((bf16[128,2048]{1,0:T(8,128)(2,1)}, bf16[128,2048]{1,0:T(8,128)(2,1)}, u32[]{:S(2)}, u32[]{:S(2)}) %collective-permute-start.3) | collective-permute-done | bytes 524320 | tf_op jit(solution)/shard_map/ppermute | solution.py:64
  77.5 2.9 put_rows.9.refs_0_
  80.4 9.3 %fusion.24.q_ref.k_ref.v_ref = bf16[1024,1024]{1,0:T(8,128)(2,1)} fusion(bf16[1024,2048]{1,0:T(8,128)(2,1)} %put_rows.9.refs_0_, bf16[2048,1536]{1,0:T(8,128)(2,1)} %all-gather.4.cloned.1.call-done), kind=kOutput, calls=%fused_computation.40 | convolution fusion | flops 4296015872 | bytes 10485760 | tf_op jit(solution)/shard_map/dot_general | solution.py:21
  91.7 1.9 fusion.42
  95.8 4.7 put_rows.10.refs_2_
  100.5 12.8 %attend.1.o_ref = bf16[1024,512]{1,0:T(8,128)(2,1)} custom-call(bf16[1024,1024]{1,0:T(8,128)(2,1)} %fusion.24.q_ref.k_ref.v_ref, bf16[1024,1024]{1,0:T(8,128)(2,1)} %fusion.24.q_ref.k_ref.v_ref, bf16[1024,1024]{1,0:T(8,128)(2,1)} %fusion.24.q_ref.k_ref.v_ref, f32[1024,128]{1,0:T(8,128)} %get-tuple-element.167.cos_ref, ...), custom_call_target="tpu_custom_call" | custom-call | flops 1000 | bytes 1000 | tf_op jit(solution)/shard_map/attend/pallas_call | solution.py:500
  114.1 3.1 put_rows.11.dy_ref.refs_1_
  117.2 2.3 convolution_convert_fusion.2
  121.7 5.1 convolution_convert_fusion.1
  126.8 4.9 collective-permute-done.9.ty_ref
  132.8 3.3 add_halves.4
  138.9 19.9 %collective-permute-done.10 = bf16[256,2048]{1,0:T(8,128)(2,1)S(1)} collective-permute-done((bf16[256,2048]{1,0:T(8,128)(2,1)}, bf16[256,2048]{1,0:T(8,128)(2,1)S(1)}, u32[]{:S(2)}, u32[]{:S(2)}) %collective-permute-start.10) | collective-permute-done | bytes 1048608 | tf_op jit(solution)/shard_map/ppermute | solution.py:64
  159.5 1.9 multiply_reduce_fusion.2
  164.0 18.9 %collective-permute-done.14.refs_1_ = bf16[256,2048]{1,0:T(8,128)(2,1)S(1)} collective-permute-done((bf16[256,2048]{1,0:T(8,128)(2,1)S(1)}, bf16[256,2048]{1,0:T(8,128)(2,1)S(1)}, u32[]{:S(2)}, u32[]{:S(2)}) %collective-permute-start.14) | collective-permute-done | bytes 1048608 | tf_op jit(solution)/shard_map/ppermute | solution.py:64
  187.9 4.6 put_rows.12.refs_2_
  192.6 2.7 collective-permute-done.15.refs_1_
  196.8 2.9 put_rows.13.xb_ref.refs_0_
  199.7 36.4 %feed_forward.2 = (bf16[1024,3072]{1,0:T(8,128)(2,1)}, f32[4,256,2048]{2,1,0:T(8,128)}, f32[4,256,2048]{2,1,0:T(8,128)}) custom-call(s32[4]{0:T(128)} %pad_add_fusion.2.order_ref, bf16[1024,2048]{1,0:T(8,128)(2,1)} %put_rows.13.xb_ref.refs_0_, bf16[1024,2048]{1,0:T(8,128)(2,1)} %put_rows.11.dy_ref.refs_1_, bf16[2048,3072]{1,0:T(8,128)(2,1)} %all-gather.6.cloned.1.call-done.w_ref), custom_call_target="tpu_custom_call" | custom-call | flops 1000 | bytes 1000 | tf_op jit(solution)/shard_map/feed_forward/pallas_call | solution.py:574
  236.1 20.4 %weight_terms.3 = bf16[2048,3072]{1,0:T(8,128)(2,1)} custom-call(s32[1]{0:T(128)} %constant.50.clone.1.parity_ref, bf16[1024,2048]{1,0:T(8,128)(2,1)} %put_rows.13.xb_ref.refs_0_, bf16[1024,2048]{1,0:T(8,128)(2,1)} %put_rows.11.dy_ref.refs_1_, bf16[1024,3072]{1,0:T(8,128)(2,1)} %get-tuple-element.77.refs_2_), custom_call_target="tpu_custom_call" | custom-call | flops 1000 | bytes 1000 | tf_op jit(solution)/shard_map/weight_terms/pallas_call | solution.py:292
  256.6 3.2 all-gather.8.cloned.1.call-done.w_ref
  259.8 21.5 %feed_forward.3 = (bf16[1024,1536]{1,0:T(8,128)(2,1)}, bf16[4,256,2048]{2,1,0:T(8,128)(2,1)}, bf16[4,256,2048]{2,1,0:T(8,128)(2,1)}) custom-call(s32[4]{0:T(128)} %pad_add_fusion.2.order_ref, bf16[1024,2048]{1,0:T(8,128)(2,1)} %put_rows.13.xb_ref.refs_0_, bf16[1024,2048]{1,0:T(8,128)(2,1)} %put_rows.11.dy_ref.refs_1_, ...), custom_call_target="tpu_custom_call" | custom-call | flops 1000 | bytes 1000 | tf_op jit(solution)/shard_map/feed_forward/pallas_call | solution.py:574
  288.0 9.3 %collective-permute-done.19.ty_ref = bf16[128,2048]{1,0:T(8,128)(2,1)S(1)} collective-permute-done((bf16[128,2048]{1,0:T(8,128)(2,1)S(1)}, bf16[128,2048]{1,0:T(8,128)(2,1)S(1)}, u32[]{:S(2)}, u32[]{:S(2)}) %collective-permute-start.19) | collective-permute-done | bytes 524320 | tf_op jit(solution)/shard_map/ppermute | solution.py:64
  298.9 9.1 %collective-permute-done.17.ty_ref = bf16[128,2048]{1,0:T(8,128)(2,1)S(1)} collective-permute-done((bf16[128,2048]{1,0:T(8,128)(2,1)S(1)}, bf16[128,2048]{1,0:T(8,128)(2,1)S(1)}, u32[]{:S(2)}, u32[]{:S(2)}) %collective-permute-start.17) | collective-permute-done | bytes 524320 | tf_op jit(solution)/shard_map/ppermute | solution.py:64
  309.3 3.4 add_halves.5
  315.1 12.4 %weight_terms.4 = bf16[2048,1536]{1,0:T(8,128)(2,1)} custom-call(s32[1]{0:T(128)} %constant.50.clone.1.parity_ref, bf16[1024,2048]{1,0:T(8,128)(2,1)} %put_rows.13.xb_ref.refs_0_, bf16[1024,2048]{1,0:T(8,128)(2,1)} %put_rows.11.dy_ref.refs_1_, bf16[1024,1536]{1,0:T(8,128)(2,1)} %get-tuple-element.87.refs_2_), custom_call_target="tpu_custom_call" | custom-call | flops 1000 | bytes 1000 | tf_op jit(solution)/shard_map/weight_terms/pallas_call | solution.py:292
  327.5 9.7 %collective-permute-done.20 = bf16[256,2048]{1,0:T(8,128)(2,1)S(1)} collective-permute-done((bf16[256,2048]{1,0:T(8,128)(2,1)}, bf16[256,2048]{1,0:T(8,128)(2,1)S(1)}, u32[]{:S(2)}, u32[]{:S(2)}) %collective-permute-start.20) | collective-permute-done | bytes 1048608 | tf_op jit(solution)/shard_map/ppermute | solution.py:64
  338.3 2.2 fusion.23
  345.5 20.7 %collective-permute-done.24.refs_1_ = bf16[256,2048]{1,0:T(8,128)(2,1)S(1)} collective-permute-done((bf16[256,2048]{1,0:T(8,128)(2,1)S(1)}, bf16[256,2048]{1,0:T(8,128)(2,1)S(1)}, u32[]{:S(2)}, u32[]{:S(2)}) %collective-permute-start.24) | collective-permute-done | bytes 1048608 | tf_op jit(solution)/shard_map/ppermute | solution.py:64
  368.1 1.7 collective-permute-start.25
  370.7 4.8 put_rows.14.refs_2_
  375.5 3.9 collective-permute-done.25.refs_1_
  381.6 2.9 put_rows.15.refs_1_
  384.5 3.4 add_halves.6
  389.5 6.2 %fusion.31.do_ref = bf16[1024,512]{1,0:T(8,128)(2,1)} fusion(bf16[1024,2048]{1,0:T(8,128)(2,1)} %put_rows.15.refs_1_, bf16[2048,1536]{1,0:T(8,128)(2,1)} %all-gather.4.cloned.1.call-done), kind=kOutput, calls=%fused_computation.46 | convolution fusion | flops 2148007936 | bytes 7340032 | tf_op jit(solution)/shard_map/dot_general | solution.py:21
  395.7 19.9 %attend_back.1 = (bf16[1024,512]{1,0:T(8,128)(2,1)}, bf16[1024,256]{1,0:T(8,128)(2,1)}, bf16[1024,256]{1,0:T(8,128)(2,1)}, f32[2,1,128]{2,1,0:T(1,128)}, f32[2,1,128]{2,1,0:T(1,128)}) custom-call(bf16[1024,1024]{1,0:T(8,128)(2,1)} %fusion.24.q_ref.k_ref.v_ref, bf16[1024,1024]{1,0:T(8,128)(2,1)} %fusion.24.q_ref.k_ref.v_ref, ...), custom_call_target="tpu_custom_call" | custom-call | flops 1000 | bytes 1000 | tf_op jit(solution)/shard_map/attend_back/pallas_call | solution.py:518
  419.3 3.1 pad_maximum_fusion.refs_2_
  422.5 12.7 %weight_terms.5 = bf16[2048,1536]{1,0:T(8,128)(2,1)} custom-call(s32[1]{0:T(128)} %constant.50.clone.1.parity_ref, bf16[1024,2048]{1,0:T(8,128)(2,1)} %put_rows.9.refs_0_, bf16[1024,2048]{1,0:T(8,128)(2,1)} %put_rows.15.refs_1_, bf16[1024,1536]{1,0:T(8,128)(2,1)} %pad_maximum_fusion.refs_2_), custom_call_target="tpu_custom_call" | custom-call | flops 1000 | bytes 1000 | tf_op jit(solution)/shard_map/weight_terms/pallas_call | solution.py:292
  436.9 8.8 %convolution_convert_fusion = bf16[1024,2048]{1,0:T(8,128)(2,1)S(1)} fusion(bf16[2048,1536]{1,0:T(8,128)(2,1)} %all-gather.4.cloned.1.call-done, bf16[256,1024]{1,0:T(8,128)(2,1)S(1)} %get-tuple-element.146, bf16[256,1024]{1,0:T(8,128)(2,1)S(1)} %get-tuple-element.147, bf16[256,1024]{1,0:T(8,128)(2,1)S(1)} %get-tuple-element.148, ...), kind=kOutput, calls=%fused_computation | convolution fusion | flops 4305453056 | bytes 10485760 | tf_op jit(solution)/shard_map/dot_general | solution.py:25
  445.8 3.0 collective-permute-done.29.refs_2_
  454.3 6.5 %reduce-scatter.6.cloned.1.call-done.refs_0_ = bf16[256,1536]{1,0:T(8,128)(2,1)} async-done(((bf16[2048,1536]{1,0:T(8,128)(2,1)}), bf16[256,1536]{1,0:T(8,128)(2,1)}) %reduce-scatter.6.cloned.1.call-update) | async-done | bytes 786448 | tf_op jit(solution)/shard_map/reduce_scatter | solution.py:333
  462.6 2.0 collective-permute-start.34
  465.6 3.6 add_halves.7
  470.1 13.3 %collective-permute-done.34 = bf16[128,3072]{1,0:T(8,128)(2,1)} collective-permute-done((bf16[128,3072]{1,0:T(8,128)(2,1)}, bf16[128,3072]{1,0:T(8,128)(2,1)}, u32[]{:S(2)}, u32[]{:S(2)}) %collective-permute-start.34) | collective-permute-done | bytes 786464 | tf_op jit(solution)/shard_map/ppermute | solution.py:64
  486.6 15.2 %collective-permute-done.32 = bf16[256,2048]{1,0:T(8,128)(2,1)} collective-permute-done((bf16[256,2048]{1,0:T(8,128)(2,1)}, bf16[256,2048]{1,0:T(8,128)(2,1)}, u32[]{:S(2)}, u32[]{:S(2)}) %collective-permute-start.32) | collective-permute-done | bytes 1048608 | tf_op jit(solution)/shard_map/ppermute | solution.py:64
  501.8 2.4 collective-permute-done.33
  505.7 2.4 convert_add_fusion.3
  510.9 3.7 collective-permute-done.37
  516.1 6.4 %place.4 = (f32[256,6144]{1,0:T(8,128)}, f32[256,6144]{1,0:T(8,128)}, f32[256,6144]{1,0:T(8,128)}) custom-call(s32[4]{0:T(128)S(1)} %copy-done.11, bf16[256,3072]{1,0:T(8,128)(2,1)S(1)} %copy-done.6, bf16[256,3072]{1,0:T(8,128)(2,1)S(1)} %collective-permute-done.28.refs_1_, bf16[256,3072]{1,0:T(8,128)(2,1)S(1)} %collective-permute-done.29.refs_2_, ...), custom_call_target="tpu_custom_call" | custom-call | flops 1000 | bytes 1000 | tf_op jit(solution)/shard_map/place/pallas_call | solution.py:622
  524.7 3.2 fusion.22
  527.9 4.9 collective-permute-done.41
  538.8 6.6 %fusion.35 = (bf16[1,256,2048]{2,1,0:T(8,128)(2,1)}, bf16[1,256,2048]{2,1,0:T(8,128)(2,1)}) fusion(f32[256,2048]{1,0:T(8,128)} %copy-done.17, bf16[1,256,2048]{2,1,0:T(8,128)(2,1)} %param.14, f32[256]{0:T(256)S(1)} %broadcast_multiply_fusion, f32[2048]{0:T(1024)S(1)} %copy-done.43, f32[256]{0:T(256)S(1)} %add_rsqrt_fusion.1, ...), kind=kLoop, calls=%fused_computation.48 | loop fusion | flops 8912896 | bytes 12603392 | tf_op jit(solution)/shard_map/broadcast_in_dim | solution.py:786
  545.4 3.6 place.5
  549.0 4.9 collective-permute-done.44
  556.1 3.1 place.6
  559.2 2.7 collective-permute-done.47.refs_0_
  (251 shorter events, 97.8 us)
Async XLA Ops:
  7.2 73.2 %all-gather.4.cloned.1.call-start = ((), (), s32[]{:S(2)}) async-start(), calls=%async_computation.3 | async-start | bytes 7077888 | tf_op jit(solution)/shard_map/all_gather | solution.py:256
  10.4 189.3 %all-gather.6.cloned.1.call-start = ((), (), s32[]{:S(2)}) async-start(), calls=%async_computation.4 | async-start | bytes 14155776 | tf_op jit(solution)/shard_map/all_gather | solution.py:256
  13.1 246.7 %all-gather.8.cloned.1.call-start = ((), (), s32[]{:S(2)}) async-start(), calls=%async_computation.5 | async-start | bytes 7077888 | tf_op jit(solution)/shard_map/all_gather | solution.py:256
  15.3 401.6 %reduce-scatter.4.cloned.1.call-start = ((), (), s32[]{:S(2)}) async-start(), calls=%async_computation.6 | async-start | bytes 14155776 | tf_op jit(solution)/shard_map/reduce_scatter | solution.py:333
  16.0 36.8 %copy-start.22 = (bf16[256,2048]{1,0:T(8,128)(2,1)}, bf16[256,2048]{1,0:T(8,128)(2,1)S(1)}, u32[]{:S(2)}) copy-start(bf16[256,2048]{1,0:T(8,128)(2,1)S(1)} %fusion.7.refs_0_) | copy-start | bytes 3145732
  16.0 27.1 %collective-permute-start.2 = (bf16[256,2048]{1,0:T(8,128)(2,1)S(1)}, bf16[256,2048]{1,0:T(8,128)(2,1)}, u32[]{:S(2)}, u32[]{:S(2)}) collective-permute-start(bf16[256,2048]{1,0:T(8,128)(2,1)S(1)} %fusion.7.refs_0_), channel_id=1, source_target_pairs={{0,8},{8,0},{16,24},{24,16},{1,9},{9,1},{17,25},{25,17},{2,10},{10... | collective-permute-start | bytes 3145736 | tf_op jit(solution)/shard_map/ppermute | solution.py:64
  19.0 28.1 %collective-permute-start = (bf16[256,2048]{1,0:T(8,128)(2,1)S(1)}, bf16[256,2048]{1,0:T(8,128)(2,1)}, u32[]{:S(2)}, u32[]{:S(2)}) collective-permute-start(bf16[256,2048]{1,0:T(8,128)(2,1)S(1)} %fusion.7.refs_0_), channel_id=1, source_target_pairs={{0,16},{8,24},{16,0},{24,8},{1,17},{9,25},{17,1},{25,9},{2,18},{10... | collective-permute-start | bytes 3145736 | tf_op jit(solution)/shard_map/ppermute | solution.py:64
  20.5 45.0 %collective-permute-start.5 = (bf16[256,2048]{1,0:T(8,128)(2,1)S(1)}, bf16[256,2048]{1,0:T(8,128)(2,1)}, u32[]{:S(2)}, u32[]{:S(2)}) collective-permute-start(bf16[256,2048]{1,0:T(8,128)(2,1)S(1)} %bitcast.59), channel_id=1, source_target_pairs={{0,8},{8,0},{16,24},{24,16},{1,9},{9,1},{17,25},{25,17},{2,10},{10... | collective-permute-start | bytes 3145736 | tf_op jit(solution)/shard_map/ppermute | solution.py:64
  21.1 46.6 %collective-permute-start.4 = (bf16[256,2048]{1,0:T(8,128)(2,1)S(1)}, bf16[256,2048]{1,0:T(8,128)(2,1)}, u32[]{:S(2)}, u32[]{:S(2)}) collective-permute-start(bf16[256,2048]{1,0:T(8,128)(2,1)S(1)} %bitcast.60), channel_id=1, source_target_pairs={{0,16},{8,24},{16,0},{24,8},{1,17},{9,25},{17,1},{25,9},{2,18},{10... | collective-permute-start | bytes 3145736 | tf_op jit(solution)/shard_map/ppermute | solution.py:64
  45.0 32.4 %collective-permute-start.3 = (bf16[128,2048]{1,0:T(8,128)(2,1)}, bf16[128,2048]{1,0:T(8,128)(2,1)}, u32[]{:S(2)}, u32[]{:S(2)}) collective-permute-start(bf16[128,2048]{1,0:T(8,128)(2,1)} %slice.159), channel_id=1, source_target_pairs={{0,16},{8,24},{16,0},{24,8},{1,17},{9,25},{17,1},{25,9},{2,18},{10... | collective-permute-start | bytes 1572872 | tf_op jit(solution)/shard_map/ppermute | solution.py:64
  49.0 28.5 %collective-permute-start.1 = (bf16[128,2048]{1,0:T(8,128)(2,1)}, bf16[128,2048]{1,0:T(8,128)(2,1)}, u32[]{:S(2)}, u32[]{:S(2)}) collective-permute-start(bf16[128,2048]{1,0:T(8,128)(2,1)} %slice.158), channel_id=1, source_target_pairs={{0,8},{8,0},{16,24},{24,16},{1,9},{9,1},{17,25},{25,17},{2,10},{10... | collective-permute-start | bytes 1572872 | tf_op jit(solution)/shard_map/ppermute | solution.py:64
  89.7 23.6 %collective-permute-start.6 = (bf16[128,2048]{1,0:T(8,128)(2,1)}, bf16[128,2048]{1,0:T(8,128)(2,1)S(1)}, u32[]{:S(2)}, u32[]{:S(2)}) collective-permute-start(bf16[128,2048]{1,0:T(8,128)(2,1)} %slice.162), channel_id=1, source_target_pairs={{0,8},{8,0},{16,24},{24,16},{1,9},{9,1},{17,25},{25,17},{2,10},{10... | collective-permute-start | bytes 1572872 | tf_op jit(solution)/shard_map/ppermute | solution.py:64
  90.0 23.2 %collective-permute-start.7 = (bf16[128,2048]{1,0:T(8,128)(2,1)}, bf16[128,2048]{1,0:T(8,128)(2,1)}, u32[]{:S(2)}, u32[]{:S(2)}) collective-permute-start(bf16[128,2048]{1,0:T(8,128)(2,1)} %slice.163), channel_id=1, source_target_pairs={{0,16},{8,24},{16,0},{24,8},{1,17},{9,25},{17,1},{25,9},{2,18},{10... | collective-permute-start | bytes 1572872 | tf_op jit(solution)/shard_map/ppermute | solution.py:64
  119.6 12.1 %collective-permute-start.9 = (bf16[128,2048]{1,0:T(8,128)(2,1)S(1)}, bf16[128,2048]{1,0:T(8,128)(2,1)S(1)}, u32[]{:S(2)}, u32[]{:S(2)}) collective-permute-start(bf16[128,2048]{1,0:T(8,128)(2,1)S(1)} %get-tuple-element.151), channel_id=1, source_target_pairs={{0,16},{8,24},{16,0},{24,8},{1,17},{9,25},{17,1},{25,9},{2,18},{10... | collective-permute-start | bytes 1572872 | tf_op jit(solution)/shard_map/ppermute | solution.py:64
  120.0 12.1 %collective-permute-start.8 = (bf16[128,2048]{1,0:T(8,128)(2,1)S(1)}, bf16[128,2048]{1,0:T(8,128)(2,1)S(1)}, u32[]{:S(2)}, u32[]{:S(2)}) collective-permute-start(bf16[128,2048]{1,0:T(8,128)(2,1)S(1)} %get-tuple-element.152), channel_id=1, source_target_pairs={{0,8},{8,0},{16,24},{24,16},{1,9},{9,1},{17,25},{25,17},{2,10},{10... | collective-permute-start | bytes 1572872 | tf_op jit(solution)/shard_map/ppermute | solution.py:64
  136.1 22.7 %collective-permute-start.10 = (bf16[256,2048]{1,0:T(8,128)(2,1)}, bf16[256,2048]{1,0:T(8,128)(2,1)S(1)}, u32[]{:S(2)}, u32[]{:S(2)}) collective-permute-start(bf16[256,2048]{1,0:T(8,128)(2,1)} %get-tuple-element.75), channel_id=1, source_target_pairs={{0,8},{8,0},{16,24},{24,16},{1,9},{9,1},{17,25},{25,17},{2,10},{10... | collective-permute-start | bytes 3145736 | tf_op jit(solution)/shard_map/ppermute | solution.py:64
  137.4 24.1 %copy-start.42 = (f32[2048]{0:T(1024)S(1)}, f32[2048]{0:T(1024)}, u32[]{:S(2)}) copy-start(f32[2048]{0:T(1024)} %param.23) | copy-start | bytes 24580
  137.4 22.1 %collective-permute-start.11 = (bf16[256,2048]{1,0:T(8,128)(2,1)}, bf16[256,2048]{1,0:T(8,128)(2,1)S(1)}, u32[]{:S(2)}, u32[]{:S(2)}) collective-permute-start(bf16[256,2048]{1,0:T(8,128)(2,1)} %get-tuple-element.76), channel_id=1, source_target_pairs={{0,16},{8,24},{16,0},{24,8},{1,17},{9,25},{17,1},{25,9},{2,18},{10... | collective-permute-start | bytes 3145736 | tf_op jit(solution)/shard_map/ppermute | solution.py:64
  161.4 179.8 %copy-start.12 = (f32[256,2048]{1,0:T(8,128)}, f32[256,2048]{1,0:T(8,128)S(1)}, u32[]{:S(2)}) copy-start(f32[256,2048]{1,0:T(8,128)S(1)} %get-tuple-element.136) | copy-start | bytes 6291460
  161.7 26.3 %copy-start.21 = (bf16[256,2048]{1,0:T(8,128)(2,1)}, bf16[256,2048]{1,0:T(8,128)(2,1)S(1)}, u32[]{:S(2)}) copy-start(bf16[256,2048]{1,0:T(8,128)(2,1)S(1)} %multiply_convert_fusion.refs_0_) | copy-start | bytes 3145732
  161.7 21.2 %collective-permute-start.14 = (bf16[256,2048]{1,0:T(8,128)(2,1)S(1)}, bf16[256,2048]{1,0:T(8,128)(2,1)S(1)}, u32[]{:S(2)}, u32[]{:S(2)}) collective-permute-start(bf16[256,2048]{1,0:T(8,128)(2,1)S(1)} %multiply_convert_fusion.refs_0_), channel_id=1, source_target_pairs={{0,8},{8,0},{16,24},{24,16},{1,9},{9,1},{17,25},{25,17},{2,10},{10... | collective-permute-start | bytes 3145736 | tf_op jit(solution)/shard_map/ppermute | solution.py:64
  162.9 23.3 %collective-permute-start.12 = (bf16[256,2048]{1,0:T(8,128)(2,1)S(1)}, bf16[256,2048]{1,0:T(8,128)(2,1)S(1)}, u32[]{:S(2)}, u32[]{:S(2)}) collective-permute-start(bf16[256,2048]{1,0:T(8,128)(2,1)S(1)} %multiply_convert_fusion.refs_0_), channel_id=1, source_target_pairs={{0,16},{8,24},{16,0},{24,8},{1,17},{9,25},{17,1},{25,9},{2,18},{10... | collective-permute-start | bytes 3145736 | tf_op jit(solution)/shard_map/ppermute | solution.py:64
  183.7 11.5 %collective-permute-start.15 = (bf16[128,2048]{1,0:T(8,128)(2,1)}, bf16[128,2048]{1,0:T(8,128)(2,1)S(1)}, u32[]{:S(2)}, u32[]{:S(2)}) collective-permute-start(bf16[128,2048]{1,0:T(8,128)(2,1)} %slice.169), channel_id=1, source_target_pairs={{0,16},{8,24},{16,0},{24,8},{1,17},{9,25},{17,1},{25,9},{2,18},{10... | collective-permute-start | bytes 1572872 | tf_op jit(solution)/shard_map/ppermute | solution.py:64
  187.3 9.5 %collective-permute-start.13 = (bf16[128,2048]{1,0:T(8,128)(2,1)}, bf16[128,2048]{1,0:T(8,128)(2,1)}, u32[]{:S(2)}, u32[]{:S(2)}) collective-permute-start(bf16[128,2048]{1,0:T(8,128)(2,1)} %slice.168), channel_id=1, source_target_pairs={{0,8},{8,0},{16,24},{24,16},{1,9},{9,1},{17,25},{25,17},{2,10},{10... | collective-permute-start | bytes 1572872 | tf_op jit(solution)/shard_map/ppermute | solution.py:64
  256.5 204.3 %reduce-scatter.6.cloned.1.call-start = ((), (), s32[]{:S(2)}) async-start(), calls=%async_computation.7 | async-start | bytes 7077888 | tf_op jit(solution)/shard_map/reduce_scatter | solution.py:333
  282.5 14.8 %collective-permute-start.19 = (bf16[128,2048]{1,0:T(8,128)(2,1)S(1)}, bf16[128,2048]{1,0:T(8,128)(2,1)S(1)}, u32[]{:S(2)}, u32[]{:S(2)}) collective-permute-start(bf16[128,2048]{1,0:T(8,128)(2,1)S(1)} %get-tuple-element.139), channel_id=1, source_target_pairs={{0,16},{8,24},{16,0},{24,8},{1,17},{9,25},{17,1},{25,9},{2,18},{10... | collective-permute-start | bytes 1572872 | tf_op jit(solution)/shard_map/ppermute | solution.py:64
  284.1 14.8 %collective-permute-start.18 = (bf16[128,2048]{1,0:T(8,128)(2,1)S(1)}, bf16[128,2048]{1,0:T(8,128)(2,1)S(1)}, u32[]{:S(2)}, u32[]{:S(2)}) collective-permute-start(bf16[128,2048]{1,0:T(8,128)(2,1)S(1)} %get-tuple-element.140), channel_id=1, source_target_pairs={{0,8},{8,0},{16,24},{24,16},{1,9},{9,1},{17,25},{25,17},{2,10},{10... | collective-permute-start | bytes 1572872 | tf_op jit(solution)/shard_map/ppermute | solution.py:64
  286.8 21.1 %collective-permute-start.17 = (bf16[128,2048]{1,0:T(8,128)(2,1)S(1)}, bf16[128,2048]{1,0:T(8,128)(2,1)S(1)}, u32[]{:S(2)}, u32[]{:S(2)}) collective-permute-start(bf16[128,2048]{1,0:T(8,128)(2,1)S(1)} %get-tuple-element.141), channel_id=1, source_target_pairs={{0,16},{8,24},{16,0},{24,8},{1,17},{9,25},{17,1},{25,9},{2,18},{10... | collective-permute-start | bytes 1572872 | tf_op jit(solution)/shard_map/ppermute | solution.py:64
  287.4 21.9 %collective-permute-start.16 = (bf16[128,2048]{1,0:T(8,128)(2,1)S(1)}, bf16[128,2048]{1,0:T(8,128)(2,1)}, u32[]{:S(2)}, u32[]{:S(2)}) collective-permute-start(bf16[128,2048]{1,0:T(8,128)(2,1)S(1)} %get-tuple-element.142), channel_id=1, source_target_pairs={{0,8},{8,0},{16,24},{24,16},{1,9},{9,1},{17,25},{25,17},{2,10},{10... | collective-permute-start | bytes 1572872 | tf_op jit(solution)/shard_map/ppermute | solution.py:64
  297.4 15.3 %copy-start.35 = (bf16[128,2048]{1,0:T(8,128)(2,1)}, bf16[128,2048]{1,0:T(8,128)(2,1)S(1)}, u32[]{:S(2)}) copy-start(bf16[128,2048]{1,0:T(8,128)(2,1)S(1)} %collective-permute-done.19.ty_ref) | copy-start | bytes 1572868
  298.9 13.8 %copy-start.36 = (bf16[128,2048]{1,0:T(8,128)(2,1)}, bf16[128,2048]{1,0:T(8,128)(2,1)S(1)}, u32[]{:S(2)}) copy-start(bf16[128,2048]{1,0:T(8,128)(2,1)S(1)} %collective-permute-done.18.tx_ref) | copy-start | bytes 1572868
  312.6 24.5 %collective-permute-start.20 = (bf16[256,2048]{1,0:T(8,128)(2,1)}, bf16[256,2048]{1,0:T(8,128)(2,1)S(1)}, u32[]{:S(2)}, u32[]{:S(2)}) collective-permute-start(bf16[256,2048]{1,0:T(8,128)(2,1)} %get-tuple-element.84), channel_id=1, source_target_pairs={{0,8},{8,0},{16,24},{24,16},{1,9},{9,1},{17,25},{25,17},{2,10},{10... | collective-permute-start | bytes 3145736 | tf_op jit(solution)/shard_map/ppermute | solution.py:64
  314.1 24.2 %collective-permute-start.21 = (bf16[256,2048]{1,0:T(8,128)(2,1)}, bf16[256,2048]{1,0:T(8,128)(2,1)}, u32[]{:S(2)}, u32[]{:S(2)}) collective-permute-start(bf16[256,2048]{1,0:T(8,128)(2,1)} %get-tuple-element.85), channel_id=1, source_target_pairs={{0,16},{8,24},{16,0},{24,8},{1,17},{9,25},{17,1},{25,9},{2,18},{10... | collective-permute-start | bytes 3145736 | tf_op jit(solution)/shard_map/ppermute | solution.py:64
  343.2 23.0 %collective-permute-start.24 = (bf16[256,2048]{1,0:T(8,128)(2,1)S(1)}, bf16[256,2048]{1,0:T(8,128)(2,1)S(1)}, u32[]{:S(2)}, u32[]{:S(2)}) collective-permute-start(bf16[256,2048]{1,0:T(8,128)(2,1)S(1)} %fusion.48.refs_0_), channel_id=1, source_target_pairs={{0,8},{8,0},{16,24},{24,16},{1,9},{9,1},{17,25},{25,17},{2,10},{10... | collective-permute-start | bytes 3145736 | tf_op jit(solution)/shard_map/ppermute | solution.py:64
  344.1 23.0 %collective-permute-start.22 = (bf16[256,2048]{1,0:T(8,128)(2,1)S(1)}, bf16[256,2048]{1,0:T(8,128)(2,1)S(1)}, u32[]{:S(2)}, u32[]{:S(2)}) collective-permute-start(bf16[256,2048]{1,0:T(8,128)(2,1)S(1)} %fusion.48.refs_0_), channel_id=1, source_target_pairs={{0,16},{8,24},{16,0},{24,8},{1,17},{9,25},{17,1},{25,9},{2,18},{10... | collective-permute-start | bytes 3145736 | tf_op jit(solution)/shard_map/ppermute | solution.py:64
  368.1 166.6 %reduce-scatter.8.cloned.1.call-start = ((), (), s32[]{:S(2)}) async-start(), calls=%async_computation.8 | async-start | bytes 7077888 | tf_op jit(solution)/shard_map/reduce_scatter | solution.py:333
  368.1 11.3 %collective-permute-start.25 = (bf16[128,2048]{1,0:T(8,128)(2,1)S(1)}, bf16[128,2048]{1,0:T(8,128)(2,1)S(1)}, u32[]{:S(2)}, u32[]{:S(2)}) collective-permute-start(bf16[128,2048]{1,0:T(8,128)(2,1)S(1)} %slice.171), channel_id=1, source_target_pairs={{0,16},{8,24},{16,0},{24,8},{1,17},{9,25},{17,1},{25,9},{2,18},{10... | collective-permute-start | bytes 1572872 | tf_op jit(solution)/shard_map/ppermute | solution.py:64
  369.8 11.0 %collective-permute-start.23 = (bf16[128,2048]{1,0:T(8,128)(2,1)S(1)}, bf16[128,2048]{1,0:T(8,128)(2,1)S(1)}, u32[]{:S(2)}, u32[]{:S(2)}) collective-permute-start(bf16[128,2048]{1,0:T(8,128)(2,1)S(1)} %slice.170), channel_id=1, source_target_pairs={{0,8},{8,0},{16,24},{24,16},{1,9},{9,1},{17,25},{25,17},{2,10},{10... | collective-permute-start | bytes 1572872 | tf_op jit(solution)/shard_map/ppermute | solution.py:64
  388.0 27.6 %collective-permute-start.26 = (bf16[256,2048]{1,0:T(8,128)(2,1)}, bf16[256,2048]{1,0:T(8,128)(2,1)S(1)}, u32[]{:S(2)}, u32[]{:S(2)}) collective-permute-start(bf16[256,2048]{1,0:T(8,128)(2,1)} %get-tuple-element.90), channel_id=1, source_target_pairs={{0,8},{8,0},{16,24},{24,16},{1,9},{9,1},{17,25},{25,17},{2,10},{10... | collective-permute-start | bytes 3145736 | tf_op jit(solution)/shard_map/ppermute | solution.py:64
  388.4 27.2 %collective-permute-start.27 = (bf16[256,2048]{1,0:T(8,128)(2,1)}, bf16[256,2048]{1,0:T(8,128)(2,1)S(1)}, u32[]{:S(2)}, u32[]{:S(2)}) collective-permute-start(bf16[256,2048]{1,0:T(8,128)(2,1)} %get-tuple-element.91), channel_id=1, source_target_pairs={{0,16},{8,24},{16,0},{24,8},{1,17},{9,25},{17,1},{25,9},{2,18},{10... | collective-permute-start | bytes 3145736 | tf_op jit(solution)/shard_map/ppermute | solution.py:64
  416.9 31.9 %collective-permute-start.29 = (bf16[256,3072]{1,0:T(8,128)(2,1)}, bf16[256,3072]{1,0:T(8,128)(2,1)S(1)}, u32[]{:S(2)}, u32[]{:S(2)}) collective-permute-start(bf16[256,3072]{1,0:T(8,128)(2,1)} %reduce-scatter.4.cloned.1.call-done.refs_0_), channel_id=1, source_target_pairs={{0,16},{8,24},{16,0},{24,8},{1,17},{9,25},{17,1},{25,9},{2,18},{10... | collective-permute-start | bytes 4718600 | tf_op jit(solution)/shard_map/ppermute | solution.py:64
  417.7 32.1 %collective-permute-start.28 = (bf16[256,3072]{1,0:T(8,128)(2,1)}, bf16[256,3072]{1,0:T(8,128)(2,1)S(1)}, u32[]{:S(2)}, u32[]{:S(2)}) collective-permute-start(bf16[256,3072]{1,0:T(8,128)(2,1)} %reduce-scatter.4.cloned.1.call-done.refs_0_), channel_id=1, source_target_pairs={{0,8},{8,0},{16,24},{24,16},{1,9},{9,1},{17,25},{25,17},{2,10},{10... | collective-permute-start | bytes 4718600 | tf_op jit(solution)/shard_map/ppermute | solution.py:64
  451.7 9.5 %collective-permute-start.31 = (bf16[128,2048]{1,0:T(8,128)(2,1)}, bf16[128,2048]{1,0:T(8,128)(2,1)}, u32[]{:S(2)}, u32[]{:S(2)}) collective-permute-start(bf16[128,2048]{1,0:T(8,128)(2,1)} %get-tuple-element.149), channel_id=1, source_target_pairs={{0,16},{8,24},{16,0},{24,8},{1,17},{9,25},{17,1},{25,9},{2,18},{10... | collective-permute-start | bytes 1572872 | tf_op jit(solution)/shard_map/ppermute | solution.py:64
  452.6 10.0 %collective-permute-start.30 = (bf16[128,2048]{1,0:T(8,128)(2,1)}, bf16[128,2048]{1,0:T(8,128)(2,1)}, u32[]{:S(2)}, u32[]{:S(2)}) collective-permute-start(bf16[128,2048]{1,0:T(8,128)(2,1)} %get-tuple-element.150), channel_id=1, source_target_pairs={{0,8},{8,0},{16,24},{24,16},{1,9},{9,1},{17,25},{25,17},{2,10},{10... | collective-permute-start | bytes 1572872 | tf_op jit(solution)/shard_map/ppermute | solution.py:64
  462.6 20.9 %collective-permute-start.34 = (bf16[128,3072]{1,0:T(8,128)(2,1)}, bf16[128,3072]{1,0:T(8,128)(2,1)}, u32[]{:S(2)}, u32[]{:S(2)}) collective-permute-start(bf16[128,3072]{1,0:T(8,128)(2,1)} %slice.173), channel_id=1, source_target_pairs={{0,8},{8,0},{16,24},{24,16},{1,9},{9,1},{17,25},{25,17},{2,10},{10... | collective-permute-start | bytes 2359304 | tf_op jit(solution)/shard_map/ppermute | solution.py:64
  464.6 20.8 %collective-permute-start.35 = (bf16[128,3072]{1,0:T(8,128)(2,1)}, bf16[128,3072]{1,0:T(8,128)(2,1)}, u32[]{:S(2)}, u32[]{:S(2)}) collective-permute-start(bf16[128,3072]{1,0:T(8,128)(2,1)} %slice.174), channel_id=1, source_target_pairs={{0,16},{8,24},{16,0},{24,8},{1,17},{9,25},{17,1},{25,9},{2,18},{10... | collective-permute-start | bytes 2359304 | tf_op jit(solution)/shard_map/ppermute | solution.py:64
  469.1 32.7 %collective-permute-start.32 = (bf16[256,2048]{1,0:T(8,128)(2,1)}, bf16[256,2048]{1,0:T(8,128)(2,1)}, u32[]{:S(2)}, u32[]{:S(2)}) collective-permute-start(bf16[256,2048]{1,0:T(8,128)(2,1)} %get-tuple-element.101), channel_id=1, source_target_pairs={{0,8},{8,0},{16,24},{24,16},{1,9},{9,1},{17,25},{25,17},{2,10},{10... | collective-permute-start | bytes 3145736 | tf_op jit(solution)/shard_map/ppermute | solution.py:64
  469.2 35.1 %collective-permute-start.33 = (bf16[256,2048]{1,0:T(8,128)(2,1)}, bf16[256,2048]{1,0:T(8,128)(2,1)}, u32[]{:S(2)}, u32[]{:S(2)}) collective-permute-start(bf16[256,2048]{1,0:T(8,128)(2,1)} %get-tuple-element.102), channel_id=1, source_target_pairs={{0,16},{8,24},{16,0},{24,8},{1,17},{9,25},{17,1},{25,9},{2,18},{10... | collective-permute-start | bytes 3145736 | tf_op jit(solution)/shard_map/ppermute | solution.py:64
  470.1 34.2 %copy-start.7 = (bf16[256,1536]{1,0:T(8,128)(2,1)S(1)}, bf16[256,1536]{1,0:T(8,128)(2,1)}, u32[]{:S(2)}) copy-start(bf16[256,1536]{1,0:T(8,128)(2,1)} %reduce-scatter.6.cloned.1.call-done.refs_0_) | copy-start | bytes 2359300
  486.6 21.6 %copy-start.16 = (bf16[1,256,2048]{2,1,0:T(8,128)(2,1)S(1)}, bf16[1,256,2048]{2,1,0:T(8,128)(2,1)}, u32[]{:S(2)}) copy-start(bf16[1,256,2048]{2,1,0:T(8,128)(2,1)} %param.14) | copy-start | bytes 3145732
  504.2 18.3 %collective-permute-start.40 = (bf16[256,1536]{1,0:T(8,128)(2,1)S(1)}, bf16[256,1536]{1,0:T(8,128)(2,1)S(1)}, u32[]{:S(2)}, u32[]{:S(2)}) collective-permute-start(bf16[256,1536]{1,0:T(8,128)(2,1)S(1)} %copy-done.7), channel_id=1, source_target_pairs={{0,16},{8,24},{16,0},{24,8},{1,17},{9,25},{17,1},{25,9},{2,18},{10... | collective-permute-start | bytes 2359304 | tf_op jit(solution)/shard_map/ppermute | solution.py:64
  505.7 16.9 %collective-permute-start.39 = (bf16[256,1536]{1,0:T(8,128)(2,1)S(1)}, bf16[256,1536]{1,0:T(8,128)(2,1)S(1)}, u32[]{:S(2)}, u32[]{:S(2)}) collective-permute-start(bf16[256,1536]{1,0:T(8,128)(2,1)S(1)} %copy-done.7), channel_id=1, source_target_pairs={{0,8},{8,0},{16,24},{24,16},{1,9},{9,1},{17,25},{25,17},{2,10},{10... | collective-permute-start | bytes 2359304 | tf_op jit(solution)/shard_map/ppermute | solution.py:64
  508.2 14.3 %copy-start.17 = (f32[256,2048]{1,0:T(8,128)}, f32[256,2048]{1,0:T(8,128)S(1)}, u32[]{:S(2)}) copy-start(f32[256,2048]{1,0:T(8,128)S(1)} %convert_add_fusion.3) | copy-start | bytes 6291460
  508.9 1.3 collective-permute-start.36
  510.1 4.4 collective-permute-start.37
  514.5 8.0 %collective-permute-start.38 = (f32[4352]{0:T(1024)S(1)}, f32[4352]{0:T(1024)S(1)}, u32[]{:S(2)}, u32[]{:S(2)}) collective-permute-start(f32[4352]{0:T(1024)S(1)} %add.145), channel_id=1, source_target_pairs={{0,4},{1,5},{2,6},{3,7},{4,0},{5,1},{6,2},{7,3},{8,12},{9,13},{10,... | collective-permute-start | bytes 52232 | tf_op jit(solution)/shard_map/ppermute | solution.py:343
  522.7 10.2 %collective-permute-start.41 = (bf16[128,1536]{1,0:T(8,128)(2,1)S(1)}, bf16[128,1536]{1,0:T(8,128)(2,1)S(1)}, u32[]{:S(2)}, u32[]{:S(2)}) collective-permute-start(bf16[128,1536]{1,0:T(8,128)(2,1)S(1)} %slice.176), channel_id=1, source_target_pairs={{0,8},{8,0},{16,24},{24,16},{1,9},{9,1},{17,25},{25,17},{2,10},{10... | collective-permute-start | bytes 1179656 | tf_op jit(solution)/shard_map/ppermute | solution.py:64
  524.2 9.8 %collective-permute-start.42 = (bf16[128,1536]{1,0:T(8,128)(2,1)S(1)}, bf16[128,1536]{1,0:T(8,128)(2,1)S(1)}, u32[]{:S(2)}, u32[]{:S(2)}) collective-permute-start(bf16[128,1536]{1,0:T(8,128)(2,1)S(1)} %slice.177), channel_id=1, source_target_pairs={{0,16},{8,24},{16,0},{24,8},{1,17},{9,25},{17,1},{25,9},{2,18},{10... | collective-permute-start | bytes 1179656 | tf_op jit(solution)/shard_map/ppermute | solution.py:64
  534.0 4.1 collective-permute-start.43
  534.7 19.3 %collective-permute-start.46 = (bf16[256,1536]{1,0:T(8,128)(2,1)}, bf16[256,1536]{1,0:T(8,128)(2,1)S(1)}, u32[]{:S(2)}, u32[]{:S(2)}) collective-permute-start(bf16[256,1536]{1,0:T(8,128)(2,1)} %reduce-scatter.8.cloned.1.call-done.refs_0_), channel_id=1, source_target_pairs={{0,8},{8,0},{16,24},{24,16},{1,9},{9,1},{17,25},{25,17},{2,10},{10... | collective-permute-start | bytes 2359304 | tf_op jit(solution)/shard_map/ppermute | solution.py:64
  536.1 17.8 %collective-permute-start.45 = (bf16[256,1536]{1,0:T(8,128)(2,1)}, bf16[256,1536]{1,0:T(8,128)(2,1)S(1)}, u32[]{:S(2)}, u32[]{:S(2)}) collective-permute-start(bf16[256,1536]{1,0:T(8,128)(2,1)} %reduce-scatter.8.cloned.1.call-done.refs_0_), channel_id=1, source_target_pairs={{0,16},{8,24},{16,0},{24,8},{1,17},{9,25},{17,1},{25,9},{2,18},{10... | collective-permute-start | bytes 2359304 | tf_op jit(solution)/shard_map/ppermute | solution.py:64
  538.2 15.7 %collective-permute-start.44 = (f32[4352]{0:T(1024)S(1)}, f32[4352]{0:T(1024)S(1)}, u32[]{:S(2)}, u32[]{:S(2)}) collective-permute-start(f32[4352]{0:T(1024)S(1)} %add.147), channel_id=1, source_target_pairs={{0,16},{8,24},{16,0},{24,8},{1,17},{9,25},{17,1},{25,9},{2,18},{10... | collective-permute-start | bytes 52232 | tf_op jit(solution)/shard_map/ppermute | solution.py:343
  554.0 7.8 %collective-permute-start.47 = (bf16[128,1536]{1,0:T(8,128)(2,1)S(1)}, bf16[128,1536]{1,0:T(8,128)(2,1)S(1)}, u32[]{:S(2)}, u32[]{:S(2)}) collective-permute-start(bf16[128,1536]{1,0:T(8,128)(2,1)S(1)} %slice.179), channel_id=1, source_target_pairs={{0,8},{8,0},{16,24},{24,16},{1,9},{9,1},{17,25},{25,17},{2,10},{10... | collective-permute-start | bytes 1179656 | tf_op jit(solution)/shard_map/ppermute | solution.py:64
  554.3 7.8 %collective-permute-start.48 = (bf16[128,1536]{1,0:T(8,128)(2,1)S(1)}, bf16[128,1536]{1,0:T(8,128)(2,1)S(1)}, u32[]{:S(2)}, u32[]{:S(2)}) collective-permute-start(bf16[128,1536]{1,0:T(8,128)(2,1)S(1)} %slice.180), channel_id=1, source_target_pairs={{0,16},{8,24},{16,0},{24,8},{1,17},{9,25},{17,1},{25,9},{2,18},{10... | collective-permute-start | bytes 1179656 | tf_op jit(solution)/shard_map/ppermute | solution.py:64
  (39 other events, 141.6 us)
Sparse Core Ops, SparseCore 0:
  10.6 67.4 all-gather.3
  79.7 115.3 all-gather.5
  196.7 62.9 all-gather.7
  261.9 127.8 reduce-scatter.3
  392.5 68.1 reduce-scatter.5
  462.9 69.0 reduce-scatter.7

commit v6 on v5

--- a/solution.py
+++ b/solution.py
@@ -104,14 +104,16 @@
         self.tx, self.ty = swap(top, 1), swap(low, 2)
         return [self.tx, self.ty]
 
-    def second(self, slots):
+    def second(self, slots, *others):
         self.slots = slots
         if not self.square:
-            every = slots.reshape(-1, slots.shape[-1])
+            every = after(slots, *others).reshape(-1, slots.shape[-1])
             self.sum = lax.psum_scatter(every, "seq", scatter_dimension=0, tiled=True)
             self.sent = [every]
             return [self.sum]
         sx, sy = add_halves(slots, self.tx, self.ty)
+        if others:
+            sx, sy, *_ = lax.optimization_barrier((sx, sy, *others))
         self.sent = [sx, sy]
         self.rx, self.ry = swap(sx, 1), swap(sy, 2)
         return [self.rx, self.ry]
@@ -736,7 +738,7 @@
         get_drl.second()
         share2 = red2.total(*get_drl.sent)
         drl = get_drl.column()
-        halves = sum_out.second(after(out, drl))
+        halves = sum_out.second(out, drl)
         d_o = dot(drl, w_out).astype(BF16)
         dq, dk, dv, q_terms, k_terms = attend_back(
             qkv, tables, start, head_gains, after(d_o, *sum_out.sent), o, q_heads, kv_heads
@@ -770,7 +772,7 @@
         get2.first()
         gains = sum_all(gains, "fsdp", fsdp_count)
         mlp = place(get1.all(), (pieces[0],) * 3, 2, 0, 3, (), seq_count)
-        get2.second(gains, *mlp)
+        get2.second(*mlp)
         get3 = Gather(after(share3, *get2.arrived()), seq_count)
         get3.first()
         mlp = place(get2.all(), (pieces[1],) * 3, 1, 2, 3, mlp, seq_count)

time: 582 us -> 581 us (level)
  the two profiles are of different devices: /device:TPU:0 before, /device:TPU:8 now
where the time goes in v6:
time: 581 us; the launch traced here: 571 us
  waiting for transfers between devices  213 us (37%)
  Pallas kernels  194 us (33%)
  starting transfers between devices  51.8 us (9%)
  local copies, waits for them, and re-layouts  34.2 us (6%)
  other arithmetic  31.8 us (5%)
  matrix products  31.7 us (5%)
  between operations  15.3 us (3%)
    ppermute x44, waiting for transfers between devices, swap(): return lax.ppermute(x, 'seq', [(s, s ^ side) for s in range(4)])  194 us
    pallas_call x2, Pallas kernels, feed_forward(): pl.pallas_call(functools.partial(feed_forward_kernel, bool(sums), piece),...  57.9 us
    ppermute x44, starting transfers between devices, swap(): return lax.ppermute(x, 'seq', [(s, s ^ side) for s in range(4)])  46.4 us
    pallas_call x3, Pallas kernels, weight_terms(): pl.pallas_call(functools.partial(terms_kernel, starts, blocks, stride), g...  45.4 us
    pallas_call x8, Pallas kernels, put_rows(): pl.pallas_call(functools.partial(put_rows_kernel, len(pieces)), grid_spec...  30.7 us
    pallas_call x1, Pallas kernels, attend_back(): pl.pallas_call(functools.partial(attend_back_kernel, ratio), grid=(kv_hea...  19.3 us
    dot_general x3, matrix products, dot_nt(): lax.dot_general(a, b, (((1,), (1,)), ((), ())), preferred_element_type=F32)  16.2 us
    dot_general x2, matrix products, dot(): return jnp.dot(a, b, preferred_element_type=F32)  15.5 us
  transfers between devices with their start and end apart: 55, of which 36 were waited for; matrix products, arithmetic and copies ran while one was open for 15% of the time, Pallas kernels for 34%

profile of v6, /device:TPU:8, one launch (start us, length us, event | category | flops | bytes accessed | tf_op | source)
XLA Modules:
  0.0 571.2 jit_solution(16375707511903078090)
XLA Ops:
  20.8 21.4 %collective-permute-done.2.refs_1_ = bf16[256,2048]{1,0:T(8,128)(2,1)} collective-permute-done((bf16[256,2048]{1,0:T(8,128)(2,1)S(1)}, bf16[256,2048]{1,0:T(8,128)(2,1)}, u32[]{:S(2)}, u32[]{:S(2)}) %collective-permute-start.2) | collective-permute-done | bytes 1048608 | tf_op jit(solution)/shard_map/ppermute | solution.py:64
  42.2 1.9 slice.159
  45.6 1.9 slice.158
  51.3 4.7 put_rows.8.refs_2_
  56.0 8.7 %collective-permute-done.5.refs_1_ = bf16[256,2048]{1,0:T(8,128)(2,1)} collective-permute-done((bf16[256,2048]{1,0:T(8,128)(2,1)S(1)}, bf16[256,2048]{1,0:T(8,128)(2,1)}, u32[]{:S(2)}, u32[]{:S(2)}) %collective-permute-start.5) | collective-permute-done | bytes 1048608 | tf_op jit(solution)/shard_map/ppermute | solution.py:64
  64.7 1.9 slice.163
  66.6 1.9 slice.162
  68.5 7.5 %collective-permute-done.3.refs_1_ = bf16[128,2048]{1,0:T(8,128)(2,1)} collective-permute-done((bf16[128,2048]{1,0:T(8,128)(2,1)}, bf16[128,2048]{1,0:T(8,128)(2,1)}, u32[]{:S(2)}, u32[]{:S(2)}) %collective-permute-start.3) | collective-permute-done | bytes 524320 | tf_op jit(solution)/shard_map/ppermute | solution.py:64
  76.0 2.9 put_rows.9.refs_0_
  78.9 9.4 %fusion.24.q_ref.k_ref.v_ref = bf16[1024,1024]{1,0:T(8,128)(2,1)} fusion(bf16[1024,2048]{1,0:T(8,128)(2,1)} %put_rows.9.refs_0_, bf16[2048,1536]{1,0:T(8,128)(2,1)} %all-gather.4.cloned.1.call-done), kind=kOutput, calls=%fused_computation.40 | convolution fusion | flops 4296015872 | bytes 10485760 | tf_op jit(solution)/shard_map/dot_general | solution.py:21
  90.2 1.9 fusion.42
  94.3 4.7 put_rows.10.refs_2_
  99.0 12.7 %attend.1.o_ref = bf16[1024,512]{1,0:T(8,128)(2,1)} custom-call(bf16[1024,1024]{1,0:T(8,128)(2,1)} %fusion.24.q_ref.k_ref.v_ref, bf16[1024,1024]{1,0:T(8,128)(2,1)} %fusion.24.q_ref.k_ref.v_ref, bf16[1024,1024]{1,0:T(8,128)(2,1)} %fusion.24.q_ref.k_ref.v_ref, f32[1024,128]{1,0:T(8,128)} %get-tuple-element.169.cos_ref, ...), custom_call_target="tpu_custom_call" | custom-call | flops 1000 | bytes 1000 | tf_op jit(solution)/shard_map/attend/pallas_call | solution.py:502
  112.5 3.2 put_rows.11.dy_ref.refs_1_
  115.7 2.3 convolution_convert_fusion.2
  120.4 5.1 convolution_convert_fusion.1
  125.5 4.7 collective-permute-done.9.ty_ref
  131.3 3.3 add_halves.4
  137.5 19.6 %collective-permute-done.10 = bf16[256,2048]{1,0:T(8,128)(2,1)S(1)} collective-permute-done((bf16[256,2048]{1,0:T(8,128)(2,1)}, bf16[256,2048]{1,0:T(8,128)(2,1)S(1)}, u32[]{:S(2)}, u32[]{:S(2)}) %collective-permute-start.10) | collective-permute-done | bytes 1048608 | tf_op jit(solution)/shard_map/ppermute | solution.py:64
  158.2 1.9 multiply_reduce_fusion.2
  162.5 19.2 %collective-permute-done.14.refs_1_ = bf16[256,2048]{1,0:T(8,128)(2,1)S(1)} collective-permute-done((bf16[256,2048]{1,0:T(8,128)(2,1)S(1)}, bf16[256,2048]{1,0:T(8,128)(2,1)S(1)}, u32[]{:S(2)}, u32[]{:S(2)}) %collective-permute-start.14) | collective-permute-done | bytes 1048608 | tf_op jit(solution)/shard_map/ppermute | solution.py:64
  184.8 1.6 collective-permute-start.13
  187.0 4.6 put_rows.12.refs_2_
  191.6 1.8 collective-permute-done.15.refs_1_
  194.3 2.9 put_rows.13.xb_ref.refs_0_
  197.2 36.4 %feed_forward.2 = (bf16[1024,3072]{1,0:T(8,128)(2,1)}, f32[4,256,2048]{2,1,0:T(8,128)}, f32[4,256,2048]{2,1,0:T(8,128)}) custom-call(s32[4]{0:T(128)} %pad_add_fusion.2.order_ref, bf16[1024,2048]{1,0:T(8,128)(2,1)} %put_rows.13.xb_ref.refs_0_, bf16[1024,2048]{1,0:T(8,128)(2,1)} %put_rows.11.dy_ref.refs_1_, bf16[2048,3072]{1,0:T(8,128)(2,1)} %all-gather.6.cloned.1.call-done.w_ref), custom_call_target="tpu_custom_call" | custom-call | flops 1000 | bytes 1000 | tf_op jit(solution)/shard_map/feed_forward/pallas_call | solution.py:576
  233.5 20.3 %weight_terms.3 = bf16[2048,3072]{1,0:T(8,128)(2,1)} custom-call(s32[1]{0:T(128)} %constant.50.clone.1.parity_ref, bf16[1024,2048]{1,0:T(8,128)(2,1)} %put_rows.13.xb_ref.refs_0_, bf16[1024,2048]{1,0:T(8,128)(2,1)} %put_rows.11.dy_ref.refs_1_, bf16[1024,3072]{1,0:T(8,128)(2,1)} %get-tuple-element.78.refs_2_), custom_call_target="tpu_custom_call" | custom-call | flops 1000 | bytes 1000 | tf_op jit(solution)/shard_map/weight_terms/pallas_call | solution.py:294
  253.9 2.1 all-gather.8.cloned.1.call-done.w_ref
  256.0 21.5 %feed_forward.3 = (bf16[1024,1536]{1,0:T(8,128)(2,1)}, bf16[4,256,2048]{2,1,0:T(8,128)(2,1)}, bf16[4,256,2048]{2,1,0:T(8,128)(2,1)}) custom-call(s32[4]{0:T(128)} %pad_add_fusion.2.order_ref, bf16[1024,2048]{1,0:T(8,128)(2,1)} %put_rows.13.xb_ref.refs_0_, bf16[1024,2048]{1,0:T(8,128)(2,1)} %put_rows.11.dy_ref.refs_1_, ...), custom_call_target="tpu_custom_call" | custom-call | flops 1000 | bytes 1000 | tf_op jit(solution)/shard_map/feed_forward/pallas_call | solution.py:576
  278.8 1.6 collective-permute-start.19
  284.3 9.3 %collective-permute-done.19.ty_ref = bf16[128,2048]{1,0:T(8,128)(2,1)S(1)} collective-permute-done((bf16[128,2048]{1,0:T(8,128)(2,1)S(1)}, bf16[128,2048]{1,0:T(8,128)(2,1)S(1)}, u32[]{:S(2)}, u32[]{:S(2)}) %collective-permute-start.19) | collective-permute-done | bytes 524320 | tf_op jit(solution)/shard_map/ppermute | solution.py:64
  295.2 9.0 %collective-permute-done.17.ty_ref = bf16[128,2048]{1,0:T(8,128)(2,1)S(1)} collective-permute-done((bf16[128,2048]{1,0:T(8,128)(2,1)S(1)}, bf16[128,2048]{1,0:T(8,128)(2,1)S(1)}, u32[]{:S(2)}, u32[]{:S(2)}) %collective-permute-start.17) | collective-permute-done | bytes 524320 | tf_op jit(solution)/shard_map/ppermute | solution.py:64
  305.5 3.5 add_halves.6
  310.9 12.4 %weight_terms.4 = bf16[2048,1536]{1,0:T(8,128)(2,1)} custom-call(s32[1]{0:T(128)} %constant.50.clone.1.parity_ref, bf16[1024,2048]{1,0:T(8,128)(2,1)} %put_rows.13.xb_ref.refs_0_, bf16[1024,2048]{1,0:T(8,128)(2,1)} %put_rows.11.dy_ref.refs_1_, bf16[1024,1536]{1,0:T(8,128)(2,1)} %get-tuple-element.90.refs_2_), custom_call_target="tpu_custom_call" | custom-call | flops 1000 | bytes 1000 | tf_op jit(solution)/shard_map/weight_terms/pallas_call | solution.py:294
  323.3 10.2 %collective-permute-done.20 = bf16[256,2048]{1,0:T(8,128)(2,1)S(1)} collective-permute-done((bf16[256,2048]{1,0:T(8,128)(2,1)}, bf16[256,2048]{1,0:T(8,128)(2,1)S(1)}, u32[]{:S(2)}, u32[]{:S(2)}) %collective-permute-start.20) | collective-permute-done | bytes 1048608 | tf_op jit(solution)/shard_map/ppermute | solution.py:64
  334.7 2.1 fusion.22
  341.2 21.4 %collective-permute-done.24.refs_1_ = bf16[256,2048]{1,0:T(8,128)(2,1)S(1)} collective-permute-done((bf16[256,2048]{1,0:T(8,128)(2,1)S(1)}, bf16[256,2048]{1,0:T(8,128)(2,1)S(1)}, u32[]{:S(2)}, u32[]{:S(2)}) %collective-permute-start.24) | collective-permute-done | bytes 1048608 | tf_op jit(solution)/shard_map/ppermute | solution.py:64
  366.5 3.3 add_halves.5
  369.8 4.8 put_rows.14.refs_2_
  377.5 2.9 put_rows.15.refs_1_
  382.1 6.2 %fusion.31.do_ref = bf16[1024,512]{1,0:T(8,128)(2,1)} fusion(bf16[1024,2048]{1,0:T(8,128)(2,1)} %put_rows.15.refs_1_, bf16[2048,1536]{1,0:T(8,128)(2,1)} %all-gather.4.cloned.1.call-done), kind=kOutput, calls=%fused_computation.46 | convolution fusion | flops 2148007936 | bytes 7340032 | tf_op jit(solution)/shard_map/dot_general | solution.py:21
  388.2 19.3 %attend_back.1 = (bf16[1024,512]{1,0:T(8,128)(2,1)}, bf16[1024,256]{1,0:T(8,128)(2,1)}, bf16[1024,256]{1,0:T(8,128)(2,1)}, f32[2,1,128]{2,1,0:T(1,128)}, f32[2,1,128]{2,1,0:T(1,128)}) custom-call(bf16[1024,1024]{1,0:T(8,128)(2,1)} %fusion.24.q_ref.k_ref.v_ref, bf16[1024,1024]{1,0:T(8,128)(2,1)} %fusion.24.q_ref.k_ref.v_ref, ...), custom_call_target="tpu_custom_call" | custom-call | flops 1000 | bytes 1000 | tf_op jit(solution)/shard_map/attend_back/pallas_call | solution.py:520
  411.3 3.2 pad_maximum_fusion.refs_2_
  414.5 12.8 %weight_terms.5 = bf16[2048,1536]{1,0:T(8,128)(2,1)} custom-call(s32[1]{0:T(128)} %constant.50.clone.1.parity_ref, bf16[1024,2048]{1,0:T(8,128)(2,1)} %put_rows.9.refs_0_, bf16[1024,2048]{1,0:T(8,128)(2,1)} %put_rows.15.refs_1_, bf16[1024,1536]{1,0:T(8,128)(2,1)} %pad_maximum_fusion.refs_2_), custom_call_target="tpu_custom_call" | custom-call | flops 1000 | bytes 1000 | tf_op jit(solution)/shard_map/weight_terms/pallas_call | solution.py:294
  429.0 8.7 %convolution_convert_fusion = bf16[1024,2048]{1,0:T(8,128)(2,1)S(1)} fusion(bf16[2048,1536]{1,0:T(8,128)(2,1)} %all-gather.4.cloned.1.call-done, bf16[256,1024]{1,0:T(8,128)(2,1)S(1)} %get-tuple-element.148, bf16[256,1024]{1,0:T(8,128)(2,1)S(1)} %get-tuple-element.149, bf16[256,1024]{1,0:T(8,128)(2,1)S(1)} %get-tuple-element.150, ...), kind=kOutput, calls=%fused_computation | convolution fusion | flops 4305453056 | bytes 10485760 | tf_op jit(solution)/shard_map/dot_general | solution.py:25
  437.8 3.6 collective-permute-done.29.refs_2_
  446.8 9.6 %reduce-scatter.6.cloned.1.call-done.refs_0_ = bf16[256,1536]{1,0:T(8,128)(2,1)} async-done(((bf16[2048,1536]{1,0:T(8,128)(2,1)}), bf16[256,1536]{1,0:T(8,128)(2,1)}) %reduce-scatter.6.cloned.1.call-update) | async-done | bytes 786448 | tf_op jit(solution)/shard_map/reduce_scatter | solution.py:335
  456.4 1.6 collective-permute-start.34
  459.5 3.3 add_halves.7
  463.9 13.1 %collective-permute-done.34 = bf16[128,3072]{1,0:T(8,128)(2,1)} collective-permute-done((bf16[128,3072]{1,0:T(8,128)(2,1)}, bf16[128,3072]{1,0:T(8,128)(2,1)}, u32[]{:S(2)}, u32[]{:S(2)}) %collective-permute-start.34) | collective-permute-done | bytes 786464 | tf_op jit(solution)/shard_map/ppermute | solution.py:64
  479.9 19.5 %collective-permute-done.32 = bf16[256,2048]{1,0:T(8,128)(2,1)} collective-permute-done((bf16[256,2048]{1,0:T(8,128)(2,1)}, bf16[256,2048]{1,0:T(8,128)(2,1)}, u32[]{:S(2)}, u32[]{:S(2)}) %collective-permute-start.32) | collective-permute-done | bytes 1048608 | tf_op jit(solution)/shard_map/ppermute | solution.py:64
  499.4 1.6 collective-permute-done.33
  503.1 2.4 convert_add_fusion.3
  508.3 6.4 %place.4 = (f32[256,6144]{1,0:T(8,128)}, f32[256,6144]{1,0:T(8,128)}, f32[256,6144]{1,0:T(8,128)}) custom-call(s32[4]{0:T(128)S(1)} %copy-done.11, bf16[256,3072]{1,0:T(8,128)(2,1)S(1)} %copy-done.6, bf16[256,3072]{1,0:T(8,128)(2,1)S(1)} %collective-permute-done.28.refs_1_, bf16[256,3072]{1,0:T(8,128)(2,1)S(1)} %collective-permute-done.29.refs_2_, ...), custom_call_target="tpu_custom_call" | custom-call | flops 1000 | bytes 1000 | tf_op jit(solution)/shard_map/place/pallas_call | solution.py:624
  514.7 2.2 collective-permute-start.38
  516.9 3.6 collective-permute-done.40.refs_2_
  523.0 3.2 fusion.23
  526.2 5.6 collective-permute-done.41
  536.9 6.5 %fusion.35 = (bf16[1,256,2048]{2,1,0:T(8,128)(2,1)}, bf16[1,256,2048]{2,1,0:T(8,128)(2,1)}) fusion(f32[256,2048]{1,0:T(8,128)} %copy-done.17, bf16[1,256,2048]{2,1,0:T(8,128)(2,1)} %param.14, f32[256]{0:T(256)S(1)} %broadcast_multiply_fusion, f32[2048]{0:T(1024)S(1)} %copy-done.44, f32[256]{0:T(256)S(1)} %add_rsqrt_fusion.1, ...), kind=kLoop, calls=%fused_computation.48 | loop fusion | flops 8912896 | bytes 12603392 | tf_op jit(solution)/shard_map/broadcast_in_dim | solution.py:788
  543.5 3.6 place.5
  547.1 4.3 collective-permute-done.44
  551.5 2.1 collective-permute-start.47
  555.4 3.1 place.6
  559.4 2.0 collective-permute-done.48.refs_1_
  (253 shorter events, 95.9 us)
Async XLA Ops:
  7.2 71.7 %all-gather.4.cloned.1.call-start = ((), (), s32[]{:S(2)}) async-start(), calls=%async_computation.3 | async-start | bytes 7077888 | tf_op jit(solution)/shard_map/all_gather | solution.py:258
  10.4 186.7 %all-gather.6.cloned.1.call-start = ((), (), s32[]{:S(2)}) async-start(), calls=%async_computation.4 | async-start | bytes 14155776 | tf_op jit(solution)/shard_map/all_gather | solution.py:258
  13.1 242.9 %all-gather.8.cloned.1.call-start = ((), (), s32[]{:S(2)}) async-start(), calls=%async_computation.5 | async-start | bytes 7077888 | tf_op jit(solution)/shard_map/all_gather | solution.py:258
  15.3 393.6 %reduce-scatter.4.cloned.1.call-start = ((), (), s32[]{:S(2)}) async-start(), calls=%async_computation.6 | async-start | bytes 14155776 | tf_op jit(solution)/shard_map/reduce_scatter | solution.py:335
  16.0 35.3 %copy-start.22 = (bf16[256,2048]{1,0:T(8,128)(2,1)}, bf16[256,2048]{1,0:T(8,128)(2,1)S(1)}, u32[]{:S(2)}) copy-start(bf16[256,2048]{1,0:T(8,128)(2,1)S(1)} %fusion.7.refs_0_) | copy-start | bytes 3145732
  16.0 26.2 %collective-permute-start.2 = (bf16[256,2048]{1,0:T(8,128)(2,1)S(1)}, bf16[256,2048]{1,0:T(8,128)(2,1)}, u32[]{:S(2)}, u32[]{:S(2)}) collective-permute-start(bf16[256,2048]{1,0:T(8,128)(2,1)S(1)} %fusion.7.refs_0_), channel_id=1, source_target_pairs={{0,8},{8,0},{16,24},{24,16},{1,9},{9,1},{17,25},{25,17},{2,10},{10... | collective-permute-start | bytes 3145736 | tf_op jit(solution)/shard_map/ppermute | solution.py:64
  17.6 28.1 %collective-permute-start = (bf16[256,2048]{1,0:T(8,128)(2,1)S(1)}, bf16[256,2048]{1,0:T(8,128)(2,1)}, u32[]{:S(2)}, u32[]{:S(2)}) collective-permute-start(bf16[256,2048]{1,0:T(8,128)(2,1)S(1)} %fusion.7.refs_0_), channel_id=1, source_target_pairs={{0,16},{8,24},{16,0},{24,8},{1,17},{9,25},{17,1},{25,9},{2,18},{10... | collective-permute-start | bytes 3145736 | tf_op jit(solution)/shard_map/ppermute | solution.py:64
  19.1 45.6 %collective-permute-start.5 = (bf16[256,2048]{1,0:T(8,128)(2,1)S(1)}, bf16[256,2048]{1,0:T(8,128)(2,1)}, u32[]{:S(2)}, u32[]{:S(2)}) collective-permute-start(bf16[256,2048]{1,0:T(8,128)(2,1)S(1)} %bitcast.59), channel_id=1, source_target_pairs={{0,8},{8,0},{16,24},{24,16},{1,9},{9,1},{17,25},{25,17},{2,10},{10... | collective-permute-start | bytes 3145736 | tf_op jit(solution)/shard_map/ppermute | solution.py:64
  19.6 47.0 %collective-permute-start.4 = (bf16[256,2048]{1,0:T(8,128)(2,1)S(1)}, bf16[256,2048]{1,0:T(8,128)(2,1)}, u32[]{:S(2)}, u32[]{:S(2)}) collective-permute-start(bf16[256,2048]{1,0:T(8,128)(2,1)S(1)} %bitcast.60), channel_id=1, source_target_pairs={{0,16},{8,24},{16,0},{24,8},{1,17},{9,25},{17,1},{25,9},{2,18},{10... | collective-permute-start | bytes 3145736 | tf_op jit(solution)/shard_map/ppermute | solution.py:64
  44.1 31.9 %collective-permute-start.3 = (bf16[128,2048]{1,0:T(8,128)(2,1)}, bf16[128,2048]{1,0:T(8,128)(2,1)}, u32[]{:S(2)}, u32[]{:S(2)}) collective-permute-start(bf16[128,2048]{1,0:T(8,128)(2,1)} %slice.159), channel_id=1, source_target_pairs={{0,16},{8,24},{16,0},{24,8},{1,17},{9,25},{17,1},{25,9},{2,18},{10... | collective-permute-start | bytes 1572872 | tf_op jit(solution)/shard_map/ppermute | solution.py:64
  47.5 28.5 %collective-permute-start.1 = (bf16[128,2048]{1,0:T(8,128)(2,1)}, bf16[128,2048]{1,0:T(8,128)(2,1)}, u32[]{:S(2)}, u32[]{:S(2)}) collective-permute-start(bf16[128,2048]{1,0:T(8,128)(2,1)} %slice.158), channel_id=1, source_target_pairs={{0,8},{8,0},{16,24},{24,16},{1,9},{9,1},{17,25},{25,17},{2,10},{10... | collective-permute-start | bytes 1572872 | tf_op jit(solution)/shard_map/ppermute | solution.py:64
  88.3 23.4 %collective-permute-start.6 = (bf16[128,2048]{1,0:T(8,128)(2,1)}, bf16[128,2048]{1,0:T(8,128)(2,1)S(1)}, u32[]{:S(2)}, u32[]{:S(2)}) collective-permute-start(bf16[128,2048]{1,0:T(8,128)(2,1)} %slice.162), channel_id=1, source_target_pairs={{0,8},{8,0},{16,24},{24,16},{1,9},{9,1},{17,25},{25,17},{2,10},{10... | collective-permute-start | bytes 1572872 | tf_op jit(solution)/shard_map/ppermute | solution.py:64
  88.7 23.0 %collective-permute-start.7 = (bf16[128,2048]{1,0:T(8,128)(2,1)}, bf16[128,2048]{1,0:T(8,128)(2,1)}, u32[]{:S(2)}, u32[]{:S(2)}) collective-permute-start(bf16[128,2048]{1,0:T(8,128)(2,1)} %slice.163), channel_id=1, source_target_pairs={{0,16},{8,24},{16,0},{24,8},{1,17},{9,25},{17,1},{25,9},{2,18},{10... | collective-permute-start | bytes 1572872 | tf_op jit(solution)/shard_map/ppermute | solution.py:64
  118.1 12.1 %collective-permute-start.9 = (bf16[128,2048]{1,0:T(8,128)(2,1)S(1)}, bf16[128,2048]{1,0:T(8,128)(2,1)S(1)}, u32[]{:S(2)}, u32[]{:S(2)}) collective-permute-start(bf16[128,2048]{1,0:T(8,128)(2,1)S(1)} %get-tuple-element.153), channel_id=1, source_target_pairs={{0,16},{8,24},{16,0},{24,8},{1,17},{9,25},{17,1},{25,9},{2,18},{10... | collective-permute-start | bytes 1572872 | tf_op jit(solution)/shard_map/ppermute | solution.py:64
  118.7 11.7 %collective-permute-start.8 = (bf16[128,2048]{1,0:T(8,128)(2,1)S(1)}, bf16[128,2048]{1,0:T(8,128)(2,1)S(1)}, u32[]{:S(2)}, u32[]{:S(2)}) collective-permute-start(bf16[128,2048]{1,0:T(8,128)(2,1)S(1)} %get-tuple-element.154), channel_id=1, source_target_pairs={{0,8},{8,0},{16,24},{24,16},{1,9},{9,1},{17,25},{25,17},{2,10},{10... | collective-permute-start | bytes 1572872 | tf_op jit(solution)/shard_map/ppermute | solution.py:64
  134.6 22.6 %collective-permute-start.10 = (bf16[256,2048]{1,0:T(8,128)(2,1)}, bf16[256,2048]{1,0:T(8,128)(2,1)S(1)}, u32[]{:S(2)}, u32[]{:S(2)}) collective-permute-start(bf16[256,2048]{1,0:T(8,128)(2,1)} %get-tuple-element.76), channel_id=1, source_target_pairs={{0,8},{8,0},{16,24},{24,16},{1,9},{9,1},{17,25},{25,17},{2,10},{10... | collective-permute-start | bytes 3145736 | tf_op jit(solution)/shard_map/ppermute | solution.py:64
  136.0 24.1 %copy-start.43 = (f32[2048]{0:T(1024)S(1)}, f32[2048]{0:T(1024)}, u32[]{:S(2)}) copy-start(f32[2048]{0:T(1024)} %param.23) | copy-start | bytes 24580
  136.0 22.2 %collective-permute-start.11 = (bf16[256,2048]{1,0:T(8,128)(2,1)}, bf16[256,2048]{1,0:T(8,128)(2,1)S(1)}, u32[]{:S(2)}, u32[]{:S(2)}) collective-permute-start(bf16[256,2048]{1,0:T(8,128)(2,1)} %get-tuple-element.77), channel_id=1, source_target_pairs={{0,16},{8,24},{16,0},{24,8},{1,17},{9,25},{17,1},{25,9},{2,18},{10... | collective-permute-start | bytes 3145736 | tf_op jit(solution)/shard_map/ppermute | solution.py:64
  160.1 177.4 %copy-start.12 = (f32[256,2048]{1,0:T(8,128)}, f32[256,2048]{1,0:T(8,128)S(1)}, u32[]{:S(2)}) copy-start(f32[256,2048]{1,0:T(8,128)S(1)} %get-tuple-element.138) | copy-start | bytes 6291460
  160.4 26.6 %copy-start.21 = (bf16[256,2048]{1,0:T(8,128)(2,1)}, bf16[256,2048]{1,0:T(8,128)(2,1)S(1)}, u32[]{:S(2)}) copy-start(bf16[256,2048]{1,0:T(8,128)(2,1)S(1)} %multiply_convert_fusion.refs_0_) | copy-start | bytes 3145732
  160.4 21.2 %collective-permute-start.14 = (bf16[256,2048]{1,0:T(8,128)(2,1)S(1)}, bf16[256,2048]{1,0:T(8,128)(2,1)S(1)}, u32[]{:S(2)}, u32[]{:S(2)}) collective-permute-start(bf16[256,2048]{1,0:T(8,128)(2,1)S(1)} %multiply_convert_fusion.refs_0_), channel_id=1, source_target_pairs={{0,8},{8,0},{16,24},{24,16},{1,9},{9,1},{17,25},{25,17},{2,10},{10... | collective-permute-start | bytes 3145736 | tf_op jit(solution)/shard_map/ppermute | solution.py:64
  161.2 22.4 %collective-permute-start.12 = (bf16[256,2048]{1,0:T(8,128)(2,1)S(1)}, bf16[256,2048]{1,0:T(8,128)(2,1)S(1)}, u32[]{:S(2)}, u32[]{:S(2)}) collective-permute-start(bf16[256,2048]{1,0:T(8,128)(2,1)S(1)} %multiply_convert_fusion.refs_0_), channel_id=1, source_target_pairs={{0,16},{8,24},{16,0},{24,8},{1,17},{9,25},{17,1},{25,9},{2,18},{10... | collective-permute-start | bytes 3145736 | tf_op jit(solution)/shard_map/ppermute | solution.py:64
  182.5 10.9 %collective-permute-start.15 = (bf16[128,2048]{1,0:T(8,128)(2,1)}, bf16[128,2048]{1,0:T(8,128)(2,1)S(1)}, u32[]{:S(2)}, u32[]{:S(2)}) collective-permute-start(bf16[128,2048]{1,0:T(8,128)(2,1)} %slice.169), channel_id=1, source_target_pairs={{0,16},{8,24},{16,0},{24,8},{1,17},{9,25},{17,1},{25,9},{2,18},{10... | collective-permute-start | bytes 1572872 | tf_op jit(solution)/shard_map/ppermute | solution.py:64
  184.8 9.5 %collective-permute-start.13 = (bf16[128,2048]{1,0:T(8,128)(2,1)}, bf16[128,2048]{1,0:T(8,128)(2,1)}, u32[]{:S(2)}, u32[]{:S(2)}) collective-permute-start(bf16[128,2048]{1,0:T(8,128)(2,1)} %slice.168), channel_id=1, source_target_pairs={{0,8},{8,0},{16,24},{24,16},{1,9},{9,1},{17,25},{25,17},{2,10},{10... | collective-permute-start | bytes 1572872 | tf_op jit(solution)/shard_map/ppermute | solution.py:64
  253.8 202.5 %reduce-scatter.6.cloned.1.call-start = ((), (), s32[]{:S(2)}) async-start(), calls=%async_computation.7 | async-start | bytes 7077888 | tf_op jit(solution)/shard_map/reduce_scatter | solution.py:335
  278.8 14.8 %collective-permute-start.19 = (bf16[128,2048]{1,0:T(8,128)(2,1)S(1)}, bf16[128,2048]{1,0:T(8,128)(2,1)S(1)}, u32[]{:S(2)}, u32[]{:S(2)}) collective-permute-start(bf16[128,2048]{1,0:T(8,128)(2,1)S(1)} %get-tuple-element.141), channel_id=1, source_target_pairs={{0,16},{8,24},{16,0},{24,8},{1,17},{9,25},{17,1},{25,9},{2,18},{10... | collective-permute-start | bytes 1572872 | tf_op jit(solution)/shard_map/ppermute | solution.py:64
  280.4 14.8 %collective-permute-start.18 = (bf16[128,2048]{1,0:T(8,128)(2,1)S(1)}, bf16[128,2048]{1,0:T(8,128)(2,1)S(1)}, u32[]{:S(2)}, u32[]{:S(2)}) collective-permute-start(bf16[128,2048]{1,0:T(8,128)(2,1)S(1)} %get-tuple-element.142), channel_id=1, source_target_pairs={{0,8},{8,0},{16,24},{24,16},{1,9},{9,1},{17,25},{25,17},{2,10},{10... | collective-permute-start | bytes 1572872 | tf_op jit(solution)/shard_map/ppermute | solution.py:64
  283.1 21.1 %collective-permute-start.17 = (bf16[128,2048]{1,0:T(8,128)(2,1)S(1)}, bf16[128,2048]{1,0:T(8,128)(2,1)S(1)}, u32[]{:S(2)}, u32[]{:S(2)}) collective-permute-start(bf16[128,2048]{1,0:T(8,128)(2,1)S(1)} %get-tuple-element.143), channel_id=1, source_target_pairs={{0,16},{8,24},{16,0},{24,8},{1,17},{9,25},{17,1},{25,9},{2,18},{10... | collective-permute-start | bytes 1572872 | tf_op jit(solution)/shard_map/ppermute | solution.py:64
  283.7 21.8 %collective-permute-start.16 = (bf16[128,2048]{1,0:T(8,128)(2,1)S(1)}, bf16[128,2048]{1,0:T(8,128)(2,1)S(1)}, u32[]{:S(2)}, u32[]{:S(2)}) collective-permute-start(bf16[128,2048]{1,0:T(8,128)(2,1)S(1)} %get-tuple-element.144), channel_id=1, source_target_pairs={{0,8},{8,0},{16,24},{24,16},{1,9},{9,1},{17,25},{25,17},{2,10},{10... | collective-permute-start | bytes 1572872 | tf_op jit(solution)/shard_map/ppermute | solution.py:64
  293.6 11.8 %copy-start.37 = (bf16[128,2048]{1,0:T(8,128)(2,1)}, bf16[128,2048]{1,0:T(8,128)(2,1)S(1)}, u32[]{:S(2)}) copy-start(bf16[128,2048]{1,0:T(8,128)(2,1)S(1)} %collective-permute-done.19.ty_ref) | copy-start | bytes 1572868
  309.0 24.5 %collective-permute-start.20 = (bf16[256,2048]{1,0:T(8,128)(2,1)}, bf16[256,2048]{1,0:T(8,128)(2,1)S(1)}, u32[]{:S(2)}, u32[]{:S(2)}) collective-permute-start(bf16[256,2048]{1,0:T(8,128)(2,1)} %get-tuple-element.87), channel_id=1, source_target_pairs={{0,8},{8,0},{16,24},{24,16},{1,9},{9,1},{17,25},{25,17},{2,10},{10... | collective-permute-start | bytes 3145736 | tf_op jit(solution)/shard_map/ppermute | solution.py:64
  310.4 24.3 %collective-permute-start.21 = (bf16[256,2048]{1,0:T(8,128)(2,1)}, bf16[256,2048]{1,0:T(8,128)(2,1)}, u32[]{:S(2)}, u32[]{:S(2)}) collective-permute-start(bf16[256,2048]{1,0:T(8,128)(2,1)} %get-tuple-element.88), channel_id=1, source_target_pairs={{0,16},{8,24},{16,0},{24,8},{1,17},{9,25},{17,1},{25,9},{2,18},{10... | collective-permute-start | bytes 3145736 | tf_op jit(solution)/shard_map/ppermute | solution.py:64
  339.5 23.2 %collective-permute-start.24 = (bf16[256,2048]{1,0:T(8,128)(2,1)S(1)}, bf16[256,2048]{1,0:T(8,128)(2,1)S(1)}, u32[]{:S(2)}, u32[]{:S(2)}) collective-permute-start(bf16[256,2048]{1,0:T(8,128)(2,1)S(1)} %fusion.48.refs_0_), channel_id=1, source_target_pairs={{0,8},{8,0},{16,24},{24,16},{1,9},{9,1},{17,25},{25,17},{2,10},{10... | collective-permute-start | bytes 3145736 | tf_op jit(solution)/shard_map/ppermute | solution.py:64
  340.4 23.1 %collective-permute-start.22 = (bf16[256,2048]{1,0:T(8,128)(2,1)S(1)}, bf16[256,2048]{1,0:T(8,128)(2,1)S(1)}, u32[]{:S(2)}, u32[]{:S(2)}) collective-permute-start(bf16[256,2048]{1,0:T(8,128)(2,1)S(1)} %fusion.48.refs_0_), channel_id=1, source_target_pairs={{0,16},{8,24},{16,0},{24,8},{1,17},{9,25},{17,1},{25,9},{2,18},{10... | collective-permute-start | bytes 3145736 | tf_op jit(solution)/shard_map/ppermute | solution.py:64
  364.5 169.1 %reduce-scatter.8.cloned.1.call-start = ((), (), s32[]{:S(2)}) async-start(), calls=%async_computation.8 | async-start | bytes 7077888 | tf_op jit(solution)/shard_map/reduce_scatter | solution.py:335
  364.5 11.1 %collective-permute-start.25 = (bf16[128,2048]{1,0:T(8,128)(2,1)S(1)}, bf16[128,2048]{1,0:T(8,128)(2,1)S(1)}, u32[]{:S(2)}, u32[]{:S(2)}) collective-permute-start(bf16[128,2048]{1,0:T(8,128)(2,1)S(1)} %slice.171), channel_id=1, source_target_pairs={{0,16},{8,24},{16,0},{24,8},{1,17},{9,25},{17,1},{25,9},{2,18},{10... | collective-permute-start | bytes 1572872 | tf_op jit(solution)/shard_map/ppermute | solution.py:64
  365.6 11.1 %collective-permute-start.23 = (bf16[128,2048]{1,0:T(8,128)(2,1)S(1)}, bf16[128,2048]{1,0:T(8,128)(2,1)S(1)}, u32[]{:S(2)}, u32[]{:S(2)}) collective-permute-start(bf16[128,2048]{1,0:T(8,128)(2,1)S(1)} %slice.170), channel_id=1, source_target_pairs={{0,8},{8,0},{16,24},{24,16},{1,9},{9,1},{17,25},{25,17},{2,10},{10... | collective-permute-start | bytes 1572872 | tf_op jit(solution)/shard_map/ppermute | solution.py:64
  380.4 27.1 %collective-permute-start.26 = (bf16[256,2048]{1,0:T(8,128)(2,1)}, bf16[256,2048]{1,0:T(8,128)(2,1)S(1)}, u32[]{:S(2)}, u32[]{:S(2)}) collective-permute-start(bf16[256,2048]{1,0:T(8,128)(2,1)} %get-tuple-element.92), channel_id=1, source_target_pairs={{0,8},{8,0},{16,24},{24,16},{1,9},{9,1},{17,25},{25,17},{2,10},{10... | collective-permute-start | bytes 3145736 | tf_op jit(solution)/shard_map/ppermute | solution.py:64
  381.0 26.6 %collective-permute-start.27 = (bf16[256,2048]{1,0:T(8,128)(2,1)}, bf16[256,2048]{1,0:T(8,128)(2,1)S(1)}, u32[]{:S(2)}, u32[]{:S(2)}) collective-permute-start(bf16[256,2048]{1,0:T(8,128)(2,1)} %get-tuple-element.93), channel_id=1, source_target_pairs={{0,16},{8,24},{16,0},{24,8},{1,17},{9,25},{17,1},{25,9},{2,18},{10... | collective-permute-start | bytes 3145736 | tf_op jit(solution)/shard_map/ppermute | solution.py:64
  408.9 32.5 %collective-permute-start.29 = (bf16[256,3072]{1,0:T(8,128)(2,1)}, bf16[256,3072]{1,0:T(8,128)(2,1)S(1)}, u32[]{:S(2)}, u32[]{:S(2)}) collective-permute-start(bf16[256,3072]{1,0:T(8,128)(2,1)} %reduce-scatter.4.cloned.1.call-done.refs_0_), channel_id=1, source_target_pairs={{0,16},{8,24},{16,0},{24,8},{1,17},{9,25},{17,1},{25,9},{2,18},{10... | collective-permute-start | bytes 4718600 | tf_op jit(solution)/shard_map/ppermute | solution.py:64
  409.9 32.5 %collective-permute-start.28 = (bf16[256,3072]{1,0:T(8,128)(2,1)}, bf16[256,3072]{1,0:T(8,128)(2,1)S(1)}, u32[]{:S(2)}, u32[]{:S(2)}) collective-permute-start(bf16[256,3072]{1,0:T(8,128)(2,1)} %reduce-scatter.4.cloned.1.call-done.refs_0_), channel_id=1, source_target_pairs={{0,8},{8,0},{16,24},{24,16},{1,9},{9,1},{17,25},{25,17},{2,10},{10... | collective-permute-start | bytes 4718600 | tf_op jit(solution)/shard_map/ppermute | solution.py:64
  444.3 12.1 %collective-permute-start.31 = (bf16[128,2048]{1,0:T(8,128)(2,1)}, bf16[128,2048]{1,0:T(8,128)(2,1)}, u32[]{:S(2)}, u32[]{:S(2)}) collective-permute-start(bf16[128,2048]{1,0:T(8,128)(2,1)} %get-tuple-element.151), channel_id=1, source_target_pairs={{0,16},{8,24},{16,0},{24,8},{1,17},{9,25},{17,1},{25,9},{2,18},{10... | collective-permute-start | bytes 1572872 | tf_op jit(solution)/shard_map/ppermute | solution.py:64
  445.2 11.2 %collective-permute-start.30 = (bf16[128,2048]{1,0:T(8,128)(2,1)}, bf16[128,2048]{1,0:T(8,128)(2,1)}, u32[]{:S(2)}, u32[]{:S(2)}) collective-permute-start(bf16[128,2048]{1,0:T(8,128)(2,1)} %get-tuple-element.152), channel_id=1, source_target_pairs={{0,8},{8,0},{16,24},{24,16},{1,9},{9,1},{17,25},{25,17},{2,10},{10... | collective-permute-start | bytes 1572872 | tf_op jit(solution)/shard_map/ppermute | solution.py:64
  456.4 20.6 %collective-permute-start.34 = (bf16[128,3072]{1,0:T(8,128)(2,1)}, bf16[128,3072]{1,0:T(8,128)(2,1)}, u32[]{:S(2)}, u32[]{:S(2)}) collective-permute-start(bf16[128,3072]{1,0:T(8,128)(2,1)} %slice.173), channel_id=1, source_target_pairs={{0,8},{8,0},{16,24},{24,16},{1,9},{9,1},{17,25},{25,17},{2,10},{10... | collective-permute-start | bytes 2359304 | tf_op jit(solution)/shard_map/ppermute | solution.py:64
  458.0 20.7 %collective-permute-start.35 = (bf16[128,3072]{1,0:T(8,128)(2,1)}, bf16[128,3072]{1,0:T(8,128)(2,1)}, u32[]{:S(2)}, u32[]{:S(2)}) collective-permute-start(bf16[128,3072]{1,0:T(8,128)(2,1)} %slice.174), channel_id=1, source_target_pairs={{0,16},{8,24},{16,0},{24,8},{1,17},{9,25},{17,1},{25,9},{2,18},{10... | collective-permute-start | bytes 2359304 | tf_op jit(solution)/shard_map/ppermute | solution.py:64
  462.8 36.6 %collective-permute-start.32 = (bf16[256,2048]{1,0:T(8,128)(2,1)}, bf16[256,2048]{1,0:T(8,128)(2,1)}, u32[]{:S(2)}, u32[]{:S(2)}) collective-permute-start(bf16[256,2048]{1,0:T(8,128)(2,1)} %get-tuple-element.103), channel_id=1, source_target_pairs={{0,8},{8,0},{16,24},{24,16},{1,9},{9,1},{17,25},{25,17},{2,10},{10... | collective-permute-start | bytes 3145736 | tf_op jit(solution)/shard_map/ppermute | solution.py:64
  463.4 37.7 %collective-permute-start.33 = (bf16[256,2048]{1,0:T(8,128)(2,1)}, bf16[256,2048]{1,0:T(8,128)(2,1)}, u32[]{:S(2)}, u32[]{:S(2)}) collective-permute-start(bf16[256,2048]{1,0:T(8,128)(2,1)} %get-tuple-element.104), channel_id=1, source_target_pairs={{0,16},{8,24},{16,0},{24,8},{1,17},{9,25},{17,1},{25,9},{2,18},{10... | collective-permute-start | bytes 3145736 | tf_op jit(solution)/shard_map/ppermute | solution.py:64
  463.9 37.2 %copy-start.7 = (bf16[256,1536]{1,0:T(8,128)(2,1)S(1)}, bf16[256,1536]{1,0:T(8,128)(2,1)}, u32[]{:S(2)}) copy-start(bf16[256,1536]{1,0:T(8,128)(2,1)} %reduce-scatter.6.cloned.1.call-done.refs_0_) | copy-start | bytes 2359300
  479.9 25.6 %copy-start.16 = (bf16[1,256,2048]{2,1,0:T(8,128)(2,1)S(1)}, bf16[1,256,2048]{2,1,0:T(8,128)(2,1)}, u32[]{:S(2)}) copy-start(bf16[1,256,2048]{2,1,0:T(8,128)(2,1)} %param.14) | copy-start | bytes 3145732
  501.1 19.4 %collective-permute-start.40 = (bf16[256,1536]{1,0:T(8,128)(2,1)S(1)}, bf16[256,1536]{1,0:T(8,128)(2,1)S(1)}, u32[]{:S(2)}, u32[]{:S(2)}) collective-permute-start(bf16[256,1536]{1,0:T(8,128)(2,1)S(1)} %copy-done.7), channel_id=1, source_target_pairs={{0,16},{8,24},{16,0},{24,8},{1,17},{9,25},{17,1},{25,9},{2,18},{10... | collective-permute-start | bytes 2359304 | tf_op jit(solution)/shard_map/ppermute | solution.py:64
  502.5 19.2 %collective-permute-start.39 = (bf16[256,1536]{1,0:T(8,128)(2,1)S(1)}, bf16[256,1536]{1,0:T(8,128)(2,1)S(1)}, u32[]{:S(2)}, u32[]{:S(2)}) collective-permute-start(bf16[256,1536]{1,0:T(8,128)(2,1)S(1)} %copy-done.7), channel_id=1, source_target_pairs={{0,8},{8,0},{16,24},{24,16},{1,9},{9,1},{17,25},{25,17},{2,10},{10... | collective-permute-start | bytes 2359304 | tf_op jit(solution)/shard_map/ppermute | solution.py:64
  506.3 1.3 collective-permute-start.36
  507.5 7.1 %collective-permute-start.37 = (f32[4352]{0:T(1024)S(1)}, f32[4352]{0:T(1024)S(1)}, u32[]{:S(2)}, u32[]{:S(2)}) collective-permute-start(f32[4352]{0:T(1024)S(1)} %fusion.47), channel_id=1, source_target_pairs={{0,2},{1,3},{2,0},{3,1},{4,6},{5,7},{6,4},{7,5},{8,10},{9,11},{10,... | collective-permute-start | bytes 52232 | tf_op jit(solution)/shard_map/ppermute | solution.py:345
  508.3 14.7 %copy-start.32 = (bf16[256,2048]{1,0:T(8,128)(2,1)S(1)}, bf16[256,2048]{1,0:T(8,128)(2,1)}, u32[]{:S(2)}) copy-start(bf16[256,2048]{1,0:T(8,128)(2,1)} %copy-done.31) | copy-start | bytes 3145732
  514.7 11.5 %collective-permute-start.38 = (f32[4352]{0:T(1024)S(1)}, f32[4352]{0:T(1024)S(1)}, u32[]{:S(2)}, u32[]{:S(2)}) collective-permute-start(f32[4352]{0:T(1024)S(1)} %add.145), channel_id=1, source_target_pairs={{0,4},{1,5},{2,6},{3,7},{4,0},{5,1},{6,2},{7,3},{8,12},{9,13},{10,... | collective-permute-start | bytes 52232 | tf_op jit(solution)/shard_map/ppermute | solution.py:345
  521.7 10.0 %collective-permute-start.41 = (bf16[128,1536]{1,0:T(8,128)(2,1)S(1)}, bf16[128,1536]{1,0:T(8,128)(2,1)S(1)}, u32[]{:S(2)}, u32[]{:S(2)}) collective-permute-start(bf16[128,1536]{1,0:T(8,128)(2,1)S(1)} %slice.176), channel_id=1, source_target_pairs={{0,8},{8,0},{16,24},{24,16},{1,9},{9,1},{17,25},{25,17},{2,10},{10... | collective-permute-start | bytes 1179656 | tf_op jit(solution)/shard_map/ppermute | solution.py:64
  522.4 9.7 %collective-permute-start.42 = (bf16[128,1536]{1,0:T(8,128)(2,1)S(1)}, bf16[128,1536]{1,0:T(8,128)(2,1)S(1)}, u32[]{:S(2)}, u32[]{:S(2)}) collective-permute-start(bf16[128,1536]{1,0:T(8,128)(2,1)S(1)} %slice.177), channel_id=1, source_target_pairs={{0,16},{8,24},{16,0},{24,8},{1,17},{9,25},{17,1},{25,9},{2,18},{10... | collective-permute-start | bytes 1179656 | tf_op jit(solution)/shard_map/ppermute | solution.py:64
  532.1 4.1 collective-permute-start.43
  533.6 17.9 %collective-permute-start.46 = (bf16[256,1536]{1,0:T(8,128)(2,1)}, bf16[256,1536]{1,0:T(8,128)(2,1)S(1)}, u32[]{:S(2)}, u32[]{:S(2)}) collective-permute-start(bf16[256,1536]{1,0:T(8,128)(2,1)} %reduce-scatter.8.cloned.1.call-done.refs_0_), channel_id=1, source_target_pairs={{0,8},{8,0},{16,24},{24,16},{1,9},{9,1},{17,25},{25,17},{2,10},{10... | collective-permute-start | bytes 2359304 | tf_op jit(solution)/shard_map/ppermute | solution.py:64
  534.1 17.4 %collective-permute-start.45 = (bf16[256,1536]{1,0:T(8,128)(2,1)}, bf16[256,1536]{1,0:T(8,128)(2,1)S(1)}, u32[]{:S(2)}, u32[]{:S(2)}) collective-permute-start(bf16[256,1536]{1,0:T(8,128)(2,1)} %reduce-scatter.8.cloned.1.call-done.refs_0_), channel_id=1, source_target_pairs={{0,16},{8,24},{16,0},{24,8},{1,17},{9,25},{17,1},{25,9},{2,18},{10... | collective-permute-start | bytes 2359304 | tf_op jit(solution)/shard_map/ppermute | solution.py:64
  536.2 15.2 %collective-permute-start.44 = (f32[4352]{0:T(1024)S(1)}, f32[4352]{0:T(1024)S(1)}, u32[]{:S(2)}, u32[]{:S(2)}) collective-permute-start(f32[4352]{0:T(1024)S(1)} %add.147), channel_id=1, source_target_pairs={{0,16},{8,24},{16,0},{24,8},{1,17},{9,25},{17,1},{25,9},{2,18},{10... | collective-permute-start | bytes 52232 | tf_op jit(solution)/shard_map/ppermute | solution.py:345
  543.5 11.9 %copy-start.10 = (s32[3]{0:T(128)S(1)}, s32[3]{0:T(128)}, u32[]{:S(2)}) copy-start(s32[3]{0:T(128)} %pad_add_fusion.1.order_ref) | copy-start | bytes 40
  551.5 7.8 %collective-permute-start.47 = (bf16[128,1536]{1,0:T(8,128)(2,1)S(1)}, bf16[128,1536]{1,0:T(8,128)(2,1)S(1)}, u32[]{:S(2)}, u32[]{:S(2)}) collective-permute-start(bf16[128,1536]{1,0:T(8,128)(2,1)S(1)} %slice.179), channel_id=1, source_target_pairs={{0,8},{8,0},{16,24},{24,16},{1,9},{9,1},{17,25},{25,17},{2,10},{10... | collective-permute-start | bytes 1179656 | tf_op jit(solution)/shard_map/ppermute | solution.py:64
  553.6 7.8 %collective-permute-start.48 = (bf16[128,1536]{1,0:T(8,128)(2,1)S(1)}, bf16[128,1536]{1,0:T(8,128)(2,1)S(1)}, u32[]{:S(2)}, u32[]{:S(2)}) collective-permute-start(bf16[128,1536]{1,0:T(8,128)(2,1)S(1)} %slice.180), channel_id=1, source_target_pairs={{0,16},{8,24},{16,0},{24,8},{1,17},{9,25},{17,1},{25,9},{2,18},{10... | collective-permute-start | bytes 1179656 | tf_op jit(solution)/shard_map/ppermute | solution.py:64
  (40 other events, 139.4 us)
Sparse Core Ops, SparseCore 0:
  10.6 63.6 all-gather.3
  75.9 114.6 all-gather.5
  192.2 63.7 all-gather.7
  258.2 127.2 reduce-scatter.3
  388.1 68.1 reduce-scatter.5
  458.5 69.0 reduce-scatter.7

commit v7 on v6

--- a/solution.py
+++ b/solution.py
@@ -755,7 +755,7 @@
         )
         get1.second(*got)
         out = resid + after(sum_out.finish(), *got)
-        share3 = red3.total(share2, *got)
+        share3 = red3.total(share2, *sum_dxa.sent)
         du, in_terms = norm_back(inputs, input_gain, after(sum_dxa.finish(), *get1.arrived()))
         d_inputs = d_resid + du
 

time: 581 us -> 580 us (level)
  the two profiles are of different devices: /device:TPU:8 before, /device:TPU:0 now
where the time goes in v7:
time: 580 us; the launch traced here: 569 us
  waiting for transfers between devices  212 us (37%)
  Pallas kernels  194 us (33%)
  starting transfers between devices  51.2 us (9%)
  local copies, waits for them, and re-layouts  33.4 us (6%)
  other arithmetic  31.9 us (6%)
  matrix products  31.6 us (5%)
  between operations  15.3 us (3%)
    ppermute x44, waiting for transfers between devices, swap(): return lax.ppermute(x, 'seq', [(s, s ^ side) for s in range(4)])  201 us
    pallas_call x2, Pallas kernels, feed_forward(): pl.pallas_call(functools.partial(feed_forward_kernel, bool(sums), piece),...  57.9 us
    ppermute x44, starting transfers between devices, swap(): return lax.ppermute(x, 'seq', [(s, s ^ side) for s in range(4)])  46.8 us
    pallas_call x3, Pallas kernels, weight_terms(): pl.pallas_call(functools.partial(terms_kernel, starts, blocks, stride), g...  45.5 us
    pallas_call x8, Pallas kernels, put_rows(): pl.pallas_call(functools.partial(put_rows_kernel, len(pieces)), grid_spec...  30.6 us
    pallas_call x1, Pallas kernels, attend_back(): pl.pallas_call(functools.partial(attend_back_kernel, ratio), grid=(kv_hea...  19.3 us
    dot_general x3, matrix products, dot_nt(): lax.dot_general(a, b, (((1,), (1,)), ((), ())), preferred_element_type=F32)  16.2 us
    dot_general x2, matrix products, dot(): return jnp.dot(a, b, preferred_element_type=F32)  15.4 us
  transfers between devices with their start and end apart: 55, of which 39 were waited for; matrix products, arithmetic and copies ran while one was open for 15% of the time, Pallas kernels for 34%

profile of v7, /device:TPU:0, one launch (start us, length us, event | category | flops | bytes accessed | tf_op | source)
XLA Modules:
  0.0 569.2 jit_solution(5511673694175206930)
XLA Ops:
  16.0 3.0 collective-permute-start.2
  21.8 21.3 %collective-permute-done.2.refs_1_ = bf16[256,2048]{1,0:T(8,128)(2,1)} collective-permute-done((bf16[256,2048]{1,0:T(8,128)(2,1)S(1)}, bf16[256,2048]{1,0:T(8,128)(2,1)}, u32[]{:S(2)}, u32[]{:S(2)}) %collective-permute-start.2) | collective-permute-done | bytes 1048608 | tf_op jit(solution)/shard_map/ppermute | solution.py:64
  43.1 1.9 slice.159
  45.0 2.0 collective-permute-start.3
  47.1 1.9 slice.158
  52.8 4.6 put_rows.8.refs_2_
  57.4 8.2 %collective-permute-done.5.refs_1_ = bf16[256,2048]{1,0:T(8,128)(2,1)} collective-permute-done((bf16[256,2048]{1,0:T(8,128)(2,1)S(1)}, bf16[256,2048]{1,0:T(8,128)(2,1)}, u32[]{:S(2)}, u32[]{:S(2)}) %collective-permute-start.5) | collective-permute-done | bytes 1048608 | tf_op jit(solution)/shard_map/ppermute | solution.py:64
  65.6 1.9 slice.163
  67.7 1.9 slice.162
  69.6 7.9 %collective-permute-done.3.refs_1_ = bf16[128,2048]{1,0:T(8,128)(2,1)} collective-permute-done((bf16[128,2048]{1,0:T(8,128)(2,1)}, bf16[128,2048]{1,0:T(8,128)(2,1)}, u32[]{:S(2)}, u32[]{:S(2)}) %collective-permute-start.3) | collective-permute-done | bytes 524320 | tf_op jit(solution)/shard_map/ppermute | solution.py:64
  77.5 2.9 put_rows.9.refs_0_
  80.4 9.3 %fusion.24.q_ref.k_ref.v_ref = bf16[1024,1024]{1,0:T(8,128)(2,1)} fusion(bf16[1024,2048]{1,0:T(8,128)(2,1)} %put_rows.9.refs_0_, bf16[2048,1536]{1,0:T(8,128)(2,1)} %all-gather.4.cloned.1.call-done), kind=kOutput, calls=%fused_computation.40 | convolution fusion | flops 4296015872 | bytes 10485760 | tf_op jit(solution)/shard_map/dot_general | solution.py:21
  90.0 1.7 collective-permute-start.7
  91.7 1.9 fusion.42
  95.7 4.7 put_rows.10.refs_2_
  100.4 12.8 %attend.1.o_ref = bf16[1024,512]{1,0:T(8,128)(2,1)} custom-call(bf16[1024,1024]{1,0:T(8,128)(2,1)} %fusion.24.q_ref.k_ref.v_ref, bf16[1024,1024]{1,0:T(8,128)(2,1)} %fusion.24.q_ref.k_ref.v_ref, bf16[1024,1024]{1,0:T(8,128)(2,1)} %fusion.24.q_ref.k_ref.v_ref, f32[1024,128]{1,0:T(8,128)} %get-tuple-element.169.cos_ref, ...), custom_call_target="tpu_custom_call" | custom-call | flops 1000 | bytes 1000 | tf_op jit(solution)/shard_map/attend/pallas_call | solution.py:502
  114.0 3.1 put_rows.11.dy_ref.refs_1_
  117.1 2.3 convolution_convert_fusion.2
  119.9 1.7 collective-permute-start.8
  121.6 5.1 convolution_convert_fusion.1
  126.7 5.0 collective-permute-done.9.ty_ref
  132.7 3.3 add_halves.4
  138.9 19.9 %collective-permute-done.10 = bf16[256,2048]{1,0:T(8,128)(2,1)S(1)} collective-permute-done((bf16[256,2048]{1,0:T(8,128)(2,1)}, bf16[256,2048]{1,0:T(8,128)(2,1)S(1)}, u32[]{:S(2)}, u32[]{:S(2)}) %collective-permute-start.10) | collective-permute-done | bytes 1048608 | tf_op jit(solution)/shard_map/ppermute | solution.py:64
  159.5 1.9 multiply_reduce_fusion.2
  163.9 19.0 %collective-permute-done.14.refs_1_ = bf16[256,2048]{1,0:T(8,128)(2,1)S(1)} collective-permute-done((bf16[256,2048]{1,0:T(8,128)(2,1)S(1)}, bf16[256,2048]{1,0:T(8,128)(2,1)S(1)}, u32[]{:S(2)}, u32[]{:S(2)}) %collective-permute-start.14) | collective-permute-done | bytes 1048608 | tf_op jit(solution)/shard_map/ppermute | solution.py:64
  187.7 4.6 put_rows.12.refs_2_
  192.3 2.9 collective-permute-done.15.refs_1_
  196.5 2.9 put_rows.13.xb_ref.refs_0_
  199.4 36.4 %feed_forward.2 = (bf16[1024,3072]{1,0:T(8,128)(2,1)}, f32[4,256,2048]{2,1,0:T(8,128)}, f32[4,256,2048]{2,1,0:T(8,128)}) custom-call(s32[4]{0:T(128)} %pad_add_fusion.2.order_ref, bf16[1024,2048]{1,0:T(8,128)(2,1)} %put_rows.13.xb_ref.refs_0_, bf16[1024,2048]{1,0:T(8,128)(2,1)} %put_rows.11.dy_ref.refs_1_, bf16[2048,3072]{1,0:T(8,128)(2,1)} %all-gather.6.cloned.1.call-done.w_ref), custom_call_target="tpu_custom_call" | custom-call | flops 1000 | bytes 1000 | tf_op jit(solution)/shard_map/feed_forward/pallas_call | solution.py:576
  235.8 20.5 %weight_terms.3 = bf16[2048,3072]{1,0:T(8,128)(2,1)} custom-call(s32[1]{0:T(128)} %constant.50.clone.1.parity_ref, bf16[1024,2048]{1,0:T(8,128)(2,1)} %put_rows.13.xb_ref.refs_0_, bf16[1024,2048]{1,0:T(8,128)(2,1)} %put_rows.11.dy_ref.refs_1_, bf16[1024,3072]{1,0:T(8,128)(2,1)} %get-tuple-element.78.refs_2_), custom_call_target="tpu_custom_call" | custom-call | flops 1000 | bytes 1000 | tf_op jit(solution)/shard_map/weight_terms/pallas_call | solution.py:294
  256.3 3.4 all-gather.8.cloned.1.call-done.w_ref
  259.8 21.5 %feed_forward.3 = (bf16[1024,1536]{1,0:T(8,128)(2,1)}, bf16[4,256,2048]{2,1,0:T(8,128)(2,1)}, bf16[4,256,2048]{2,1,0:T(8,128)(2,1)}) custom-call(s32[4]{0:T(128)} %pad_add_fusion.2.order_ref, bf16[1024,2048]{1,0:T(8,128)(2,1)} %put_rows.13.xb_ref.refs_0_, bf16[1024,2048]{1,0:T(8,128)(2,1)} %put_rows.11.dy_ref.refs_1_, ...), custom_call_target="tpu_custom_call" | custom-call | flops 1000 | bytes 1000 | tf_op jit(solution)/shard_map/feed_forward/pallas_call | solution.py:576
  288.1 9.3 %collective-permute-done.19.ty_ref = bf16[128,2048]{1,0:T(8,128)(2,1)S(1)} collective-permute-done((bf16[128,2048]{1,0:T(8,128)(2,1)S(1)}, bf16[128,2048]{1,0:T(8,128)(2,1)S(1)}, u32[]{:S(2)}, u32[]{:S(2)}) %collective-permute-start.19) | collective-permute-done | bytes 524320 | tf_op jit(solution)/shard_map/ppermute | solution.py:64
  298.9 9.1 %collective-permute-done.17.ty_ref = bf16[128,2048]{1,0:T(8,128)(2,1)S(1)} collective-permute-done((bf16[128,2048]{1,0:T(8,128)(2,1)S(1)}, bf16[128,2048]{1,0:T(8,128)(2,1)S(1)}, u32[]{:S(2)}, u32[]{:S(2)}) %collective-permute-start.17) | collective-permute-done | bytes 524320 | tf_op jit(solution)/shard_map/ppermute | solution.py:64
  309.2 3.5 add_halves.6
  314.7 12.3 %weight_terms.4 = bf16[2048,1536]{1,0:T(8,128)(2,1)} custom-call(s32[1]{0:T(128)} %constant.50.clone.1.parity_ref, bf16[1024,2048]{1,0:T(8,128)(2,1)} %put_rows.13.xb_ref.refs_0_, bf16[1024,2048]{1,0:T(8,128)(2,1)} %put_rows.11.dy_ref.refs_1_, bf16[1024,1536]{1,0:T(8,128)(2,1)} %get-tuple-element.90.refs_2_), custom_call_target="tpu_custom_call" | custom-call | flops 1000 | bytes 1000 | tf_op jit(solution)/shard_map/weight_terms/pallas_call | solution.py:294
  327.0 10.3 %collective-permute-done.20 = bf16[256,2048]{1,0:T(8,128)(2,1)S(1)} collective-permute-done((bf16[256,2048]{1,0:T(8,128)(2,1)}, bf16[256,2048]{1,0:T(8,128)(2,1)S(1)}, u32[]{:S(2)}, u32[]{:S(2)}) %collective-permute-start.20) | collective-permute-done | bytes 1048608 | tf_op jit(solution)/shard_map/ppermute | solution.py:64
  338.6 2.1 fusion.22
  345.0 21.6 %collective-permute-done.24.refs_1_ = bf16[256,2048]{1,0:T(8,128)(2,1)S(1)} collective-permute-done((bf16[256,2048]{1,0:T(8,128)(2,1)S(1)}, bf16[256,2048]{1,0:T(8,128)(2,1)S(1)}, u32[]{:S(2)}, u32[]{:S(2)}) %collective-permute-start.24) | collective-permute-done | bytes 1048608 | tf_op jit(solution)/shard_map/ppermute | solution.py:64
  370.3 3.3 add_halves.5
  373.6 4.8 put_rows.14.refs_2_
  381.3 2.9 put_rows.15.refs_1_
  385.9 6.2 %fusion.31.do_ref = bf16[1024,512]{1,0:T(8,128)(2,1)} fusion(bf16[1024,2048]{1,0:T(8,128)(2,1)} %put_rows.15.refs_1_, bf16[2048,1536]{1,0:T(8,128)(2,1)} %all-gather.4.cloned.1.call-done), kind=kOutput, calls=%fused_computation.46 | convolution fusion | flops 2148007936 | bytes 7340032 | tf_op jit(solution)/shard_map/dot_general | solution.py:21
  392.1 19.3 %attend_back.1 = (bf16[1024,512]{1,0:T(8,128)(2,1)}, bf16[1024,256]{1,0:T(8,128)(2,1)}, bf16[1024,256]{1,0:T(8,128)(2,1)}, f32[2,1,128]{2,1,0:T(1,128)}, f32[2,1,128]{2,1,0:T(1,128)}) custom-call(bf16[1024,1024]{1,0:T(8,128)(2,1)} %fusion.24.q_ref.k_ref.v_ref, bf16[1024,1024]{1,0:T(8,128)(2,1)} %fusion.24.q_ref.k_ref.v_ref, ...), custom_call_target="tpu_custom_call" | custom-call | flops 1000 | bytes 1000 | tf_op jit(solution)/shard_map/attend_back/pallas_call | solution.py:520
  415.1 3.1 pad_maximum_fusion.refs_2_
  418.2 12.7 %weight_terms.5 = bf16[2048,1536]{1,0:T(8,128)(2,1)} custom-call(s32[1]{0:T(128)} %constant.50.clone.1.parity_ref, bf16[1024,2048]{1,0:T(8,128)(2,1)} %put_rows.9.refs_0_, bf16[1024,2048]{1,0:T(8,128)(2,1)} %put_rows.15.refs_1_, bf16[1024,1536]{1,0:T(8,128)(2,1)} %pad_maximum_fusion.refs_2_), custom_call_target="tpu_custom_call" | custom-call | flops 1000 | bytes 1000 | tf_op jit(solution)/shard_map/weight_terms/pallas_call | solution.py:294
  430.9 1.6 slice-done
  432.7 8.8 %convolution_convert_fusion = bf16[1024,2048]{1,0:T(8,128)(2,1)S(1)} fusion(bf16[2048,1536]{1,0:T(8,128)(2,1)} %all-gather.4.cloned.1.call-done, bf16[256,1024]{1,0:T(8,128)(2,1)S(1)} %get-tuple-element.148, bf16[256,1024]{1,0:T(8,128)(2,1)S(1)} %get-tuple-element.149, bf16[256,1024]{1,0:T(8,128)(2,1)S(1)} %get-tuple-element.150, ...), kind=kOutput, calls=%fused_computation | convolution fusion | flops 4305453056 | bytes 10485760 | tf_op jit(solution)/shard_map/dot_general | solution.py:25
  441.6 3.8 collective-permute-done.29.refs_2_
  449.8 6.8 %collective-permute-done.31.ty_ref = bf16[128,2048]{1,0:T(8,128)(2,1)S(1)} collective-permute-done((bf16[128,2048]{1,0:T(8,128)(2,1)S(1)}, bf16[128,2048]{1,0:T(8,128)(2,1)S(1)}, u32[]{:S(2)}, u32[]{:S(2)}) %collective-permute-start.31) | collective-permute-done | bytes 524320 | tf_op jit(solution)/shard_map/ppermute | solution.py:64
  457.6 3.4 add_halves.7
  461.0 1.6 collective-permute-start.34
  465.2 16.7 %collective-permute-done.34 = bf16[128,3072]{1,0:T(8,128)(2,1)} collective-permute-done((bf16[128,3072]{1,0:T(8,128)(2,1)}, bf16[128,3072]{1,0:T(8,128)(2,1)}, u32[]{:S(2)}, u32[]{:S(2)}) %collective-permute-start.34) | collective-permute-done | bytes 786464 | tf_op jit(solution)/shard_map/ppermute | solution.py:64
  484.6 16.2 %collective-permute-done.32 = bf16[256,2048]{1,0:T(8,128)(2,1)} collective-permute-done((bf16[256,2048]{1,0:T(8,128)(2,1)}, bf16[256,2048]{1,0:T(8,128)(2,1)}, u32[]{:S(2)}, u32[]{:S(2)}) %collective-permute-start.32) | collective-permute-done | bytes 1048608 | tf_op jit(solution)/shard_map/ppermute | solution.py:64
  500.8 2.2 collective-permute-done.33
  504.7 2.5 convert_add_fusion.3
  510.6 6.4 %place.4 = (f32[256,6144]{1,0:T(8,128)}, f32[256,6144]{1,0:T(8,128)}, f32[256,6144]{1,0:T(8,128)}) custom-call(s32[4]{0:T(128)S(1)} %copy-done.11, bf16[256,3072]{1,0:T(8,128)(2,1)S(1)} %copy-done.6, bf16[256,3072]{1,0:T(8,128)(2,1)S(1)} %collective-permute-done.28.refs_1_, bf16[256,3072]{1,0:T(8,128)(2,1)S(1)} %collective-permute-done.29.refs_2_, ...), custom_call_target="tpu_custom_call" | custom-call | flops 1000 | bytes 1000 | tf_op jit(solution)/shard_map/place/pallas_call | solution.py:624
  520.9 3.2 fusion.23
  524.1 5.1 collective-permute-done.41
  535.6 6.6 %fusion.35 = (bf16[1,256,2048]{2,1,0:T(8,128)(2,1)}, bf16[1,256,2048]{2,1,0:T(8,128)(2,1)}) fusion(f32[256,2048]{1,0:T(8,128)} %copy-done.17, bf16[1,256,2048]{2,1,0:T(8,128)(2,1)} %param.14, f32[256]{0:T(256)S(1)} %broadcast_multiply_fusion, f32[2048]{0:T(1024)S(1)} %copy-done.45, f32[256]{0:T(256)S(1)} %add_rsqrt_fusion.1, ...), kind=kLoop, calls=%fused_computation.48 | loop fusion | flops 8912896 | bytes 12603392 | tf_op jit(solution)/shard_map/broadcast_in_dim | solution.py:788
  542.2 3.6 place.5
  545.8 5.6 collective-permute-done.44
  554.3 3.1 place.6
  557.4 1.9 collective-permute-done.47.refs_0_
  (255 shorter events, 93.2 us)
Async XLA Ops:
  7.2 73.2 %all-gather.4.cloned.1.call-start = ((), (), s32[]{:S(2)}) async-start(), calls=%async_computation.3 | async-start | bytes 7077888 | tf_op jit(solution)/shard_map/all_gather | solution.py:258
  10.4 189.0 %all-gather.6.cloned.1.call-start = ((), (), s32[]{:S(2)}) async-start(), calls=%async_computation.4 | async-start | bytes 14155776 | tf_op jit(solution)/shard_map/all_gather | solution.py:258
  13.1 246.7 %all-gather.8.cloned.1.call-start = ((), (), s32[]{:S(2)}) async-start(), calls=%async_computation.5 | async-start | bytes 7077888 | tf_op jit(solution)/shard_map/all_gather | solution.py:258
  15.3 397.4 %reduce-scatter.4.cloned.1.call-start = ((), (), s32[]{:S(2)}) async-start(), calls=%async_computation.6 | async-start | bytes 14155776 | tf_op jit(solution)/shard_map/reduce_scatter | solution.py:335
  16.0 36.8 %copy-start.22 = (bf16[256,2048]{1,0:T(8,128)(2,1)}, bf16[256,2048]{1,0:T(8,128)(2,1)S(1)}, u32[]{:S(2)}) copy-start(bf16[256,2048]{1,0:T(8,128)(2,1)S(1)} %fusion.7.refs_0_) | copy-start | bytes 3145732
  16.0 27.1 %collective-permute-start.2 = (bf16[256,2048]{1,0:T(8,128)(2,1)S(1)}, bf16[256,2048]{1,0:T(8,128)(2,1)}, u32[]{:S(2)}, u32[]{:S(2)}) collective-permute-start(bf16[256,2048]{1,0:T(8,128)(2,1)S(1)} %fusion.7.refs_0_), channel_id=1, source_target_pairs={{0,8},{8,0},{16,24},{24,16},{1,9},{9,1},{17,25},{25,17},{2,10},{10... | collective-permute-start | bytes 3145736 | tf_op jit(solution)/shard_map/ppermute | solution.py:64
  19.0 28.1 %collective-permute-start = (bf16[256,2048]{1,0:T(8,128)(2,1)S(1)}, bf16[256,2048]{1,0:T(8,128)(2,1)}, u32[]{:S(2)}, u32[]{:S(2)}) collective-permute-start(bf16[256,2048]{1,0:T(8,128)(2,1)S(1)} %fusion.7.refs_0_), channel_id=1, source_target_pairs={{0,16},{8,24},{16,0},{24,8},{1,17},{9,25},{17,1},{25,9},{2,18},{10... | collective-permute-start | bytes 3145736 | tf_op jit(solution)/shard_map/ppermute | solution.py:64
  20.5 45.0 %collective-permute-start.5 = (bf16[256,2048]{1,0:T(8,128)(2,1)S(1)}, bf16[256,2048]{1,0:T(8,128)(2,1)}, u32[]{:S(2)}, u32[]{:S(2)}) collective-permute-start(bf16[256,2048]{1,0:T(8,128)(2,1)S(1)} %bitcast.59), channel_id=1, source_target_pairs={{0,8},{8,0},{16,24},{24,16},{1,9},{9,1},{17,25},{25,17},{2,10},{10... | collective-permute-start | bytes 3145736 | tf_op jit(solution)/shard_map/ppermute | solution.py:64
  21.1 46.6 %collective-permute-start.4 = (bf16[256,2048]{1,0:T(8,128)(2,1)S(1)}, bf16[256,2048]{1,0:T(8,128)(2,1)}, u32[]{:S(2)}, u32[]{:S(2)}) collective-permute-start(bf16[256,2048]{1,0:T(8,128)(2,1)S(1)} %bitcast.60), channel_id=1, source_target_pairs={{0,16},{8,24},{16,0},{24,8},{1,17},{9,25},{17,1},{25,9},{2,18},{10... | collective-permute-start | bytes 3145736 | tf_op jit(solution)/shard_map/ppermute | solution.py:64
  45.0 32.4 %collective-permute-start.3 = (bf16[128,2048]{1,0:T(8,128)(2,1)}, bf16[128,2048]{1,0:T(8,128)(2,1)}, u32[]{:S(2)}, u32[]{:S(2)}) collective-permute-start(bf16[128,2048]{1,0:T(8,128)(2,1)} %slice.159), channel_id=1, source_target_pairs={{0,16},{8,24},{16,0},{24,8},{1,17},{9,25},{17,1},{25,9},{2,18},{10... | collective-permute-start | bytes 1572872 | tf_op jit(solution)/shard_map/ppermute | solution.py:64
  49.0 28.5 %collective-permute-start.1 = (bf16[128,2048]{1,0:T(8,128)(2,1)}, bf16[128,2048]{1,0:T(8,128)(2,1)}, u32[]{:S(2)}, u32[]{:S(2)}) collective-permute-start(bf16[128,2048]{1,0:T(8,128)(2,1)} %slice.158), channel_id=1, source_target_pairs={{0,8},{8,0},{16,24},{24,16},{1,9},{9,1},{17,25},{25,17},{2,10},{10... | collective-permute-start | bytes 1572872 | tf_op jit(solution)/shard_map/ppermute | solution.py:64
  89.6 23.6 %collective-permute-start.6 = (bf16[128,2048]{1,0:T(8,128)(2,1)}, bf16[128,2048]{1,0:T(8,128)(2,1)S(1)}, u32[]{:S(2)}, u32[]{:S(2)}) collective-permute-start(bf16[128,2048]{1,0:T(8,128)(2,1)} %slice.162), channel_id=1, source_target_pairs={{0,8},{8,0},{16,24},{24,16},{1,9},{9,1},{17,25},{25,17},{2,10},{10... | collective-permute-start | bytes 1572872 | tf_op jit(solution)/shard_map/ppermute | solution.py:64
  90.0 23.2 %collective-permute-start.7 = (bf16[128,2048]{1,0:T(8,128)(2,1)}, bf16[128,2048]{1,0:T(8,128)(2,1)}, u32[]{:S(2)}, u32[]{:S(2)}) collective-permute-start(bf16[128,2048]{1,0:T(8,128)(2,1)} %slice.163), channel_id=1, source_target_pairs={{0,16},{8,24},{16,0},{24,8},{1,17},{9,25},{17,1},{25,9},{2,18},{10... | collective-permute-start | bytes 1572872 | tf_op jit(solution)/shard_map/ppermute | solution.py:64
  119.6 12.1 %collective-permute-start.9 = (bf16[128,2048]{1,0:T(8,128)(2,1)S(1)}, bf16[128,2048]{1,0:T(8,128)(2,1)S(1)}, u32[]{:S(2)}, u32[]{:S(2)}) collective-permute-start(bf16[128,2048]{1,0:T(8,128)(2,1)S(1)} %get-tuple-element.153), channel_id=1, source_target_pairs={{0,16},{8,24},{16,0},{24,8},{1,17},{9,25},{17,1},{25,9},{2,18},{10... | collective-permute-start | bytes 1572872 | tf_op jit(solution)/shard_map/ppermute | solution.py:64
  119.9 12.1 %collective-permute-start.8 = (bf16[128,2048]{1,0:T(8,128)(2,1)S(1)}, bf16[128,2048]{1,0:T(8,128)(2,1)S(1)}, u32[]{:S(2)}, u32[]{:S(2)}) collective-permute-start(bf16[128,2048]{1,0:T(8,128)(2,1)S(1)} %get-tuple-element.154), channel_id=1, source_target_pairs={{0,8},{8,0},{16,24},{24,16},{1,9},{9,1},{17,25},{25,17},{2,10},{10... | collective-permute-start | bytes 1572872 | tf_op jit(solution)/shard_map/ppermute | solution.py:64
  136.0 22.7 %collective-permute-start.10 = (bf16[256,2048]{1,0:T(8,128)(2,1)}, bf16[256,2048]{1,0:T(8,128)(2,1)S(1)}, u32[]{:S(2)}, u32[]{:S(2)}) collective-permute-start(bf16[256,2048]{1,0:T(8,128)(2,1)} %get-tuple-element.76), channel_id=1, source_target_pairs={{0,8},{8,0},{16,24},{24,16},{1,9},{9,1},{17,25},{25,17},{2,10},{10... | collective-permute-start | bytes 3145736 | tf_op jit(solution)/shard_map/ppermute | solution.py:64
  137.3 24.1 %copy-start.44 = (f32[2048]{0:T(1024)S(1)}, f32[2048]{0:T(1024)}, u32[]{:S(2)}) copy-start(f32[2048]{0:T(1024)} %param.23) | copy-start | bytes 24580
  137.3 22.2 %collective-permute-start.11 = (bf16[256,2048]{1,0:T(8,128)(2,1)}, bf16[256,2048]{1,0:T(8,128)(2,1)S(1)}, u32[]{:S(2)}, u32[]{:S(2)}) collective-permute-start(bf16[256,2048]{1,0:T(8,128)(2,1)} %get-tuple-element.77), channel_id=1, source_target_pairs={{0,16},{8,24},{16,0},{24,8},{1,17},{9,25},{17,1},{25,9},{2,18},{10... | collective-permute-start | bytes 3145736 | tf_op jit(solution)/shard_map/ppermute | solution.py:64
  161.4 180.1 %copy-start.12 = (f32[256,2048]{1,0:T(8,128)}, f32[256,2048]{1,0:T(8,128)S(1)}, u32[]{:S(2)}) copy-start(f32[256,2048]{1,0:T(8,128)S(1)} %get-tuple-element.138) | copy-start | bytes 6291460
  161.7 26.0 %copy-start.21 = (bf16[256,2048]{1,0:T(8,128)(2,1)}, bf16[256,2048]{1,0:T(8,128)(2,1)S(1)}, u32[]{:S(2)}) copy-start(bf16[256,2048]{1,0:T(8,128)(2,1)S(1)} %multiply_convert_fusion.refs_0_) | copy-start | bytes 3145732
  161.7 21.2 %collective-permute-start.14 = (bf16[256,2048]{1,0:T(8,128)(2,1)S(1)}, bf16[256,2048]{1,0:T(8,128)(2,1)S(1)}, u32[]{:S(2)}, u32[]{:S(2)}) collective-permute-start(bf16[256,2048]{1,0:T(8,128)(2,1)S(1)} %multiply_convert_fusion.refs_0_), channel_id=1, source_target_pairs={{0,8},{8,0},{16,24},{24,16},{1,9},{9,1},{17,25},{25,17},{2,10},{10... | collective-permute-start | bytes 3145736 | tf_op jit(solution)/shard_map/ppermute | solution.py:64
  162.8 23.1 %collective-permute-start.12 = (bf16[256,2048]{1,0:T(8,128)(2,1)S(1)}, bf16[256,2048]{1,0:T(8,128)(2,1)S(1)}, u32[]{:S(2)}, u32[]{:S(2)}) collective-permute-start(bf16[256,2048]{1,0:T(8,128)(2,1)S(1)} %multiply_convert_fusion.refs_0_), channel_id=1, source_target_pairs={{0,16},{8,24},{16,0},{24,8},{1,17},{9,25},{17,1},{25,9},{2,18},{10... | collective-permute-start | bytes 3145736 | tf_op jit(solution)/shard_map/ppermute | solution.py:64
  183.8 11.4 %collective-permute-start.15 = (bf16[128,2048]{1,0:T(8,128)(2,1)}, bf16[128,2048]{1,0:T(8,128)(2,1)S(1)}, u32[]{:S(2)}, u32[]{:S(2)}) collective-permute-start(bf16[128,2048]{1,0:T(8,128)(2,1)} %slice.169), channel_id=1, source_target_pairs={{0,16},{8,24},{16,0},{24,8},{1,17},{9,25},{17,1},{25,9},{2,18},{10... | collective-permute-start | bytes 1572872 | tf_op jit(solution)/shard_map/ppermute | solution.py:64
  187.0 9.5 %collective-permute-start.13 = (bf16[128,2048]{1,0:T(8,128)(2,1)}, bf16[128,2048]{1,0:T(8,128)(2,1)}, u32[]{:S(2)}, u32[]{:S(2)}) collective-permute-start(bf16[128,2048]{1,0:T(8,128)(2,1)} %slice.168), channel_id=1, source_target_pairs={{0,8},{8,0},{16,24},{24,16},{1,9},{9,1},{17,25},{25,17},{2,10},{10... | collective-permute-start | bytes 1572872 | tf_op jit(solution)/shard_map/ppermute | solution.py:64
  256.3 204.7 %reduce-scatter.6.cloned.1.call-start = ((), (), s32[]{:S(2)}) async-start(), calls=%async_computation.7 | async-start | bytes 7077888 | tf_op jit(solution)/shard_map/reduce_scatter | solution.py:335
  282.6 14.8 %collective-permute-start.19 = (bf16[128,2048]{1,0:T(8,128)(2,1)S(1)}, bf16[128,2048]{1,0:T(8,128)(2,1)S(1)}, u32[]{:S(2)}, u32[]{:S(2)}) collective-permute-start(bf16[128,2048]{1,0:T(8,128)(2,1)S(1)} %get-tuple-element.141), channel_id=1, source_target_pairs={{0,16},{8,24},{16,0},{24,8},{1,17},{9,25},{17,1},{25,9},{2,18},{10... | collective-permute-start | bytes 1572872 | tf_op jit(solution)/shard_map/ppermute | solution.py:64
  284.1 14.8 %collective-permute-start.18 = (bf16[128,2048]{1,0:T(8,128)(2,1)S(1)}, bf16[128,2048]{1,0:T(8,128)(2,1)S(1)}, u32[]{:S(2)}, u32[]{:S(2)}) collective-permute-start(bf16[128,2048]{1,0:T(8,128)(2,1)S(1)} %get-tuple-element.142), channel_id=1, source_target_pairs={{0,8},{8,0},{16,24},{24,16},{1,9},{9,1},{17,25},{25,17},{2,10},{10... | collective-permute-start | bytes 1572872 | tf_op jit(solution)/shard_map/ppermute | solution.py:64
  286.8 21.2 %collective-permute-start.17 = (bf16[128,2048]{1,0:T(8,128)(2,1)S(1)}, bf16[128,2048]{1,0:T(8,128)(2,1)S(1)}, u32[]{:S(2)}, u32[]{:S(2)}) collective-permute-start(bf16[128,2048]{1,0:T(8,128)(2,1)S(1)} %get-tuple-element.143), channel_id=1, source_target_pairs={{0,16},{8,24},{16,0},{24,8},{1,17},{9,25},{17,1},{25,9},{2,18},{10... | collective-permute-start | bytes 1572872 | tf_op jit(solution)/shard_map/ppermute | solution.py:64
  287.4 21.8 %collective-permute-start.16 = (bf16[128,2048]{1,0:T(8,128)(2,1)S(1)}, bf16[128,2048]{1,0:T(8,128)(2,1)S(1)}, u32[]{:S(2)}, u32[]{:S(2)}) collective-permute-start(bf16[128,2048]{1,0:T(8,128)(2,1)S(1)} %get-tuple-element.144), channel_id=1, source_target_pairs={{0,8},{8,0},{16,24},{24,16},{1,9},{9,1},{17,25},{25,17},{2,10},{10... | collective-permute-start | bytes 1572872 | tf_op jit(solution)/shard_map/ppermute | solution.py:64
  297.4 11.8 %copy-start.37 = (bf16[128,2048]{1,0:T(8,128)(2,1)}, bf16[128,2048]{1,0:T(8,128)(2,1)S(1)}, u32[]{:S(2)}) copy-start(bf16[128,2048]{1,0:T(8,128)(2,1)S(1)} %collective-permute-done.19.ty_ref) | copy-start | bytes 1572868
  312.7 24.6 %collective-permute-start.20 = (bf16[256,2048]{1,0:T(8,128)(2,1)}, bf16[256,2048]{1,0:T(8,128)(2,1)S(1)}, u32[]{:S(2)}, u32[]{:S(2)}) collective-permute-start(bf16[256,2048]{1,0:T(8,128)(2,1)} %get-tuple-element.87), channel_id=1, source_target_pairs={{0,8},{8,0},{16,24},{24,16},{1,9},{9,1},{17,25},{25,17},{2,10},{10... | collective-permute-start | bytes 3145736 | tf_op jit(solution)/shard_map/ppermute | solution.py:64
  314.2 24.4 %collective-permute-start.21 = (bf16[256,2048]{1,0:T(8,128)(2,1)}, bf16[256,2048]{1,0:T(8,128)(2,1)}, u32[]{:S(2)}, u32[]{:S(2)}) collective-permute-start(bf16[256,2048]{1,0:T(8,128)(2,1)} %get-tuple-element.88), channel_id=1, source_target_pairs={{0,16},{8,24},{16,0},{24,8},{1,17},{9,25},{17,1},{25,9},{2,18},{10... | collective-permute-start | bytes 3145736 | tf_op jit(solution)/shard_map/ppermute | solution.py:64
  343.5 23.2 %collective-permute-start.24 = (bf16[256,2048]{1,0:T(8,128)(2,1)S(1)}, bf16[256,2048]{1,0:T(8,128)(2,1)S(1)}, u32[]{:S(2)}, u32[]{:S(2)}) collective-permute-start(bf16[256,2048]{1,0:T(8,128)(2,1)S(1)} %fusion.48.refs_0_), channel_id=1, source_target_pairs={{0,8},{8,0},{16,24},{24,16},{1,9},{9,1},{17,25},{25,17},{2,10},{10... | collective-permute-start | bytes 3145736 | tf_op jit(solution)/shard_map/ppermute | solution.py:64
  344.4 23.1 %collective-permute-start.22 = (bf16[256,2048]{1,0:T(8,128)(2,1)S(1)}, bf16[256,2048]{1,0:T(8,128)(2,1)S(1)}, u32[]{:S(2)}, u32[]{:S(2)}) collective-permute-start(bf16[256,2048]{1,0:T(8,128)(2,1)S(1)} %fusion.48.refs_0_), channel_id=1, source_target_pairs={{0,16},{8,24},{16,0},{24,8},{1,17},{9,25},{17,1},{25,9},{2,18},{10... | collective-permute-start | bytes 3145736 | tf_op jit(solution)/shard_map/ppermute | solution.py:64
  368.5 163.5 %reduce-scatter.8.cloned.1.call-start = ((), (), s32[]{:S(2)}) async-start(), calls=%async_computation.8 | async-start | bytes 7077888 | tf_op jit(solution)/shard_map/reduce_scatter | solution.py:335
  368.5 11.0 %collective-permute-start.25 = (bf16[128,2048]{1,0:T(8,128)(2,1)S(1)}, bf16[128,2048]{1,0:T(8,128)(2,1)S(1)}, u32[]{:S(2)}, u32[]{:S(2)}) collective-permute-start(bf16[128,2048]{1,0:T(8,128)(2,1)S(1)} %slice.171), channel_id=1, source_target_pairs={{0,16},{8,24},{16,0},{24,8},{1,17},{9,25},{17,1},{25,9},{2,18},{10... | collective-permute-start | bytes 1572872 | tf_op jit(solution)/shard_map/ppermute | solution.py:64
  369.4 11.1 %collective-permute-start.23 = (bf16[128,2048]{1,0:T(8,128)(2,1)S(1)}, bf16[128,2048]{1,0:T(8,128)(2,1)S(1)}, u32[]{:S(2)}, u32[]{:S(2)}) collective-permute-start(bf16[128,2048]{1,0:T(8,128)(2,1)S(1)} %slice.170), channel_id=1, source_target_pairs={{0,8},{8,0},{16,24},{24,16},{1,9},{9,1},{17,25},{25,17},{2,10},{10... | collective-permute-start | bytes 1572872 | tf_op jit(solution)/shard_map/ppermute | solution.py:64
  384.2 27.2 %collective-permute-start.26 = (bf16[256,2048]{1,0:T(8,128)(2,1)}, bf16[256,2048]{1,0:T(8,128)(2,1)S(1)}, u32[]{:S(2)}, u32[]{:S(2)}) collective-permute-start(bf16[256,2048]{1,0:T(8,128)(2,1)} %get-tuple-element.92), channel_id=1, source_target_pairs={{0,8},{8,0},{16,24},{24,16},{1,9},{9,1},{17,25},{25,17},{2,10},{10... | collective-permute-start | bytes 3145736 | tf_op jit(solution)/shard_map/ppermute | solution.py:64
  384.8 26.6 %collective-permute-start.27 = (bf16[256,2048]{1,0:T(8,128)(2,1)}, bf16[256,2048]{1,0:T(8,128)(2,1)S(1)}, u32[]{:S(2)}, u32[]{:S(2)}) collective-permute-start(bf16[256,2048]{1,0:T(8,128)(2,1)} %get-tuple-element.93), channel_id=1, source_target_pairs={{0,16},{8,24},{16,0},{24,8},{1,17},{9,25},{17,1},{25,9},{2,18},{10... | collective-permute-start | bytes 3145736 | tf_op jit(solution)/shard_map/ppermute | solution.py:64
  412.7 32.7 %collective-permute-start.29 = (bf16[256,3072]{1,0:T(8,128)(2,1)}, bf16[256,3072]{1,0:T(8,128)(2,1)S(1)}, u32[]{:S(2)}, u32[]{:S(2)}) collective-permute-start(bf16[256,3072]{1,0:T(8,128)(2,1)} %reduce-scatter.4.cloned.1.call-done.refs_0_), channel_id=1, source_target_pairs={{0,16},{8,24},{16,0},{24,8},{1,17},{9,25},{17,1},{25,9},{2,18},{10... | collective-permute-start | bytes 4718600 | tf_op jit(solution)/shard_map/ppermute | solution.py:64
  413.7 32.6 %collective-permute-start.28 = (bf16[256,3072]{1,0:T(8,128)(2,1)}, bf16[256,3072]{1,0:T(8,128)(2,1)S(1)}, u32[]{:S(2)}, u32[]{:S(2)}) collective-permute-start(bf16[256,3072]{1,0:T(8,128)(2,1)} %reduce-scatter.4.cloned.1.call-done.refs_0_), channel_id=1, source_target_pairs={{0,8},{8,0},{16,24},{24,16},{1,9},{9,1},{17,25},{25,17},{2,10},{10... | collective-permute-start | bytes 4718600 | tf_op jit(solution)/shard_map/ppermute | solution.py:64
  447.3 9.2 %collective-permute-start.31 = (bf16[128,2048]{1,0:T(8,128)(2,1)S(1)}, bf16[128,2048]{1,0:T(8,128)(2,1)S(1)}, u32[]{:S(2)}, u32[]{:S(2)}) collective-permute-start(bf16[128,2048]{1,0:T(8,128)(2,1)S(1)} %get-tuple-element.151), channel_id=1, source_target_pairs={{0,16},{8,24},{16,0},{24,8},{1,17},{9,25},{17,1},{25,9},{2,18},{10... | collective-permute-start | bytes 1572872 | tf_op jit(solution)/shard_map/ppermute | solution.py:64
  448.3 9.3 %collective-permute-start.30 = (bf16[128,2048]{1,0:T(8,128)(2,1)S(1)}, bf16[128,2048]{1,0:T(8,128)(2,1)}, u32[]{:S(2)}, u32[]{:S(2)}) collective-permute-start(bf16[128,2048]{1,0:T(8,128)(2,1)S(1)} %get-tuple-element.152), channel_id=1, source_target_pairs={{0,8},{8,0},{16,24},{24,16},{1,9},{9,1},{17,25},{25,17},{2,10},{10... | collective-permute-start | bytes 1572872 | tf_op jit(solution)/shard_map/ppermute | solution.py:64
  461.0 20.9 %collective-permute-start.34 = (bf16[128,3072]{1,0:T(8,128)(2,1)}, bf16[128,3072]{1,0:T(8,128)(2,1)}, u32[]{:S(2)}, u32[]{:S(2)}) collective-permute-start(bf16[128,3072]{1,0:T(8,128)(2,1)} %slice.173), channel_id=1, source_target_pairs={{0,8},{8,0},{16,24},{24,16},{1,9},{9,1},{17,25},{25,17},{2,10},{10... | collective-permute-start | bytes 2359304 | tf_op jit(solution)/shard_map/ppermute | solution.py:64
  462.6 20.8 %collective-permute-start.35 = (bf16[128,3072]{1,0:T(8,128)(2,1)}, bf16[128,3072]{1,0:T(8,128)(2,1)}, u32[]{:S(2)}, u32[]{:S(2)}) collective-permute-start(bf16[128,3072]{1,0:T(8,128)(2,1)} %slice.174), channel_id=1, source_target_pairs={{0,16},{8,24},{16,0},{24,8},{1,17},{9,25},{17,1},{25,9},{2,18},{10... | collective-permute-start | bytes 2359304 | tf_op jit(solution)/shard_map/ppermute | solution.py:64
  463.8 37.0 %collective-permute-start.32 = (bf16[256,2048]{1,0:T(8,128)(2,1)}, bf16[256,2048]{1,0:T(8,128)(2,1)}, u32[]{:S(2)}, u32[]{:S(2)}) collective-permute-start(bf16[256,2048]{1,0:T(8,128)(2,1)} %get-tuple-element.103), channel_id=1, source_target_pairs={{0,8},{8,0},{16,24},{24,16},{1,9},{9,1},{17,25},{25,17},{2,10},{10... | collective-permute-start | bytes 3145736 | tf_op jit(solution)/shard_map/ppermute | solution.py:64
  464.4 38.6 %collective-permute-start.33 = (bf16[256,2048]{1,0:T(8,128)(2,1)}, bf16[256,2048]{1,0:T(8,128)(2,1)}, u32[]{:S(2)}, u32[]{:S(2)}) collective-permute-start(bf16[256,2048]{1,0:T(8,128)(2,1)} %get-tuple-element.104), channel_id=1, source_target_pairs={{0,16},{8,24},{16,0},{24,8},{1,17},{9,25},{17,1},{25,9},{2,18},{10... | collective-permute-start | bytes 3145736 | tf_op jit(solution)/shard_map/ppermute | solution.py:64
  465.2 37.8 %copy-start.7 = (bf16[256,1536]{1,0:T(8,128)(2,1)S(1)}, bf16[256,1536]{1,0:T(8,128)(2,1)}, u32[]{:S(2)}) copy-start(bf16[256,1536]{1,0:T(8,128)(2,1)} %reduce-scatter.6.cloned.1.call-done.refs_0_) | copy-start | bytes 2359300
  484.6 22.6 %copy-start.16 = (bf16[1,256,2048]{2,1,0:T(8,128)(2,1)S(1)}, bf16[1,256,2048]{2,1,0:T(8,128)(2,1)}, u32[]{:S(2)}) copy-start(bf16[1,256,2048]{2,1,0:T(8,128)(2,1)} %param.14) | copy-start | bytes 3145732
  503.0 15.7 %collective-permute-start.40 = (bf16[256,1536]{1,0:T(8,128)(2,1)S(1)}, bf16[256,1536]{1,0:T(8,128)(2,1)S(1)}, u32[]{:S(2)}, u32[]{:S(2)}) collective-permute-start(bf16[256,1536]{1,0:T(8,128)(2,1)S(1)} %copy-done.7), channel_id=1, source_target_pairs={{0,16},{8,24},{16,0},{24,8},{1,17},{9,25},{17,1},{25,9},{2,18},{10... | collective-permute-start | bytes 2359304 | tf_op jit(solution)/shard_map/ppermute | solution.py:64
  504.2 14.9 %collective-permute-start.39 = (bf16[256,1536]{1,0:T(8,128)(2,1)S(1)}, bf16[256,1536]{1,0:T(8,128)(2,1)S(1)}, u32[]{:S(2)}, u32[]{:S(2)}) collective-permute-start(bf16[256,1536]{1,0:T(8,128)(2,1)S(1)} %copy-done.7), channel_id=1, source_target_pairs={{0,8},{8,0},{16,24},{24,16},{1,9},{9,1},{17,25},{25,17},{2,10},{10... | collective-permute-start | bytes 2359304 | tf_op jit(solution)/shard_map/ppermute | solution.py:64
  507.9 1.3 collective-permute-start.36
  509.2 7.9 %collective-permute-start.37 = (f32[4352]{0:T(1024)S(1)}, f32[4352]{0:T(1024)S(1)}, u32[]{:S(2)}, u32[]{:S(2)}) collective-permute-start(f32[4352]{0:T(1024)S(1)} %fusion.47), channel_id=1, source_target_pairs={{0,2},{1,3},{2,0},{3,1},{4,6},{5,7},{6,4},{7,5},{8,10},{9,11},{10,... | collective-permute-start | bytes 52232 | tf_op jit(solution)/shard_map/ppermute | solution.py:345
  510.6 10.3 %copy-start.32 = (bf16[256,2048]{1,0:T(8,128)(2,1)S(1)}, bf16[256,2048]{1,0:T(8,128)(2,1)}, u32[]{:S(2)}) copy-start(bf16[256,2048]{1,0:T(8,128)(2,1)} %copy-done.31) | copy-start | bytes 3145732
  517.1 7.0 %collective-permute-start.38 = (f32[4352]{0:T(1024)S(1)}, f32[4352]{0:T(1024)S(1)}, u32[]{:S(2)}, u32[]{:S(2)}) collective-permute-start(f32[4352]{0:T(1024)S(1)} %add.145), channel_id=1, source_target_pairs={{0,4},{1,5},{2,6},{3,7},{4,0},{5,1},{6,2},{7,3},{8,12},{9,13},{10,... | collective-permute-start | bytes 52232 | tf_op jit(solution)/shard_map/ppermute | solution.py:345
  519.1 10.0 %collective-permute-start.41 = (bf16[128,1536]{1,0:T(8,128)(2,1)S(1)}, bf16[128,1536]{1,0:T(8,128)(2,1)S(1)}, u32[]{:S(2)}, u32[]{:S(2)}) collective-permute-start(bf16[128,1536]{1,0:T(8,128)(2,1)S(1)} %slice.176), channel_id=1, source_target_pairs={{0,8},{8,0},{16,24},{24,16},{1,9},{9,1},{17,25},{25,17},{2,10},{10... | collective-permute-start | bytes 1179656 | tf_op jit(solution)/shard_map/ppermute | solution.py:64
  520.1 10.3 %collective-permute-start.42 = (bf16[128,1536]{1,0:T(8,128)(2,1)S(1)}, bf16[128,1536]{1,0:T(8,128)(2,1)S(1)}, u32[]{:S(2)}, u32[]{:S(2)}) collective-permute-start(bf16[128,1536]{1,0:T(8,128)(2,1)S(1)} %slice.177), channel_id=1, source_target_pairs={{0,16},{8,24},{16,0},{24,8},{1,17},{9,25},{17,1},{25,9},{2,18},{10... | collective-permute-start | bytes 1179656 | tf_op jit(solution)/shard_map/ppermute | solution.py:64
  530.4 4.5 collective-permute-start.43
  532.0 19.4 %collective-permute-start.46 = (bf16[256,1536]{1,0:T(8,128)(2,1)}, bf16[256,1536]{1,0:T(8,128)(2,1)S(1)}, u32[]{:S(2)}, u32[]{:S(2)}) collective-permute-start(bf16[256,1536]{1,0:T(8,128)(2,1)} %reduce-scatter.8.cloned.1.call-done.refs_0_), channel_id=1, source_target_pairs={{0,8},{8,0},{16,24},{24,16},{1,9},{9,1},{17,25},{25,17},{2,10},{10... | collective-permute-start | bytes 2359304 | tf_op jit(solution)/shard_map/ppermute | solution.py:64
  533.4 18.0 %collective-permute-start.45 = (bf16[256,1536]{1,0:T(8,128)(2,1)}, bf16[256,1536]{1,0:T(8,128)(2,1)S(1)}, u32[]{:S(2)}, u32[]{:S(2)}) collective-permute-start(bf16[256,1536]{1,0:T(8,128)(2,1)} %reduce-scatter.8.cloned.1.call-done.refs_0_), channel_id=1, source_target_pairs={{0,16},{8,24},{16,0},{24,8},{1,17},{9,25},{17,1},{25,9},{2,18},{10... | collective-permute-start | bytes 2359304 | tf_op jit(solution)/shard_map/ppermute | solution.py:64
  535.0 16.4 %collective-permute-start.44 = (f32[4352]{0:T(1024)S(1)}, f32[4352]{0:T(1024)S(1)}, u32[]{:S(2)}, u32[]{:S(2)}) collective-permute-start(f32[4352]{0:T(1024)S(1)} %add.147), channel_id=1, source_target_pairs={{0,16},{8,24},{16,0},{24,8},{1,17},{9,25},{17,1},{25,9},{2,18},{10... | collective-permute-start | bytes 52232 | tf_op jit(solution)/shard_map/ppermute | solution.py:345
  542.2 12.1 %copy-start.10 = (s32[3]{0:T(128)S(1)}, s32[3]{0:T(128)}, u32[]{:S(2)}) copy-start(s32[3]{0:T(128)} %pad_add_fusion.1.order_ref) | copy-start | bytes 40
  551.5 7.8 %collective-permute-start.47 = (bf16[128,1536]{1,0:T(8,128)(2,1)S(1)}, bf16[128,1536]{1,0:T(8,128)(2,1)S(1)}, u32[]{:S(2)}, u32[]{:S(2)}) collective-permute-start(bf16[128,1536]{1,0:T(8,128)(2,1)S(1)} %slice.179), channel_id=1, source_target_pairs={{0,8},{8,0},{16,24},{24,16},{1,9},{9,1},{17,25},{25,17},{2,10},{10... | collective-permute-start | bytes 1179656 | tf_op jit(solution)/shard_map/ppermute | solution.py:64
  551.7 7.8 %collective-permute-start.48 = (bf16[128,1536]{1,0:T(8,128)(2,1)S(1)}, bf16[128,1536]{1,0:T(8,128)(2,1)S(1)}, u32[]{:S(2)}, u32[]{:S(2)}) collective-permute-start(bf16[128,1536]{1,0:T(8,128)(2,1)S(1)} %slice.180), channel_id=1, source_target_pairs={{0,16},{8,24},{16,0},{24,8},{1,17},{9,25},{17,1},{25,9},{2,18},{10... | collective-permute-start | bytes 1179656 | tf_op jit(solution)/shard_map/ppermute | solution.py:64
  (41 other events, 142.1 us)
Sparse Core Ops, SparseCore 0:
  10.6 67.4 all-gather.3
  79.7 115.3 all-gather.5
  196.7 62.9 all-gather.7
  261.9 127.8 reduce-scatter.3
  392.5 68.1 reduce-scatter.5
  462.9 69.0 reduce-scatter.7
